TPU v7x, 32 devices: a whole 2x2x4 slice. The times are simulated.
32 devices in a mesh: gx: 2 (over y), gy: 16 (over z, x, core).
Axes of the slice: x: 2, y: 2, z: 4, core: 2. Of those that a mesh axis runs over, the one named last changes fastest.
Arguments:
- duals: float32 [16, 4, 64, 128], P(None, 'gx', 'gy'), may hold values from -6 to 6
- residual: float32 [16, 4, 64, 128], P(None, 'gx', 'gy')
- direction: float32 [16, 4, 64, 128], P(None, 'gx', 'gy'), may hold values from -6 to 6
- prev_rho: float32 [16], replicated, may hold values from 16384 to 65536
- dual_schur: float32 [4, 64, 256, 256], P('gx', 'gy'), as said below
- coupling: float32 [4, 64, 8, 256], P('gx', 'gy'), may hold values from -0.75 to 0.75
- coarse_inverse: float32 [2, 384, 384], P('gx'), as said below
- edge_map: int32 [4, 64, 256], P('gx', 'gy'), may hold values from 0 to 255, each once within a row
- corner_slot: int32 [4, 64, 8], P('gx', 'gy'), may hold values from 0 to 384, as said below
- active: int32 [4, 64, 128], P('gx', 'gy'), may hold values 0 or 1
- scaling: float32 [4, 64, 128], P('gx', 'gy'), may hold values from 0.25 to 1
Outputs:
- new_duals: float32 [16, 4, 64, 128], P(None, 'gx', 'gy')
- new_residual: float32 [16, 4, 64, 128], P(None, 'gx', 'gy')
- new_direction: float32 [16, 4, 64, 128], P(None, 'gx', 'gy')
Inputs may be any that keep to these rules, and one draw needn't show every extreme that they name: Each subdomain's block of dual_schur and each region's block of coarse_inverse is symmetric positive definite. `coarse_inverse`: each region's block is symmetric positive definite. `corner_slot`: slots number the corner dofs of a region; a corner shared by subdomains of one region has one slot; 384 marks corners on the clamped bottom edge, which have no dof.
All inputs are finite; a program needn't handle non-finite values. No bound on the sum of `active` on one device may be relied on, other than what follows from the above.
Results may differ from a plain program's by a relative error of at most 0.00014.
Values sent between devices are 32-bit elements; how exact they have to be, the bound alone decides.
No kernel may reach another device: no remote copies, remote signals or barrier semaphores. Data moves between devices by JAX's collectives and lax.ppermute only.
A program may use at most 64 MiB of HBM per device.

v0:
```python
import jax
import jax.numpy as jnp
from jax import lax
from jax.sharding import PartitionSpec as P

ITERS = 6


def passed_along(value, axis, by):
    peers = lax.axis_size(axis)
    pairs = [(i, i + by) for i in range(peers) if 0 <= i + by < peers]
    return lax.ppermute(value, axis, pairs)


def across_x(slab, offset):
    return passed_along(slab, "gx", offset)


def across_y(slab, offset):
    return passed_along(slab, "gy", offset)


def case_sum(values):
    return lax.psum(values, ("gx", "gy"))


def shards(
    duals,
    residual,
    direction,
    prev_rho,
    dual_schur,
    coupling,
    coarse_inverse,
    edge_map,
    corner_slot,
    active,
    scaling,
):
    high = lax.Precision.HIGHEST
    cases, span_x, span_y, owned = duals.shape
    half = owned // 2
    width_c = coarse_inverse.shape[-1]
    columns = lax.axis_index("gx") * span_x + jnp.arange(span_x)
    rowset = lax.axis_index("gy") * span_y + jnp.arange(span_y)
    east_ok = jnp.broadcast_to(
        (columns < span_x * lax.axis_size("gx") - 1)[:, None, None], (span_x, span_y, half)
    )
    north_ok = jnp.broadcast_to(
        (rowset < span_y * lax.axis_size("gy") - 1)[None, :, None], (span_x, span_y, half)
    )
    keep = active.astype(jnp.float32) * jnp.concatenate([east_ok, north_ok], -1).astype(jnp.float32)
    inverse = jnp.argsort(edge_map, axis=-1)
    onehot = (corner_slot[..., None] == jnp.arange(width_c, dtype=jnp.int32)).astype(jnp.float32)
    region_inv = coarse_inverse[0]
    lam = duals
    res = residual
    pprev = keep * direction
    rho_old = prev_rho
    for step in range(ITERS):
        zvec = keep * scaling * res
        rho = case_sum(jnp.sum(res * zvec, axis=(1, 2, 3)))
        beta = rho / rho_old
        pvec = zvec + beta[:, None, None, None] * pprev
        part_e = pvec[..., :half]
        part_n = pvec[..., half:]
        from_west = across_x(part_e[:, -1].reshape(cases, span_y * half), 1).reshape(
            cases, 1, span_y, half
        )
        west = -jnp.concatenate([from_west, part_e[:, :-1]], 1)
        from_south = across_y(part_n[:, :, -1].reshape(cases, span_x * half), 1).reshape(
            cases, span_x, 1, half
        )
        south = -jnp.concatenate([from_south, part_n[:, :, :-1]], 2)
        edge_vec = jnp.concatenate([west, part_e, south, part_n], -1)
        local = jnp.take_along_axis(edge_vec, edge_map[None], -1)
        work = jnp.einsum("xyij,kxyj->kxyi", dual_schur, local, precision=high)
        corner_val = jnp.einsum("xycj,kxyj->kxyc", coupling, local, precision=high)
        partial_total = jnp.einsum("kxyc,xycn->kn", corner_val, onehot, precision=high)
        total = lax.psum(partial_total, "gy")
        solved = jnp.einsum("nm,km->kn", region_inv, total, precision=high)
        back = jnp.einsum("xycn,kn->kxyc", onehot, solved, precision=high)
        work = work + jnp.einsum("xycj,kxyc->kxyj", coupling, back, precision=high)
        work_edge = jnp.take_along_axis(work, inverse[None], -1)
        west_w = work_edge[..., :half]
        east_w = work_edge[..., half : 2 * half]
        south_w = work_edge[..., 2 * half : 3 * half]
        north_w = work_edge[..., 3 * half :]
        from_east = across_x(west_w[:, 0].reshape(cases, span_y * half), -1).reshape(
            cases, 1, span_y, half
        )
        east_nb = jnp.concatenate([west_w[:, 1:], from_east], 1)
        from_north = across_y(south_w[:, :, 0].reshape(cases, span_x * half), -1).reshape(
            cases, span_x, 1, half
        )
        north_nb = jnp.concatenate([south_w[:, :, 1:], from_north], 2)
        qvec = jnp.concatenate([east_w - east_nb, north_w - north_nb], -1) * keep
        alpha = rho / case_sum(jnp.sum(pvec * qvec, axis=(1, 2, 3)))
        lam = lam + alpha[:, None, None, None] * pvec
        res = res - alpha[:, None, None, None] * qvec
        rho_old = rho
        pprev = pvec
    return (lam, res, pprev)


def solution(mesh):
    placed = (
        P(None, "gx", "gy", None),
        P(None, "gx", "gy", None),
        P(None, "gx", "gy", None),
        P(),
        P("gx", "gy", None, None),
        P("gx", "gy", None, None),
        P("gx", None, None),
        P("gx", "gy", None),
        P("gx", "gy", None),
        P("gx", "gy", None),
        P("gx", "gy", None),
    )
    return jax.shard_map(
        shards,
        mesh=mesh,
        in_specs=placed,
        out_specs=(P(None, "gx", "gy", None), P(None, "gx", "gy", None), P(None, "gx", "gy", None)),
        check_vma=False,
    )
```

profile of v0, /device:TPU:0, one launch (start us, length us, event | category | flops | bytes accessed | tf_op | source)
XLA Modules:
  0.0 1377.1 jit_solution(17021217025992527875)
XLA Ops:
  9.3 42.0 %psum.126 = f32[16]{0:T(128)S(1)} all-reduce(f32[16]{0:T(128)S(1)} %fusion.42), channel_id=1, replica_groups=mesh['gx'=2,'gy'=16] {'gx','gy'}, use_global_device_ids=true, to_apply=%region_1.2 | all-reduce | flops 16 | bytes 128 | tf_op jit(solution)/shard_map/psum | solution.py:24
  67.3 31.6 %gather_fusion = f32[2048,16]{1,0:T(8,128)} fusion(f32[16,2,4,256]{0,3,2,1:T(8,128)} %copy.75, s32[2048]{0:T(1024)S(1)} %bitcast.287), kind=kCustom, calls=%fused_computation.clone | custom fusion | bytes 286720 | tf_op jit(solution)/shard_map/jit(take_along_axis)/gather | solution.py:76
  100.9 58.7 %psum.127 = f32[16,384]{1,0:T(8,128)S(1)} all-reduce(f32[16,384]{1,0:T(8,128)S(1)} %convolution_bitcast_fusion.11), channel_id=1, replica_groups=mesh['gx'=2,'gy'=16] {'gy'}, use_global_device_ids=true, to_apply=%region_2.0 | all-reduce | flops 6144 | bytes 49152 | tf_op jit(solution)/shard_map/psum | solution.py:80
  203.3 36.9 %psum.128 = f32[16]{0:T(128)S(1)} all-reduce(f32[16]{0:T(128)S(1)} %multiply_reduce_fusion.5), channel_id=1, replica_groups=mesh['gx'=2,'gy'=16] {'gx','gy'}, use_global_device_ids=true, to_apply=%region_5.7 | all-reduce | flops 16 | bytes 128 | tf_op jit(solution)/shard_map/psum | solution.py:24
  240.5 42.4 %psum.129 = f32[16]{0:T(128)S(1)} all-reduce(f32[16]{0:T(128)S(1)} %get-tuple-element.23), channel_id=1, replica_groups=mesh['gx'=2,'gy'=16] {'gx','gy'}, use_global_device_ids=true, to_apply=%region_7.9 | all-reduce | flops 16 | bytes 128 | tf_op jit(solution)/shard_map/psum | solution.py:24
  291.9 31.6 %gather_fusion.2 = f32[2048,16]{1,0:T(8,128)} fusion(f32[16,2,4,256]{0,3,2,1:T(8,128)} %copy.89, s32[2048]{0:T(1024)S(1)} %bitcast.288), kind=kCustom, calls=%fused_computation.2.clone | custom fusion | bytes 286720 | tf_op jit(solution)/shard_map/jit(take_along_axis)/gather | solution.py:76
  325.5 58.1 %psum.130 = f32[16,384]{1,0:T(8,128)S(1)} all-reduce(f32[16,384]{1,0:T(8,128)S(1)} %convolution_bitcast_fusion.10), channel_id=1, replica_groups=mesh['gx'=2,'gy'=16] {'gy'}, use_global_device_ids=true, to_apply=%region_8.10 | all-reduce | flops 6144 | bytes 49152 | tf_op jit(solution)/shard_map/psum | solution.py:80
  427.2 36.9 %psum.131 = f32[16]{0:T(128)S(1)} all-reduce(f32[16]{0:T(128)S(1)} %multiply_reduce_fusion.4), channel_id=1, replica_groups=mesh['gx'=2,'gy'=16] {'gx','gy'}, use_global_device_ids=true, to_apply=%region_10.12 | all-reduce | flops 16 | bytes 128 | tf_op jit(solution)/shard_map/psum | solution.py:24
  464.4 42.4 %psum.132 = f32[16]{0:T(128)S(1)} all-reduce(f32[16]{0:T(128)S(1)} %get-tuple-element.21), channel_id=1, replica_groups=mesh['gx'=2,'gy'=16] {'gx','gy'}, use_global_device_ids=true, to_apply=%region_12.14 | all-reduce | flops 16 | bytes 128 | tf_op jit(solution)/shard_map/psum | solution.py:24
  515.8 31.6 %gather_fusion.4 = f32[2048,16]{1,0:T(8,128)} fusion(f32[16,2,4,256]{0,3,2,1:T(8,128)} %copy.101, s32[2048]{0:T(1024)S(1)} %bitcast.289), kind=kCustom, calls=%fused_computation.4.clone | custom fusion | bytes 286720 | tf_op jit(solution)/shard_map/jit(take_along_axis)/gather | solution.py:76
  549.4 57.8 %psum.133 = f32[16,384]{1,0:T(8,128)S(1)} all-reduce(f32[16,384]{1,0:T(8,128)S(1)} %convolution_bitcast_fusion.9), channel_id=1, replica_groups=mesh['gx'=2,'gy'=16] {'gy'}, use_global_device_ids=true, to_apply=%region_13.15 | all-reduce | flops 6144 | bytes 49152 | tf_op jit(solution)/shard_map/psum | solution.py:80
  650.9 36.9 %psum.134 = f32[16]{0:T(128)S(1)} all-reduce(f32[16]{0:T(128)S(1)} %multiply_reduce_fusion.3), channel_id=1, replica_groups=mesh['gx'=2,'gy'=16] {'gx','gy'}, use_global_device_ids=true, to_apply=%region_15.17 | all-reduce | flops 16 | bytes 128 | tf_op jit(solution)/shard_map/psum | solution.py:24
  688.0 42.6 %psum.135 = f32[16]{0:T(128)S(1)} all-reduce(f32[16]{0:T(128)S(1)} %get-tuple-element.19), channel_id=1, replica_groups=mesh['gx'=2,'gy'=16] {'gx','gy'}, use_global_device_ids=true, to_apply=%region_17.19 | all-reduce | flops 16 | bytes 128 | tf_op jit(solution)/shard_map/psum | solution.py:24
  741.1 31.6 %gather_fusion.6 = f32[2048,16]{1,0:T(8,128)} fusion(f32[16,2,4,256]{0,3,2,1:T(8,128)} %copy.113, s32[2048]{0:T(1024)S(1)} %bitcast.290), kind=kCustom, calls=%fused_computation.6.clone | custom fusion | bytes 286720 | tf_op jit(solution)/shard_map/jit(take_along_axis)/gather | solution.py:76
  774.7 57.8 %psum.136 = f32[16,384]{1,0:T(8,128)S(1)} all-reduce(f32[16,384]{1,0:T(8,128)S(1)} %convolution_bitcast_fusion.8), channel_id=1, replica_groups=mesh['gx'=2,'gy'=16] {'gy'}, use_global_device_ids=true, to_apply=%region_18.20 | all-reduce | flops 6144 | bytes 49152 | tf_op jit(solution)/shard_map/psum | solution.py:80
  876.2 36.9 %psum.137 = f32[16]{0:T(128)S(1)} all-reduce(f32[16]{0:T(128)S(1)} %multiply_reduce_fusion.2), channel_id=1, replica_groups=mesh['gx'=2,'gy'=16] {'gx','gy'}, use_global_device_ids=true, to_apply=%region_20.22 | all-reduce | flops 16 | bytes 128 | tf_op jit(solution)/shard_map/psum | solution.py:24
  913.3 42.4 %psum.138 = f32[16]{0:T(128)S(1)} all-reduce(f32[16]{0:T(128)S(1)} %get-tuple-element.17), channel_id=1, replica_groups=mesh['gx'=2,'gy'=16] {'gx','gy'}, use_global_device_ids=true, to_apply=%region_22.24 | all-reduce | flops 16 | bytes 128 | tf_op jit(solution)/shard_map/psum | solution.py:24
  966.2 31.6 %gather_fusion.8 = f32[2048,16]{1,0:T(8,128)} fusion(f32[16,2,4,256]{0,3,2,1:T(8,128)} %copy.125, s32[2048]{0:T(1024)S(1)} %bitcast.291), kind=kCustom, calls=%fused_computation.8.clone | custom fusion | bytes 286720 | tf_op jit(solution)/shard_map/jit(take_along_axis)/gather | solution.py:76
  999.8 58.1 %psum.139 = f32[16,384]{1,0:T(8,128)S(1)} all-reduce(f32[16,384]{1,0:T(8,128)S(1)} %convolution_bitcast_fusion.7), channel_id=1, replica_groups=mesh['gx'=2,'gy'=16] {'gy'}, use_global_device_ids=true, to_apply=%region_23.25 | all-reduce | flops 6144 | bytes 49152 | tf_op jit(solution)/shard_map/psum | solution.py:80
  1104.8 36.9 %psum.140 = f32[16]{0:T(128)S(1)} all-reduce(f32[16]{0:T(128)S(1)} %multiply_reduce_fusion.1), channel_id=1, replica_groups=mesh['gx'=2,'gy'=16] {'gx','gy'}, use_global_device_ids=true, to_apply=%region_25.27 | all-reduce | flops 16 | bytes 128 | tf_op jit(solution)/shard_map/psum | solution.py:24
  1142.8 42.4 %psum.141 = f32[16]{0:T(128)S(1)} all-reduce(f32[16]{0:T(128)S(1)} %get-tuple-element.15), channel_id=1, replica_groups=mesh['gx'=2,'gy'=16] {'gx','gy'}, use_global_device_ids=true, to_apply=%region_27.29 | all-reduce | flops 16 | bytes 128 | tf_op jit(solution)/shard_map/psum | solution.py:24
  1195.7 31.6 %gather_fusion.10 = f32[2048,16]{1,0:T(8,128)} fusion(f32[16,2,4,256]{0,3,2,1:T(8,128)} %copy.137, s32[2048]{0:T(1024)S(1)} %bitcast.292), kind=kCustom, calls=%fused_computation.10.clone | custom fusion | bytes 286720 | tf_op jit(solution)/shard_map/jit(take_along_axis)/gather | solution.py:76
  1229.3 57.8 %psum.142 = f32[16,384]{1,0:T(8,128)S(1)} all-reduce(f32[16,384]{1,0:T(8,128)S(1)} %convolution_bitcast_fusion.6), channel_id=1, replica_groups=mesh['gx'=2,'gy'=16] {'gy'}, use_global_device_ids=true, to_apply=%region_28.30 | all-reduce | flops 6144 | bytes 49152 | tf_op jit(solution)/shard_map/psum | solution.py:80
  1331.4 36.9 %psum.143 = f32[16]{0:T(128)S(1)} all-reduce(f32[16]{0:T(128)S(1)} %multiply_reduce_fusion), channel_id=1, replica_groups=mesh['gx'=2,'gy'=16] {'gx','gy'}, use_global_device_ids=true, to_apply=%region_30.32 | all-reduce | flops 16 | bytes 128 | tf_op jit(solution)/shard_map/psum | solution.py:24
  (366 shorter events, 347.6 us)
Async XLA Ops:
  53.0 12.7 collective-permute-start
  57.4 8.2 collective-permute-start.1
  197.3 5.6 collective-permute-start.2
  198.7 3.1 collective-permute-start.3
  283.2 5.7 collective-permute-start.5
  284.7 5.6 collective-permute-start.4
  421.2 5.6 collective-permute-start.6
  422.6 3.1 collective-permute-start.7
  507.1 5.7 collective-permute-start.9
  508.6 5.6 collective-permute-start.8
  644.8 5.6 collective-permute-start.10
  646.2 3.1 collective-permute-start.11
  731.6 5.7 collective-permute-start.13
  733.1 5.6 collective-permute-start.12
  870.1 5.6 collective-permute-start.14
  871.5 3.1 collective-permute-start.15
  956.7 5.7 collective-permute-start.17
  958.2 5.6 collective-permute-start.16
  1098.7 5.6 collective-permute-start.18
  1100.1 3.1 collective-permute-start.19
  1186.1 5.7 collective-permute-start.21
  1187.6 5.6 collective-permute-start.20
  1324.7 5.6 collective-permute-start.22
  1326.1 3.1 collective-permute-start.23
  (19 other events, 1316.7 us)
Sparse Core Ops, SparseCore 0:
  59.4 4.4 sort.21.cloned.1.call-done
  (1 shorter events, 0.0 us)
where the time goes:
time: 1390 us; the launch traced here: 1380 us
  blocking collectives  824 us (59%)
  local copies, waits for them, and re-layouts  429 us (31%)
  starting transfers between devices  48 us (3%)
  waiting for transfers between devices  23.6 us (2%)
  matrix products  21.9 us (2%)
  between operations  15.7 us (1%)
  other arithmetic  15 us (1%)
    psum x12, blocking collectives, case_sum(): return lax.psum(values, ('gx', 'gy'))  476 us
    psum x6, blocking collectives, shards(): total = lax.psum(partial_total, 'gy')  348 us
    gather x12, local copies, waits for them, and re-layouts, shards(): work_edge = jnp.take_along_axis(work, inverse[None], -1)  199 us
    gather x12, local copies, waits for them, and re-layouts, shards(): local = jnp.take_along_axis(edge_vec, edge_map[None], -1)  199 us
    ppermute x24, starting transfers between devices, passed_along(): return lax.ppermute(value, axis, pairs)  48 us
  transfers between devices with their start and end apart: 24, of which 17 were waited for; matrix products, arithmetic and copies ran while one was open for 0% of the time, Pallas kernels for 0%

commit v1 on v0

v1 whole, which is shorter than its diff:
```python
import jax
import jax.numpy as jnp
from jax import lax
from jax.sharding import PartitionSpec as P

ITERS = 6
HIGH = lax.Precision.HIGH
EXACT = lax.Precision.HIGHEST
BOTH = ("gx", "gy")


def pairs_from(first, peers):
    return [(i, i + 1) for i in range(first, peers - 1, 2)]


def both_ways(pairs):
    return pairs + [(b, a) for a, b in pairs]


def up_gy(value, peers):
    even = lax.ppermute(value, "gy", pairs_from(0, peers))
    odd = lax.ppermute(value, "gy", pairs_from(1, peers))
    return jnp.where(lax.axis_index("gy") % 2 == 1, even, odd)


def swap_gy(low, high, peers):
    is_even = lax.axis_index("gy") % 2 == 0
    first = lax.ppermute(jnp.where(is_even, high, low), "gy", both_ways(pairs_from(0, peers)))
    second = lax.ppermute(jnp.where(is_even, low, high), "gy", both_ways(pairs_from(1, peers)))
    return jnp.where(is_even, second, first), jnp.where(is_even, first, second)


def swap_gx(low, high, peers):
    if peers == 2:
        is_first = lax.axis_index("gx") == 0
        got = lax.ppermute(jnp.where(is_first, high, low), "gx", [(0, 1), (1, 0)])
        zero = jnp.zeros_like(got)
        return jnp.where(is_first, zero, got), jnp.where(is_first, got, zero)
    below = lax.ppermute(high, "gx", [(i, i + 1) for i in range(peers - 1)])
    above = lax.ppermute(low, "gx", [(i + 1, i) for i in range(peers - 1)])
    return below, above


def everywhere(block, axes):
    sent = jnp.broadcast_to(block[None], (lax.axis_size(axes),) + block.shape)
    return lax.all_to_all(sent, axes, 0, 0, tiled=False)


def shards(
    duals, residual, direction, prev_rho, dual_schur, coupling, coarse_inverse, edge_map, corner_slot, active, scaling
):
    cases, span_x, span_y, owned = duals.shape
    half = owned // 2
    full = 2 * owned
    corners = coupling.shape[2]
    width_c = coarse_inverse.shape[-1]
    peers_x, peers_y = lax.axis_size("gx"), lax.axis_size("gy")
    whole = peers_x == 2
    axes = BOTH if whole else "gy"
    regions = peers_x if whole else 1
    peers = regions * peers_y
    here_x, here_y = lax.axis_index("gx"), lax.axis_index("gy")
    used = 2 * (span_x + 1) * (span_y + 1)
    slots = used + 2

    columns = here_x * span_x + jnp.arange(span_x)
    rowset = here_y * span_y + jnp.arange(span_y)
    east_ok = jnp.broadcast_to((columns < span_x * peers_x - 1)[:, None, None], (span_x, span_y, half))
    north_ok = jnp.broadcast_to((rowset < span_y * peers_y - 1)[None, :, None], (span_x, span_y, half))
    keep_own = active.astype(jnp.float32) * jnp.concatenate([east_ok, north_ok], -1).astype(jnp.float32)
    scale_own = keep_own * scaling

    by_place = lambda v: jnp.transpose(v, (1, 2, 0, 3))
    lam = by_place(duals)
    p = keep_own[:, :, None] * by_place(direction)
    stacked = jnp.concatenate([by_place(residual), p, scale_own[:, :, None], keep_own[:, :, None]], 2)
    part_e, part_n = stacked[..., :half], stacked[..., half:]
    from_west = lax.ppermute(part_e[-1], "gx", [(i, i + 1) for i in range(peers_x - 1)])
    from_south = up_gy(part_n[:, -1], peers_y)
    west = jnp.concatenate([from_west[None], part_e[:-1]], 0)
    south = jnp.concatenate([from_south[:, None], part_n[:, :-1]], 1)
    stacked = jnp.concatenate([west, part_e, south, part_n], -1)
    r = stacked[:, :, :cases]
    p_all = stacked[:, :, cases : 2 * cases]
    scale = stacked[:, :, 2 * cases : 2 * cases + 1]
    keep = stacked[:, :, 2 * cases + 1 :]

    sign = jnp.concatenate([-jnp.ones(half), jnp.ones(half), -jnp.ones(half), jnp.ones(half)]).astype(jnp.float32)
    place = (edge_map[..., None] == jnp.arange(full, dtype=jnp.int32)).astype(jnp.float32) * sign
    schur = jnp.einsum("xyij,xyjf->xyif", dual_schur, place, precision=EXACT)
    schur = jnp.einsum("xyie,xyif->xyef", place, schur, precision=EXACT)
    couple = jnp.einsum("xycj,xyjf->xycf", coupling, place, precision=EXACT)

    flat = corner_slot.reshape(-1)
    count = flat.shape[0]
    order = jnp.arange(count)
    same = flat[:, None] == flat[None, :]
    first = ~jnp.any(same & (order[None, :] < order[:, None]), 1) & (flat != width_c)
    rank = jnp.sum((flat[None, :] < flat[:, None]) & first[None, :], 1)
    local_slot = jnp.arange(slots)
    compact = ((rank[:, None] == local_slot) & (flat != width_c)[:, None]).astype(jnp.float32)
    named = jnp.where(
        jnp.any(compact > 0, 0), jnp.max(compact * flat[:, None].astype(jnp.float32), 0), float(width_c)
    )
    compact = compact.reshape(span_x, span_y, corners, slots)
    gather_c = jnp.einsum("xycs,xycf->xysf", compact, couple, precision=EXACT)

    blocks = lambda a: (a[..., :half], a[..., half : 2 * half], a[..., 2 * half : 3 * half], a[..., 3 * half :])

    def jump(y, from_w, from_e, from_s, from_n):
        w, e, s, n = blocks(y)
        w_nb = jnp.concatenate([from_w[None], e[:-1]], 0)
        e_nb = jnp.concatenate([w[1:], from_e[None]], 0)
        s_nb = jnp.concatenate([from_s[:, None], n[:, :-1]], 1)
        n_nb = jnp.concatenate([s[:, 1:], from_n[:, None]], 1)
        return jnp.concatenate([w + w_nb, e + e_nb, s + s_nb, n + n_nb], -1)

    def rims(y):
        w, e, s, n = blocks(y)
        return w[0], e[-1], s[:, 0], n[:, -1]

    def exchange(y):
        w, e, s, n = rims(y)
        from_w, from_e = swap_gx(w, e, peers_x)
        from_s, from_n = swap_gy(s, n, peers_y)
        return from_w, from_e, from_s, from_n

    def put(rim, name):
        zero = jnp.zeros((span_x, span_y, rim.shape[-2], half), jnp.float32)
        parts = [zero, zero, zero, zero]
        if name == 0:
            parts[0] = zero.at[0].set(rim)
        elif name == 1:
            parts[1] = zero.at[-1].set(rim)
        elif name == 2:
            parts[2] = zero.at[:, 0].set(rim)
        else:
            parts[3] = zero.at[:, -1].set(rim)
        return jnp.concatenate(parts, -1)

    nb = exchange(gather_c)
    none = [jnp.zeros_like(v) for v in nb]
    spread = jnp.concatenate([jump(gather_c, *none)] + [put(v, i) for i, v in enumerate(nb)], 2)
    spread = spread * keep

    region_inv = coarse_inverse[0]

    def local_part(v):
        y = jnp.einsum("xykj,xyji->xyki", v, schur, precision=HIGH)
        c = jnp.einsum("xykj,xysj->ks", v, gather_c[:, :, :used], precision=HIGH)
        return y, c

    def over_cases(a, b):
        return jnp.sum(a * b, axis=(0, 1, 3))

    def pack(c, one, two):
        return jnp.concatenate([c, one[:, None], two[:, None]], 1).reshape(-1, 128)

    def unpack(got):
        got = got.reshape(peers, cases, slots)
        sums = jnp.sum(got[:, :, used:], 0)
        return jnp.transpose(got, (1, 0, 2)).reshape(cases, regions, peers_y, slots), sums[:, 0], sums[:, 1]

    def own_part(a):
        return jnp.concatenate([a[..., half : 2 * half], a[..., 3 * half :]], -1)

    u = scale * r
    both = jnp.concatenate([u, p_all], 2)
    y, c = local_part(both)
    yu, yp = y[:, :, :cases], y[:, :, cases:]
    rho_part = over_cases(own_part(r), own_part(u))
    names = jnp.concatenate([named, jnp.zeros(4 * 128 - slots, jnp.float32)]).reshape(4, 128)
    block = jnp.concatenate(
        [pack(c[:cases], rho_part, over_cases(u, yu)), pack(c[cases:], over_cases(p_all, yu), over_cases(p_all, yp)), names]
    )
    got = everywhere(block, axes)
    from_all = exchange(y)

    rows = cases * slots // 128
    slot_of = got[:, 2 * rows :].reshape(peers, -1)[:, :slots].reshape(regions, peers_y * slots)

    if whole:
        other = lax.ppermute(region_inv, "gx", [(0, 1), (1, 0)])
        inverses = jnp.where(here_x == 0, jnp.stack([region_inv, other]), jnp.stack([other, region_inv]))
    else:
        inverses = region_inv[None]
    pick = (slot_of[..., None] == jnp.arange(width_c, dtype=jnp.float32)).astype(jnp.float32)
    dense = jnp.einsum("ran,rnm->ram", pick, inverses, precision=EXACT)
    dense = jnp.einsum("ram,rbm->rab", dense, pick, precision=EXACT)

    def solve(c_all):
        flat_c = c_all.reshape(cases, regions, peers_y * slots)
        sol = jnp.einsum("kra,rab->krb", flat_c, dense, precision=HIGH)
        return flat_c, sol

    def total(a, b):
        return jnp.sum(a * b, (1, 2))

    def over_gx(*sums):
        return sums if whole else tuple(lax.psum(jnp.stack(sums), "gx"))

    def at(sol, ix, dy):
        sol = sol.reshape(cases, regions, peers_y, slots)
        iy = jnp.clip(here_y + dy, 0, peers_y - 1)
        return lax.dynamic_slice(sol, (0, ix, iy, 0), (cases, 1, 1, slots))[:, 0, 0]

    def beside(sol):
        if whole:
            return at(sol, 0, 0), at(sol, 1, 0)
        mine = at(sol, 0, 0)
        return swap_gx(mine, mine, peers_x)

    def coarse_part(sol):
        mine = here_x if whole else 0
        near = jnp.concatenate([at(sol, mine, 0), *beside(sol), at(sol, mine, -1), at(sol, mine, 1)], 1)
        return jnp.einsum("kn,xynj->xykj", near, spread, precision=HIGH)

    cu, rho, delta = unpack(got[:, :rows])
    cp, cross, eta = unpack(got[:, rows : 2 * rows])
    cu, su = solve(cu)
    cp, sp = solve(cp)
    delta, cross, eta = delta + total(cu, su), cross + total(cu, sp), eta + total(cp, sp)
    rho, delta, cross, eta = over_gx(rho, delta, cross, eta)
    f_both = keep * jump(y, *from_all)
    w = f_both[:, :, :cases] + coarse_part(su)
    s = f_both[:, :, cases:] + coarse_part(sp)

    wide = lambda a: a[None, None, :, None]
    beta = rho / prev_rho
    skew = cross + beta * eta
    pi = delta + 2.0 * beta * skew - beta * beta * eta
    for step in range(ITERS):
        if step > 0:
            u = scale * r
            y, c = local_part(u)
            block = pack(c, over_cases(own_part(r), own_part(u)), over_cases(u, y))
            got = everywhere(block, axes)
            from_all = exchange(y)
            rho_old = rho
            c_all, rho, delta = unpack(got)
            c_all, sol = solve(c_all)
            rho, delta = over_gx(rho, delta + total(c_all, sol))
            w = keep * jump(y, *from_all) + coarse_part(sol)
            skew = beta * skew
            beta = rho / rho_old
            pi = delta + 2.0 * beta * skew - beta * beta * pi
        alpha = rho / pi
        p = own_part(u) + wide(beta) * p
        s = w + wide(beta) * s
        lam = lam + wide(alpha) * p
        r = r - wide(alpha) * s
    back = lambda v: jnp.transpose(v, (2, 0, 1, 3))
    return back(lam), back(own_part(r)), back(p)


def solution(mesh):
    placed = (
        P(None, "gx", "gy", None),
        P(None, "gx", "gy", None),
        P(None, "gx", "gy", None),
        P(),
        P("gx", "gy", None, None),
        P("gx", "gy", None, None),
        P("gx", None, None),
        P("gx", "gy", None),
        P("gx", "gy", None),
        P("gx", "gy", None),
        P("gx", "gy", None),
    )
    return jax.shard_map(
        shards,
        mesh=mesh,
        in_specs=placed,
        out_specs=(P(None, "gx", "gy", None), P(None, "gx", "gy", None), P(None, "gx", "gy", None)),
        check_vma=False,
    )
```

time: 1390 us -> 358 us (0.26)
  blocking collectives: 824 us -> 0 us
  local copies, waits for them, and re-layouts: 429 us -> 122 us
  other arithmetic: 15 us -> 69.4 us
  matrix products: 21.9 us -> 64.9 us
  starting transfers between devices: 48 us -> 70.4 us
  between operations: 15.7 us -> 1.79 us
    psum x18 -> x0, blocking collectives: 824 us -> none  [the longest x12 476 us: case_sum(): return lax.psum(values, ('gx', 'gy'))]
    gather x24 -> x0, local copies, waits for them, and re-layouts: 398 us -> none  [the longest x12 199 us: shards(): work_edge = jnp.take_along_axis(work, inverse[None], -1)]
    dot_general x36 -> x32, matrix products: 21.9 us -> 64.9 us  [the longest x7 21.2 us: solve(): sol = jnp.einsum('kra,rab->krb', flat_c, dense, precision=HIGH)]
    broadcast_in_dim x2 -> x27, local copies, waits for them, and re-layouts: 0.15 us -> 29.9 us  [the longest x14 15.6 us: pack(): return jnp.concatenate([c, one[:, None], two[:, None]], 1).reshape(-1, 128)]
    all_to_all x0 -> x6, starting transfers between devices: none -> 27.7 us  [everywhere(): return lax.all_to_all(sent, axes, 0, 0, tiled=False)]
    reshape x48 -> x17, local copies, waits for them, and re-layouts: 2.05 us -> 21.7 us  [the longest x7 10.8 us: at(): sol = sol.reshape(cases, regions, peers_y, slots)]
    slice x66 -> x32, local copies, waits for them, and re-layouts: 3.77 us -> 21.6 us  [the longest x12 7.91 us: own_part(): return jnp.concatenate([a[..., half:2 * half], a[..., 3 * half:]], -1)]
    all_to_all x0 -> x6, waiting for transfers between devices: none -> 16 us  [everywhere(): return lax.all_to_all(sent, axes, 0, 0, tiled=False)]
  transfers between devices with their start and end apart: 24 -> 31, of which waited for: 17 -> 11; matrix products, arithmetic and copies ran while one was open for 0% -> 25% of each run, Pallas kernels for 0% -> 0%
where the time goes in v1:
time: 358 us; the launch traced here: 353 us
  local copies, waits for them, and re-layouts  122 us (34%)
  starting transfers between devices  70.4 us (20%)
  other arithmetic  69.4 us (19%)
  matrix products  64.9 us (18%)
  waiting for transfers between devices  24.2 us (7%)
    all_to_all x6, starting transfers between devices, everywhere(): return lax.all_to_all(sent, axes, 0, 0, tiled=False)  27.7 us
    dot_general x7, matrix products, solve(): sol = jnp.einsum('kra,rab->krb', flat_c, dense, precision=HIGH)  21.2 us
    all_to_all x6, waiting for transfers between devices, everywhere(): return lax.all_to_all(sent, axes, 0, 0, tiled=False)  16 us
    broadcast_in_dim x14, local copies, waits for them, and re-layouts, pack(): return jnp.concatenate([c, one[:, None], two[:, None]], 1).reshape(-1, 128)  15.6 us
    dot_general x7, matrix products, coarse_part(): return jnp.einsum('kn,xynj->xykj', near, spread, precision=HIGH)  14.3 us
    broadcast_in_dim x11, local copies, waits for them, and re-layouts, everywhere(): sent = jnp.broadcast_to(block[None], (lax.axis_size(axes),) + block.shape)  14.1 us
    transpose x7, local copies, waits for them, and re-layouts, unpack(): jnp.transpose(got, (1, 0, 2)).reshape(cases, regions, peers_y, slots)  12.2 us
    ppermute x7, starting transfers between devices, swap_gy(): lax.ppermute(jnp.where(is_even, high, low), 'gy', both_ways(pairs_from(0,...  11.8 us
  transfers between devices with their start and end apart: 31, of which 11 were waited for; matrix products, arithmetic and copies ran while one was open for 25% of the time, Pallas kernels for 0%

profile of v1, /device:TPU:0, one launch (start us, length us, event | category | flops | bytes accessed | tf_op | source)
XLA Modules:
  0.0 352.7 jit_solution(13838618729549407235)
XLA Ops:
  4.6 6.8 %collective-permute-start.1 = (f32[2,34,64]{2,1,0:T(8,128)}, f32[2,34,64]{2,1,0:T(8,128)}, u32[]{:S(2)}, u32[]{:S(2)}) collective-permute-start(f32[2,34,64]{2,1,0:T(8,128)} %slice_bitcast_fusion.3), channel_id=1, source_target_pairs={{0,1},{2,3},{4,5},{6,7},{8,9},{10,11},{12,13},{14,15},{16,17},{18,... | collective-permute-start | bytes 52232 | tf_op jit(solution)/shard_map/ppermute | solution.py:21
  12.1 4.0 %collective-permute-start = (f32[4,34,64]{2,1,0:T(8,128)}, f32[4,34,64]{2,1,0:T(8,128)}, u32[]{:S(2)}, u32[]{:S(2)}) collective-permute-start(f32[4,34,64]{2,1,0:T(8,128)} %get-tuple-element.182), channel_id=1, source_target_pairs={{0,16},{1,17},{2,18},{3,19},{4,20},{5,21},{6,22},{7,23},{8,24},{9,... | collective-permute-start | bytes 104456 | tf_op jit(solution)/shard_map/ppermute | solution.py:78
  18.1 3.0 fusion.4
  26.2 2.3 fusion.2
  28.5 3.7 %fusion = f32[2,4,256,256]{3,2,1,0:T(8,128)} fusion(f32[2,4,256,256]{3,2,1,0:T(8,128)S(1)} %fusion.2, f32[256]{0:T(256)S(1)} %copy-done.60, s32[2,4,256]{2,1,0:T(4,128)S(1)} %copy-done.45), kind=kOutput, calls=%fused_computation | convolution fusion | flops 1611661312 | bytes 4203520 | tf_op jit(solution)/shard_map/xyie,xyif->xyef/dot_general | solution.py:91
  51.6 4.3 %collective-permute-start.6 = (f32[2,32,64]{2,1,0:T(8,128)}, f32[2,32,64]{2,1,0:T(8,128)}, u32[]{:S(2)}, u32[]{:S(2)}) collective-permute-start(f32[2,32,64]{2,1,0:T(8,128)} %get-tuple-element.172), channel_id=1, source_target_pairs={{0,1},{2,3},{4,5},{6,7},{8,9},{10,11},{12,13},{14,15},{1,0},{3,2},... | collective-permute-start | bytes 49160 | tf_op jit(solution)/shard_map/ppermute | solution.py:28
  57.3 6.7 %all-to-all-start = ((f32[32,12,128]{2,1,0:T(8,128)}), f32[32,12,128]{2,1,0:T(8,128)}, u32[]{:S(2)}, u32[]{:S(2)}) async-start(f32[32,12,128]{2,1,0:T(8,128)} %broadcast_in_dim.229), calls=%async_computation | async-start | bytes 524288 | tf_op jit(solution)/shard_map/all_to_all | solution.py:46
  67.9 6.2 %all-to-all-done = f32[32,12,128]{2,1,0:T(8,128)} async-done(((f32[32,12,128]{2,1,0:T(8,128)}), f32[32,12,128]{2,1,0:T(8,128)}, u32[]{:S(2)}, u32[]{:S(2)}) %all-to-all-start) | async-done | bytes 196640 | tf_op jit(solution)/shard_map/all_to_all | solution.py:46
  88.7 3.4 fusion.7
  97.0 3.5 %multiply_reduce_fusion.13 = (f32[16]{0:T(128)}, f32[16]{0:T(128)}, f32[16]{0:T(128)}, f32[16,2,512]{2,0,1:T(8,128)}) fusion(f32[16,2,512]{2,1,0:T(2,128)S(1)} %reshape_reshape.21, f32[16,2,512]{2,0,1:T(8,128)S(1)} %convolution_bitcast_fusion.13, f32[16,2,512]{2,1,0:T(2,128)} %reshape_reshape.22, f32[2,512,512]{2,1,0:T(8,128)} %copy-done.1), kind=kOutput, calls=%fused_computation.204 | convolution fusion | flops 50429904 | bytes 2359488 | tf_op jit(solution)/shard_map/kra,rab->krb/dot_general | solution.py:193
  121.0 2.3 collective-permute-start.12
  127.4 3.3 all-to-all-start.1
  145.1 3.5 %multiply_reduce_fusion.11 = (f32[16]{0:T(128)}, f32[16,2,512]{2,0,1:T(8,128)}) fusion(f32[16,2,512]{2,1,0:T(2,128)} %reshape_reshape.23, f32[2,512,512]{2,1,0:T(8,128)} %copy-done.1), kind=kOutput, calls=%fused_computation.197 | convolution fusion | flops 50364400 | bytes 2228288 | tf_op jit(solution)/shard_map/kra,rab->krb/dot_general | solution.py:193
  174.9 4.7 %all-to-all-start.2 = ((f32[32,4,128]{2,1,0:T(4,128)}), f32[32,4,128]{2,1,0:T(4,128)}, u32[]{:S(2)}, u32[]{:S(2)}) async-start(f32[32,4,128]{2,1,0:T(4,128)} %broadcast_in_dim.245), calls=%async_computation.2 | async-start | bytes 131072 | tf_op jit(solution)/shard_map/all_to_all | solution.py:46
  193.7 3.5 multiply_reduce_fusion.10
  203.3 2.3 broadcast_multiply_fusion.3
  223.4 4.4 %all-to-all-start.3 = ((f32[32,4,128]{2,1,0:T(4,128)}), f32[32,4,128]{2,1,0:T(4,128)}, u32[]{:S(2)}, u32[]{:S(2)}) async-start(f32[32,4,128]{2,1,0:T(4,128)} %broadcast_in_dim.253), calls=%async_computation.3 | async-start | bytes 131072 | tf_op jit(solution)/shard_map/all_to_all | solution.py:46
  242.3 3.5 %multiply_reduce_fusion.9 = (f32[16]{0:T(128)}, f32[16,2,512]{2,0,1:T(8,128)}) fusion(f32[16,2,512]{2,1,0:T(2,128)} %reshape_reshape.25, f32[2,512,512]{2,1,0:T(8,128)} %copy-done.1), kind=kOutput, calls=%fused_computation.193 | convolution fusion | flops 50364400 | bytes 2228288 | tf_op jit(solution)/shard_map/kra,rab->krb/dot_general | solution.py:193
  272.0 4.4 %all-to-all-start.4 = ((f32[32,4,128]{2,1,0:T(4,128)}), f32[32,4,128]{2,1,0:T(4,128)}, u32[]{:S(2)}, u32[]{:S(2)}) async-start(f32[32,4,128]{2,1,0:T(4,128)} %broadcast_in_dim.261), calls=%async_computation.4 | async-start | bytes 131072 | tf_op jit(solution)/shard_map/all_to_all | solution.py:46
  290.8 3.5 %multiply_reduce_fusion.8 = (f32[16]{0:T(128)}, f32[16,2,512]{2,0,1:T(8,128)}) fusion(f32[16,2,512]{2,1,0:T(2,128)} %reshape_reshape.26, f32[2,512,512]{2,1,0:T(8,128)} %copy-done.1), kind=kOutput, calls=%fused_computation.191 | convolution fusion | flops 50364400 | bytes 2228288 | tf_op jit(solution)/shard_map/kra,rab->krb/dot_general | solution.py:193
  300.4 2.4 broadcast_multiply_fusion.1
  320.8 4.2 %all-to-all-start.5 = ((f32[32,4,128]{2,1,0:T(4,128)}), f32[32,4,128]{2,1,0:T(4,128)}, u32[]{:S(2)}, u32[]{:S(2)}) async-start(f32[32,4,128]{2,1,0:T(4,128)} %broadcast_in_dim.269), calls=%async_computation.5 | async-start | bytes 131072 | tf_op jit(solution)/shard_map/all_to_all | solution.py:46
  328.1 4.0 %all-to-all-done.5 = f32[32,4,128]{2,1,0:T(4,128)} async-done(((f32[32,4,128]{2,1,0:T(4,128)}), f32[32,4,128]{2,1,0:T(4,128)}, u32[]{:S(2)}, u32[]{:S(2)}) %all-to-all-start.5) | async-done | bytes 65568 | tf_op jit(solution)/shard_map/all_to_all | solution.py:46
  338.7 3.0 multiply_reduce_fusion.7
  (405 shorter events, 257.9 us)
Async XLA Ops:
  3.4 33.6 %collective-permute-start.2 = (f32[2,34,64]{2,1,0:T(8,128)}, f32[2,34,64]{2,1,0:T(8,128)}, u32[]{:S(2)}, u32[]{:S(2)}) collective-permute-start(f32[2,34,64]{2,1,0:T(8,128)} %slice_bitcast_fusion.3), channel_id=1, source_target_pairs={{1,2},{3,4},{5,6},{7,8},{9,10},{11,12},{13,14},{17,18},{19,20},{21... | collective-permute-start | bytes 52232 | tf_op jit(solution)/shard_map/ppermute | solution.py:22
  4.6 32.3 %collective-permute-start.1 = (f32[2,34,64]{2,1,0:T(8,128)}, f32[2,34,64]{2,1,0:T(8,128)}, u32[]{:S(2)}, u32[]{:S(2)}) collective-permute-start(f32[2,34,64]{2,1,0:T(8,128)} %slice_bitcast_fusion.3), channel_id=1, source_target_pairs={{0,1},{2,3},{4,5},{6,7},{8,9},{10,11},{12,13},{14,15},{16,17},{18,... | collective-permute-start | bytes 52232 | tf_op jit(solution)/shard_map/ppermute | solution.py:21
  12.1 26.9 %collective-permute-start = (f32[4,34,64]{2,1,0:T(8,128)}, f32[4,34,64]{2,1,0:T(8,128)}, u32[]{:S(2)}, u32[]{:S(2)}) collective-permute-start(f32[4,34,64]{2,1,0:T(8,128)} %get-tuple-element.182), channel_id=1, source_target_pairs={{0,16},{1,17},{2,18},{3,19},{4,20},{5,21},{6,22},{7,23},{8,24},{9,... | collective-permute-start | bytes 104456 | tf_op jit(solution)/shard_map/ppermute | solution.py:78
  22.2 11.8 %collective-permute-start.9 = (f32[2,32,64]{2,1,0:T(8,128)}, f32[2,32,64]{2,1,0:T(8,128)}, u32[]{:S(2)}, u32[]{:S(2)}) collective-permute-start(f32[2,32,64]{2,1,0:T(8,128)} %select_bitcast_fusion.17), channel_id=1, source_target_pairs={{0,1},{2,3},{4,5},{6,7},{8,9},{10,11},{12,13},{14,15},{1,0},{3,2},... | collective-permute-start | bytes 49160 | tf_op jit(solution)/shard_map/ppermute | solution.py:28
  22.9 11.2 %collective-permute-start.8 = (f32[2,32,64]{2,1,0:T(8,128)}, f32[2,32,64]{2,1,0:T(8,128)}, u32[]{:S(2)}, u32[]{:S(2)}) collective-permute-start(f32[2,32,64]{2,1,0:T(8,128)} %fusion.88), channel_id=1, source_target_pairs={{1,2},{3,4},{5,6},{7,8},{9,10},{11,12},{13,14},{2,1},{4,3},{6,5},{... | collective-permute-start | bytes 49160 | tf_op jit(solution)/shard_map/ppermute | solution.py:29
  34.2 54.6 %collective-permute-start.3 = (f32[384,384]{1,0:T(8,128)}, f32[384,384]{1,0:T(8,128)}, u32[]{:S(2)}, u32[]{:S(2)}) collective-permute-start(f32[384,384]{1,0:T(8,128)} %bitcast.561), channel_id=1, source_target_pairs={{0,16},{16,0},{1,17},{17,1},{2,18},{18,2},{3,19},{19,3},{4,20},{20... | collective-permute-start | bytes 1769480 | tf_op jit(solution)/shard_map/ppermute | solution.py:183
  50.3 13.7 %collective-permute-start.5 = (f32[2,32,64]{2,1,0:T(8,128)}, f32[2,32,64]{2,1,0:T(8,128)}, u32[]{:S(2)}, u32[]{:S(2)}) collective-permute-start(f32[2,32,64]{2,1,0:T(8,128)} %get-tuple-element.171), channel_id=1, source_target_pairs={{1,2},{3,4},{5,6},{7,8},{9,10},{11,12},{13,14},{2,1},{4,3},{6,5},{... | collective-permute-start | bytes 49160 | tf_op jit(solution)/shard_map/ppermute | solution.py:29
  51.6 12.4 %collective-permute-start.6 = (f32[2,32,64]{2,1,0:T(8,128)}, f32[2,32,64]{2,1,0:T(8,128)}, u32[]{:S(2)}, u32[]{:S(2)}) collective-permute-start(f32[2,32,64]{2,1,0:T(8,128)} %get-tuple-element.172), channel_id=1, source_target_pairs={{0,1},{2,3},{4,5},{6,7},{8,9},{10,11},{12,13},{14,15},{1,0},{3,2},... | collective-permute-start | bytes 49160 | tf_op jit(solution)/shard_map/ppermute | solution.py:28
  57.3 16.8 %all-to-all-start = ((f32[32,12,128]{2,1,0:T(8,128)}), f32[32,12,128]{2,1,0:T(8,128)}, u32[]{:S(2)}, u32[]{:S(2)}) async-start(f32[32,12,128]{2,1,0:T(8,128)} %broadcast_in_dim.229), calls=%async_computation | async-start | bytes 524288 | tf_op jit(solution)/shard_map/all_to_all | solution.py:46
  119.7 12.6 %collective-permute-start.11 = (f32[2,16,64]{2,1,0:T(8,128)}, f32[2,16,64]{2,1,0:T(8,128)}, u32[]{:S(2)}, u32[]{:S(2)}) collective-permute-start(f32[2,16,64]{2,1,0:T(8,128)} %get-tuple-element.261), channel_id=1, source_target_pairs={{1,2},{3,4},{5,6},{7,8},{9,10},{11,12},{13,14},{2,1},{4,3},{6,5},{... | collective-permute-start | bytes 24584 | tf_op jit(solution)/shard_map/ppermute | solution.py:29
  121.0 11.4 %collective-permute-start.12 = (f32[2,16,64]{2,1,0:T(8,128)}, f32[2,16,64]{2,1,0:T(8,128)}, u32[]{:S(2)}, u32[]{:S(2)}) collective-permute-start(f32[2,16,64]{2,1,0:T(8,128)} %get-tuple-element.262), channel_id=1, source_target_pairs={{0,1},{2,3},{4,5},{6,7},{8,9},{10,11},{12,13},{14,15},{1,0},{3,2},... | collective-permute-start | bytes 24584 | tf_op jit(solution)/shard_map/ppermute | solution.py:28
  168.2 12.9 %collective-permute-start.14 = (f32[2,16,64]{2,1,0:T(8,128)}, f32[2,16,64]{2,1,0:T(8,128)}, u32[]{:S(2)}, u32[]{:S(2)}) collective-permute-start(f32[2,16,64]{2,1,0:T(8,128)} %get-tuple-element.246), channel_id=1, source_target_pairs={{1,2},{3,4},{5,6},{7,8},{9,10},{11,12},{13,14},{2,1},{4,3},{6,5},{... | collective-permute-start | bytes 24584 | tf_op jit(solution)/shard_map/ppermute | solution.py:29
  169.5 11.6 %collective-permute-start.15 = (f32[2,16,64]{2,1,0:T(8,128)}, f32[2,16,64]{2,1,0:T(8,128)}, u32[]{:S(2)}, u32[]{:S(2)}) collective-permute-start(f32[2,16,64]{2,1,0:T(8,128)} %get-tuple-element.247), channel_id=1, source_target_pairs={{0,1},{2,3},{4,5},{6,7},{8,9},{10,11},{12,13},{14,15},{1,0},{3,2},... | collective-permute-start | bytes 24584 | tf_op jit(solution)/shard_map/ppermute | solution.py:28
  174.9 11.8 %all-to-all-start.2 = ((f32[32,4,128]{2,1,0:T(4,128)}), f32[32,4,128]{2,1,0:T(4,128)}, u32[]{:S(2)}, u32[]{:S(2)}) async-start(f32[32,4,128]{2,1,0:T(4,128)} %broadcast_in_dim.245), calls=%async_computation.2 | async-start | bytes 131072 | tf_op jit(solution)/shard_map/all_to_all | solution.py:46
  216.8 12.8 %collective-permute-start.17 = (f32[2,16,64]{2,1,0:T(8,128)}, f32[2,16,64]{2,1,0:T(8,128)}, u32[]{:S(2)}, u32[]{:S(2)}) collective-permute-start(f32[2,16,64]{2,1,0:T(8,128)} %get-tuple-element.231), channel_id=1, source_target_pairs={{1,2},{3,4},{5,6},{7,8},{9,10},{11,12},{13,14},{2,1},{4,3},{6,5},{... | collective-permute-start | bytes 24584 | tf_op jit(solution)/shard_map/ppermute | solution.py:29
  218.0 11.6 %collective-permute-start.18 = (f32[2,16,64]{2,1,0:T(8,128)}, f32[2,16,64]{2,1,0:T(8,128)}, u32[]{:S(2)}, u32[]{:S(2)}) collective-permute-start(f32[2,16,64]{2,1,0:T(8,128)} %get-tuple-element.232), channel_id=1, source_target_pairs={{0,1},{2,3},{4,5},{6,7},{8,9},{10,11},{12,13},{14,15},{1,0},{3,2},... | collective-permute-start | bytes 24584 | tf_op jit(solution)/shard_map/ppermute | solution.py:28
  223.4 11.8 %all-to-all-start.3 = ((f32[32,4,128]{2,1,0:T(4,128)}), f32[32,4,128]{2,1,0:T(4,128)}, u32[]{:S(2)}, u32[]{:S(2)}) async-start(f32[32,4,128]{2,1,0:T(4,128)} %broadcast_in_dim.253), calls=%async_computation.3 | async-start | bytes 131072 | tf_op jit(solution)/shard_map/all_to_all | solution.py:46
  265.3 12.8 %collective-permute-start.20 = (f32[2,16,64]{2,1,0:T(8,128)}, f32[2,16,64]{2,1,0:T(8,128)}, u32[]{:S(2)}, u32[]{:S(2)}) collective-permute-start(f32[2,16,64]{2,1,0:T(8,128)} %get-tuple-element.216), channel_id=1, source_target_pairs={{1,2},{3,4},{5,6},{7,8},{9,10},{11,12},{13,14},{2,1},{4,3},{6,5},{... | collective-permute-start | bytes 24584 | tf_op jit(solution)/shard_map/ppermute | solution.py:29
  266.6 11.6 %collective-permute-start.21 = (f32[2,16,64]{2,1,0:T(8,128)}, f32[2,16,64]{2,1,0:T(8,128)}, u32[]{:S(2)}, u32[]{:S(2)}) collective-permute-start(f32[2,16,64]{2,1,0:T(8,128)} %get-tuple-element.217), channel_id=1, source_target_pairs={{0,1},{2,3},{4,5},{6,7},{8,9},{10,11},{12,13},{14,15},{1,0},{3,2},... | collective-permute-start | bytes 24584 | tf_op jit(solution)/shard_map/ppermute | solution.py:28
  272.0 11.8 %all-to-all-start.4 = ((f32[32,4,128]{2,1,0:T(4,128)}), f32[32,4,128]{2,1,0:T(4,128)}, u32[]{:S(2)}, u32[]{:S(2)}) async-start(f32[32,4,128]{2,1,0:T(4,128)} %broadcast_in_dim.261), calls=%async_computation.4 | async-start | bytes 131072 | tf_op jit(solution)/shard_map/all_to_all | solution.py:46
  309.1 15.9 %collective-permute-start.23 = (f32[2,16,64]{2,1,0:T(8,128)}, f32[2,16,64]{2,1,0:T(8,128)}, u32[]{:S(2)}, u32[]{:S(2)}) collective-permute-start(f32[2,16,64]{2,1,0:T(8,128)} %get-tuple-element.197), channel_id=1, source_target_pairs={{1,2},{3,4},{5,6},{7,8},{9,10},{11,12},{13,14},{2,1},{4,3},{6,5},{... | collective-permute-start | bytes 24584 | tf_op jit(solution)/shard_map/ppermute | solution.py:29
  310.3 14.7 %collective-permute-start.24 = (f32[2,16,64]{2,1,0:T(8,128)}, f32[2,16,64]{2,1,0:T(8,128)}, u32[]{:S(2)}, u32[]{:S(2)}) collective-permute-start(f32[2,16,64]{2,1,0:T(8,128)} %get-tuple-element.198), channel_id=1, source_target_pairs={{0,1},{2,3},{4,5},{6,7},{8,9},{10,11},{12,13},{14,15},{1,0},{3,2},... | collective-permute-start | bytes 24584 | tf_op jit(solution)/shard_map/ppermute | solution.py:28
  311.6 14.2 %collective-permute-start.22 = (f32[4,16,64]{2,1,0:T(8,128)}, f32[4,16,64]{2,1,0:T(8,128)}, u32[]{:S(2)}, u32[]{:S(2)}) collective-permute-start(f32[4,16,64]{2,1,0:T(8,128)} %get-tuple-element.194), channel_id=1, source_target_pairs={{0,16},{16,0},{1,17},{17,1},{2,18},{18,2},{3,19},{19,3},{4,20},{20... | collective-permute-start | bytes 49160 | tf_op jit(solution)/shard_map/ppermute | solution.py:36
  320.8 11.3 %all-to-all-start.5 = ((f32[32,4,128]{2,1,0:T(4,128)}), f32[32,4,128]{2,1,0:T(4,128)}, u32[]{:S(2)}, u32[]{:S(2)}) async-start(f32[32,4,128]{2,1,0:T(4,128)} %broadcast_in_dim.269), calls=%async_computation.5 | async-start | bytes 131072 | tf_op jit(solution)/shard_map/all_to_all | solution.py:46
  (70 other events, 426.1 us)

commit v2 on v1

--- a/solution.py
+++ b/solution.py
@@ -1,6 +1,8 @@
 import jax
 import jax.numpy as jnp
 from jax import lax
+from jax.experimental import pallas as pl
+from jax.experimental.pallas import tpu as pltpu
 from jax.sharding import PartitionSpec as P
 
 ITERS = 6
@@ -46,7 +48,7 @@
     return lax.all_to_all(sent, axes, 0, 0, tiled=False)
 
 
-def shards(
+def general(
     duals, residual, direction, prev_rho, dual_schur, coupling, coarse_inverse, edge_map, corner_slot, active, scaling
 ):
     cases, span_x, span_y, owned = duals.shape
@@ -253,6 +255,585 @@
     return back(lam), back(own_part(r)), back(p)
 
 
+F32, BF16 = jnp.float32, jnp.bfloat16
+SPAN_X, SPAN_Y = 2, 4
+SUBS = SPAN_X * SPAN_Y
+CASES = 16
+SLOTS = 32
+USED = 2 * (SPAN_X + 1) * (SPAN_Y + 1)
+CAST = 40
+LIMIT = 16 * 1024 * 1024
+
+
+def iota(shape, dim):
+    return lax.broadcasted_iota(jnp.int32, shape, dim)
+
+
+def split(v):
+    high = v.astype(BF16)
+    return high, (v - high.astype(F32)).astype(BF16)
+
+
+def dot(a, b):
+    return jnp.dot(a, b, preferred_element_type=F32)
+
+
+def dot_split(v, high, low):
+    n = v.shape[0]
+    vh, vl = split(v)
+    wide = dot(jnp.concatenate([vh, vl], 0), high)
+    return wide[:n] + wide[n:] + dot(vh, low)
+
+
+def dot_exact(v, ones):
+    n = v.shape[0]
+    vh, vl = split(v)
+    wide = dot(jnp.concatenate([vh, vl], 0), ones)
+    return wide[:n] + wide[n:]
+
+
+def odd(i):
+    return (i // SPAN_Y + i % SPAN_Y) % 2
+
+
+def lower(rows):
+    return iota((rows, 128), 1) < 64
+
+
+def packs(ys):
+    rows = ys[0].shape[0]
+    low = lower(rows)
+    column = lambda x: [
+        jnp.where(low, ys[x * SPAN_Y + t][:, :128], ys[x * SPAN_Y + t + 1][:, :128]) for t in range(0, SPAN_Y, 2)
+    ]
+    row = lambda y: jnp.where(low, ys[y][:, 128:], ys[SPAN_Y + y][:, 128:])
+    return column(0), column(SPAN_X - 1), row(0), row(SPAN_Y - 1)
+
+
+def send(ys, x_ref, a_ref, b_ref, at):
+    rows = pl.ds(at, ys[0].shape[0])
+    west, east, south, north = packs(ys)
+    first = lax.axis_index("gx") == 0
+    even = lax.axis_index("gy") % 2 == 0
+    for t in range(SPAN_Y // 2):
+        x_ref[t, rows, :] = jnp.where(first, east[t], west[t])
+    a_ref[rows, :] = jnp.where(even, north, south)
+    b_ref[rows, :] = jnp.where(even, south, north)
+
+
+def received(x_ref, a_ref, b_ref, at, n):
+    rows = pl.ds(at, n)
+    first = lax.axis_index("gx") == 0
+    even = lax.axis_index("gy") % 2 == 0
+    xs = [x_ref[t, rows, :] for t in range(SPAN_Y // 2)]
+    a, b = a_ref[rows, :], b_ref[rows, :]
+    zero = jnp.zeros_like(a)
+    return (
+        [jnp.where(first, zero, v) for v in xs],
+        [jnp.where(first, v, zero) for v in xs],
+        jnp.where(even, b, a),
+        jnp.where(even, a, b),
+    )
+
+
+def across(ys, nb, rows):
+    low = lower(rows)
+    zero = jnp.zeros((rows, 128), F32)
+    inside = lambda x, y, part: zero if ys is None else ys[x * SPAN_Y + y][:, part * 128 : part * 128 + 128]
+    out = []
+    for x in range(SPAN_X):
+        for y in range(SPAN_Y):
+            beyond = lambda v: zero if nb is None else v()
+            west = inside(x - 1, y, 0) if x else beyond(lambda: nb[0][y // 2])
+            east = inside(x + 1, y, 0) if x < SPAN_X - 1 else beyond(lambda: nb[1][y // 2])
+            south = inside(x, y - 1, 1) if y else beyond(lambda: nb[2])
+            north = inside(x, y + 1, 1) if y < SPAN_Y - 1 else beyond(lambda: nb[3])
+            if (x + y) % 2:
+                west, east, south, north = east, west, north, south
+            out.append(jnp.concatenate([jnp.where(low, west, east), jnp.where(low, south, north)], 1))
+    return out
+
+
+def owned_lanes(i, rows):
+    lane = iota((rows, 256), 1) % 128
+    return lane < 64 if odd(i) else lane >= 64
+
+
+def spread_owned(v, i):
+    zero = jnp.zeros_like(v)
+    low = lower(v.shape[0])
+    turned = pltpu.roll(v, 64, 1)
+    if odd(i):
+        return jnp.concatenate([jnp.where(low, v, zero), jnp.where(low, turned, zero)], 1)
+    return jnp.concatenate([jnp.where(low, zero, turned), jnp.where(low, zero, v)], 1)
+
+
+def take_owned(v, i):
+    low = lower(v.shape[0])
+    if odd(i):
+        return jnp.where(low, v[:, :128], pltpu.roll(v[:, 128:], 64, 1))
+    return jnp.where(low, pltpu.roll(v[:, :128], 64, 1), v[:, 128:])
+
+
+def start_kernel(res_ref, dir_ref, act_ref, scale_ref, own_ref, x_ref, a_ref, b_ref):
+    gx, gy = lax.axis_index("gx"), lax.axis_index("gy")
+    last_x = gx * SPAN_X + SPAN_X - 1 == lax.axis_size("gx") * SPAN_X - 1
+    last_y = gy * SPAN_Y + SPAN_Y - 1 == lax.axis_size("gy") * SPAN_Y - 1
+    east = iota((1, 128), 1) < 64
+    ys = []
+    for i in range(SUBS):
+        x, y = i // SPAN_Y, i % SPAN_Y
+        keep = act_ref[i : i + 1, :].astype(F32)
+        if x == SPAN_X - 1:
+            keep = jnp.where(jnp.logical_and(last_x, east), 0.0, keep)
+        if y == SPAN_Y - 1:
+            keep = jnp.where(jnp.logical_and(last_y, jnp.logical_not(east)), 0.0, keep)
+        mine = pl.ds(i, CASES, stride=SUBS)
+        v = jnp.concatenate(
+            [
+                res_ref[mine, :],
+                dir_ref[mine, :] * keep,
+                scale_ref[i : i + 1, :] * keep,
+                keep,
+                jnp.zeros((CAST - 2 * CASES - 2, 128), F32),
+            ],
+            0,
+        )
+        v = spread_owned(v, i)
+        own_ref[i] = v
+        ys.append(v)
+    send(ys, x_ref, a_ref, b_ref, 0)
+
+
+def operator_kernel(schur_ref, couple_ref, map_ref, slot_ref, high_ref, low_ref, cc_ref, wh_ref, wl_ref, name_ref):
+    none = 384
+    slot = slot_ref[...].astype(F32)
+    eye = iota((8, 8), 0) == iota((8, 8), 1)
+    column = jnp.concatenate(
+        [jnp.sum(jnp.where(eye, jnp.broadcast_to(slot[i : i + 1, :], (8, 8)), 0.0), 1, keepdims=True) for i in range(SUBS)], 0
+    )
+    row = jnp.concatenate([slot[i : i + 1, :] for i in range(SUBS)], 1)
+    count = SUBS * 8
+    earlier = iota((count, count), 1) < iota((count, count), 0)
+    again = jnp.sum(jnp.where(jnp.logical_and(column == row, earlier), 1.0, 0.0), 1, keepdims=True)
+    first = jnp.where(jnp.logical_and(again == 0.0, column != float(none)), 1.0, 0.0)
+    first_row = jnp.sum(
+        jnp.where(jnp.logical_and(column == row, iota((count, count), 0) < iota((count, count), 1)), 1.0, 0.0), 0, keepdims=True
+    )
+    first_row = jnp.where(jnp.logical_and(first_row == 0.0, row != float(none)), 1.0, 0.0)
+    rank = jnp.sum(jnp.where(row < column, first_row, 0.0), 1, keepdims=True)
+    hit = jnp.where(rank == iota((count, 128), 1).astype(F32), first, 0.0)
+    name_ref[...] = jnp.broadcast_to(
+        jnp.where(jnp.sum(hit, 0, keepdims=True) > 0.0, jnp.sum(hit * column, 0, keepdims=True), float(none)), (8, 128)
+    )
+    sub = iota((256, 256), 0)
+    west = (sub // 64) % 2 == 0
+    all_cc = []
+    for i in range(SUBS):
+        spots = map_ref[i : i + 1, :]
+        if odd(i):
+            spots = jnp.where((spots // 64) % 2 == 0, spots + 64, spots - 64)
+        sign = jnp.where(west, 1.0, -1.0) if odd(i) else jnp.where(west, -1.0, 1.0)
+        place = jnp.where(sub == spots, sign, 0.0).astype(BF16)
+        mine = slot[i : i + 1, :]
+        number = jnp.sum(jnp.where(column < mine, first, 0.0), 0, keepdims=True)
+        compact = jnp.where(
+            jnp.logical_and(number == iota((SLOTS, 8), 0).astype(F32), mine != float(none)), 1.0, 0.0
+        )
+        cc = jnp.dot(compact, couple_ref[i], precision=EXACT, preferred_element_type=F32)
+        c1, rest = split(cc)
+        c2, c3 = split(cc - c1.astype(F32))
+        s1, s2 = split(schur_ref[i])
+        tall = lax.dot_general(
+            jnp.concatenate([s1, s2, c1, c2, c3], 0), place, (((1,), (1,)), ((), ())), preferred_element_type=F32
+        )
+        high_ref[i] = dot(place, tall[:256].astype(BF16)).astype(BF16)
+        low_ref[i] = dot(place, tall[256:512].astype(BF16)).astype(BF16)
+        cc = tall[512 : 512 + SLOTS] + tall[512 + SLOTS : 512 + 2 * SLOTS] + tall[512 + 2 * SLOTS :]
+        cc_ref[i] = cc
+        all_cc.append(cc)
+    wh_ref[...], wl_ref[...] = split(jnp.transpose(jnp.concatenate(all_cc, 0)))
+
+
+def inverse_kernel(mine_ref, other_ref, high_ref, low_ref):
+    first = lax.axis_index("gx") == 0
+    mine, other = mine_ref[...], other_ref[...]
+    high_ref[0], low_ref[0] = split(jnp.where(first, mine, other))
+    high_ref[1], low_ref[1] = split(jnp.where(first, other, mine))
+
+
+def spread_kernel(cc_ref, name_ref, mk_ref, x_ref, a_ref, b_ref, high_ref, low_ref, near_ref):
+    at = 2 * CASES
+    cc = [cc_ref[i] for i in range(SUBS)]
+    inside = across(cc, None, SLOTS)
+    nb = received(x_ref, a_ref, b_ref, at, SLOTS)
+    blank = jnp.zeros((SLOTS, 128), F32)
+    blanks = [blank] * (SPAN_Y // 2)
+    even = lax.axis_index("gy") % 2 == 0
+    by_x = across(None, (nb[0], nb[1], blank, blank), SLOTS)
+    a_low, a_high = jnp.where(even, 0.0, 1.0), jnp.where(even, 1.0, 0.0)
+    by_a = across(None, (blanks, blanks, nb[2] * a_low, nb[3] * a_high), SLOTS)
+    by_b = across(None, (blanks, blanks, nb[2] * a_high, nb[3] * a_low), SLOTS)
+    for i in range(SUBS):
+        keep = mk_ref[i, 1:2, :]
+        whole = jnp.concatenate([cc[i] + inside[i], by_a[i], by_b[i], by_x[i]], 0) * keep
+        high_ref[i], low_ref[i] = split(whole)
+    named = pl.ds(at + SLOTS, 1)
+    group = iota((1, 128), 1) // SLOTS
+    turn = lambda v, g: pltpu.roll(jnp.broadcast_to(v, (8, 128)), g * SLOTS, 1)[0:1]
+    names = [turn(name_ref[0:1, :], 0), turn(a_ref[named, :], 1), turn(b_ref[named, :], 2), turn(x_ref[0, named, :], 3)]
+    wanted = jnp.where(group == 0, names[0], jnp.where(group == 1, names[1], jnp.where(group == 2, names[2], names[3])))
+    found = iota((384, 128), 0).astype(F32) == wanted
+    mine = jnp.where(iota((384, 128), 1) < 3 * SLOTS, 1.0, 0.0)
+    gx = lax.axis_index("gx")
+    for region in range(2):
+        near_ref[region] = jnp.where(found, jnp.where(gx == region, mine, 1.0 - mine), 0.0).astype(BF16)
+
+
+def local_part(us, rs, high_ref, low_ref, wh_ref, wl_ref):
+    ys = [dot_split(us[i], high_ref[i], low_ref[i]) for i in range(SUBS)]
+    n = us[0].shape[0]
+    corner = dot_split(jnp.concatenate(us, 0), wh_ref[...], wl_ref[...])
+    group = iota((n, 128), 1) // SLOTS
+    total = jnp.zeros((n, 128), F32)
+    for i in range(SUBS):
+        part = corner[n * i : n * i + n, 128 * (i // 4) : 128 * (i // 4) + 128]
+        total = total + jnp.where(group == i % 4, part, 0.0)
+    total = total + pltpu.roll(total, 64, 1)
+    total = total + pltpu.roll(total, 32, 1)
+    return ys, total
+
+
+def over_lanes(terms):
+    total = terms[0]
+    for t in terms[1:]:
+        total = total + t
+    return jnp.sum(total[:, :128] + total[:, 128:], 1, keepdims=True)
+
+
+def packed(corner, one, two):
+    slot = iota((CASES, 128), 1) % SLOTS
+    full = jnp.where(slot == USED, one, jnp.where(slot == USED + 1, two, corner))
+    group = iota((4, 128), 1) // SLOTS
+    out = jnp.zeros((4, 128), F32)
+    for b in range(4):
+        out = jnp.where(group == b, full[4 * b : 4 * b + 4], out)
+    return out
+
+
+def by_slot(vs):
+    group = iota((8, 128), 1) // SLOTS
+    out = []
+    for region in range(2):
+        rows = []
+        for b in range(4):
+            halves = []
+            for h in range(2):
+                acc = None
+                for q in range(4):
+                    v = vs[8 * region + 4 * h + q]
+                    turned = v if q == b else pltpu.roll(v, (SLOTS * (q - b)) % 128, 1)
+                    acc = turned if acc is None else jnp.where(group == q, turned, acc)
+                halves.append(acc)
+            rows.append(jnp.concatenate(halves, 1))
+        out.append(jnp.concatenate(rows, 0))
+    return out
+
+
+def inner(vs):
+    total = vs[0]
+    for v in vs[1:]:
+        total = total + v
+    total = total[:4] + total[4:]
+    tall = jnp.concatenate([total] * 4, 0)
+    lane, row = iota((CASES, 128), 1), iota((CASES, 128), 0)
+    column = lambda s: jnp.sum(jnp.where(lane == SLOTS * (row // 4) + s, tall, 0.0), 1, keepdims=True)
+    return column(USED), column(USED + 1)
+
+
+def first_of_pairs(v):
+    return jnp.concatenate([v[8 * b : 8 * b + 4] for b in range(v.shape[0] // 8)], 0)
+
+
+def solve(spots, pick_ref, gh_ref, gl_ref, near_ref):
+    totals, sols, near = [], [], None
+    for region in range(2):
+        v = spots[region]
+        n = v.shape[0]
+        even = dot_exact(v, pick_ref[region, 0])
+        odds = dot_exact(v, pick_ref[region, 1])
+        z = jnp.where((iota((n, 384), 0) // 4) % 2 == 0, even, odds).reshape(n // 8, 8, 384)
+        total = (z + pltpu.roll(z, 4, 1)).reshape(n, 384)
+        sol = dot_split(total, gh_ref[region], gl_ref[region])
+        part = dot_exact(sol, near_ref[region])
+        near = part if near is None else near + part
+        totals.append(total)
+        sols.append(sol)
+    return totals, sols, near
+
+
+def energy(totals, sols):
+    both = totals[0] * sols[0] + totals[1] * sols[1]
+    return first_of_pairs(jnp.sum(both, 1, keepdims=True))
+
+
+def emit(rs, mk_ref, high_ref, low_ref, wh_ref, wl_ref, block_ref, y_ref, x_ref, a_ref, b_ref):
+    us = [mk_ref[i, 0:1, :] * rs[i] for i in range(SUBS)]
+    ys, corner = local_part(us, rs, high_ref, low_ref, wh_ref, wl_ref)
+    send(ys, x_ref, a_ref, b_ref, 0)
+    rho = over_lanes([jnp.where(owned_lanes(i, CASES), rs[i] * us[i], 0.0) for i in range(SUBS)])
+    delta = over_lanes([us[i] * ys[i] for i in range(SUBS)])
+    block = packed(corner, rho, delta)
+    twice = jnp.concatenate([block, block], 0)
+    for j in range(16):
+        block_ref[j] = twice
+    for i in range(SUBS):
+        y_ref[i] = ys[i]
+
+
+def first_kernel(
+    own_ref, x_ref, a_ref, b_ref, high_ref, low_ref, cc_ref, wh_ref, wl_ref, name_ref,
+    r_ref, p_ref, mk_ref, y_ref, block_ref, sx_ref, sa_ref, sb_ref,
+):
+    own = [own_ref[i] for i in range(SUBS)]
+    other = across(own, received(x_ref, a_ref, b_ref, 0, CAST), CAST)
+    rs, vs = [], []
+    for i in range(SUBS):
+        full = own[i] + other[i]
+        rs.append(full[:CASES])
+        r_ref[i] = full[:CASES]
+        p_ref[i] = full[CASES : 2 * CASES]
+        mk_ref[i] = full[2 * CASES : 2 * CASES + 8]
+        vs.append(jnp.concatenate([full[2 * CASES : 2 * CASES + 1] * full[:CASES], full[CASES : 2 * CASES]], 0))
+    ys, corner = local_part(vs, rs, high_ref, low_ref, wh_ref, wl_ref)
+    names = name_ref[...]
+    send([jnp.concatenate([ys[i], cc_ref[i]], 0) for i in range(SUBS)], sx_ref, sa_ref, sb_ref, 0)
+    at = pl.ds(2 * CASES + SLOTS, 8)
+    for t in range(SPAN_Y // 2):
+        sx_ref[t, at, :] = names
+    sa_ref[at, :] = names
+    sb_ref[at, :] = names
+    us = [v[:CASES] for v in vs]
+    ps = [v[CASES:] for v in vs]
+    rho = over_lanes([jnp.where(owned_lanes(i, CASES), rs[i] * us[i], 0.0) for i in range(SUBS)])
+    delta = over_lanes([us[i] * ys[i][:CASES] for i in range(SUBS)])
+    cross = over_lanes([ps[i] * ys[i][:CASES] for i in range(SUBS)])
+    eta = over_lanes([ps[i] * ys[i][CASES:] for i in range(SUBS)])
+    one, two = packed(corner[:CASES], rho, delta), packed(corner[CASES:], cross, eta)
+    blocks = [
+        jnp.concatenate([one, two], 0),
+        jnp.concatenate([names[:4], one], 0),
+        jnp.concatenate([two, names[:4]], 0),
+    ]
+    for j in range(16):
+        for t in range(3):
+            block_ref[3 * j + t] = blocks[t]
+    for i in range(SUBS):
+        y_ref[i] = ys[i]
+
+
+def column_of(row):
+    eye = iota((CASES, CASES), 0) == iota((CASES, CASES), 1)
+    return jnp.sum(jnp.where(eye, jnp.broadcast_to(row, (CASES, CASES)), 0.0), 1, keepdims=True)
+
+
+def keep_scalars(scal_ref, values):
+    for t, v in enumerate(values):
+        scal_ref[t] = jnp.broadcast_to(v, (CASES, 128))
+
+
+def second_kernel(
+    got_ref, x_ref, a_ref, b_ref, y_ref, r_ref, p_ref, mk_ref, dual_ref, rho_ref, gh_ref, gl_ref, near_ref, dh_ref, dl_ref,
+    high_ref, low_ref, wh_ref, wl_ref,
+    pick_ref, ro_ref, so_ref, po_ref, lo_ref, scal_ref, block_ref, yo_ref, sx_ref, sa_ref, sb_ref,
+):
+    top = iota((8, 128), 0) < 4
+    us, ps, names = [], [], []
+    for j in range(16):
+        v = [got_ref[3 * j + t] for t in range(3)]
+        us.append(jnp.where(top, v[0], v[1]))
+        ps.append(pltpu.roll(jnp.where(top, v[2], v[0]), 4, 0))
+        names.append((v[1], pltpu.roll(v[2], 4, 0)))
+    group = iota((8, 128), 1) // SLOTS
+    for region in range(2):
+        for par in range(2):
+            halves = []
+            for h in range(2):
+                acc = None
+                for q in range(4):
+                    v = names[8 * region + 4 * h + q][par]
+                    turned = pltpu.roll(v, SLOTS * q, 1) if q else v
+                    acc = turned if acc is None else jnp.where(group == q, turned, acc)
+                halves.append(acc[0:1])
+            wanted = jnp.concatenate(halves, 1)
+            hit = jnp.where(iota((384, 256), 0).astype(F32) == wanted, 1.0, 0.0)
+            pick_ref[region, par] = jnp.transpose(hit).astype(BF16)
+    lhs_u, lhs_p = by_slot(us), by_slot(ps)
+    n = lhs_u[0].shape[0]
+    totals, sols, near = solve(
+        [jnp.concatenate([lhs_u[t], lhs_p[t]], 0) for t in range(2)], pick_ref, gh_ref, gl_ref, near_ref
+    )
+    of_u, of_p = lambda vs: [v[:n] for v in vs], lambda vs: [v[n:] for v in vs]
+    rho, delta = inner(us)
+    cross, eta = inner(ps)
+    delta = delta + energy(of_u(totals), of_u(sols))
+    cross = cross + energy(of_p(totals), of_u(sols))
+    eta = eta + energy(of_p(totals), of_p(sols))
+    near = first_of_pairs(near)
+    beta = rho / column_of(rho_ref[...])
+    skew = cross + beta * eta
+    pi = delta + 2.0 * beta * skew - beta * beta * eta
+    alpha = rho / pi
+    ys = [y_ref[i] for i in range(SUBS)]
+    other = across(ys, received(x_ref, a_ref, b_ref, 0, 2 * CASES), 2 * CASES)
+    rs = []
+    for i in range(SUBS):
+        f = mk_ref[i, 1:2, :] * (ys[i] + other[i]) + dot_split(near, dh_ref[i], dl_ref[i])
+        r = r_ref[i]
+        p = mk_ref[i, 0:1, :] * r + beta * p_ref[i]
+        s = f[:CASES] + beta * f[CASES:]
+        r = r - alpha * s
+        rs.append(r)
+        ro_ref[i], so_ref[i], po_ref[i] = r, s, p
+        lo_ref[i] = spread_owned(dual_ref[pl.ds(i, CASES, stride=SUBS), :], i) + alpha * p
+    keep_scalars(scal_ref, (rho, pi, beta, skew))
+    emit(rs, mk_ref, high_ref, low_ref, wh_ref, wl_ref, block_ref, yo_ref, sx_ref, sa_ref, sb_ref)
+
+
+def absorb(got_ref, x_ref, a_ref, b_ref, y_ref, r_ref, s_ref, p_ref, l_ref, scal_ref, mk_ref, pick_ref, gh_ref, gl_ref, near_ref, dh_ref, dl_ref):
+    vs = [got_ref[j] for j in range(16)]
+    totals, sols, near = solve(by_slot(vs), pick_ref, gh_ref, gl_ref, near_ref)
+    rho, delta = inner(vs)
+    delta = delta + energy(totals, sols)
+    near = first_of_pairs(near)
+    rho_old, pi, beta, skew = (scal_ref[t][:, 0:1] for t in range(4))
+    skew = beta * skew
+    beta = rho / rho_old
+    pi = delta + 2.0 * beta * skew - beta * beta * pi
+    alpha = rho / pi
+    ys = [y_ref[i] for i in range(SUBS)]
+    other = across(ys, received(x_ref, a_ref, b_ref, 0, CASES), CASES)
+    out = []
+    for i in range(SUBS):
+        f = mk_ref[i, 1:2, :] * (ys[i] + other[i]) + dot_split(near, dh_ref[i], dl_ref[i])
+        r = r_ref[i]
+        p = mk_ref[i, 0:1, :] * r + beta * p_ref[i]
+        s = f + beta * s_ref[i]
+        out.append((r - alpha * s, s, p, l_ref[i] + alpha * p))
+    return out, (rho, pi, beta, skew)
+
+
+def round_kernel(
+    got_ref, x_ref, a_ref, b_ref, y_ref, r_ref, s_ref, p_ref, l_ref, scal_ref, mk_ref, pick_ref, gh_ref, gl_ref, near_ref,
+    dh_ref, dl_ref, high_ref, low_ref, wh_ref, wl_ref,
+    ro_ref, so_ref, po_ref, lo_ref, scalo_ref, block_ref, yo_ref, sx_ref, sa_ref, sb_ref,
+):
+    out, scalars = absorb(
+        got_ref, x_ref, a_ref, b_ref, y_ref, r_ref, s_ref, p_ref, l_ref, scal_ref, mk_ref, pick_ref, gh_ref, gl_ref, near_ref,
+        dh_ref, dl_ref,
+    )
+    for i, (r, s, p, lam) in enumerate(out):
+        ro_ref[i], so_ref[i], po_ref[i], lo_ref[i] = r, s, p, lam
+    keep_scalars(scalo_ref, scalars)
+    emit([v[0] for v in out], mk_ref, high_ref, low_ref, wh_ref, wl_ref, block_ref, yo_ref, sx_ref, sa_ref, sb_ref)
+
+
+def last_kernel(
+    got_ref, x_ref, a_ref, b_ref, y_ref, r_ref, s_ref, p_ref, l_ref, scal_ref, mk_ref, pick_ref, gh_ref, gl_ref, near_ref,
+    dh_ref, dl_ref, lo_ref, ro_ref, po_ref,
+):
+    out, _ = absorb(
+        got_ref, x_ref, a_ref, b_ref, y_ref, r_ref, s_ref, p_ref, l_ref, scal_ref, mk_ref, pick_ref, gh_ref, gl_ref, near_ref,
+        dh_ref, dl_ref,
+    )
+    for i, (r, _, p, lam) in enumerate(out):
+        mine = pl.ds(i, CASES, stride=SUBS)
+        lo_ref[mine, :] = take_owned(lam, i)
+        ro_ref[mine, :] = take_owned(r, i)
+        po_ref[mine, :] = take_owned(p, i)
+
+
+def call(kernel, args, outs):
+    vmem = pl.BlockSpec(memory_space=pltpu.VMEM)
+    return pl.pallas_call(
+        kernel,
+        out_shape=[jax.ShapeDtypeStruct(shape, kind) for shape, kind in outs],
+        in_specs=[vmem] * len(args),
+        out_specs=[vmem] * len(outs),
+        compiler_params=pltpu.CompilerParams(vmem_limit_bytes=LIMIT),
+    )(*args)
+
+
+def trade(x, a, b):
+    peers = lax.axis_size("gy")
+    return (
+        lax.ppermute(x, "gx", [(0, 1), (1, 0)]),
+        lax.ppermute(a, "gy", both_ways(pairs_from(0, peers))),
+        lax.ppermute(b, "gy", both_ways(pairs_from(1, peers))),
+    )
+
+
+def two_regions(
+    duals, residual, direction, prev_rho, dual_schur, coupling, coarse_inverse, edge_map, corner_slot, active, scaling
+):
+    native = lambda v: v.reshape(CASES * SUBS, 128)
+    by_sub = lambda v: v.reshape((SUBS,) + v.shape[2:])
+    width = coarse_inverse.shape[-1]
+    sends = lambda rows: [((SPAN_Y // 2, rows, 128), F32), ((rows, 128), F32), ((rows, 128), F32)]
+    state = ((SUBS, CASES, 256), F32)
+
+    other = lax.ppermute(coarse_inverse[0], "gx", [(0, 1), (1, 0)])
+    own, *out = call(
+        start_kernel,
+        [native(residual), native(direction), by_sub(active), by_sub(scaling)],
+        [((SUBS, CAST, 256), F32)] + sends(CAST),
+    )
+    come = trade(*out)
+    matrix = ((SUBS, 256, 256), BF16)
+    high, low, cc, wh, wl, names = call(
+        operator_kernel,
+        [by_sub(dual_schur), by_sub(coupling), by_sub(edge_map), by_sub(corner_slot)],
+        [matrix, matrix, ((SUBS, SLOTS, 256), F32), ((256, 256), BF16), ((256, 256), BF16), ((8, 128), F32)],
+    )
+    square = ((2, width, width), BF16)
+    gh, gl = call(inverse_kernel, [coarse_inverse[0], other], [square, square])
+    rows = 2 * CASES + SLOTS + 8
+    r, p, mk, y, block, *out = call(
+        first_kernel,
+        [own, *come, high, low, cc, wh, wl, names],
+        [state, state, ((SUBS, 8, 256), F32), ((SUBS, 2 * CASES, 256), F32), ((48, 8, 128), F32)] + sends(rows),
+    )
+    got = lax.all_to_all(block.reshape(32, 12, 128), BOTH, 0, 0, tiled=False).reshape(48, 8, 128)
+    come = trade(*out)
+    wide = ((SUBS, 128, 256), BF16)
+    dh, dl, near = call(spread_kernel, [cc, names, mk, *come], [wide, wide, ((2, width, 128), BF16)])
+    weights = [high, low, wh, wl]
+    onward = [state, state, state, state, ((4, CASES, 128), F32), ((16, 8, 128), F32), state] + sends(CASES)
+    pick, r, s, p, lam, scal, block, y, *out = call(
+        second_kernel,
+        [got, *come, y, r, p, mk, native(duals), prev_rho.reshape(1, CASES), gh, gl, near, dh, dl, *weights],
+        [((2, 2, 256, width), BF16)] + onward,
+    )
+    for step in range(1, ITERS):
+        got = lax.all_to_all(block.reshape(32, 4, 128), BOTH, 0, 0, tiled=False).reshape(16, 8, 128)
+        come = trade(*out)
+        args = [got, *come, y, r, s, p, lam, scal, mk, pick, gh, gl, near, dh, dl]
+        if step < ITERS - 1:
+            r, s, p, lam, scal, block, y, *out = call(round_kernel, args + weights, onward)
+        else:
+            plain = ((CASES * SUBS, 128), F32)
+            results = call(last_kernel, args, [plain, plain, plain])
+    return tuple(v.reshape(duals.shape) for v in results)
+
+
+def shards(*args):
+    cases, span_x, span_y, owned = args[0].shape
+    fits = (cases, span_x, span_y, owned, args[6].shape[-1]) == (CASES, SPAN_X, SPAN_Y, 128, 384)
+    if fits and lax.axis_size("gx") == 2 and lax.axis_size("gy") == 16:
+        return two_regions(*args)
+    return general(*args)
+
+
 def solution(mesh):
     placed = (
         P(None, "gx", "gy", None),

time: 358 us -> 227 us (0.63)
  other arithmetic: 69.4 us -> 0 us
  matrix products: 64.9 us -> 0 us
  starting transfers between devices: 70.4 us -> 50.4 us
  Pallas kernels: 0 us -> 19 us
  local copies, waits for them, and re-layouts: 122 us -> 127 us
    unnamed x133 -> x324, local copies, waits for them, and re-layouts: 4.1 us -> 125 us
    dot_general x32 -> x0, matrix products: 64.9 us -> none  [the longest x7 21.2 us: solve(): sol = jnp.einsum('kra,rab->krb', flat_c, dense, precision=HIGH)]
    broadcast_in_dim x27 -> x0, local copies, waits for them, and re-layouts: 29.9 us -> none  [the longest x14 15.6 us: pack(): return jnp.concatenate([c, one[:, None], two[:, None]], 1).reshape(-1, 128)]
    ppermute x25 -> x22, starting transfers between devices: 42.6 us -> 18.6 us  [the longest x7 10.8 us: trade(): lax.ppermute(x, 'gx', [(0, 1), (1, 0)])]
    slice x32 -> x0, local copies, waits for them, and re-layouts: 21.6 us -> none  [the longest x12 7.91 us: own_part(): return jnp.concatenate([a[..., half:2 * half], a[..., 3 * half:]], -1)]
    reshape x17 -> x3, local copies, waits for them, and re-layouts: 21.7 us -> 2.14 us  [the longest x1 0.72 us: two_regions(): lax.all_to_all(block.reshape(32, 12, 128), BOTH, 0, 0, tiled=False)]
    pallas_call x0 -> x11, Pallas kernels: none -> 19 us  [call(): pl.pallas_call(kernel, out_shape=[jax.ShapeDtypeStruct(shape, kind) for s...]
    reduce_sum x15 -> x0, other arithmetic: 17.3 us -> none  [the longest x7 9.5 us: over_cases(): return jnp.sum(a * b, axis=(0, 1, 3))]
  transfers between devices with their start and end apart: 31 -> 28, of which waited for: 11 -> 15; matrix products, arithmetic and copies ran while one was open for 25% -> 1% of each run, Pallas kernels for 0% -> 2%
where the time goes in v2:
time: 227 us; the launch traced here: 224 us
  local copies, waits for them, and re-layouts  127 us (56%)
  starting transfers between devices  50.4 us (22%)
  waiting for transfers between devices  26.3 us (12%)
  Pallas kernels  19 us (8%)
    unnamed x324, local copies, waits for them, and re-layouts  125 us
    all_to_all x5, starting transfers between devices, two_regions(): lax.all_to_all(block.reshape(32, 4, 128), BOTH, 0, 0, tiled=False)  25.7 us
    pallas_call x11, Pallas kernels, call(): pl.pallas_call(kernel, out_shape=[jax.ShapeDtypeStruct(shape, kind) for s...  19 us
    all_to_all x5, waiting for transfers between devices, two_regions(): lax.all_to_all(block.reshape(32, 4, 128), BOTH, 0, 0, tiled=False)  15.5 us
    ppermute x7, starting transfers between devices, trade(): lax.ppermute(x, 'gx', [(0, 1), (1, 0)])  10.8 us
    all_to_all x1, starting transfers between devices, two_regions(): lax.all_to_all(block.reshape(32, 12, 128), BOTH, 0, 0, tiled=False)  6.07 us
    ppermute x7, waiting for transfers between devices, trade(): lax.ppermute(x, 'gx', [(0, 1), (1, 0)])  5.88 us
    ppermute x7, starting transfers between devices, trade(): lax.ppermute(b, 'gy', both_ways(pairs_from(1, peers)))  4.75 us
  transfers between devices with their start and end apart: 28, of which 15 were waited for; matrix products, arithmetic and copies ran while one was open for 1% of the time, Pallas kernels for 2%

profile of v2, /device:TPU:0, one launch (start us, length us, event | category | flops | bytes accessed | tf_op | source)
XLA Modules:
  0.0 223.7 jit_solution(12108038816761275838)
XLA Ops:
  0.6 3.0 %collective-permute-start.6 = (f32[384,384]{1,0:T(8,128)}, f32[384,384]{1,0:T(8,128)S(1)}, u32[]{:S(2)}, u32[]{:S(2)}) collective-permute-start(f32[384,384]{1,0:T(8,128)} %bitcast.24), channel_id=1, source_target_pairs={{0,16},{16,0},{1,17},{17,1},{2,18},{18,2},{3,19},{19,3},{4,20},{20... | collective-permute-start | bytes 1769480 | tf_op jit(solution)/shard_map/ppermute | solution.py:785
  11.5 2.9 %shard_map.131 = (bf16[8,256,256]{2,1,0:T(8,128)(2,1)S(1)}, bf16[8,256,256]{2,1,0:T(8,128)(2,1)S(1)}, f32[8,32,256]{2,1,0:T(8,128)S(1)}, bf16[256,256]{1,0:T(8,1...) custom-call(f32[8,256,256]{2,1,0:T(8,128)S(1)} %bitcast.23, f32[8,8,256]{2,1,0:T(8,128)S(1)} %bitcast.28, ...), custom_call_target="tpu_custom_call" | custom-call | tf_op jit(solution)/shard_map/pallas_call | solution.py:758
  15.7 2.4 %collective-permute-done.x_ref = f32[2,40,128]{2,1,0:T(8,128)S(1)} collective-permute-done((f32[2,40,128]{2,1,0:T(8,128)S(1)}, f32[2,40,128]{2,1,0:T(8,128)S(1)}, u32[]{:S(2)}, u32[]{:S(2)}) %collective-permute-start) | collective-permute-done | bytes 40992 | tf_op jit(solution)/shard_map/ppermute | solution.py:770
  27.0 6.1 %all-to-all-start = ((f32[32,12,128]{2,1,0:T(8,128)}), f32[32,12,128]{2,1,0:T(8,128)S(1)}, u32[]{:S(2)}, u32[]{:S(2)}) async-start(f32[32,12,128]{2,1,0:T(8,128)} %reshape.89), calls=%async_computation | async-start | bytes 524288 | tf_op jit(solution)/shard_map/all_to_all | solution.py:806
  33.1 1.8 collective-permute-start.3
  36.4 2.7 %collective-permute-done.3.x_ref = f32[2,72,128]{2,1,0:T(8,128)S(1)} collective-permute-done((f32[2,72,128]{2,1,0:T(8,128)}, f32[2,72,128]{2,1,0:T(8,128)S(1)}, u32[]{:S(2)}, u32[]{:S(2)}) %collective-permute-start.3) | collective-permute-done | bytes 73760 | tf_op jit(solution)/shard_map/ppermute | solution.py:770
  58.2 2.1 shard_map.135
  67.5 6.0 %all-to-all-start.1 = ((f32[32,4,128]{2,1,0:T(4,128)}), f32[32,4,128]{2,1,0:T(4,128)}, u32[]{:S(2)}, u32[]{:S(2)}) async-start(f32[32,4,128]{2,1,0:T(4,128)} %bitcast.35), calls=%async_computation.1 | async-start | bytes 131072 | tf_op jit(solution)/shard_map/all_to_all | solution.py:818
  73.6 1.8 collective-permute-start.7
  77.9 3.0 %all-to-all-done.1 = f32[32,4,128]{2,1,0:T(4,128)} async-done(((f32[32,4,128]{2,1,0:T(4,128)}), f32[32,4,128]{2,1,0:T(4,128)}, u32[]{:S(2)}, u32[]{:S(2)}) %all-to-all-start.1) | async-done | bytes 65568 | tf_op jit(solution)/shard_map/all_to_all | solution.py:818
  92.7 2.7 %shard_map.136 = (f32[8,16,256]{2,1,0:T(8,128)S(1)}, f32[8,16,256]{2,1,0:T(8,128)S(1)}, f32[8,16,256]{2,1,0:T(8,128)S(1)}, f32[8,16,256]{2,1,0:T(8,128)S(1)}, f3...) custom-call(f32[16,8,128]{2,1,0:T(8,128)} %bitcast.11.got_ref, ...), custom_call_target="tpu_custom_call" | custom-call | tf_op jit(solution)/shard_map/pallas_call | solution.py:758
  101.7 5.0 %all-to-all-start.2 = ((f32[32,4,128]{2,1,0:T(4,128)}), f32[32,4,128]{2,1,0:T(4,128)}, u32[]{:S(2)}, u32[]{:S(2)}) async-start(f32[32,4,128]{2,1,0:T(4,128)} %bitcast.32), calls=%async_computation.2 | async-start | bytes 131072 | tf_op jit(solution)/shard_map/all_to_all | solution.py:818
  111.0 3.0 %all-to-all-done.2 = f32[32,4,128]{2,1,0:T(4,128)} async-done(((f32[32,4,128]{2,1,0:T(4,128)}), f32[32,4,128]{2,1,0:T(4,128)}, u32[]{:S(2)}, u32[]{:S(2)}) %all-to-all-start.2) | async-done | bytes 65568 | tf_op jit(solution)/shard_map/all_to_all | solution.py:818
  125.8 2.7 %shard_map.137 = (f32[8,16,256]{2,1,0:T(8,128)S(1)}, f32[8,16,256]{2,1,0:T(8,128)S(1)}, f32[8,16,256]{2,1,0:T(8,128)S(1)}, f32[8,16,256]{2,1,0:T(8,128)S(1)}, f3...) custom-call(f32[16,8,128]{2,1,0:T(8,128)} %bitcast.13.got_ref, ...), custom_call_target="tpu_custom_call" | custom-call | tf_op jit(solution)/shard_map/pallas_call | solution.py:758
  134.8 5.0 %all-to-all-start.3 = ((f32[32,4,128]{2,1,0:T(4,128)}), f32[32,4,128]{2,1,0:T(4,128)}, u32[]{:S(2)}, u32[]{:S(2)}) async-start(f32[32,4,128]{2,1,0:T(4,128)} %bitcast.33), calls=%async_computation.3 | async-start | bytes 131072 | tf_op jit(solution)/shard_map/all_to_all | solution.py:818
  144.1 3.0 %all-to-all-done.3 = f32[32,4,128]{2,1,0:T(4,128)} async-done(((f32[32,4,128]{2,1,0:T(4,128)}), f32[32,4,128]{2,1,0:T(4,128)}, u32[]{:S(2)}, u32[]{:S(2)}) %all-to-all-start.3) | async-done | bytes 65568 | tf_op jit(solution)/shard_map/all_to_all | solution.py:818
  158.8 2.7 %shard_map.138 = (f32[8,16,256]{2,1,0:T(8,128)S(1)}, f32[8,16,256]{2,1,0:T(8,128)S(1)}, f32[8,16,256]{2,1,0:T(8,128)S(1)}, f32[8,16,256]{2,1,0:T(8,128)S(1)}, f3...) custom-call(f32[16,8,128]{2,1,0:T(8,128)} %bitcast.15.got_ref, ...), custom_call_target="tpu_custom_call" | custom-call | tf_op jit(solution)/shard_map/pallas_call | solution.py:758
  167.9 5.0 %all-to-all-start.4 = ((f32[32,4,128]{2,1,0:T(4,128)}), f32[32,4,128]{2,1,0:T(4,128)}, u32[]{:S(2)}, u32[]{:S(2)}) async-start(f32[32,4,128]{2,1,0:T(4,128)} %bitcast.34), calls=%async_computation.4 | async-start | bytes 131072 | tf_op jit(solution)/shard_map/all_to_all | solution.py:818
  177.2 3.0 %all-to-all-done.4 = f32[32,4,128]{2,1,0:T(4,128)} async-done(((f32[32,4,128]{2,1,0:T(4,128)}), f32[32,4,128]{2,1,0:T(4,128)}, u32[]{:S(2)}, u32[]{:S(2)}) %all-to-all-start.4) | async-done | bytes 65568 | tf_op jit(solution)/shard_map/all_to_all | solution.py:818
  191.9 2.7 %shard_map.139 = (f32[8,16,256]{2,1,0:T(8,128)S(1)}, f32[8,16,256]{2,1,0:T(8,128)S(1)}, f32[8,16,256]{2,1,0:T(8,128)S(1)}, f32[8,16,256]{2,1,0:T(8,128)S(1)}, f3...) custom-call(f32[16,8,128]{2,1,0:T(8,128)} %bitcast.17.got_ref, ...), custom_call_target="tpu_custom_call" | custom-call | tf_op jit(solution)/shard_map/pallas_call | solution.py:758
  201.0 4.8 %all-to-all-start.5 = ((f32[32,4,128]{2,1,0:T(4,128)}), f32[32,4,128]{2,1,0:T(4,128)S(1)}, u32[]{:S(2)}, u32[]{:S(2)}) async-start(f32[32,4,128]{2,1,0:T(4,128)} %bitcast.31), calls=%async_computation.5 | async-start | bytes 131072 | tf_op jit(solution)/shard_map/all_to_all | solution.py:818
  205.8 1.8 collective-permute-start.19
  209.9 3.4 %all-to-all-done.5 = f32[32,4,128]{2,1,0:T(4,128)S(1)} async-done(((f32[32,4,128]{2,1,0:T(4,128)}), f32[32,4,128]{2,1,0:T(4,128)S(1)}, u32[]{:S(2)}, u32[]{:S(2)}) %all-to-all-start.5) | async-done | bytes 65568 | tf_op jit(solution)/shard_map/all_to_all | solution.py:818
  221.7 2.0 shard_map.140
  (370 shorter events, 144.1 us)
Async XLA Ops:
  0.6 43.5 %collective-permute-start.6 = (f32[384,384]{1,0:T(8,128)}, f32[384,384]{1,0:T(8,128)S(1)}, u32[]{:S(2)}, u32[]{:S(2)}) collective-permute-start(f32[384,384]{1,0:T(8,128)} %bitcast.24), channel_id=1, source_target_pairs={{0,16},{16,0},{1,17},{17,1},{2,18},{18,2},{3,19},{19,3},{4,20},{20... | collective-permute-start | bytes 1769480 | tf_op jit(solution)/shard_map/ppermute | solution.py:785
  6.8 11.2 %collective-permute-start = (f32[2,40,128]{2,1,0:T(8,128)S(1)}, f32[2,40,128]{2,1,0:T(8,128)S(1)}, u32[]{:S(2)}, u32[]{:S(2)}) collective-permute-start(f32[2,40,128]{2,1,0:T(8,128)S(1)} %get-tuple-element.81), channel_id=1, source_target_pairs={{0,16},{16,0},{1,17},{17,1},{2,18},{18,2},{3,19},{19,3},{4,20},{20... | collective-permute-start | bytes 122888 | tf_op jit(solution)/shard_map/ppermute | solution.py:770
  6.9 7.5 %collective-permute-start.1 = (f32[40,128]{1,0:T(8,128)S(1)}, f32[40,128]{1,0:T(8,128)S(1)}, u32[]{:S(2)}, u32[]{:S(2)}) collective-permute-start(f32[40,128]{1,0:T(8,128)S(1)} %get-tuple-element.82), channel_id=1, source_target_pairs={{0,1},{2,3},{4,5},{6,7},{8,9},{10,11},{12,13},{14,15},{1,0},{3,2},... | collective-permute-start | bytes 61448 | tf_op jit(solution)/shard_map/ppermute | solution.py:771
  7.0 8.1 %collective-permute-start.2 = (f32[40,128]{1,0:T(8,128)S(1)}, f32[40,128]{1,0:T(8,128)S(1)}, u32[]{:S(2)}, u32[]{:S(2)}) collective-permute-start(f32[40,128]{1,0:T(8,128)S(1)} %get-tuple-element.83), channel_id=1, source_target_pairs={{1,2},{3,4},{5,6},{7,8},{9,10},{11,12},{13,14},{2,1},{4,3},{6,5},{... | collective-permute-start | bytes 61448 | tf_op jit(solution)/shard_map/ppermute | solution.py:772
  27.0 16.4 %all-to-all-start = ((f32[32,12,128]{2,1,0:T(8,128)}), f32[32,12,128]{2,1,0:T(8,128)S(1)}, u32[]{:S(2)}, u32[]{:S(2)}) async-start(f32[32,12,128]{2,1,0:T(8,128)} %reshape.89), calls=%async_computation | async-start | bytes 524288 | tf_op jit(solution)/shard_map/all_to_all | solution.py:806
  33.1 5.9 %collective-permute-start.3 = (f32[2,72,128]{2,1,0:T(8,128)}, f32[2,72,128]{2,1,0:T(8,128)S(1)}, u32[]{:S(2)}, u32[]{:S(2)}) collective-permute-start(f32[2,72,128]{2,1,0:T(8,128)} %copy-done.144), channel_id=1, source_target_pairs={{0,16},{16,0},{1,17},{17,1},{2,18},{18,2},{3,19},{19,3},{4,20},{20... | collective-permute-start | bytes 221192 | tf_op jit(solution)/shard_map/ppermute | solution.py:770
  34.9 1.4 collective-permute-start.4
  34.9 1.4 collective-permute-start.5
  67.5 13.4 %all-to-all-start.1 = ((f32[32,4,128]{2,1,0:T(4,128)}), f32[32,4,128]{2,1,0:T(4,128)}, u32[]{:S(2)}, u32[]{:S(2)}) async-start(f32[32,4,128]{2,1,0:T(4,128)} %bitcast.35), calls=%async_computation.1 | async-start | bytes 131072 | tf_op jit(solution)/shard_map/all_to_all | solution.py:818
  73.6 4.3 %collective-permute-start.7 = (f32[2,16,128]{2,1,0:T(8,128)}, f32[2,16,128]{2,1,0:T(8,128)S(1)}, u32[]{:S(2)}, u32[]{:S(2)}) collective-permute-start(f32[2,16,128]{2,1,0:T(8,128)} %copy-done.151), channel_id=1, source_target_pairs={{0,16},{16,0},{1,17},{17,1},{2,18},{18,2},{3,19},{19,3},{4,20},{20... | collective-permute-start | bytes 49160 | tf_op jit(solution)/shard_map/ppermute | solution.py:770
  75.3 1.4 collective-permute-start.8
  75.3 2.0 collective-permute-start.9
  101.7 12.3 %all-to-all-start.2 = ((f32[32,4,128]{2,1,0:T(4,128)}), f32[32,4,128]{2,1,0:T(4,128)}, u32[]{:S(2)}, u32[]{:S(2)}) async-start(f32[32,4,128]{2,1,0:T(4,128)} %bitcast.32), calls=%async_computation.2 | async-start | bytes 131072 | tf_op jit(solution)/shard_map/all_to_all | solution.py:818
  106.7 4.3 %collective-permute-start.10 = (f32[2,16,128]{2,1,0:T(8,128)}, f32[2,16,128]{2,1,0:T(8,128)S(1)}, u32[]{:S(2)}, u32[]{:S(2)}) collective-permute-start(f32[2,16,128]{2,1,0:T(8,128)} %copy-done.148), channel_id=1, source_target_pairs={{0,16},{16,0},{1,17},{17,1},{2,18},{18,2},{3,19},{19,3},{4,20},{20... | collective-permute-start | bytes 49160 | tf_op jit(solution)/shard_map/ppermute | solution.py:770
  108.4 1.4 collective-permute-start.11
  108.4 2.0 collective-permute-start.12
  134.8 12.3 %all-to-all-start.3 = ((f32[32,4,128]{2,1,0:T(4,128)}), f32[32,4,128]{2,1,0:T(4,128)}, u32[]{:S(2)}, u32[]{:S(2)}) async-start(f32[32,4,128]{2,1,0:T(4,128)} %bitcast.33), calls=%async_computation.3 | async-start | bytes 131072 | tf_op jit(solution)/shard_map/all_to_all | solution.py:818
  139.8 4.3 %collective-permute-start.13 = (f32[2,16,128]{2,1,0:T(8,128)}, f32[2,16,128]{2,1,0:T(8,128)S(1)}, u32[]{:S(2)}, u32[]{:S(2)}) collective-permute-start(f32[2,16,128]{2,1,0:T(8,128)} %copy-done.149), channel_id=1, source_target_pairs={{0,16},{16,0},{1,17},{17,1},{2,18},{18,2},{3,19},{19,3},{4,20},{20... | collective-permute-start | bytes 49160 | tf_op jit(solution)/shard_map/ppermute | solution.py:770
  141.5 2.0 collective-permute-start.15
  167.9 12.3 %all-to-all-start.4 = ((f32[32,4,128]{2,1,0:T(4,128)}), f32[32,4,128]{2,1,0:T(4,128)}, u32[]{:S(2)}, u32[]{:S(2)}) async-start(f32[32,4,128]{2,1,0:T(4,128)} %bitcast.34), calls=%async_computation.4 | async-start | bytes 131072 | tf_op jit(solution)/shard_map/all_to_all | solution.py:818
  172.8 4.3 %collective-permute-start.16 = (f32[2,16,128]{2,1,0:T(8,128)}, f32[2,16,128]{2,1,0:T(8,128)S(1)}, u32[]{:S(2)}, u32[]{:S(2)}) collective-permute-start(f32[2,16,128]{2,1,0:T(8,128)} %copy-done.150), channel_id=1, source_target_pairs={{0,16},{16,0},{1,17},{17,1},{2,18},{18,2},{3,19},{19,3},{4,20},{20... | collective-permute-start | bytes 49160 | tf_op jit(solution)/shard_map/ppermute | solution.py:770
  174.6 2.0 collective-permute-start.18
  201.0 12.2 %all-to-all-start.5 = ((f32[32,4,128]{2,1,0:T(4,128)}), f32[32,4,128]{2,1,0:T(4,128)S(1)}, u32[]{:S(2)}, u32[]{:S(2)}) async-start(f32[32,4,128]{2,1,0:T(4,128)} %bitcast.31), calls=%async_computation.5 | async-start | bytes 131072 | tf_op jit(solution)/shard_map/all_to_all | solution.py:818
  205.8 4.0 %collective-permute-start.19 = (f32[2,16,128]{2,1,0:T(8,128)}, f32[2,16,128]{2,1,0:T(8,128)S(1)}, u32[]{:S(2)}, u32[]{:S(2)}) collective-permute-start(f32[2,16,128]{2,1,0:T(8,128)} %copy-done.147), channel_id=1, source_target_pairs={{0,16},{16,0},{1,17},{17,1},{2,18},{18,2},{3,19},{19,3},{4,20},{20... | collective-permute-start | bytes 49160 | tf_op jit(solution)/shard_map/ppermute | solution.py:770
  (166 other events, 158.7 us)

commit v3 on v2

--- a/solution.py
+++ b/solution.py
@@ -278,7 +278,11 @@
     return jnp.dot(a, b, preferred_element_type=F32)
 
 
-def dot_split(v, high, low):
+def dot_turned(a, b):
+    return lax.dot_general(a, b, (((1,), (1,)), ((), ())), preferred_element_type=F32)
+
+
+def dot_split(v, high, low, dot=dot):
     n = v.shape[0]
     vh, vl = split(v)
     wide = dot(jnp.concatenate([vh, vl], 0), high)
@@ -321,12 +325,15 @@
     b_ref[rows, :] = jnp.where(even, south, north)
 
 
-def received(x_ref, a_ref, b_ref, at, n):
+def received(x_ref, a_ref, b_ref, at, n, side=None):
     rows = pl.ds(at, n)
     first = lax.axis_index("gx") == 0
     even = lax.axis_index("gy") % 2 == 0
     xs = [x_ref[t, rows, :] for t in range(SPAN_Y // 2)]
     a, b = a_ref[rows, :], b_ref[rows, :]
+    if side is not None:
+        a, b = a + side[:, :128], b + side[:, 128:256]
+        xs = [xs[t] + side[:, 256 + 128 * t : 384 + 128 * t] for t in range(SPAN_Y // 2)]
     zero = jnp.zeros_like(a)
     return (
         [jnp.where(first, zero, v) for v in xs],
@@ -405,7 +412,7 @@
     send(ys, x_ref, a_ref, b_ref, 0)
 
 
-def operator_kernel(schur_ref, couple_ref, map_ref, slot_ref, high_ref, low_ref, cc_ref, wh_ref, wl_ref, name_ref):
+def operator_kernel(schur_ref, couple_ref, map_ref, slot_ref, high_ref, low_ref, cc_ref, ch_ref, cl_ref, name_ref):
     none = 384
     slot = slot_ref[...].astype(F32)
     eye = iota((8, 8), 0) == iota((8, 8), 1)
@@ -428,9 +435,8 @@
     )
     sub = iota((256, 256), 0)
     west = (sub // 64) % 2 == 0
-    all_cc = []
     for i in range(SUBS):
-        spots = map_ref[i : i + 1, :]
+        spots = map_ref[i // SPAN_Y, i % SPAN_Y : i % SPAN_Y + 1, :]
         if odd(i):
             spots = jnp.where((spots // 64) % 2 == 0, spots + 64, spots - 64)
         sign = jnp.where(west, 1.0, -1.0) if odd(i) else jnp.where(west, -1.0, 1.0)
@@ -444,15 +450,12 @@
         c1, rest = split(cc)
         c2, c3 = split(cc - c1.astype(F32))
         s1, s2 = split(schur_ref[i])
-        tall = lax.dot_general(
-            jnp.concatenate([s1, s2, c1, c2, c3], 0), place, (((1,), (1,)), ((), ())), preferred_element_type=F32
-        )
+        tall = dot_turned(jnp.concatenate([s1, s2, c1, c2, c3], 0), place)
         high_ref[i] = dot(place, tall[:256].astype(BF16)).astype(BF16)
         low_ref[i] = dot(place, tall[256:512].astype(BF16)).astype(BF16)
         cc = tall[512 : 512 + SLOTS] + tall[512 + SLOTS : 512 + 2 * SLOTS] + tall[512 + 2 * SLOTS :]
         cc_ref[i] = cc
-        all_cc.append(cc)
-    wh_ref[...], wl_ref[...] = split(jnp.transpose(jnp.concatenate(all_cc, 0)))
+        ch_ref[i], cl_ref[i] = split(cc)
 
 
 def inverse_kernel(mine_ref, other_ref, high_ref, low_ref):
@@ -462,38 +465,46 @@
     high_ref[1], low_ref[1] = split(jnp.where(first, other, mine))
 
 
-def spread_kernel(cc_ref, name_ref, mk_ref, x_ref, a_ref, b_ref, high_ref, low_ref, near_ref):
-    at = 2 * CASES
-    cc = [cc_ref[i] for i in range(SUBS)]
-    inside = across(cc, None, SLOTS)
-    nb = received(x_ref, a_ref, b_ref, at, SLOTS)
-    blank = jnp.zeros((SLOTS, 128), F32)
-    blanks = [blank] * (SPAN_Y // 2)
-    even = lax.axis_index("gy") % 2 == 0
-    by_x = across(None, (nb[0], nb[1], blank, blank), SLOTS)
-    a_low, a_high = jnp.where(even, 0.0, 1.0), jnp.where(even, 1.0, 0.0)
-    by_a = across(None, (blanks, blanks, nb[2] * a_low, nb[3] * a_high), SLOTS)
-    by_b = across(None, (blanks, blanks, nb[2] * a_high, nb[3] * a_low), SLOTS)
-    for i in range(SUBS):
-        keep = mk_ref[i, 1:2, :]
-        whole = jnp.concatenate([cc[i] + inside[i], by_a[i], by_b[i], by_x[i]], 0) * keep
-        high_ref[i], low_ref[i] = split(whole)
-    named = pl.ds(at + SLOTS, 1)
-    group = iota((1, 128), 1) // SLOTS
-    turn = lambda v, g: pltpu.roll(jnp.broadcast_to(v, (8, 128)), g * SLOTS, 1)[0:1]
-    names = [turn(name_ref[0:1, :], 0), turn(a_ref[named, :], 1), turn(b_ref[named, :], 2), turn(x_ref[0, named, :], 3)]
-    wanted = jnp.where(group == 0, names[0], jnp.where(group == 1, names[1], jnp.where(group == 2, names[2], names[3])))
-    found = iota((384, 128), 0).astype(F32) == wanted
+def near_names(name_ref, x_ref, a_ref, b_ref, near_ref):
+    named = pl.ds(2 * CASES + SLOTS, 8)
+    group = iota((8, 128), 1) // SLOTS
+    turn = lambda v, g: jnp.where(group == g, pltpu.roll(v, g * SLOTS, 1), 0.0)
+    wanted = name_ref[...] + 0.0
+    wanted = jnp.where(group == 0, wanted, turn(a_ref[named, :], 1) + turn(b_ref[named, :], 2) + turn(x_ref[0, named, :], 3))
+    found = iota((384, 128), 0).astype(F32) == wanted[0:1]
     mine = jnp.where(iota((384, 128), 1) < 3 * SLOTS, 1.0, 0.0)
     gx = lax.axis_index("gx")
     for region in range(2):
         near_ref[region] = jnp.where(found, jnp.where(gx == region, mine, 1.0 - mine), 0.0).astype(BF16)
 
 
-def local_part(us, rs, high_ref, low_ref, wh_ref, wl_ref):
+def near_spread(x_ref, a_ref, b_ref, nh_ref, nl_ref):
+    rows = pl.ds(2 * CASES, SLOTS)
+    blank = jnp.zeros((SLOTS, 128), F32)
+    parts = [
+        [blank] * 4,
+        [a_ref[rows, :], blank, blank, blank],
+        [blank, b_ref[rows, :], blank, blank],
+        [blank, blank, x_ref[0, rows, :], x_ref[1, rows, :]],
+    ]
+    nh_ref[...], nl_ref[...] = split(jnp.concatenate([jnp.concatenate(row, 1) for row in parts], 0))
+
+
+def operator(ys, x_ref, a_ref, b_ref, near, mk_ref, ch_ref, cl_ref, nh_ref, nl_ref):
+    n = ys[0].shape[0]
+    side = dot_split(near, nh_ref[...], nl_ref[...])
+    west, east, south, north = received(x_ref, a_ref, b_ref, 0, n, side)
+    mine = near[:, :SLOTS]
+    ys = [ys[i] + dot_split(mine, ch_ref[i], cl_ref[i]) for i in range(SUBS)]
+    other = across(ys, (west, east, south, north), n)
+    return [mk_ref[i, 1:2, :] * (ys[i] + other[i]) for i in range(SUBS)]
+
+
+def local_part(us, high_ref, low_ref, ch_ref, cl_ref):
     ys = [dot_split(us[i], high_ref[i], low_ref[i]) for i in range(SUBS)]
     n = us[0].shape[0]
-    corner = dot_split(jnp.concatenate(us, 0), wh_ref[...], wl_ref[...])
+    couple = lambda ref: jnp.concatenate([ref[i] for i in range(SUBS)], 0)
+    corner = dot_split(jnp.concatenate(us, 0), couple(ch_ref), couple(cl_ref), dot_turned)
     group = iota((n, 128), 1) // SLOTS
     total = jnp.zeros((n, 128), F32)
     for i in range(SUBS):
@@ -577,22 +588,24 @@
     return first_of_pairs(jnp.sum(both, 1, keepdims=True))
 
 
-def emit(rs, mk_ref, high_ref, low_ref, wh_ref, wl_ref, block_ref, y_ref, x_ref, a_ref, b_ref):
+def emit(rs, mk_ref, high_ref, low_ref, ch_ref, cl_ref, block_ref, y_ref, x_ref, a_ref, b_ref):
     us = [mk_ref[i, 0:1, :] * rs[i] for i in range(SUBS)]
-    ys, corner = local_part(us, rs, high_ref, low_ref, wh_ref, wl_ref)
+    ys, corner = local_part(us, high_ref, low_ref, ch_ref, cl_ref)
     send(ys, x_ref, a_ref, b_ref, 0)
+    for i in range(SUBS):
+        y_ref[i] = ys[i]
+    for ref in (x_ref, a_ref, b_ref, y_ref):
+        ref.flush()
     rho = over_lanes([jnp.where(owned_lanes(i, CASES), rs[i] * us[i], 0.0) for i in range(SUBS)])
     delta = over_lanes([us[i] * ys[i] for i in range(SUBS)])
     block = packed(corner, rho, delta)
     twice = jnp.concatenate([block, block], 0)
     for j in range(16):
         block_ref[j] = twice
-    for i in range(SUBS):
-        y_ref[i] = ys[i]
 
 
 def first_kernel(
-    own_ref, x_ref, a_ref, b_ref, high_ref, low_ref, cc_ref, wh_ref, wl_ref, name_ref,
+    own_ref, x_ref, a_ref, b_ref, high_ref, low_ref, cc_ref, ch_ref, cl_ref, name_ref,
     r_ref, p_ref, mk_ref, y_ref, block_ref, sx_ref, sa_ref, sb_ref,
 ):
     own = [own_ref[i] for i in range(SUBS)]
@@ -605,7 +618,7 @@
         p_ref[i] = full[CASES : 2 * CASES]
         mk_ref[i] = full[2 * CASES : 2 * CASES + 8]
         vs.append(jnp.concatenate([full[2 * CASES : 2 * CASES + 1] * full[:CASES], full[CASES : 2 * CASES]], 0))
-    ys, corner = local_part(vs, rs, high_ref, low_ref, wh_ref, wl_ref)
+    ys, corner = local_part(vs, high_ref, low_ref, ch_ref, cl_ref)
     names = name_ref[...]
     send([jnp.concatenate([ys[i], cc_ref[i]], 0) for i in range(SUBS)], sx_ref, sa_ref, sb_ref, 0)
     at = pl.ds(2 * CASES + SLOTS, 8)
@@ -643,10 +656,12 @@
 
 
 def second_kernel(
-    got_ref, x_ref, a_ref, b_ref, y_ref, r_ref, p_ref, mk_ref, dual_ref, rho_ref, gh_ref, gl_ref, near_ref, dh_ref, dl_ref,
-    high_ref, low_ref, wh_ref, wl_ref,
-    pick_ref, ro_ref, so_ref, po_ref, lo_ref, scal_ref, block_ref, yo_ref, sx_ref, sa_ref, sb_ref,
+    got_ref, x_ref, a_ref, b_ref, y_ref, r_ref, p_ref, mk_ref, dual_ref, rho_ref, gh_ref, gl_ref, name_ref,
+    high_ref, low_ref, ch_ref, cl_ref,
+    pick_ref, near_ref, nh_ref, nl_ref, ro_ref, so_ref, po_ref, lo_ref, scal_ref, block_ref, yo_ref, sx_ref, sa_ref, sb_ref,
 ):
+    near_names(name_ref, x_ref, a_ref, b_ref, near_ref)
+    near_spread(x_ref, a_ref, b_ref, nh_ref, nl_ref)
     top = iota((8, 128), 0) < 4
     us, ps, names = [], [], []
     for j in range(16):
@@ -684,12 +699,10 @@
     skew = cross + beta * eta
     pi = delta + 2.0 * beta * skew - beta * beta * eta
     alpha = rho / pi
-    ys = [y_ref[i] for i in range(SUBS)]
-    other = across(ys, received(x_ref, a_ref, b_ref, 0, 2 * CASES), 2 * CASES)
+    fs = operator([y_ref[i] for i in range(SUBS)], x_ref, a_ref, b_ref, near, mk_ref, ch_ref, cl_ref, nh_ref, nl_ref)
     rs = []
     for i in range(SUBS):
-        f = mk_ref[i, 1:2, :] * (ys[i] + other[i]) + dot_split(near, dh_ref[i], dl_ref[i])
-        r = r_ref[i]
+        f, r = fs[i], r_ref[i]
         p = mk_ref[i, 0:1, :] * r + beta * p_ref[i]
         s = f[:CASES] + beta * f[CASES:]
         r = r - alpha * s
@@ -697,10 +710,12 @@
         ro_ref[i], so_ref[i], po_ref[i] = r, s, p
         lo_ref[i] = spread_owned(dual_ref[pl.ds(i, CASES, stride=SUBS), :], i) + alpha * p
     keep_scalars(scal_ref, (rho, pi, beta, skew))
-    emit(rs, mk_ref, high_ref, low_ref, wh_ref, wl_ref, block_ref, yo_ref, sx_ref, sa_ref, sb_ref)
-
-
-def absorb(got_ref, x_ref, a_ref, b_ref, y_ref, r_ref, s_ref, p_ref, l_ref, scal_ref, mk_ref, pick_ref, gh_ref, gl_ref, near_ref, dh_ref, dl_ref):
+    for ref in (pick_ref, near_ref, nh_ref, nl_ref, ro_ref, so_ref, po_ref, lo_ref, scal_ref):
+        ref.flush()
+    emit(rs, mk_ref, high_ref, low_ref, ch_ref, cl_ref, block_ref, yo_ref, sx_ref, sa_ref, sb_ref)
+
+
+def absorb(got_ref, x_ref, a_ref, b_ref, y_ref, r_ref, s_ref, p_ref, l_ref, scal_ref, mk_ref, pick_ref, gh_ref, gl_ref, near_ref, nh_ref, nl_ref, ch_ref, cl_ref):
     vs = [got_ref[j] for j in range(16)]
     totals, sols, near = solve(by_slot(vs), pick_ref, gh_ref, gl_ref, near_ref)
     rho, delta = inner(vs)
@@ -711,40 +726,40 @@
     beta = rho / rho_old
     pi = delta + 2.0 * beta * skew - beta * beta * pi
     alpha = rho / pi
-    ys = [y_ref[i] for i in range(SUBS)]
-    other = across(ys, received(x_ref, a_ref, b_ref, 0, CASES), CASES)
+    fs = operator([y_ref[i] for i in range(SUBS)], x_ref, a_ref, b_ref, near, mk_ref, ch_ref, cl_ref, nh_ref, nl_ref)
     out = []
     for i in range(SUBS):
-        f = mk_ref[i, 1:2, :] * (ys[i] + other[i]) + dot_split(near, dh_ref[i], dl_ref[i])
         r = r_ref[i]
         p = mk_ref[i, 0:1, :] * r + beta * p_ref[i]
-        s = f + beta * s_ref[i]
+        s = fs[i] + beta * s_ref[i]
         out.append((r - alpha * s, s, p, l_ref[i] + alpha * p))
     return out, (rho, pi, beta, skew)
 
 
 def round_kernel(
     got_ref, x_ref, a_ref, b_ref, y_ref, r_ref, s_ref, p_ref, l_ref, scal_ref, mk_ref, pick_ref, gh_ref, gl_ref, near_ref,
-    dh_ref, dl_ref, high_ref, low_ref, wh_ref, wl_ref,
+    nh_ref, nl_ref, ch_ref, cl_ref, high_ref, low_ref,
     ro_ref, so_ref, po_ref, lo_ref, scalo_ref, block_ref, yo_ref, sx_ref, sa_ref, sb_ref,
 ):
     out, scalars = absorb(
         got_ref, x_ref, a_ref, b_ref, y_ref, r_ref, s_ref, p_ref, l_ref, scal_ref, mk_ref, pick_ref, gh_ref, gl_ref, near_ref,
-        dh_ref, dl_ref,
+        nh_ref, nl_ref, ch_ref, cl_ref,
     )
     for i, (r, s, p, lam) in enumerate(out):
         ro_ref[i], so_ref[i], po_ref[i], lo_ref[i] = r, s, p, lam
     keep_scalars(scalo_ref, scalars)
-    emit([v[0] for v in out], mk_ref, high_ref, low_ref, wh_ref, wl_ref, block_ref, yo_ref, sx_ref, sa_ref, sb_ref)
+    for ref in (ro_ref, so_ref, po_ref, lo_ref, scalo_ref):
+        ref.flush()
+    emit([v[0] for v in out], mk_ref, high_ref, low_ref, ch_ref, cl_ref, block_ref, yo_ref, sx_ref, sa_ref, sb_ref)
 
 
 def last_kernel(
     got_ref, x_ref, a_ref, b_ref, y_ref, r_ref, s_ref, p_ref, l_ref, scal_ref, mk_ref, pick_ref, gh_ref, gl_ref, near_ref,
-    dh_ref, dl_ref, lo_ref, ro_ref, po_ref,
+    nh_ref, nl_ref, ch_ref, cl_ref, lo_ref, ro_ref, po_ref,
 ):
     out, _ = absorb(
         got_ref, x_ref, a_ref, b_ref, y_ref, r_ref, s_ref, p_ref, l_ref, scal_ref, mk_ref, pick_ref, gh_ref, gl_ref, near_ref,
-        dh_ref, dl_ref,
+        nh_ref, nl_ref, ch_ref, cl_ref,
     )
     for i, (r, _, p, lam) in enumerate(out):
         mine = pl.ds(i, CASES, stride=SUBS)
@@ -753,13 +768,82 @@
         po_ref[mine, :] = take_owned(p, i)
 
 
-def call(kernel, args, outs):
-    vmem = pl.BlockSpec(memory_space=pltpu.VMEM)
+class Fetched:
+    def __init__(self, source, buffer, semaphore):
+        self.buffer = buffer
+        self.copy = pltpu.make_async_copy(source, buffer, semaphore)
+        self.copy.start()
+        self.here = False
+
+    def __getitem__(self, index):
+        if not self.here:
+            self.copy.wait()
+            self.here = True
+        return self.buffer[index]
+
+
+class Stored:
+    def __init__(self, target, buffer, semaphore):
+        self.buffer = buffer
+        self.copy = pltpu.make_async_copy(buffer, target, semaphore)
+        self.sent = False
+
+    def __setitem__(self, index, value):
+        self.buffer[index] = value
+
+    def __getitem__(self, index):
+        return self.buffer[index]
+
+    def flush(self):
+        if not self.sent:
+            self.copy.start()
+            self.sent = True
+
+
+class Kept:
+    def __init__(self, ref):
+        self.ref = ref
+
+    def __setitem__(self, index, value):
+        self.ref[index] = value
+
+    def flush(self):
+        pass
+
+
+def call(kernel, args, outs, kept=(), kept_out=()):
+    moved = [i for i in range(len(args)) if i not in kept]
+    written = [i for i in range(len(outs)) if i not in kept_out]
+
+    def body(*refs):
+        ins, results = refs[: len(args)], refs[len(args) : len(args) + len(outs)]
+        buffers, (in_sem, out_sem) = refs[len(args) + len(outs) : -2], refs[-2:]
+        fetched, stored = list(ins), [Kept(ref) for ref in results]
+        for t, i in enumerate(moved):
+            fetched[i] = Fetched(ins[i], buffers[t], in_sem.at[t])
+        for t, i in enumerate(written):
+            stored[i] = Stored(results[i], buffers[len(moved) + t], out_sem.at[t])
+        kernel(*fetched, *stored)
+        for i in written:
+            stored[i].flush()
+        for i in moved:
+            if not fetched[i].here:
+                fetched[i].copy.wait()
+        for i in written:
+            stored[i].copy.wait()
+
+    place = lambda held: pl.BlockSpec(memory_space=pltpu.VMEM if held else pltpu.HBM)
+    args = [a if i in kept else pltpu.with_memory_space_constraint(a, pltpu.HBM) for i, a in enumerate(args)]
     return pl.pallas_call(
-        kernel,
-        out_shape=[jax.ShapeDtypeStruct(shape, kind) for shape, kind in outs],
-        in_specs=[vmem] * len(args),
-        out_specs=[vmem] * len(outs),
+        body,
+        out_shape=[
+            jax.ShapeDtypeStruct(*out) if i in kept_out else pltpu.HBM(*out) for i, out in enumerate(outs)
+        ],
+        in_specs=[place(i in kept) for i in range(len(args))],
+        out_specs=[place(i in kept_out) for i in range(len(outs))],
+        scratch_shapes=[pltpu.VMEM(args[i].shape, args[i].dtype) for i in moved]
+        + [pltpu.VMEM(*outs[i]) for i in written]
+        + [pltpu.SemaphoreType.DMA((max(len(moved), 1),)), pltpu.SemaphoreType.DMA((max(len(written), 1),))],
         compiler_params=pltpu.CompilerParams(vmem_limit_bytes=LIMIT),
     )(*args)
 
@@ -790,39 +874,42 @@
     )
     come = trade(*out)
     matrix = ((SUBS, 256, 256), BF16)
-    high, low, cc, wh, wl, names = call(
+    couple = ((SUBS, SLOTS, 256), BF16)
+    high, low, cc, ch, cl, names = call(
         operator_kernel,
-        [by_sub(dual_schur), by_sub(coupling), by_sub(edge_map), by_sub(corner_slot)],
-        [matrix, matrix, ((SUBS, SLOTS, 256), F32), ((256, 256), BF16), ((256, 256), BF16), ((8, 128), F32)],
+        [by_sub(dual_schur), by_sub(coupling), edge_map, by_sub(corner_slot)],
+        [matrix, matrix, ((SUBS, SLOTS, 256), F32), couple, couple, ((8, 128), F32)],
+        kept_out=(0, 1),
     )
     square = ((2, width, width), BF16)
-    gh, gl = call(inverse_kernel, [coarse_inverse[0], other], [square, square])
+    gh, gl = call(inverse_kernel, [coarse_inverse[0], other], [square, square], kept_out=(0, 1))
     rows = 2 * CASES + SLOTS + 8
     r, p, mk, y, block, *out = call(
         first_kernel,
-        [own, *come, high, low, cc, wh, wl, names],
+        [own, *come, high, low, cc, ch, cl, names],
         [state, state, ((SUBS, 8, 256), F32), ((SUBS, 2 * CASES, 256), F32), ((48, 8, 128), F32)] + sends(rows),
+        kept=(4, 5),
     )
     got = lax.all_to_all(block.reshape(32, 12, 128), BOTH, 0, 0, tiled=False).reshape(48, 8, 128)
     come = trade(*out)
-    wide = ((SUBS, 128, 256), BF16)
-    dh, dl, near = call(spread_kernel, [cc, names, mk, *come], [wide, wide, ((2, width, 128), BF16)])
-    weights = [high, low, wh, wl]
+    side = ((128, 512), BF16)
+    weights = [ch, cl, high, low]
     onward = [state, state, state, state, ((4, CASES, 128), F32), ((16, 8, 128), F32), state] + sends(CASES)
-    pick, r, s, p, lam, scal, block, y, *out = call(
+    pick, near, nh, nl, r, s, p, lam, scal, block, y, *out = call(
         second_kernel,
-        [got, *come, y, r, p, mk, native(duals), prev_rho.reshape(1, CASES), gh, gl, near, dh, dl, *weights],
-        [((2, 2, 256, width), BF16)] + onward,
+        [got, *come, y, r, p, mk, native(duals), prev_rho.reshape(1, CASES), gh, gl, names, high, low, ch, cl],
+        [((2, 2, 256, width), BF16), ((2, width, 128), BF16), side, side] + onward,
+        kept=(10, 11, 13, 14),
     )
     for step in range(1, ITERS):
         got = lax.all_to_all(block.reshape(32, 4, 128), BOTH, 0, 0, tiled=False).reshape(16, 8, 128)
         come = trade(*out)
-        args = [got, *come, y, r, s, p, lam, scal, mk, pick, gh, gl, near, dh, dl]
+        args = [got, *come, y, r, s, p, lam, scal, mk, pick, gh, gl, near, nh, nl, ch, cl]
         if step < ITERS - 1:
-            r, s, p, lam, scal, block, y, *out = call(round_kernel, args + weights, onward)
+            r, s, p, lam, scal, block, y, *out = call(round_kernel, args + [high, low], onward, kept=(12, 13, 19, 20))
         else:
             plain = ((CASES * SUBS, 128), F32)
-            results = call(last_kernel, args, [plain, plain, plain])
+            results = call(last_kernel, args, [plain, plain, plain], kept=(12, 13))
     return tuple(v.reshape(duals.shape) for v in results)
 
 

time: 227 us -> 132 us (0.58); the launches traced: 224 us -> 131 us
  local copies, waits for them, and re-layouts: 127 us -> 6.72 us
  Pallas kernels: 19 us -> 39.9 us
  waiting for transfers between devices: 26.3 us -> 38.9 us
  starting transfers between devices: 50.4 us -> 44.5 us
    unnamed x324 -> x52, local copies, waits for them, and re-layouts: 125 us -> 4.39 us
    pallas_call x11 -> x10, Pallas kernels: 19 us -> 39.9 us  [call(): pl.pallas_call(body, out_shape=[jax.ShapeDtypeStruct(*out) if i in kept_o...]
    all_to_all x1, waiting for transfers between devices: 0.67 us -> 7.8 us  [two_regions(): lax.all_to_all(block.reshape(32, 12, 128), BOTH, 0, 0, tiled=False)]
    all_to_all x5, starting transfers between devices: 25.7 us -> 19.9 us  [two_regions(): lax.all_to_all(block.reshape(32, 4, 128), BOTH, 0, 0, tiled=False)]
    ppermute x7, waiting for transfers between devices: 5.88 us -> 10.8 us  [trade(): lax.ppermute(x, 'gx', [(0, 1), (1, 0)])]
  transfers between devices with their start and end apart: 28 -> 28, of which waited for: 15 -> 17; matrix products, arithmetic and copies ran while one was open for 1% -> 2% of each run, Pallas kernels for 2% -> 9%
where the time goes in v3:
time: 132 us; the launch traced here: 131 us
  starting transfers between devices  44.5 us (34%)
  Pallas kernels  39.9 us (30%)
  waiting for transfers between devices  38.9 us (29%)
  local copies, waits for them, and re-layouts  6.72 us (5%)
    pallas_call x10, Pallas kernels, call(): pl.pallas_call(body, out_shape=[jax.ShapeDtypeStruct(*out) if i in kept_o...  39.9 us
    all_to_all x5, starting transfers between devices, two_regions(): lax.all_to_all(block.reshape(32, 4, 128), BOTH, 0, 0, tiled=False)  19.9 us
    all_to_all x5, waiting for transfers between devices, two_regions(): lax.all_to_all(block.reshape(32, 4, 128), BOTH, 0, 0, tiled=False)  16.7 us
    ppermute x7, starting transfers between devices, trade(): lax.ppermute(x, 'gx', [(0, 1), (1, 0)])  10.8 us
    ppermute x7, waiting for transfers between devices, trade(): lax.ppermute(x, 'gx', [(0, 1), (1, 0)])  10.8 us
    all_to_all x1, waiting for transfers between devices, two_regions(): lax.all_to_all(block.reshape(32, 12, 128), BOTH, 0, 0, tiled=False)  7.8 us
    all_to_all x1, starting transfers between devices, two_regions(): lax.all_to_all(block.reshape(32, 12, 128), BOTH, 0, 0, tiled=False)  6.07 us
    ppermute x7, starting transfers between devices, trade(): lax.ppermute(b, 'gy', both_ways(pairs_from(1, peers)))  4.56 us
  transfers between devices with their start and end apart: 28, of which 17 were waited for; matrix products, arithmetic and copies ran while one was open for 2% of the time, Pallas kernels for 9%

profile of v3, /device:TPU:0, one launch (start us, length us, event | category | flops | bytes accessed | tf_op | source)
XLA Modules:
  0.0 131.1 jit_solution(17847682145071297835)
XLA Ops:
  0.6 3.0 %collective-permute-start.6 = (f32[384,384]{1,0:T(8,128)}, f32[384,384]{1,0:T(8,128)}, u32[]{:S(2)}, u32[]{:S(2)}) collective-permute-start(f32[384,384]{1,0:T(8,128)} %bitcast.24), channel_id=1, source_target_pairs={{0,16},{16,0},{1,17},{17,1},{2,18},{18,2},{3,19},{19,3},{4,20},{20... | collective-permute-start | bytes 1769480 | tf_op jit(solution)/shard_map/ppermute | solution.py:869
  6.3 5.3 %shard_map.131 = (bf16[8,256,256]{2,1,0:T(8,128)(2,1)S(1)}, bf16[8,256,256]{2,1,0:T(8,128)(2,1)S(1)}, f32[8,32,256]{2,1,0:T(8,128)}, bf16[8,32,256]{2,1,0:T(8,12...) custom-call(f32[8,256,256]{2,1,0:T(8,128)} %bitcast.23, f32[8,8,256]{2,1,0:T(8,128)} %bitcast.32, ...), custom_call_target="tpu_custom_call" | custom-call | tf_op jit(solution)/shard_map/pallas_call | solution.py:837
  11.6 6.5 %collective-permute-done.refs_1_ = f32[2,40,128]{2,1,0:T(8,128)S(1)} collective-permute-done((f32[2,40,128]{2,1,0:T(8,128)}, f32[2,40,128]{2,1,0:T(8,128)S(1)}, u32[]{:S(2)}, u32[]{:S(2)}) %collective-permute-start) | collective-permute-done | bytes 40992 | tf_op jit(solution)/shard_map/ppermute | solution.py:854
  18.7 3.0 %shard_map.132 = (f32[8,16,256]{2,1,0:T(8,128)}, f32[8,16,256]{2,1,0:T(8,128)}, f32[8,8,256]{2,1,0:T(8,128)}, f32[8,32,256]{2,1,0:T(8,128)}, f32[48,8,128]{2,1,0...) custom-call(f32[8,40,256]{2,1,0:T(8,128)} %get-tuple-element.80.refs_0_, ...), custom_call_target="tpu_custom_call" | custom-call | tf_op jit(solution)/shard_map/pallas_call | solution.py:837
  23.4 6.1 %all-to-all-start = ((f32[32,12,128]{2,1,0:T(8,128)}), f32[32,12,128]{2,1,0:T(8,128)S(1)}, u32[]{:S(2)}, u32[]{:S(2)}) async-start(f32[32,12,128]{2,1,0:T(8,128)} %reshape.85), calls=%async_computation | async-start | bytes 524288 | tf_op jit(solution)/shard_map/all_to_all | solution.py:893
  31.9 7.8 %all-to-all-done = f32[32,12,128]{2,1,0:T(8,128)S(1)} async-done(((f32[32,12,128]{2,1,0:T(8,128)}), f32[32,12,128]{2,1,0:T(8,128)S(1)}, u32[]{:S(2)}, u32[]{:S(2)}) %all-to-all-start) | async-done | bytes 196640 | tf_op jit(solution)/shard_map/all_to_all | solution.py:893
  42.6 5.0 %shard_map.134 = (bf16[2,2,256,384]{3,2,1,0:T(8,128)(2,1)}, bf16[2,384,128]{2,1,0:T(8,128)(2,1)}, bf16[128,512]{1,0:T(8,128)(2,1)}, bf16[128,512]{1,0:T(8,128)(2...) custom-call(f32[48,8,128]{2,1,0:T(8,128)} %reshape.86.refs_0_, ...), custom_call_target="tpu_custom_call" | custom-call | tf_op jit(solution)/shard_map/pallas_call | solution.py:837
  47.7 2.6 %all-to-all-start.1 = ((f32[32,4,128]{2,1,0:T(4,128)}), f32[32,4,128]{2,1,0:T(4,128)S(1)}, u32[]{:S(2)}, u32[]{:S(2)}) async-start(f32[32,4,128]{2,1,0:T(4,128)} %bitcast.35), calls=%async_computation.1 | async-start | bytes 131072 | tf_op jit(solution)/shard_map/all_to_all | solution.py:905
  54.3 3.4 %all-to-all-done.1 = f32[32,4,128]{2,1,0:T(4,128)S(1)} async-done(((f32[32,4,128]{2,1,0:T(4,128)}), f32[32,4,128]{2,1,0:T(4,128)S(1)}, u32[]{:S(2)}, u32[]{:S(2)}) %all-to-all-start.1) | async-done | bytes 65568 | tf_op jit(solution)/shard_map/all_to_all | solution.py:905
  58.3 4.8 %shard_map.135 = (f32[8,16,256]{2,1,0:T(8,128)}, f32[8,16,256]{2,1,0:T(8,128)}, f32[8,16,256]{2,1,0:T(8,128)}, f32[8,16,256]{2,1,0:T(8,128)}, f32[4,16,128]{2,1,...) custom-call(f32[16,8,128]{2,1,0:T(8,128)} %bitcast.28, ...), custom_call_target="tpu_custom_call" | custom-call | tf_op jit(solution)/shard_map/pallas_call | solution.py:837
  63.1 4.3 %all-to-all-start.2 = ((f32[32,4,128]{2,1,0:T(4,128)}), f32[32,4,128]{2,1,0:T(4,128)S(1)}, u32[]{:S(2)}, u32[]{:S(2)}) async-start(f32[32,4,128]{2,1,0:T(4,128)} %bitcast.37), calls=%async_computation.2 | async-start | bytes 131072 | tf_op jit(solution)/shard_map/all_to_all | solution.py:905
  67.4 1.8 %collective-permute-start.10 = (f32[2,16,128]{2,1,0:T(8,128)}, f32[2,16,128]{2,1,0:T(8,128)S(1)}, u32[]{:S(2)}, u32[]{:S(2)}) collective-permute-start(f32[2,16,128]{2,1,0:T(8,128)} %get-tuple-element.115), channel_id=1, source_target_pairs={{0,16},{16,0},{1,17},{17,1},{2,18},{18,2},{3,19},{19,3},{4,20},{20... | collective-permute-start | bytes 49160 | tf_op jit(solution)/shard_map/ppermute | solution.py:854
  71.5 3.4 %all-to-all-done.2 = f32[32,4,128]{2,1,0:T(4,128)S(1)} async-done(((f32[32,4,128]{2,1,0:T(4,128)}), f32[32,4,128]{2,1,0:T(4,128)S(1)}, u32[]{:S(2)}, u32[]{:S(2)}) %all-to-all-start.2) | async-done | bytes 65568 | tf_op jit(solution)/shard_map/all_to_all | solution.py:905
  75.5 4.8 %shard_map.136 = (f32[8,16,256]{2,1,0:T(8,128)}, f32[8,16,256]{2,1,0:T(8,128)}, f32[8,16,256]{2,1,0:T(8,128)}, f32[8,16,256]{2,1,0:T(8,128)}, f32[4,16,128]{2,1,...) custom-call(f32[16,8,128]{2,1,0:T(8,128)} %bitcast.29, ...), custom_call_target="tpu_custom_call" | custom-call | tf_op jit(solution)/shard_map/pallas_call | solution.py:837
  80.3 4.3 %all-to-all-start.3 = ((f32[32,4,128]{2,1,0:T(4,128)}), f32[32,4,128]{2,1,0:T(4,128)S(1)}, u32[]{:S(2)}, u32[]{:S(2)}) async-start(f32[32,4,128]{2,1,0:T(4,128)} %bitcast.38), calls=%async_computation.3 | async-start | bytes 131072 | tf_op jit(solution)/shard_map/all_to_all | solution.py:905
  88.7 3.4 %all-to-all-done.3 = f32[32,4,128]{2,1,0:T(4,128)S(1)} async-done(((f32[32,4,128]{2,1,0:T(4,128)}), f32[32,4,128]{2,1,0:T(4,128)S(1)}, u32[]{:S(2)}, u32[]{:S(2)}) %all-to-all-start.3) | async-done | bytes 65568 | tf_op jit(solution)/shard_map/all_to_all | solution.py:905
  92.7 4.8 %shard_map.137 = (f32[8,16,256]{2,1,0:T(8,128)}, f32[8,16,256]{2,1,0:T(8,128)}, f32[8,16,256]{2,1,0:T(8,128)}, f32[8,16,256]{2,1,0:T(8,128)}, f32[4,16,128]{2,1,...) custom-call(f32[16,8,128]{2,1,0:T(8,128)} %bitcast.30, ...), custom_call_target="tpu_custom_call" | custom-call | tf_op jit(solution)/shard_map/pallas_call | solution.py:837
  97.5 4.5 %all-to-all-start.4 = ((f32[32,4,128]{2,1,0:T(4,128)}), f32[32,4,128]{2,1,0:T(4,128)S(1)}, u32[]{:S(2)}, u32[]{:S(2)}) async-start(f32[32,4,128]{2,1,0:T(4,128)} %bitcast.39), calls=%async_computation.4 | async-start | bytes 131072 | tf_op jit(solution)/shard_map/all_to_all | solution.py:905
  106.0 3.2 %all-to-all-done.4 = f32[32,4,128]{2,1,0:T(4,128)S(1)} async-done(((f32[32,4,128]{2,1,0:T(4,128)}), f32[32,4,128]{2,1,0:T(4,128)S(1)}, u32[]{:S(2)}, u32[]{:S(2)}) %all-to-all-start.4) | async-done | bytes 65568 | tf_op jit(solution)/shard_map/all_to_all | solution.py:905
  109.8 4.8 %shard_map.138 = (f32[8,16,256]{2,1,0:T(8,128)}, f32[8,16,256]{2,1,0:T(8,128)}, f32[8,16,256]{2,1,0:T(8,128)}, f32[8,16,256]{2,1,0:T(8,128)}, f32[4,16,128]{2,1,...) custom-call(f32[16,8,128]{2,1,0:T(8,128)} %bitcast.26, ...), custom_call_target="tpu_custom_call" | custom-call | tf_op jit(solution)/shard_map/pallas_call | solution.py:837
  114.6 4.3 %all-to-all-start.5 = ((f32[32,4,128]{2,1,0:T(4,128)}), f32[32,4,128]{2,1,0:T(4,128)S(1)}, u32[]{:S(2)}, u32[]{:S(2)}) async-start(f32[32,4,128]{2,1,0:T(4,128)} %bitcast.36), calls=%async_computation.5 | async-start | bytes 131072 | tf_op jit(solution)/shard_map/all_to_all | solution.py:905
  119.0 1.8 %collective-permute-start.19 = (f32[2,16,128]{2,1,0:T(8,128)}, f32[2,16,128]{2,1,0:T(8,128)S(1)}, u32[]{:S(2)}, u32[]{:S(2)}) collective-permute-start(f32[2,16,128]{2,1,0:T(8,128)} %get-tuple-element.145), channel_id=1, source_target_pairs={{0,16},{16,0},{1,17},{17,1},{2,18},{18,2},{3,19},{19,3},{4,20},{20... | collective-permute-start | bytes 49160 | tf_op jit(solution)/shard_map/ppermute | solution.py:854
  123.0 3.4 %all-to-all-done.5 = f32[32,4,128]{2,1,0:T(4,128)S(1)} async-done(((f32[32,4,128]{2,1,0:T(4,128)}), f32[32,4,128]{2,1,0:T(4,128)S(1)}, u32[]{:S(2)}, u32[]{:S(2)}) %all-to-all-start.5) | async-done | bytes 65568 | tf_op jit(solution)/shard_map/all_to_all | solution.py:905
  127.0 4.0 %shard_map.139 = (f32[128,128]{1,0:T(8,128)}, f32[128,128]{1,0:T(8,128)}, f32[128,128]{1,0:T(8,128)}) custom-call(f32[16,8,128]{2,1,0:T(8,128)} %bitcast.27, f32[2,16,128]{2,1,0:T(8,128)} %copy-done.12, f32[16,128]{1,0:T(8,128)} %copy-done.17, f32[16,128]{1,0:T(8,128)} %copy-done.22, f32[8,16,256]{2,1,0:T(8,128)} %get-tuple-element.148.refs_4_, ...), custom_call_target="tpu_custom_call" | custom-call | tf_op jit(solution)/shard_map/pallas_call | solution.py:837
  (96 shorter events, 29.8 us)
Async XLA Ops:
  0.6 39.8 %collective-permute-start.6 = (f32[384,384]{1,0:T(8,128)}, f32[384,384]{1,0:T(8,128)}, u32[]{:S(2)}, u32[]{:S(2)}) collective-permute-start(f32[384,384]{1,0:T(8,128)} %bitcast.24), channel_id=1, source_target_pairs={{0,16},{16,0},{1,17},{17,1},{2,18},{18,2},{3,19},{19,3},{4,20},{20... | collective-permute-start | bytes 1769480 | tf_op jit(solution)/shard_map/ppermute | solution.py:869
  5.5 12.6 %collective-permute-start = (f32[2,40,128]{2,1,0:T(8,128)}, f32[2,40,128]{2,1,0:T(8,128)S(1)}, u32[]{:S(2)}, u32[]{:S(2)}) collective-permute-start(f32[2,40,128]{2,1,0:T(8,128)} %get-tuple-element.81), channel_id=1, source_target_pairs={{0,16},{16,0},{1,17},{17,1},{2,18},{18,2},{3,19},{19,3},{4,20},{20... | collective-permute-start | bytes 122888 | tf_op jit(solution)/shard_map/ppermute | solution.py:854
  5.5 6.0 %collective-permute-start.1 = (f32[40,128]{1,0:T(8,128)}, f32[40,128]{1,0:T(8,128)S(1)}, u32[]{:S(2)}, u32[]{:S(2)}) collective-permute-start(f32[40,128]{1,0:T(8,128)} %get-tuple-element.82), channel_id=1, source_target_pairs={{0,1},{2,3},{4,5},{6,7},{8,9},{10,11},{12,13},{14,15},{1,0},{3,2},... | collective-permute-start | bytes 61448 | tf_op jit(solution)/shard_map/ppermute | solution.py:855
  5.6 6.0 %collective-permute-start.2 = (f32[40,128]{1,0:T(8,128)}, f32[40,128]{1,0:T(8,128)S(1)}, u32[]{:S(2)}, u32[]{:S(2)}) collective-permute-start(f32[40,128]{1,0:T(8,128)} %get-tuple-element.83), channel_id=1, source_target_pairs={{1,2},{3,4},{5,6},{7,8},{9,10},{11,12},{13,14},{2,1},{4,3},{6,5},{... | collective-permute-start | bytes 61448 | tf_op jit(solution)/shard_map/ppermute | solution.py:856
  23.4 16.4 %all-to-all-start = ((f32[32,12,128]{2,1,0:T(8,128)}), f32[32,12,128]{2,1,0:T(8,128)S(1)}, u32[]{:S(2)}, u32[]{:S(2)}) async-start(f32[32,12,128]{2,1,0:T(8,128)} %reshape.85), calls=%async_computation | async-start | bytes 524288 | tf_op jit(solution)/shard_map/all_to_all | solution.py:893
  29.4 12.6 %collective-permute-start.3 = (f32[2,72,128]{2,1,0:T(8,128)}, f32[2,72,128]{2,1,0:T(8,128)S(1)}, u32[]{:S(2)}, u32[]{:S(2)}) collective-permute-start(f32[2,72,128]{2,1,0:T(8,128)} %get-tuple-element.91), channel_id=1, source_target_pairs={{0,16},{16,0},{1,17},{17,1},{2,18},{18,2},{3,19},{19,3},{4,20},{20... | collective-permute-start | bytes 221192 | tf_op jit(solution)/shard_map/ppermute | solution.py:854
  31.3 10.7 %collective-permute-start.4 = (f32[72,128]{1,0:T(8,128)}, f32[72,128]{1,0:T(8,128)S(1)}, u32[]{:S(2)}, u32[]{:S(2)}) collective-permute-start(f32[72,128]{1,0:T(8,128)} %get-tuple-element.92), channel_id=1, source_target_pairs={{0,1},{2,3},{4,5},{6,7},{8,9},{10,11},{12,13},{14,15},{1,0},{3,2},... | collective-permute-start | bytes 110600 | tf_op jit(solution)/shard_map/ppermute | solution.py:855
  31.3 10.7 %collective-permute-start.5 = (f32[72,128]{1,0:T(8,128)}, f32[72,128]{1,0:T(8,128)S(1)}, u32[]{:S(2)}, u32[]{:S(2)}) collective-permute-start(f32[72,128]{1,0:T(8,128)} %get-tuple-element.93), channel_id=1, source_target_pairs={{1,2},{3,4},{5,6},{7,8},{9,10},{11,12},{13,14},{2,1},{4,3},{6,5},{... | collective-permute-start | bytes 110600 | tf_op jit(solution)/shard_map/ppermute | solution.py:856
  47.7 10.0 %all-to-all-start.1 = ((f32[32,4,128]{2,1,0:T(4,128)}), f32[32,4,128]{2,1,0:T(4,128)S(1)}, u32[]{:S(2)}, u32[]{:S(2)}) async-start(f32[32,4,128]{2,1,0:T(4,128)} %bitcast.35), calls=%async_computation.1 | async-start | bytes 131072 | tf_op jit(solution)/shard_map/all_to_all | solution.py:905
  50.3 4.0 %collective-permute-start.7 = (f32[2,16,128]{2,1,0:T(8,128)}, f32[2,16,128]{2,1,0:T(8,128)S(1)}, u32[]{:S(2)}, u32[]{:S(2)}) collective-permute-start(f32[2,16,128]{2,1,0:T(8,128)} %get-tuple-element.101), channel_id=1, source_target_pairs={{0,16},{16,0},{1,17},{17,1},{2,18},{18,2},{3,19},{19,3},{4,20},{20... | collective-permute-start | bytes 49160 | tf_op jit(solution)/shard_map/ppermute | solution.py:854
  52.0 1.4 %collective-permute-start.8 = (f32[16,128]{1,0:T(8,128)}, f32[16,128]{1,0:T(8,128)S(1)}, u32[]{:S(2)}, u32[]{:S(2)}) collective-permute-start(f32[16,128]{1,0:T(8,128)} %get-tuple-element.102), channel_id=1, source_target_pairs={{0,1},{2,3},{4,5},{6,7},{8,9},{10,11},{12,13},{14,15},{1,0},{3,2},... | collective-permute-start | bytes 24584 | tf_op jit(solution)/shard_map/ppermute | solution.py:855
  52.0 1.4 %collective-permute-start.9 = (f32[16,128]{1,0:T(8,128)}, f32[16,128]{1,0:T(8,128)S(1)}, u32[]{:S(2)}, u32[]{:S(2)}) collective-permute-start(f32[16,128]{1,0:T(8,128)} %get-tuple-element.103), channel_id=1, source_target_pairs={{1,2},{3,4},{5,6},{7,8},{9,10},{11,12},{13,14},{2,1},{4,3},{6,5},{... | collective-permute-start | bytes 24584 | tf_op jit(solution)/shard_map/ppermute | solution.py:856
  63.1 11.7 %all-to-all-start.2 = ((f32[32,4,128]{2,1,0:T(4,128)}), f32[32,4,128]{2,1,0:T(4,128)S(1)}, u32[]{:S(2)}, u32[]{:S(2)}) async-start(f32[32,4,128]{2,1,0:T(4,128)} %bitcast.37), calls=%async_computation.2 | async-start | bytes 131072 | tf_op jit(solution)/shard_map/all_to_all | solution.py:905
  67.4 4.0 %collective-permute-start.10 = (f32[2,16,128]{2,1,0:T(8,128)}, f32[2,16,128]{2,1,0:T(8,128)S(1)}, u32[]{:S(2)}, u32[]{:S(2)}) collective-permute-start(f32[2,16,128]{2,1,0:T(8,128)} %get-tuple-element.115), channel_id=1, source_target_pairs={{0,16},{16,0},{1,17},{17,1},{2,18},{18,2},{3,19},{19,3},{4,20},{20... | collective-permute-start | bytes 49160 | tf_op jit(solution)/shard_map/ppermute | solution.py:854
  69.3 1.4 %collective-permute-start.12 = (f32[16,128]{1,0:T(8,128)}, f32[16,128]{1,0:T(8,128)S(1)}, u32[]{:S(2)}, u32[]{:S(2)}) collective-permute-start(f32[16,128]{1,0:T(8,128)} %get-tuple-element.117), channel_id=1, source_target_pairs={{1,2},{3,4},{5,6},{7,8},{9,10},{11,12},{13,14},{2,1},{4,3},{6,5},{... | collective-permute-start | bytes 24584 | tf_op jit(solution)/shard_map/ppermute | solution.py:856
  80.3 11.7 %all-to-all-start.3 = ((f32[32,4,128]{2,1,0:T(4,128)}), f32[32,4,128]{2,1,0:T(4,128)S(1)}, u32[]{:S(2)}, u32[]{:S(2)}) async-start(f32[32,4,128]{2,1,0:T(4,128)} %bitcast.38), calls=%async_computation.3 | async-start | bytes 131072 | tf_op jit(solution)/shard_map/all_to_all | solution.py:905
  84.6 4.0 %collective-permute-start.13 = (f32[2,16,128]{2,1,0:T(8,128)}, f32[2,16,128]{2,1,0:T(8,128)S(1)}, u32[]{:S(2)}, u32[]{:S(2)}) collective-permute-start(f32[2,16,128]{2,1,0:T(8,128)} %get-tuple-element.125), channel_id=1, source_target_pairs={{0,16},{16,0},{1,17},{17,1},{2,18},{18,2},{3,19},{19,3},{4,20},{20... | collective-permute-start | bytes 49160 | tf_op jit(solution)/shard_map/ppermute | solution.py:854
  86.5 1.4 %collective-permute-start.15 = (f32[16,128]{1,0:T(8,128)}, f32[16,128]{1,0:T(8,128)S(1)}, u32[]{:S(2)}, u32[]{:S(2)}) collective-permute-start(f32[16,128]{1,0:T(8,128)} %get-tuple-element.127), channel_id=1, source_target_pairs={{1,2},{3,4},{5,6},{7,8},{9,10},{11,12},{13,14},{2,1},{4,3},{6,5},{... | collective-permute-start | bytes 24584 | tf_op jit(solution)/shard_map/ppermute | solution.py:856
  97.5 11.7 %all-to-all-start.4 = ((f32[32,4,128]{2,1,0:T(4,128)}), f32[32,4,128]{2,1,0:T(4,128)S(1)}, u32[]{:S(2)}, u32[]{:S(2)}) async-start(f32[32,4,128]{2,1,0:T(4,128)} %bitcast.39), calls=%async_computation.4 | async-start | bytes 131072 | tf_op jit(solution)/shard_map/all_to_all | solution.py:905
  102.0 4.0 %collective-permute-start.16 = (f32[2,16,128]{2,1,0:T(8,128)}, f32[2,16,128]{2,1,0:T(8,128)S(1)}, u32[]{:S(2)}, u32[]{:S(2)}) collective-permute-start(f32[2,16,128]{2,1,0:T(8,128)} %get-tuple-element.135), channel_id=1, source_target_pairs={{0,16},{16,0},{1,17},{17,1},{2,18},{18,2},{3,19},{19,3},{4,20},{20... | collective-permute-start | bytes 49160 | tf_op jit(solution)/shard_map/ppermute | solution.py:854
  103.6 1.4 %collective-permute-start.18 = (f32[16,128]{1,0:T(8,128)}, f32[16,128]{1,0:T(8,128)S(1)}, u32[]{:S(2)}, u32[]{:S(2)}) collective-permute-start(f32[16,128]{1,0:T(8,128)} %get-tuple-element.137), channel_id=1, source_target_pairs={{1,2},{3,4},{5,6},{7,8},{9,10},{11,12},{13,14},{2,1},{4,3},{6,5},{... | collective-permute-start | bytes 24584 | tf_op jit(solution)/shard_map/ppermute | solution.py:856
  114.6 11.7 %all-to-all-start.5 = ((f32[32,4,128]{2,1,0:T(4,128)}), f32[32,4,128]{2,1,0:T(4,128)S(1)}, u32[]{:S(2)}, u32[]{:S(2)}) async-start(f32[32,4,128]{2,1,0:T(4,128)} %bitcast.36), calls=%async_computation.5 | async-start | bytes 131072 | tf_op jit(solution)/shard_map/all_to_all | solution.py:905
  119.0 4.0 %collective-permute-start.19 = (f32[2,16,128]{2,1,0:T(8,128)}, f32[2,16,128]{2,1,0:T(8,128)S(1)}, u32[]{:S(2)}, u32[]{:S(2)}) collective-permute-start(f32[2,16,128]{2,1,0:T(8,128)} %get-tuple-element.145), channel_id=1, source_target_pairs={{0,16},{16,0},{1,17},{17,1},{2,18},{18,2},{3,19},{19,3},{4,20},{20... | collective-permute-start | bytes 49160 | tf_op jit(solution)/shard_map/ppermute | solution.py:854
  120.8 1.4 %collective-permute-start.21 = (f32[16,128]{1,0:T(8,128)}, f32[16,128]{1,0:T(8,128)S(1)}, u32[]{:S(2)}, u32[]{:S(2)}) collective-permute-start(f32[16,128]{1,0:T(8,128)} %get-tuple-element.147), channel_id=1, source_target_pairs={{1,2},{3,4},{5,6},{7,8},{9,10},{11,12},{13,14},{2,1},{4,3},{6,5},{... | collective-permute-start | bytes 24584 | tf_op jit(solution)/shard_map/ppermute | solution.py:856
  (30 other events, 82.9 us)

commit v4 on v3

--- a/solution.py
+++ b/solution.py
@@ -263,6 +263,7 @@
 USED = 2 * (SPAN_X + 1) * (SPAN_Y + 1)
 CAST = 40
 LIMIT = 16 * 1024 * 1024
+UPPER = [(i, j) for i in range(3) for j in range(i, 3)]
 
 
 def iota(shape, dim):
@@ -382,7 +383,9 @@
     return jnp.where(low, pltpu.roll(v[:, :128], 64, 1), v[:, 128:])
 
 
-def start_kernel(res_ref, dir_ref, act_ref, scale_ref, own_ref, x_ref, a_ref, b_ref):
+def start_kernel(res_ref, dir_ref, act_ref, scale_ref, *refs):
+    inverse_ref, own_ref, x_ref, a_ref, b_ref = refs[4:9]
+    upper_ref = refs[13]
     gx, gy = lax.axis_index("gx"), lax.axis_index("gy")
     last_x = gx * SPAN_X + SPAN_X - 1 == lax.axis_size("gx") * SPAN_X - 1
     last_y = gy * SPAN_Y + SPAN_Y - 1 == lax.axis_size("gy") * SPAN_Y - 1
@@ -410,9 +413,15 @@
         own_ref[i] = v
         ys.append(v)
     send(ys, x_ref, a_ref, b_ref, 0)
-
-
-def operator_kernel(schur_ref, couple_ref, map_ref, slot_ref, high_ref, low_ref, cc_ref, ch_ref, cl_ref, name_ref):
+    for ref in (x_ref, a_ref, b_ref):
+        ref.flush()
+    for t, (i, j) in enumerate(UPPER):
+        upper_ref[t] = inverse_ref[128 * i : 128 * i + 128, 128 * j : 128 * j + 128]
+
+
+def operator_kernel(
+    schur_ref, couple_ref, map_ref, slot_ref, high_ref, low_ref, cc_ref, ch_ref, cl_ref, name_ref,
+):
     none = 384
     slot = slot_ref[...].astype(F32)
     eye = iota((8, 8), 0) == iota((8, 8), 1)
@@ -451,16 +460,19 @@
         c2, c3 = split(cc - c1.astype(F32))
         s1, s2 = split(schur_ref[i])
         tall = dot_turned(jnp.concatenate([s1, s2, c1, c2, c3], 0), place)
-        high_ref[i] = dot(place, tall[:256].astype(BF16)).astype(BF16)
-        low_ref[i] = dot(place, tall[256:512].astype(BF16)).astype(BF16)
+        high, low = (dot(place, tall[t : t + 256].astype(BF16)).astype(BF16) for t in (0, 256))
+        high_ref[i], low_ref[i] = high, low
         cc = tall[512 : 512 + SLOTS] + tall[512 + SLOTS : 512 + 2 * SLOTS] + tall[512 + 2 * SLOTS :]
         cc_ref[i] = cc
         ch_ref[i], cl_ref[i] = split(cc)
 
 
-def inverse_kernel(mine_ref, other_ref, high_ref, low_ref):
+def inverse_kernel(mine_ref, upper_ref, high_ref, low_ref):
     first = lax.axis_index("gx") == 0
-    mine, other = mine_ref[...], other_ref[...]
+    mine = mine_ref[...]
+    blocks = {spot: upper_ref[t] for t, spot in enumerate(UPPER)}
+    side = lambda i, j: blocks[i, j] if i <= j else jnp.transpose(blocks[j, i])
+    other = jnp.concatenate([jnp.concatenate([side(i, j) for j in range(3)], 1) for i in range(3)], 0)
     high_ref[0], low_ref[0] = split(jnp.where(first, mine, other))
     high_ref[1], low_ref[1] = split(jnp.where(first, other, mine))
 
@@ -606,7 +618,7 @@
 
 def first_kernel(
     own_ref, x_ref, a_ref, b_ref, high_ref, low_ref, cc_ref, ch_ref, cl_ref, name_ref,
-    r_ref, p_ref, mk_ref, y_ref, block_ref, sx_ref, sa_ref, sb_ref,
+    r_ref, p_ref, mk_ref, y_ref, block_ref, sx_ref, sa_ref, sb_ref, high_out_ref, low_out_ref,
 ):
     own = [own_ref[i] for i in range(SUBS)]
     other = across(own, received(x_ref, a_ref, b_ref, 0, CAST), CAST)
@@ -807,32 +819,44 @@
     def __setitem__(self, index, value):
         self.ref[index] = value
 
+    def __getitem__(self, index):
+        return self.ref[index]
+
     def flush(self):
         pass
 
 
-def call(kernel, args, outs, kept=(), kept_out=()):
-    moved = [i for i in range(len(args)) if i not in kept]
-    written = [i for i in range(len(outs)) if i not in kept_out]
+def call(kernel, args, outs, kept=(), kept_out=(), raw=(), through=None, flops=None):
+    through = through or {}
+    moved = [i for i in range(len(args)) if i not in kept and i not in raw]
+    written = [i for i in range(len(outs)) if i not in kept_out and i not in through]
 
     def body(*refs):
         ins, results = refs[: len(args)], refs[len(args) : len(args) + len(outs)]
-        buffers, (in_sem, out_sem) = refs[len(args) + len(outs) : -2], refs[-2:]
+        buffers, (in_sem, out_sem, through_sem) = refs[len(args) + len(outs) : -3], refs[-3:]
         fetched, stored = list(ins), [Kept(ref) for ref in results]
         for t, i in enumerate(moved):
             fetched[i] = Fetched(ins[i], buffers[t], in_sem.at[t])
         for t, i in enumerate(written):
             stored[i] = Stored(results[i], buffers[len(moved) + t], out_sem.at[t])
+        passing = [
+            pltpu.make_async_copy(source(ins), results[i], through_sem.at[t]) for t, (i, source) in enumerate(through.items())
+        ]
+        for copy in passing:
+            copy.start()
         kernel(*fetched, *stored)
         for i in written:
             stored[i].flush()
         for i in moved:
             if not fetched[i].here:
                 fetched[i].copy.wait()
+        for copy in passing:
+            copy.wait()
         for i in written:
             stored[i].copy.wait()
 
     place = lambda held: pl.BlockSpec(memory_space=pltpu.VMEM if held else pltpu.HBM)
+    semaphores = lambda n: pltpu.SemaphoreType.DMA((max(n, 1),))
     args = [a if i in kept else pltpu.with_memory_space_constraint(a, pltpu.HBM) for i, a in enumerate(args)]
     return pl.pallas_call(
         body,
@@ -843,8 +867,9 @@
         out_specs=[place(i in kept_out) for i in range(len(outs))],
         scratch_shapes=[pltpu.VMEM(args[i].shape, args[i].dtype) for i in moved]
         + [pltpu.VMEM(*outs[i]) for i in written]
-        + [pltpu.SemaphoreType.DMA((max(len(moved), 1),)), pltpu.SemaphoreType.DMA((max(len(written), 1),))],
+        + [semaphores(len(moved)), semaphores(len(written)), semaphores(len(through))],
         compiler_params=pltpu.CompilerParams(vmem_limit_bytes=LIMIT),
+        cost_estimate=flops and pl.CostEstimate(flops=flops, bytes_accessed=flops // 512, transcendentals=0),
     )(*args)
 
 
@@ -866,50 +891,61 @@
     sends = lambda rows: [((SPAN_Y // 2, rows, 128), F32), ((rows, 128), F32), ((rows, 128), F32)]
     state = ((SUBS, CASES, 256), F32)
 
-    other = lax.ppermute(coarse_inverse[0], "gx", [(0, 1), (1, 0)])
-    own, *out = call(
+    raw = [by_sub(dual_schur), by_sub(coupling), edge_map, by_sub(corner_slot)]
+    own, *out, schur, coupled, placed, slotted, inverse = call(
         start_kernel,
-        [native(residual), native(direction), by_sub(active), by_sub(scaling)],
-        [((SUBS, CAST, 256), F32)] + sends(CAST),
+        [native(residual), native(direction), by_sub(active), by_sub(scaling), *raw, coarse_inverse[0]],
+        [((SUBS, CAST, 256), F32)] + sends(CAST) + [(v.shape, v.dtype) for v in raw] + [((len(UPPER), 128, 128), F32)],
+        kept_out=(0, 4, 5, 6, 7),
+        raw=(4, 5, 6, 7),
+        through={4: lambda v: v[4], 5: lambda v: v[5], 6: lambda v: v[6], 7: lambda v: v[7]},
     )
     come = trade(*out)
+    other = lax.ppermute(inverse, "gx", [(0, 1), (1, 0)])
     matrix = ((SUBS, 256, 256), BF16)
     couple = ((SUBS, SLOTS, 256), BF16)
     high, low, cc, ch, cl, names = call(
         operator_kernel,
-        [by_sub(dual_schur), by_sub(coupling), edge_map, by_sub(corner_slot)],
+        [schur, coupled, placed, slotted],
         [matrix, matrix, ((SUBS, SLOTS, 256), F32), couple, couple, ((8, 128), F32)],
-        kept_out=(0, 1),
-    )
-    square = ((2, width, width), BF16)
-    gh, gl = call(inverse_kernel, [coarse_inverse[0], other], [square, square], kept_out=(0, 1))
+        kept=range(4),
+        kept_out=range(6),
+        flops=5 * 10**9,
+    )
     rows = 2 * CASES + SLOTS + 8
-    r, p, mk, y, block, *out = call(
+    r, p, mk, y, block, *out, high, low = call(
         first_kernel,
         [own, *come, high, low, cc, ch, cl, names],
-        [state, state, ((SUBS, 8, 256), F32), ((SUBS, 2 * CASES, 256), F32), ((48, 8, 128), F32)] + sends(rows),
-        kept=(4, 5),
-    )
-    got = lax.all_to_all(block.reshape(32, 12, 128), BOTH, 0, 0, tiled=False).reshape(48, 8, 128)
+        [state, state, ((SUBS, 8, 256), F32), ((SUBS, 2 * CASES, 256), F32), ((48, 8, 128), F32)]
+        + sends(rows)
+        + [matrix, matrix],
+        kept=range(10),
+        kept_out=(2, 3),
+        through={8: lambda v: v[4], 9: lambda v: v[5]},
+    )
+    got = lax.all_to_all(block.reshape(32, 3, 4, 128), BOTH, 0, 0, tiled=False).reshape(48, 8, 128)
     come = trade(*out)
+    square = ((2, width, width), BF16)
+    gh, gl = call(inverse_kernel, [coarse_inverse[0], other], [square, square], kept_out=(0, 1), flops=10**9)
     side = ((128, 512), BF16)
-    weights = [ch, cl, high, low]
     onward = [state, state, state, state, ((4, CASES, 128), F32), ((16, 8, 128), F32), state] + sends(CASES)
     pick, near, nh, nl, r, s, p, lam, scal, block, y, *out = call(
         second_kernel,
         [got, *come, y, r, p, mk, native(duals), prev_rho.reshape(1, CASES), gh, gl, names, high, low, ch, cl],
         [((2, 2, 256, width), BF16), ((2, width, 128), BF16), side, side] + onward,
-        kept=(10, 11, 13, 14),
+        kept=(0, 1, 2, 3, 4, 7, 10, 11, 12, 15, 16),
+        kept_out=(0, 1, 2, 3, 8, 10),
     )
     for step in range(1, ITERS):
         got = lax.all_to_all(block.reshape(32, 4, 128), BOTH, 0, 0, tiled=False).reshape(16, 8, 128)
         come = trade(*out)
         args = [got, *come, y, r, s, p, lam, scal, mk, pick, gh, gl, near, nh, nl, ch, cl]
+        kept = (0, 1, 2, 3, 4, *range(9, 19))
         if step < ITERS - 1:
-            r, s, p, lam, scal, block, y, *out = call(round_kernel, args + [high, low], onward, kept=(12, 13, 19, 20))
+            r, s, p, lam, scal, block, y, *out = call(round_kernel, args + [high, low], onward, kept, kept_out=(4, 6))
         else:
             plain = ((CASES * SUBS, 128), F32)
-            results = call(last_kernel, args, [plain, plain, plain], kept=(12, 13))
+            results = call(last_kernel, args, [plain, plain, plain], kept)
     return tuple(v.reshape(duals.shape) for v in results)
 
 

time: 132 us -> 112 us (0.85)
  waiting for transfers between devices: 38.9 us -> 28.8 us
  Pallas kernels: 39.9 us -> 33.3 us
  local copies, waits for them, and re-layouts: 6.72 us -> 0.75 us
  starting transfers between devices: 44.5 us -> 47.2 us
    pallas_call x10, Pallas kernels: 39.9 us -> 33.3 us  [call(): pl.pallas_call(body, out_shape=[jax.ShapeDtypeStruct(*out) if i in kept_o...]
    ppermute x7, waiting for transfers between devices: 10.8 us -> 5.12 us  [trade(): lax.ppermute(x, 'gx', [(0, 1), (1, 0)])]
    all_to_all x1, waiting for transfers between devices: 7.8 us -> 3.24 us  [two_regions(): lax.all_to_all(block.reshape(32, 3, 4, 128), BOTH, 0, 0, tiled=False)]
    unnamed x52 -> x2, local copies, waits for them, and re-layouts: 4.39 us -> 0.75 us
    ppermute x7, starting transfers between devices: 10.8 us -> 14 us  [trade(): lax.ppermute(x, 'gx', [(0, 1), (1, 0)])]
    ppermute x1, starting transfers between devices: 3.03 us -> 0.16 us  [two_regions(): other = lax.ppermute(inverse, 'gx', [(0, 1), (1, 0)])]
    reshape x2 -> x0, local copies, waits for them, and re-layouts: 2.33 us -> none  [the longest x1 1.64 us: two_regions(): block.reshape(32, 12, 128)]
    all_to_all x1, starting transfers between devices: 6.07 us -> 8.15 us  [two_regions(): lax.all_to_all(block.reshape(32, 3, 4, 128), BOTH, 0, 0, tiled=False)]
  transfers between devices with their start and end apart: 28 -> 28, of which waited for: 17 -> 17; matrix products, arithmetic and copies ran while one was open for 2% -> 0% of each run, Pallas kernels for 9% -> 5%
where the time goes in v4:
time: 112 us; the launch traced here: 111 us
  starting transfers between devices  47.2 us (42%)
  Pallas kernels  33.3 us (30%)
  waiting for transfers between devices  28.8 us (26%)
    pallas_call x10, Pallas kernels, call(): pl.pallas_call(body, out_shape=[jax.ShapeDtypeStruct(*out) if i in kept_o...  33.3 us
    all_to_all x5, starting transfers between devices, two_regions(): lax.all_to_all(block.reshape(32, 4, 128), BOTH, 0, 0, tiled=False)  20.2 us
    all_to_all x5, waiting for transfers between devices, two_regions(): lax.all_to_all(block.reshape(32, 4, 128), BOTH, 0, 0, tiled=False)  16.8 us
    ppermute x7, starting transfers between devices, trade(): lax.ppermute(x, 'gx', [(0, 1), (1, 0)])  14 us
    all_to_all x1, starting transfers between devices, two_regions(): lax.all_to_all(block.reshape(32, 3, 4, 128), BOTH, 0, 0, tiled=False)  8.15 us
    ppermute x7, waiting for transfers between devices, trade(): lax.ppermute(x, 'gx', [(0, 1), (1, 0)])  5.12 us
    ppermute x7, starting transfers between devices, trade(): lax.ppermute(b, 'gy', both_ways(pairs_from(1, peers)))  4.55 us
    ppermute x7, waiting for transfers between devices, trade(): lax.ppermute(a, 'gy', both_ways(pairs_from(0, peers)))  3.62 us
  transfers between devices with their start and end apart: 28, of which 17 were waited for; matrix products, arithmetic and copies ran while one was open for 0% of the time, Pallas kernels for 5%

profile of v4, /device:TPU:0, one launch (start us, length us, event | category | flops | bytes accessed | tf_op | source)
XLA Modules:
  0.0 110.8 jit_solution(1330310155419285220)
XLA Ops:
  0.6 2.7 %shard_map.130 = (f32[8,40,256]{2,1,0:T(8,128)S(1)}, f32[2,40,128]{2,1,0:T(8,128)}, f32[40,128]{1,0:T(8,128)}, f32[40,128]{1,0:T(8,128)}, f32[8,256,256]{2,1,0:T...) custom-call(f32[128,128]{1,0:T(8,128)} %bitcast.36, ...), custom_call_target="tpu_custom_call" | custom-call | tf_op jit(solution)/shard_map/pallas_call | solution.py:861
  3.3 3.0 %collective-permute-start = (f32[2,40,128]{2,1,0:T(8,128)}, f32[2,40,128]{2,1,0:T(8,128)S(1)}, u32[]{:S(2)}, u32[]{:S(2)}) collective-permute-start(f32[2,40,128]{2,1,0:T(8,128)} %get-tuple-element.88), channel_id=1, source_target_pairs={{0,16},{16,0},{1,17},{17,1},{2,18},{18,2},{3,19},{19,3},{4,20},{20... | collective-permute-start | bytes 122888 | tf_op jit(solution)/shard_map/ppermute | solution.py:879
  7.2 3.0 %shard_map.131 = (bf16[8,256,256]{2,1,0:T(8,128)(2,1)S(1)}, bf16[8,256,256]{2,1,0:T(8,128)(2,1)S(1)}, f32[8,32,256]{2,1,0:T(8,128)S(1)}, bf16[8,32,256]{2,1,0:T(...) custom-call(f32[8,256,256]{2,1,0:T(8,128)S(1)} %get-tuple-element.91.refs_0_, ...), custom_call_target="tpu_custom_call" | custom-call | flops 5000000000 | bytes 9765625 | tf_op jit(solution)/shard_map/pallas_call | solution.py:861
  11.9 8.2 %all-to-all-start = ((f32[32,3,4,128]{3,2,1,0:T(4,128)}), f32[32,3,4,128]{3,2,1,0:T(4,128)S(1)}, u32[]{:S(2)}, u32[]{:S(2)}) async-start(f32[32,3,4,128]{3,2,1,0:T(4,128)} %bitcast.34), calls=%async_computation | async-start | bytes 393216 | tf_op jit(solution)/shard_map/all_to_all | solution.py:926
  20.0 1.8 %collective-permute-start.3 = (f32[2,72,128]{2,1,0:T(8,128)}, f32[2,72,128]{2,1,0:T(8,128)S(1)}, u32[]{:S(2)}, u32[]{:S(2)}) collective-permute-start(f32[2,72,128]{2,1,0:T(8,128)} %get-tuple-element.102), channel_id=1, source_target_pairs={{0,16},{16,0},{1,17},{17,1},{2,18},{18,2},{3,19},{19,3},{4,20},{20... | collective-permute-start | bytes 221192 | tf_op jit(solution)/shard_map/ppermute | solution.py:879
  25.7 3.2 %all-to-all-done = f32[32,3,4,128]{3,2,1,0:T(4,128)S(1)} async-done(((f32[32,3,4,128]{3,2,1,0:T(4,128)}), f32[32,3,4,128]{3,2,1,0:T(4,128)S(1)}, u32[]{:S(2)}, u32[]{:S(2)}) %all-to-all-start) | async-done | bytes 196640 | tf_op jit(solution)/shard_map/all_to_all | solution.py:926
  28.9 4.1 %shard_map.134 = (bf16[2,2,256,384]{3,2,1,0:T(8,128)(2,1)S(1)}, bf16[2,384,128]{2,1,0:T(8,128)(2,1)S(1)}, bf16[128,512]{1,0:T(8,128)(2,1)S(1)}, bf16[128,512]{1,...) custom-call(f32[48,8,128]{2,1,0:T(8,128)S(1)} %bitcast.25, ...), custom_call_target="tpu_custom_call" | custom-call | tf_op jit(solution)/shard_map/pallas_call | solution.py:861
  33.1 3.1 %all-to-all-start.1 = ((f32[32,4,128]{2,1,0:T(4,128)}), f32[32,4,128]{2,1,0:T(4,128)S(1)}, u32[]{:S(2)}, u32[]{:S(2)}) async-start(f32[32,4,128]{2,1,0:T(4,128)} %bitcast.39), calls=%async_computation.1 | async-start | bytes 131072 | tf_op jit(solution)/shard_map/all_to_all | solution.py:940
  36.2 1.8 %collective-permute-start.7 = (f32[2,16,128]{2,1,0:T(8,128)}, f32[2,16,128]{2,1,0:T(8,128)S(1)}, u32[]{:S(2)}, u32[]{:S(2)}) collective-permute-start(f32[2,16,128]{2,1,0:T(8,128)} %get-tuple-element.115), channel_id=1, source_target_pairs={{0,16},{16,0},{1,17},{17,1},{2,18},{18,2},{3,19},{19,3},{4,20},{20... | collective-permute-start | bytes 49160 | tf_op jit(solution)/shard_map/ppermute | solution.py:879
  40.3 3.4 %all-to-all-done.1 = f32[32,4,128]{2,1,0:T(4,128)S(1)} async-done(((f32[32,4,128]{2,1,0:T(4,128)}), f32[32,4,128]{2,1,0:T(4,128)S(1)}, u32[]{:S(2)}, u32[]{:S(2)}) %all-to-all-start.1) | async-done | bytes 65568 | tf_op jit(solution)/shard_map/all_to_all | solution.py:940
  43.6 4.3 %shard_map.135 = (f32[8,16,256]{2,1,0:T(8,128)}, f32[8,16,256]{2,1,0:T(8,128)}, f32[8,16,256]{2,1,0:T(8,128)}, f32[8,16,256]{2,1,0:T(8,128)}, f32[4,16,128]{2,1,...) custom-call(f32[16,8,128]{2,1,0:T(8,128)S(1)} %bitcast.28, ...), custom_call_target="tpu_custom_call" | custom-call | tf_op jit(solution)/shard_map/pallas_call | solution.py:861
  48.0 4.3 %all-to-all-start.2 = ((f32[32,4,128]{2,1,0:T(4,128)}), f32[32,4,128]{2,1,0:T(4,128)S(1)}, u32[]{:S(2)}, u32[]{:S(2)}) async-start(f32[32,4,128]{2,1,0:T(4,128)} %bitcast.41), calls=%async_computation.2 | async-start | bytes 131072 | tf_op jit(solution)/shard_map/all_to_all | solution.py:940
  56.3 3.4 %all-to-all-done.2 = f32[32,4,128]{2,1,0:T(4,128)S(1)} async-done(((f32[32,4,128]{2,1,0:T(4,128)}), f32[32,4,128]{2,1,0:T(4,128)S(1)}, u32[]{:S(2)}, u32[]{:S(2)}) %all-to-all-start.2) | async-done | bytes 65568 | tf_op jit(solution)/shard_map/all_to_all | solution.py:940
  59.7 4.3 %shard_map.136 = (f32[8,16,256]{2,1,0:T(8,128)}, f32[8,16,256]{2,1,0:T(8,128)}, f32[8,16,256]{2,1,0:T(8,128)}, f32[8,16,256]{2,1,0:T(8,128)}, f32[4,16,128]{2,1,...) custom-call(f32[16,8,128]{2,1,0:T(8,128)S(1)} %bitcast.29, ...), custom_call_target="tpu_custom_call" | custom-call | tf_op jit(solution)/shard_map/pallas_call | solution.py:861
  64.0 4.3 %all-to-all-start.3 = ((f32[32,4,128]{2,1,0:T(4,128)}), f32[32,4,128]{2,1,0:T(4,128)S(1)}, u32[]{:S(2)}, u32[]{:S(2)}) async-start(f32[32,4,128]{2,1,0:T(4,128)} %bitcast.42), calls=%async_computation.3 | async-start | bytes 131072 | tf_op jit(solution)/shard_map/all_to_all | solution.py:940
  72.4 3.4 %all-to-all-done.3 = f32[32,4,128]{2,1,0:T(4,128)S(1)} async-done(((f32[32,4,128]{2,1,0:T(4,128)}), f32[32,4,128]{2,1,0:T(4,128)S(1)}, u32[]{:S(2)}, u32[]{:S(2)}) %all-to-all-start.3) | async-done | bytes 65568 | tf_op jit(solution)/shard_map/all_to_all | solution.py:940
  75.7 4.3 %shard_map.137 = (f32[8,16,256]{2,1,0:T(8,128)}, f32[8,16,256]{2,1,0:T(8,128)}, f32[8,16,256]{2,1,0:T(8,128)}, f32[8,16,256]{2,1,0:T(8,128)}, f32[4,16,128]{2,1,...) custom-call(f32[16,8,128]{2,1,0:T(8,128)S(1)} %bitcast.30, ...), custom_call_target="tpu_custom_call" | custom-call | tf_op jit(solution)/shard_map/pallas_call | solution.py:861
  80.1 4.3 %all-to-all-start.4 = ((f32[32,4,128]{2,1,0:T(4,128)}), f32[32,4,128]{2,1,0:T(4,128)S(1)}, u32[]{:S(2)}, u32[]{:S(2)}) async-start(f32[32,4,128]{2,1,0:T(4,128)} %bitcast.43), calls=%async_computation.4 | async-start | bytes 131072 | tf_op jit(solution)/shard_map/all_to_all | solution.py:940
  84.4 1.8 %collective-permute-start.16 = (f32[2,16,128]{2,1,0:T(8,128)}, f32[2,16,128]{2,1,0:T(8,128)S(1)}, u32[]{:S(2)}, u32[]{:S(2)}) collective-permute-start(f32[2,16,128]{2,1,0:T(8,128)} %get-tuple-element.149), channel_id=1, source_target_pairs={{0,16},{16,0},{1,17},{17,1},{2,18},{18,2},{3,19},{19,3},{4,20},{20... | collective-permute-start | bytes 49160 | tf_op jit(solution)/shard_map/ppermute | solution.py:879
  88.4 3.4 %all-to-all-done.4 = f32[32,4,128]{2,1,0:T(4,128)S(1)} async-done(((f32[32,4,128]{2,1,0:T(4,128)}), f32[32,4,128]{2,1,0:T(4,128)S(1)}, u32[]{:S(2)}, u32[]{:S(2)}) %all-to-all-start.4) | async-done | bytes 65568 | tf_op jit(solution)/shard_map/all_to_all | solution.py:940
  91.8 4.3 %shard_map.138 = (f32[8,16,256]{2,1,0:T(8,128)}, f32[8,16,256]{2,1,0:T(8,128)}, f32[8,16,256]{2,1,0:T(8,128)}, f32[8,16,256]{2,1,0:T(8,128)}, f32[4,16,128]{2,1,...) custom-call(f32[16,8,128]{2,1,0:T(8,128)S(1)} %bitcast.26, ...), custom_call_target="tpu_custom_call" | custom-call | tf_op jit(solution)/shard_map/pallas_call | solution.py:861
  96.1 4.3 %all-to-all-start.5 = ((f32[32,4,128]{2,1,0:T(4,128)}), f32[32,4,128]{2,1,0:T(4,128)S(1)}, u32[]{:S(2)}, u32[]{:S(2)}) async-start(f32[32,4,128]{2,1,0:T(4,128)} %bitcast.40), calls=%async_computation.5 | async-start | bytes 131072 | tf_op jit(solution)/shard_map/all_to_all | solution.py:940
  104.4 3.4 %all-to-all-done.5 = f32[32,4,128]{2,1,0:T(4,128)S(1)} async-done(((f32[32,4,128]{2,1,0:T(4,128)}), f32[32,4,128]{2,1,0:T(4,128)S(1)}, u32[]{:S(2)}, u32[]{:S(2)}) %all-to-all-start.5) | async-done | bytes 65568 | tf_op jit(solution)/shard_map/all_to_all | solution.py:940
  107.8 3.0 %shard_map.139 = (f32[128,128]{1,0:T(8,128)}, f32[128,128]{1,0:T(8,128)}, f32[128,128]{1,0:T(8,128)}) custom-call(f32[16,8,128]{2,1,0:T(8,128)S(1)} %bitcast.27, f32[2,16,128]{2,1,0:T(8,128)S(1)} %collective-permute-done.19.refs_1_, f32[16,128]{1,0:T(8,128)S(1)} %collective-permute-done.20.refs_2_, f32[16,128]{1,0:T(8,128)S(1)} %collective-permute-done.21.refs_3_, ...), custom_call_target="tpu_custom_call" | custom-call | tf_op jit(solution)/shard_map/pallas_call | solution.py:861
  (44 shorter events, 22.8 us)
Async XLA Ops:
  3.3 6.9 %collective-permute-start = (f32[2,40,128]{2,1,0:T(8,128)}, f32[2,40,128]{2,1,0:T(8,128)S(1)}, u32[]{:S(2)}, u32[]{:S(2)}) collective-permute-start(f32[2,40,128]{2,1,0:T(8,128)} %get-tuple-element.88), channel_id=1, source_target_pairs={{0,16},{16,0},{1,17},{17,1},{2,18},{18,2},{3,19},{19,3},{4,20},{20... | collective-permute-start | bytes 122888 | tf_op jit(solution)/shard_map/ppermute | solution.py:879
  6.4 3.8 %collective-permute-start.1 = (f32[40,128]{1,0:T(8,128)}, f32[40,128]{1,0:T(8,128)S(1)}, u32[]{:S(2)}, u32[]{:S(2)}) collective-permute-start(f32[40,128]{1,0:T(8,128)} %get-tuple-element.89), channel_id=1, source_target_pairs={{0,1},{2,3},{4,5},{6,7},{8,9},{10,11},{12,13},{14,15},{1,0},{3,2},... | collective-permute-start | bytes 61448 | tf_op jit(solution)/shard_map/ppermute | solution.py:880
  6.4 3.8 %collective-permute-start.2 = (f32[40,128]{1,0:T(8,128)}, f32[40,128]{1,0:T(8,128)S(1)}, u32[]{:S(2)}, u32[]{:S(2)}) collective-permute-start(f32[40,128]{1,0:T(8,128)} %get-tuple-element.90), channel_id=1, source_target_pairs={{1,2},{3,4},{5,6},{7,8},{9,10},{11,12},{13,14},{2,1},{4,3},{6,5},{... | collective-permute-start | bytes 61448 | tf_op jit(solution)/shard_map/ppermute | solution.py:881
  7.0 15.5 %collective-permute-start.6 = (f32[6,128,128]{2,1,0:T(8,128)}, f32[6,128,128]{2,1,0:T(8,128)S(1)}, u32[]{:S(2)}, u32[]{:S(2)}) collective-permute-start(f32[6,128,128]{2,1,0:T(8,128)} %get-tuple-element.109), channel_id=1, source_target_pairs={{0,16},{16,0},{1,17},{17,1},{2,18},{18,2},{3,19},{19,3},{4,20},{20... | collective-permute-start | bytes 1179656 | tf_op jit(solution)/shard_map/ppermute | solution.py:904
  11.9 17.1 %all-to-all-start = ((f32[32,3,4,128]{3,2,1,0:T(4,128)}), f32[32,3,4,128]{3,2,1,0:T(4,128)S(1)}, u32[]{:S(2)}, u32[]{:S(2)}) async-start(f32[32,3,4,128]{3,2,1,0:T(4,128)} %bitcast.34), calls=%async_computation | async-start | bytes 393216 | tf_op jit(solution)/shard_map/all_to_all | solution.py:926
  20.0 5.7 %collective-permute-start.3 = (f32[2,72,128]{2,1,0:T(8,128)}, f32[2,72,128]{2,1,0:T(8,128)S(1)}, u32[]{:S(2)}, u32[]{:S(2)}) collective-permute-start(f32[2,72,128]{2,1,0:T(8,128)} %get-tuple-element.102), channel_id=1, source_target_pairs={{0,16},{16,0},{1,17},{17,1},{2,18},{18,2},{3,19},{19,3},{4,20},{20... | collective-permute-start | bytes 221192 | tf_op jit(solution)/shard_map/ppermute | solution.py:879
  21.9 2.9 %collective-permute-start.4 = (f32[72,128]{1,0:T(8,128)}, f32[72,128]{1,0:T(8,128)S(1)}, u32[]{:S(2)}, u32[]{:S(2)}) collective-permute-start(f32[72,128]{1,0:T(8,128)} %get-tuple-element.103), channel_id=1, source_target_pairs={{0,1},{2,3},{4,5},{6,7},{8,9},{10,11},{12,13},{14,15},{1,0},{3,2},... | collective-permute-start | bytes 110600 | tf_op jit(solution)/shard_map/ppermute | solution.py:880
  21.9 2.9 %collective-permute-start.5 = (f32[72,128]{1,0:T(8,128)}, f32[72,128]{1,0:T(8,128)S(1)}, u32[]{:S(2)}, u32[]{:S(2)}) collective-permute-start(f32[72,128]{1,0:T(8,128)} %get-tuple-element.104), channel_id=1, source_target_pairs={{1,2},{3,4},{5,6},{7,8},{9,10},{11,12},{13,14},{2,1},{4,3},{6,5},{... | collective-permute-start | bytes 110600 | tf_op jit(solution)/shard_map/ppermute | solution.py:881
  33.1 10.5 %all-to-all-start.1 = ((f32[32,4,128]{2,1,0:T(4,128)}), f32[32,4,128]{2,1,0:T(4,128)S(1)}, u32[]{:S(2)}, u32[]{:S(2)}) async-start(f32[32,4,128]{2,1,0:T(4,128)} %bitcast.39), calls=%async_computation.1 | async-start | bytes 131072 | tf_op jit(solution)/shard_map/all_to_all | solution.py:940
  36.2 4.0 %collective-permute-start.7 = (f32[2,16,128]{2,1,0:T(8,128)}, f32[2,16,128]{2,1,0:T(8,128)S(1)}, u32[]{:S(2)}, u32[]{:S(2)}) collective-permute-start(f32[2,16,128]{2,1,0:T(8,128)} %get-tuple-element.115), channel_id=1, source_target_pairs={{0,16},{16,0},{1,17},{17,1},{2,18},{18,2},{3,19},{19,3},{4,20},{20... | collective-permute-start | bytes 49160 | tf_op jit(solution)/shard_map/ppermute | solution.py:879
  38.1 1.4 %collective-permute-start.8 = (f32[16,128]{1,0:T(8,128)}, f32[16,128]{1,0:T(8,128)S(1)}, u32[]{:S(2)}, u32[]{:S(2)}) collective-permute-start(f32[16,128]{1,0:T(8,128)} %get-tuple-element.116), channel_id=1, source_target_pairs={{0,1},{2,3},{4,5},{6,7},{8,9},{10,11},{12,13},{14,15},{1,0},{3,2},... | collective-permute-start | bytes 24584 | tf_op jit(solution)/shard_map/ppermute | solution.py:880
  38.1 1.4 %collective-permute-start.9 = (f32[16,128]{1,0:T(8,128)}, f32[16,128]{1,0:T(8,128)S(1)}, u32[]{:S(2)}, u32[]{:S(2)}) collective-permute-start(f32[16,128]{1,0:T(8,128)} %get-tuple-element.117), channel_id=1, source_target_pairs={{1,2},{3,4},{5,6},{7,8},{9,10},{11,12},{13,14},{2,1},{4,3},{6,5},{... | collective-permute-start | bytes 24584 | tf_op jit(solution)/shard_map/ppermute | solution.py:881
  48.0 11.7 %all-to-all-start.2 = ((f32[32,4,128]{2,1,0:T(4,128)}), f32[32,4,128]{2,1,0:T(4,128)S(1)}, u32[]{:S(2)}, u32[]{:S(2)}) async-start(f32[32,4,128]{2,1,0:T(4,128)} %bitcast.41), calls=%async_computation.2 | async-start | bytes 131072 | tf_op jit(solution)/shard_map/all_to_all | solution.py:940
  52.3 4.0 %collective-permute-start.10 = (f32[2,16,128]{2,1,0:T(8,128)}, f32[2,16,128]{2,1,0:T(8,128)S(1)}, u32[]{:S(2)}, u32[]{:S(2)}) collective-permute-start(f32[2,16,128]{2,1,0:T(8,128)} %get-tuple-element.129), channel_id=1, source_target_pairs={{0,16},{16,0},{1,17},{17,1},{2,18},{18,2},{3,19},{19,3},{4,20},{20... | collective-permute-start | bytes 49160 | tf_op jit(solution)/shard_map/ppermute | solution.py:879
  54.1 1.4 %collective-permute-start.11 = (f32[16,128]{1,0:T(8,128)}, f32[16,128]{1,0:T(8,128)S(1)}, u32[]{:S(2)}, u32[]{:S(2)}) collective-permute-start(f32[16,128]{1,0:T(8,128)} %get-tuple-element.130), channel_id=1, source_target_pairs={{0,1},{2,3},{4,5},{6,7},{8,9},{10,11},{12,13},{14,15},{1,0},{3,2},... | collective-permute-start | bytes 24584 | tf_op jit(solution)/shard_map/ppermute | solution.py:880
  54.1 1.4 %collective-permute-start.12 = (f32[16,128]{1,0:T(8,128)}, f32[16,128]{1,0:T(8,128)S(1)}, u32[]{:S(2)}, u32[]{:S(2)}) collective-permute-start(f32[16,128]{1,0:T(8,128)} %get-tuple-element.131), channel_id=1, source_target_pairs={{1,2},{3,4},{5,6},{7,8},{9,10},{11,12},{13,14},{2,1},{4,3},{6,5},{... | collective-permute-start | bytes 24584 | tf_op jit(solution)/shard_map/ppermute | solution.py:881
  64.0 11.7 %all-to-all-start.3 = ((f32[32,4,128]{2,1,0:T(4,128)}), f32[32,4,128]{2,1,0:T(4,128)S(1)}, u32[]{:S(2)}, u32[]{:S(2)}) async-start(f32[32,4,128]{2,1,0:T(4,128)} %bitcast.42), calls=%async_computation.3 | async-start | bytes 131072 | tf_op jit(solution)/shard_map/all_to_all | solution.py:940
  68.3 4.0 %collective-permute-start.13 = (f32[2,16,128]{2,1,0:T(8,128)}, f32[2,16,128]{2,1,0:T(8,128)S(1)}, u32[]{:S(2)}, u32[]{:S(2)}) collective-permute-start(f32[2,16,128]{2,1,0:T(8,128)} %get-tuple-element.139), channel_id=1, source_target_pairs={{0,16},{16,0},{1,17},{17,1},{2,18},{18,2},{3,19},{19,3},{4,20},{20... | collective-permute-start | bytes 49160 | tf_op jit(solution)/shard_map/ppermute | solution.py:879
  70.1 1.4 %collective-permute-start.15 = (f32[16,128]{1,0:T(8,128)}, f32[16,128]{1,0:T(8,128)S(1)}, u32[]{:S(2)}, u32[]{:S(2)}) collective-permute-start(f32[16,128]{1,0:T(8,128)} %get-tuple-element.141), channel_id=1, source_target_pairs={{1,2},{3,4},{5,6},{7,8},{9,10},{11,12},{13,14},{2,1},{4,3},{6,5},{... | collective-permute-start | bytes 24584 | tf_op jit(solution)/shard_map/ppermute | solution.py:881
  80.1 11.7 %all-to-all-start.4 = ((f32[32,4,128]{2,1,0:T(4,128)}), f32[32,4,128]{2,1,0:T(4,128)S(1)}, u32[]{:S(2)}, u32[]{:S(2)}) async-start(f32[32,4,128]{2,1,0:T(4,128)} %bitcast.43), calls=%async_computation.4 | async-start | bytes 131072 | tf_op jit(solution)/shard_map/all_to_all | solution.py:940
  84.4 4.0 %collective-permute-start.16 = (f32[2,16,128]{2,1,0:T(8,128)}, f32[2,16,128]{2,1,0:T(8,128)S(1)}, u32[]{:S(2)}, u32[]{:S(2)}) collective-permute-start(f32[2,16,128]{2,1,0:T(8,128)} %get-tuple-element.149), channel_id=1, source_target_pairs={{0,16},{16,0},{1,17},{17,1},{2,18},{18,2},{3,19},{19,3},{4,20},{20... | collective-permute-start | bytes 49160 | tf_op jit(solution)/shard_map/ppermute | solution.py:879
  86.2 1.4 %collective-permute-start.17 = (f32[16,128]{1,0:T(8,128)}, f32[16,128]{1,0:T(8,128)S(1)}, u32[]{:S(2)}, u32[]{:S(2)}) collective-permute-start(f32[16,128]{1,0:T(8,128)} %get-tuple-element.150), channel_id=1, source_target_pairs={{0,1},{2,3},{4,5},{6,7},{8,9},{10,11},{12,13},{14,15},{1,0},{3,2},... | collective-permute-start | bytes 24584 | tf_op jit(solution)/shard_map/ppermute | solution.py:880
  96.1 11.7 %all-to-all-start.5 = ((f32[32,4,128]{2,1,0:T(4,128)}), f32[32,4,128]{2,1,0:T(4,128)S(1)}, u32[]{:S(2)}, u32[]{:S(2)}) async-start(f32[32,4,128]{2,1,0:T(4,128)} %bitcast.40), calls=%async_computation.5 | async-start | bytes 131072 | tf_op jit(solution)/shard_map/all_to_all | solution.py:940
  100.4 4.0 %collective-permute-start.19 = (f32[2,16,128]{2,1,0:T(8,128)}, f32[2,16,128]{2,1,0:T(8,128)S(1)}, u32[]{:S(2)}, u32[]{:S(2)}) collective-permute-start(f32[2,16,128]{2,1,0:T(8,128)} %get-tuple-element.159), channel_id=1, source_target_pairs={{0,16},{16,0},{1,17},{17,1},{2,18},{18,2},{3,19},{19,3},{4,20},{20... | collective-permute-start | bytes 49160 | tf_op jit(solution)/shard_map/ppermute | solution.py:879
  (5 other events, 6.3 us)

commit v5 on v4

--- a/solution.py
+++ b/solution.py
@@ -385,7 +385,7 @@
 
 def start_kernel(res_ref, dir_ref, act_ref, scale_ref, *refs):
     inverse_ref, own_ref, x_ref, a_ref, b_ref = refs[4:9]
-    upper_ref = refs[13]
+    upper_ref, p_ref = refs[13:15]
     gx, gy = lax.axis_index("gx"), lax.axis_index("gy")
     last_x = gx * SPAN_X + SPAN_X - 1 == lax.axis_size("gx") * SPAN_X - 1
     last_y = gy * SPAN_Y + SPAN_Y - 1 == lax.axis_size("gy") * SPAN_Y - 1
@@ -399,10 +399,12 @@
         if y == SPAN_Y - 1:
             keep = jnp.where(jnp.logical_and(last_y, jnp.logical_not(east)), 0.0, keep)
         mine = pl.ds(i, CASES, stride=SUBS)
+        p = dir_ref[mine, :] * keep
+        p_ref[mine, :] = p
         v = jnp.concatenate(
             [
                 res_ref[mine, :],
-                dir_ref[mine, :] * keep,
+                p,
                 scale_ref[i : i + 1, :] * keep,
                 keep,
                 jnp.zeros((CAST - 2 * CASES - 2, 128), F32),
@@ -467,17 +469,19 @@
         ch_ref[i], cl_ref[i] = split(cc)
 
 
-def inverse_kernel(mine_ref, upper_ref, high_ref, low_ref):
+def inverse_kernel(mine_ref, upper_ref, high_ref, low_ref, high_out_ref, low_out_ref):
     first = lax.axis_index("gx") == 0
     mine = mine_ref[...]
     blocks = {spot: upper_ref[t] for t, spot in enumerate(UPPER)}
     side = lambda i, j: blocks[i, j] if i <= j else jnp.transpose(blocks[j, i])
     other = jnp.concatenate([jnp.concatenate([side(i, j) for j in range(3)], 1) for i in range(3)], 0)
-    high_ref[0], low_ref[0] = split(jnp.where(first, mine, other))
-    high_ref[1], low_ref[1] = split(jnp.where(first, other, mine))
-
-
-def near_names(name_ref, x_ref, a_ref, b_ref, near_ref):
+    for region, v in enumerate((jnp.where(first, mine, other), jnp.where(first, other, mine))):
+        high, low = split(v)
+        high_ref[region], low_ref[region] = high, low
+        high_out_ref[region], low_out_ref[region] = high, low
+
+
+def near_names(name_ref, x_ref, a_ref, b_ref):
     named = pl.ds(2 * CASES + SLOTS, 8)
     group = iota((8, 128), 1) // SLOTS
     turn = lambda v, g: jnp.where(group == g, pltpu.roll(v, g * SLOTS, 1), 0.0)
@@ -486,45 +490,47 @@
     found = iota((384, 128), 0).astype(F32) == wanted[0:1]
     mine = jnp.where(iota((384, 128), 1) < 3 * SLOTS, 1.0, 0.0)
     gx = lax.axis_index("gx")
-    for region in range(2):
-        near_ref[region] = jnp.where(found, jnp.where(gx == region, mine, 1.0 - mine), 0.0).astype(BF16)
+    return [jnp.where(found, jnp.where(gx == region, mine, 1.0 - mine), 0.0).astype(BF16) for region in range(2)]
 
 
 def near_spread(x_ref, a_ref, b_ref, nh_ref, nl_ref):
     rows = pl.ds(2 * CASES, SLOTS)
-    blank = jnp.zeros((SLOTS, 128), F32)
-    parts = [
-        [blank] * 4,
-        [a_ref[rows, :], blank, blank, blank],
-        [blank, b_ref[rows, :], blank, blank],
-        [blank, blank, x_ref[0, rows, :], x_ref[1, rows, :]],
-    ]
-    nh_ref[...], nl_ref[...] = split(jnp.concatenate([jnp.concatenate(row, 1) for row in parts], 0))
+    nh_ref[...], nl_ref[...] = split(
+        jnp.concatenate([a_ref[rows, :], b_ref[rows, :], x_ref[0, rows, :], x_ref[1, rows, :]], 1)
+    )
 
 
 def operator(ys, x_ref, a_ref, b_ref, near, mk_ref, ch_ref, cl_ref, nh_ref, nl_ref):
     n = ys[0].shape[0]
-    side = dot_split(near, nh_ref[...], nl_ref[...])
+    high, low = nh_ref[...], nl_ref[...]
+    side = jnp.concatenate(
+        [
+            dot_split(near[g], high[:, at : at + width], low[:, at : at + width])
+            for g, at, width in ((1, 0, 128), (2, 128, 128), (3, 256, 256))
+        ],
+        1,
+    )
     west, east, south, north = received(x_ref, a_ref, b_ref, 0, n, side)
-    mine = near[:, :SLOTS]
-    ys = [ys[i] + dot_split(mine, ch_ref[i], cl_ref[i]) for i in range(SUBS)]
+    ys = [ys[i] + dot_split(near[0], ch_ref[i], cl_ref[i]) for i in range(SUBS)]
     other = across(ys, (west, east, south, north), n)
     return [mk_ref[i, 1:2, :] * (ys[i] + other[i]) for i in range(SUBS)]
 
 
-def local_part(us, high_ref, low_ref, ch_ref, cl_ref):
-    ys = [dot_split(us[i], high_ref[i], low_ref[i]) for i in range(SUBS)]
-    n = us[0].shape[0]
+def corners(us, ch_ref, cl_ref):
     couple = lambda ref: jnp.concatenate([ref[i] for i in range(SUBS)], 0)
     corner = dot_split(jnp.concatenate(us, 0), couple(ch_ref), couple(cl_ref), dot_turned)
+    n = us[0].shape[0]
     group = iota((n, 128), 1) // SLOTS
     total = jnp.zeros((n, 128), F32)
     for i in range(SUBS):
         part = corner[n * i : n * i + n, 128 * (i // 4) : 128 * (i // 4) + 128]
         total = total + jnp.where(group == i % 4, part, 0.0)
     total = total + pltpu.roll(total, 64, 1)
-    total = total + pltpu.roll(total, 32, 1)
-    return ys, total
+    return total + pltpu.roll(total, 32, 1)
+
+
+def by_schur(us, high_ref, low_ref):
+    return [dot_split(us[i], high_ref[i], low_ref[i]) for i in range(SUBS)]
 
 
 def over_lanes(terms):
@@ -595,6 +601,62 @@
     return totals, sols, near
 
 
+def swap_pairs(v):
+    rows, lanes = v.shape
+    return pltpu.roll(v.reshape(rows // 8, 8, lanes), 4, 1).reshape(rows, lanes)
+
+
+def ahead(region, t):
+    gx, gy = lax.axis_index("gx"), lax.axis_index("gy")
+    return 8 * lax.rem(gx + region, 2) + lax.rem(gy // 2 + t, 8)
+
+
+def dense_kernel(got_ref, gh_ref, gl_ref, dh_ref, dl_ref):
+    group = iota((8, 128), 1) // SLOTS
+    for region in range(2):
+        hits = []
+        for par in range(2):
+            halves = []
+            for h in range(2):
+                acc = None
+                for q in range(4):
+                    v = got_ref[3 * ahead(region, 4 * h + q) + 1 + par]
+                    v = v if par == 0 else pltpu.roll(v, 4, 0)
+                    turned = pltpu.roll(v, SLOTS * q, 1) if q else v
+                    acc = turned if acc is None else jnp.where(group == q, turned, acc)
+                halves.append(acc[0:1])
+            wanted = jnp.concatenate(halves, 1)
+            hits.append(jnp.where(iota((384, 256), 0).astype(F32) == wanted, 1.0, 0.0))
+        picks = jnp.concatenate(hits, 1).astype(BF16)
+        rows = [jnp.transpose(hit).astype(BF16) for hit in hits]
+        which = lax.rem(lax.axis_index("gx") + region, 2)
+        for whole_ref, out_ref in ((gh_ref, dh_ref), (gl_ref, dl_ref)):
+            half = dot(whole_ref[which], picks).astype(BF16)
+            for par in range(2):
+                out_ref[region, par] = dot(rows[par], half).astype(BF16)
+
+
+def solve_dense(spots, dh_ref, dl_ref):
+    total, sols = None, []
+    for region in range(2):
+        v = spots[region]
+        one, two = (dot_split(v, dh_ref[region, par], dl_ref[region, par]) for par in range(2))
+        first = (iota(v.shape, 0) // 4) % 2 == 0
+        sol = jnp.where(first, one[:, :256] + swap_pairs(two[:, :256]), two[:, 256:] + swap_pairs(one[:, 256:]))
+        total = v * sol if total is None else total + v * sol
+        sols.append(sol)
+    total = jnp.sum(total, 1, keepdims=True)
+    halves = lambda v: [jnp.concatenate([v[8 * b + at : 8 * b + at + 4] for b in range(4)], 0) for at in (0, 4)]
+    total = sum(halves(total))
+    even = lax.axis_index("gy") % 2 == 0
+    (a, b), (c, d) = halves(sols[0]), halves(sols[1][:, :128])
+    here = jnp.where(even, a[:, :128], b[:, :128])
+    pair = jnp.where(even, b[:, :128], a[:, :128])
+    beyond = jnp.where(even, pltpu.roll(b[:, 128:], SLOTS, 1), pltpu.roll(a[:, :128], 128 - SLOTS, 1))
+    along = jnp.where(even, c, d)
+    return total, [v[:, :SLOTS] for v in (here, pair, beyond, along)]
+
+
 def energy(totals, sols):
     both = totals[0] * sols[0] + totals[1] * sols[1]
     return first_of_pairs(jnp.sum(both, 1, keepdims=True))
@@ -602,13 +664,14 @@
 
 def emit(rs, mk_ref, high_ref, low_ref, ch_ref, cl_ref, block_ref, y_ref, x_ref, a_ref, b_ref):
     us = [mk_ref[i, 0:1, :] * rs[i] for i in range(SUBS)]
-    ys, corner = local_part(us, high_ref, low_ref, ch_ref, cl_ref)
+    corner = corners(us, ch_ref, cl_ref)
+    rho = over_lanes([jnp.where(owned_lanes(i, CASES), rs[i] * us[i], 0.0) for i in range(SUBS)])
+    ys = by_schur(us, high_ref, low_ref)
     send(ys, x_ref, a_ref, b_ref, 0)
     for i in range(SUBS):
         y_ref[i] = ys[i]
     for ref in (x_ref, a_ref, b_ref, y_ref):
         ref.flush()
-    rho = over_lanes([jnp.where(owned_lanes(i, CASES), rs[i] * us[i], 0.0) for i in range(SUBS)])
     delta = over_lanes([us[i] * ys[i] for i in range(SUBS)])
     block = packed(corner, rho, delta)
     twice = jnp.concatenate([block, block], 0)
@@ -618,7 +681,7 @@
 
 def first_kernel(
     own_ref, x_ref, a_ref, b_ref, high_ref, low_ref, cc_ref, ch_ref, cl_ref, name_ref,
-    r_ref, p_ref, mk_ref, y_ref, block_ref, sx_ref, sa_ref, sb_ref, high_out_ref, low_out_ref,
+    r_ref, mk_ref, y_ref, block_ref, sx_ref, sa_ref, sb_ref, high_out_ref, low_out_ref,
 ):
     own = [own_ref[i] for i in range(SUBS)]
     other = across(own, received(x_ref, a_ref, b_ref, 0, CAST), CAST)
@@ -627,10 +690,10 @@
         full = own[i] + other[i]
         rs.append(full[:CASES])
         r_ref[i] = full[:CASES]
-        p_ref[i] = full[CASES : 2 * CASES]
         mk_ref[i] = full[2 * CASES : 2 * CASES + 8]
         vs.append(jnp.concatenate([full[2 * CASES : 2 * CASES + 1] * full[:CASES], full[CASES : 2 * CASES]], 0))
-    ys, corner = local_part(vs, high_ref, low_ref, ch_ref, cl_ref)
+    corner = corners(vs, ch_ref, cl_ref)
+    ys = by_schur(vs, high_ref, low_ref)
     names = name_ref[...]
     send([jnp.concatenate([ys[i], cc_ref[i]], 0) for i in range(SUBS)], sx_ref, sa_ref, sb_ref, 0)
     at = pl.ds(2 * CASES + SLOTS, 8)
@@ -668,11 +731,11 @@
 
 
 def second_kernel(
-    got_ref, x_ref, a_ref, b_ref, y_ref, r_ref, p_ref, mk_ref, dual_ref, rho_ref, gh_ref, gl_ref, name_ref,
+    got_ref, x_ref, a_ref, b_ref, y_ref, r_ref, mk_ref, p_ref, l_ref, rho_ref, gh_ref, gl_ref, name_ref,
     high_ref, low_ref, ch_ref, cl_ref,
-    pick_ref, near_ref, nh_ref, nl_ref, ro_ref, so_ref, po_ref, lo_ref, scal_ref, block_ref, yo_ref, sx_ref, sa_ref, sb_ref,
+    nh_ref, nl_ref, po_ref, lo_ref, ro_ref, so_ref, scal_ref, block_ref, yo_ref, sx_ref, sa_ref, sb_ref,
 ):
-    near_names(name_ref, x_ref, a_ref, b_ref, near_ref)
+    near_ref, pick_ref = near_names(name_ref, x_ref, a_ref, b_ref), {}
     near_spread(x_ref, a_ref, b_ref, nh_ref, nl_ref)
     top = iota((8, 128), 0) < 4
     us, ps, names = [], [], []
@@ -707,6 +770,7 @@
     cross = cross + energy(of_p(totals), of_u(sols))
     eta = eta + energy(of_p(totals), of_p(sols))
     near = first_of_pairs(near)
+    near = [(pltpu.roll(near, 128 - SLOTS * g, 1) if g else near)[:, :SLOTS] for g in range(4)]
     beta = rho / column_of(rho_ref[...])
     skew = cross + beta * eta
     pi = delta + 2.0 * beta * skew - beta * beta * eta
@@ -715,69 +779,68 @@
     rs = []
     for i in range(SUBS):
         f, r = fs[i], r_ref[i]
-        p = mk_ref[i, 0:1, :] * r + beta * p_ref[i]
         s = f[:CASES] + beta * f[CASES:]
         r = r - alpha * s
         rs.append(r)
-        ro_ref[i], so_ref[i], po_ref[i] = r, s, p
-        lo_ref[i] = spread_owned(dual_ref[pl.ds(i, CASES, stride=SUBS), :], i) + alpha * p
-    keep_scalars(scal_ref, (rho, pi, beta, skew))
-    for ref in (pick_ref, near_ref, nh_ref, nl_ref, ro_ref, so_ref, po_ref, lo_ref, scal_ref):
-        ref.flush()
+        ro_ref[i], so_ref[i] = r, s
+    scalars = rho, pi, beta, skew, alpha
+    keep_scalars(scal_ref, scalars)
+    so_ref.flush()
+    track(r_ref, scalars, mk_ref, p_ref, l_ref, po_ref, lo_ref)
     emit(rs, mk_ref, high_ref, low_ref, ch_ref, cl_ref, block_ref, yo_ref, sx_ref, sa_ref, sb_ref)
 
 
-def absorb(got_ref, x_ref, a_ref, b_ref, y_ref, r_ref, s_ref, p_ref, l_ref, scal_ref, mk_ref, pick_ref, gh_ref, gl_ref, near_ref, nh_ref, nl_ref, ch_ref, cl_ref):
-    vs = [got_ref[j] for j in range(16)]
-    totals, sols, near = solve(by_slot(vs), pick_ref, gh_ref, gl_ref, near_ref)
+def absorb(got_ref, x_ref, a_ref, b_ref, y_ref, r_ref, s_ref, scal_ref, mk_ref, dh_ref, dl_ref, nh_ref, nl_ref, ch_ref, cl_ref):
+    vs = [got_ref[ahead(region, t)] for region in range(2) for t in range(8)]
+    coarse, near = solve_dense(by_slot(vs), dh_ref, dl_ref)
     rho, delta = inner(vs)
-    delta = delta + energy(totals, sols)
-    near = first_of_pairs(near)
+    delta = delta + coarse
     rho_old, pi, beta, skew = (scal_ref[t][:, 0:1] for t in range(4))
     skew = beta * skew
     beta = rho / rho_old
     pi = delta + 2.0 * beta * skew - beta * beta * pi
     alpha = rho / pi
     fs = operator([y_ref[i] for i in range(SUBS)], x_ref, a_ref, b_ref, near, mk_ref, ch_ref, cl_ref, nh_ref, nl_ref)
-    out = []
+    ss = [fs[i] + beta * s_ref[i] for i in range(SUBS)]
+    rs = [r_ref[i] - alpha * ss[i] for i in range(SUBS)]
+    return rs, ss, (rho, pi, beta, skew, alpha)
+
+
+def track(r_ref, scalars, mk_ref, p_ref, l_ref, po_ref, lo_ref):
+    _, _, beta, _, alpha = scalars
     for i in range(SUBS):
-        r = r_ref[i]
-        p = mk_ref[i, 0:1, :] * r + beta * p_ref[i]
-        s = fs[i] + beta * s_ref[i]
-        out.append((r - alpha * s, s, p, l_ref[i] + alpha * p))
-    return out, (rho, pi, beta, skew)
+        mine = pl.ds(i, CASES, stride=SUBS)
+        p = take_owned(mk_ref[i, 0:1, :] * r_ref[i], i) + beta * p_ref[mine, :]
+        po_ref[mine, :] = p
+        lo_ref[mine, :] = l_ref[mine, :] + alpha * p
 
 
 def round_kernel(
-    got_ref, x_ref, a_ref, b_ref, y_ref, r_ref, s_ref, p_ref, l_ref, scal_ref, mk_ref, pick_ref, gh_ref, gl_ref, near_ref,
-    nh_ref, nl_ref, ch_ref, cl_ref, high_ref, low_ref,
-    ro_ref, so_ref, po_ref, lo_ref, scalo_ref, block_ref, yo_ref, sx_ref, sa_ref, sb_ref,
+    got_ref, x_ref, a_ref, b_ref, y_ref, r_ref, s_ref, scal_ref, mk_ref, dh_ref, dl_ref,
+    nh_ref, nl_ref, ch_ref, cl_ref, p_ref, l_ref, high_ref, low_ref,
+    po_ref, lo_ref, ro_ref, so_ref, scalo_ref, block_ref, yo_ref, sx_ref, sa_ref, sb_ref,
 ):
-    out, scalars = absorb(
-        got_ref, x_ref, a_ref, b_ref, y_ref, r_ref, s_ref, p_ref, l_ref, scal_ref, mk_ref, pick_ref, gh_ref, gl_ref, near_ref,
-        nh_ref, nl_ref, ch_ref, cl_ref,
-    )
-    for i, (r, s, p, lam) in enumerate(out):
-        ro_ref[i], so_ref[i], po_ref[i], lo_ref[i] = r, s, p, lam
+    rs, ss, scalars = absorb(
+        got_ref, x_ref, a_ref, b_ref, y_ref, r_ref, s_ref, scal_ref, mk_ref, dh_ref, dl_ref, nh_ref, nl_ref, ch_ref, cl_ref
+    )
+    for i in range(SUBS):
+        ro_ref[i], so_ref[i] = rs[i], ss[i]
+    so_ref.flush()
     keep_scalars(scalo_ref, scalars)
-    for ref in (ro_ref, so_ref, po_ref, lo_ref, scalo_ref):
-        ref.flush()
-    emit([v[0] for v in out], mk_ref, high_ref, low_ref, ch_ref, cl_ref, block_ref, yo_ref, sx_ref, sa_ref, sb_ref)
+    track(r_ref, scalars, mk_ref, p_ref, l_ref, po_ref, lo_ref)
+    emit(rs, mk_ref, high_ref, low_ref, ch_ref, cl_ref, block_ref, yo_ref, sx_ref, sa_ref, sb_ref)
 
 
 def last_kernel(
-    got_ref, x_ref, a_ref, b_ref, y_ref, r_ref, s_ref, p_ref, l_ref, scal_ref, mk_ref, pick_ref, gh_ref, gl_ref, near_ref,
-    nh_ref, nl_ref, ch_ref, cl_ref, lo_ref, ro_ref, po_ref,
+    got_ref, x_ref, a_ref, b_ref, y_ref, r_ref, s_ref, scal_ref, mk_ref, dh_ref, dl_ref, nh_ref, nl_ref, ch_ref, cl_ref,
+    p_ref, l_ref, lo_ref, ro_ref, po_ref,
 ):
-    out, _ = absorb(
-        got_ref, x_ref, a_ref, b_ref, y_ref, r_ref, s_ref, p_ref, l_ref, scal_ref, mk_ref, pick_ref, gh_ref, gl_ref, near_ref,
-        nh_ref, nl_ref, ch_ref, cl_ref,
-    )
-    for i, (r, _, p, lam) in enumerate(out):
-        mine = pl.ds(i, CASES, stride=SUBS)
-        lo_ref[mine, :] = take_owned(lam, i)
-        ro_ref[mine, :] = take_owned(r, i)
-        po_ref[mine, :] = take_owned(p, i)
+    rs, _, scalars = absorb(
+        got_ref, x_ref, a_ref, b_ref, y_ref, r_ref, s_ref, scal_ref, mk_ref, dh_ref, dl_ref, nh_ref, nl_ref, ch_ref, cl_ref
+    )
+    track(r_ref, scalars, mk_ref, p_ref, l_ref, po_ref, lo_ref)
+    for i in range(SUBS):
+        ro_ref[pl.ds(i, CASES, stride=SUBS), :] = take_owned(rs[i], i)
 
 
 class Fetched:
@@ -787,10 +850,34 @@
         self.copy.start()
         self.here = False
 
+    def wait(self):
+        self.copy.wait()
+        self.here = True
+
     def __getitem__(self, index):
         if not self.here:
-            self.copy.wait()
-            self.here = True
+            self.wait()
+        return self.buffer[index]
+
+
+class FetchedPieces:
+    def __init__(self, source, buffer, semaphore, count):
+        self.buffer = buffer
+        step = buffer.shape[0] // count
+        self.parts = [
+            Fetched(source.at[pl.ds(i * step, step)], buffer.at[pl.ds(i * step, step)], semaphore.at[i])
+            for i in range(count)
+        ]
+        self.here = False
+
+    def wait(self):
+        for part in self.parts:
+            part.copy.wait()
+        self.here = True
+
+    def __getitem__(self, index):
+        if not self.here:
+            self.wait()
         return self.buffer[index]
 
 
@@ -826,8 +913,8 @@
         pass
 
 
-def call(kernel, args, outs, kept=(), kept_out=(), raw=(), through=None, flops=None):
-    through = through or {}
+def call(kernel, args, outs, kept=(), kept_out=(), raw=(), through=None, flops=None, late=0, pieces=None):
+    through, pieces = through or {}, pieces or {}
     moved = [i for i in range(len(args)) if i not in kept and i not in raw]
     written = [i for i in range(len(outs)) if i not in kept_out and i not in through]
 
@@ -835,8 +922,12 @@
         ins, results = refs[: len(args)], refs[len(args) : len(args) + len(outs)]
         buffers, (in_sem, out_sem, through_sem) = refs[len(args) + len(outs) : -3], refs[-3:]
         fetched, stored = list(ins), [Kept(ref) for ref in results]
-        for t, i in enumerate(moved):
-            fetched[i] = Fetched(ins[i], buffers[t], in_sem.at[t])
+        for i in sorted(moved, key=lambda i: i not in pieces):
+            t, at = moved.index(i), sum(pieces.get(m, 1) for m in moved[: moved.index(i)])
+            if i in pieces:
+                fetched[i] = FetchedPieces(ins[i], buffers[t], in_sem.at[pl.ds(at, pieces[i])], pieces[i])
+            else:
+                fetched[i] = Fetched(ins[i], buffers[t], in_sem.at[at])
         for t, i in enumerate(written):
             stored[i] = Stored(results[i], buffers[len(moved) + t], out_sem.at[t])
         passing = [
@@ -844,12 +935,20 @@
         ]
         for copy in passing:
             copy.start()
+        if moved or passing:
+            spot = (0,) * (len(outs[-1 - late][0]) - 2)
+            blank = stored[-1 - late]
+
+            @pl.when(lax.axis_index("gx") >= 0)
+            def _():
+                blank[spot] = jnp.zeros(outs[-1 - late][0][-2:], outs[-1 - late][1])
+
         kernel(*fetched, *stored)
         for i in written:
             stored[i].flush()
         for i in moved:
             if not fetched[i].here:
-                fetched[i].copy.wait()
+                fetched[i].wait()
         for copy in passing:
             copy.wait()
         for i in written:
@@ -867,7 +966,7 @@
         out_specs=[place(i in kept_out) for i in range(len(outs))],
         scratch_shapes=[pltpu.VMEM(args[i].shape, args[i].dtype) for i in moved]
         + [pltpu.VMEM(*outs[i]) for i in written]
-        + [semaphores(len(moved)), semaphores(len(written)), semaphores(len(through))],
+        + [semaphores(sum(pieces.get(i, 1) for i in moved)), semaphores(len(written)), semaphores(len(through))],
         compiler_params=pltpu.CompilerParams(vmem_limit_bytes=LIMIT),
         cost_estimate=flops and pl.CostEstimate(flops=flops, bytes_accessed=flops // 512, transcendentals=0),
     )(*args)
@@ -890,12 +989,13 @@
     width = coarse_inverse.shape[-1]
     sends = lambda rows: [((SPAN_Y // 2, rows, 128), F32), ((rows, 128), F32), ((rows, 128), F32)]
     state = ((SUBS, CASES, 256), F32)
+    plain = ((CASES * SUBS, 128), F32)
 
     raw = [by_sub(dual_schur), by_sub(coupling), edge_map, by_sub(corner_slot)]
-    own, *out, schur, coupled, placed, slotted, inverse = call(
+    own, *out, schur, coupled, placed, slotted, inverse, p = call(
         start_kernel,
         [native(residual), native(direction), by_sub(active), by_sub(scaling), *raw, coarse_inverse[0]],
-        [((SUBS, CAST, 256), F32)] + sends(CAST) + [(v.shape, v.dtype) for v in raw] + [((len(UPPER), 128, 128), F32)],
+        [((SUBS, CAST, 256), F32)] + sends(CAST) + [(v.shape, v.dtype) for v in raw] + [((len(UPPER), 128, 128), F32), plain],
         kept_out=(0, 4, 5, 6, 7),
         raw=(4, 5, 6, 7),
         through={4: lambda v: v[4], 5: lambda v: v[5], 6: lambda v: v[6], 7: lambda v: v[7]},
@@ -913,38 +1013,45 @@
         flops=5 * 10**9,
     )
     rows = 2 * CASES + SLOTS + 8
-    r, p, mk, y, block, *out, high, low = call(
+    r, mk, y, block, *out, high, low = call(
         first_kernel,
         [own, *come, high, low, cc, ch, cl, names],
-        [state, state, ((SUBS, 8, 256), F32), ((SUBS, 2 * CASES, 256), F32), ((48, 8, 128), F32)]
+        [state, ((SUBS, 8, 256), F32), ((SUBS, 2 * CASES, 256), F32), ((48, 8, 128), F32)]
         + sends(rows)
         + [matrix, matrix],
         kept=range(10),
-        kept_out=(2, 3),
-        through={8: lambda v: v[4], 9: lambda v: v[5]},
+        kept_out=(0, 1, 2),
+        through={7: lambda v: v[4], 8: lambda v: v[5]},
+        late=2,
     )
     got = lax.all_to_all(block.reshape(32, 3, 4, 128), BOTH, 0, 0, tiled=False).reshape(48, 8, 128)
     come = trade(*out)
     square = ((2, width, width), BF16)
-    gh, gl = call(inverse_kernel, [coarse_inverse[0], other], [square, square], kept_out=(0, 1), flops=10**9)
-    side = ((128, 512), BF16)
-    onward = [state, state, state, state, ((4, CASES, 128), F32), ((16, 8, 128), F32), state] + sends(CASES)
-    pick, near, nh, nl, r, s, p, lam, scal, block, y, *out = call(
+    gh, gl, gh_far, gl_far = call(
+        inverse_kernel, [coarse_inverse[0], other], [square] * 4, kept=(1,), kept_out=(0, 1), flops=10**9
+    )
+    side = ((SLOTS, 512), BF16)
+    onward = [plain, plain, state, state, ((5, CASES, 128), F32), ((16, 8, 128), F32), state] + sends(CASES)
+    nh, nl, p, lam, r, s, scal, block, y, *out = call(
         second_kernel,
-        [got, *come, y, r, p, mk, native(duals), prev_rho.reshape(1, CASES), gh, gl, names, high, low, ch, cl],
-        [((2, 2, 256, width), BF16), ((2, width, 128), BF16), side, side] + onward,
-        kept=(0, 1, 2, 3, 4, 7, 10, 11, 12, 15, 16),
-        kept_out=(0, 1, 2, 3, 8, 10),
-    )
+        [got, *come, y, r, mk, p, native(duals), prev_rho.reshape(1, CASES), gh, gl, names, high, low, ch, cl],
+        [side, side] + onward,
+        kept=(0, 1, 2, 3, 4, 5, 6, 10, 11, 12, 15, 16),
+        kept_out=(0, 1, 2, 3, 4, 6, 8),
+        late=3,
+    )
+    dense = ((2, 2, 256, 512), BF16)
+    dh, dl = call(dense_kernel, [got, gh_far, gl_far], [dense, dense], kept_out=(0, 1), flops=3 * 10**9)
     for step in range(1, ITERS):
         got = lax.all_to_all(block.reshape(32, 4, 128), BOTH, 0, 0, tiled=False).reshape(16, 8, 128)
         come = trade(*out)
-        args = [got, *come, y, r, s, p, lam, scal, mk, pick, gh, gl, near, nh, nl, ch, cl]
-        kept = (0, 1, 2, 3, 4, *range(9, 19))
+        args = [got, *come, y, r, s, scal, mk, dh, dl, nh, nl, ch, cl, p, lam]
+        kept = (*range(6), *range(7, 17))
         if step < ITERS - 1:
-            r, s, p, lam, scal, block, y, *out = call(round_kernel, args + [high, low], onward, kept, kept_out=(4, 6))
+            p, lam, r, s, scal, block, y, *out = call(
+                round_kernel, args + [high, low], onward, kept, kept_out=(0, 1, 2, 4, 6), late=3
+            )
         else:
-            plain = ((CASES * SUBS, 128), F32)
             results = call(last_kernel, args, [plain, plain, plain], kept)
     return tuple(v.reshape(duals.shape) for v in results)
 

time: 112 us -> 105 us (0.938)
  waiting for transfers between devices: 28.8 us -> 24.7 us
  Pallas kernels: 33.3 us -> 30.1 us
  starting transfers between devices: 47.2 us -> 48.5 us
    pallas_call x10 -> x11, Pallas kernels: 33.3 us -> 30.1 us  [call(): pl.pallas_call(body, out_shape=[jax.ShapeDtypeStruct(*out) if i in kept_o...]
    all_to_all x5, waiting for transfers between devices: 16.8 us -> 14.4 us  [two_regions(): lax.all_to_all(block.reshape(32, 4, 128), BOTH, 0, 0, tiled=False)]
    all_to_all x5, starting transfers between devices: 20.2 us -> 21.6 us  [two_regions(): lax.all_to_all(block.reshape(32, 4, 128), BOTH, 0, 0, tiled=False)]
  transfers between devices with their start and end apart: 28 -> 28, of which waited for: 17 -> 15; matrix products, arithmetic and copies ran while one was open for 0% -> 0% of each run, Pallas kernels for 5% -> 10%
where the time goes in v5:
time: 105 us; the launch traced here: 104 us
  starting transfers between devices  48.5 us (46%)
  Pallas kernels  30.1 us (29%)
  waiting for transfers between devices  24.7 us (24%)
  between operations  1.07 us (1%)
    pallas_call x11, Pallas kernels, call(): pl.pallas_call(body, out_shape=[jax.ShapeDtypeStruct(*out) if i in kept_o...  30.1 us
    all_to_all x5, starting transfers between devices, two_regions(): lax.all_to_all(block.reshape(32, 4, 128), BOTH, 0, 0, tiled=False)  21.6 us
    all_to_all x5, waiting for transfers between devices, two_regions(): lax.all_to_all(block.reshape(32, 4, 128), BOTH, 0, 0, tiled=False)  14.4 us
    ppermute x7, starting transfers between devices, trade(): lax.ppermute(x, 'gx', [(0, 1), (1, 0)])  14 us
    all_to_all x1, starting transfers between devices, two_regions(): lax.all_to_all(block.reshape(32, 3, 4, 128), BOTH, 0, 0, tiled=False)  8.15 us
    ppermute x7, starting transfers between devices, trade(): lax.ppermute(b, 'gy', both_ways(pairs_from(1, peers)))  4.55 us
    ppermute x7, waiting for transfers between devices, trade(): lax.ppermute(x, 'gx', [(0, 1), (1, 0)])  4.12 us
    all_to_all x1, waiting for transfers between devices, two_regions(): lax.all_to_all(block.reshape(32, 3, 4, 128), BOTH, 0, 0, tiled=False)  3.24 us
  transfers between devices with their start and end apart: 28, of which 15 were waited for; matrix products, arithmetic and copies ran while one was open for 0% of the time, Pallas kernels for 10%

profile of v5, /device:TPU:0, one launch (start us, length us, event | category | flops | bytes accessed | tf_op | source)
XLA Modules:
  0.0 104.4 jit_solution(8575050787011262695)
XLA Ops:
  0.6 2.7 %shard_map.130 = (f32[8,40,256]{2,1,0:T(8,128)S(1)}, f32[2,40,128]{2,1,0:T(8,128)}, f32[40,128]{1,0:T(8,128)}, f32[40,128]{1,0:T(8,128)}, f32[8,256,256]{2,1,0:T...) custom-call(f32[128,128]{1,0:T(8,128)} %bitcast.37, ...), custom_call_target="tpu_custom_call" | custom-call | tf_op jit(solution)/shard_map/pallas_call | solution.py:960
  3.4 3.0 %collective-permute-start = (f32[2,40,128]{2,1,0:T(8,128)}, f32[2,40,128]{2,1,0:T(8,128)S(1)}, u32[]{:S(2)}, u32[]{:S(2)}) collective-permute-start(f32[2,40,128]{2,1,0:T(8,128)} %get-tuple-element.90), channel_id=1, source_target_pairs={{0,16},{16,0},{1,17},{17,1},{2,18},{18,2},{3,19},{19,3},{4,20},{20... | collective-permute-start | bytes 122888 | tf_op jit(solution)/shard_map/ppermute | solution.py:978
  7.2 3.0 %shard_map.131 = (bf16[8,256,256]{2,1,0:T(8,128)(2,1)S(1)}, bf16[8,256,256]{2,1,0:T(8,128)(2,1)S(1)}, f32[8,32,256]{2,1,0:T(8,128)S(1)}, bf16[8,32,256]{2,1,0:T(...) custom-call(f32[8,256,256]{2,1,0:T(8,128)S(1)} %get-tuple-element.93.refs_0_, ...), custom_call_target="tpu_custom_call" | custom-call | flops 5000000000 | bytes 9765625 | tf_op jit(solution)/shard_map/pallas_call | solution.py:960
  11.8 8.2 %all-to-all-start = ((f32[32,3,4,128]{3,2,1,0:T(4,128)}), f32[32,3,4,128]{3,2,1,0:T(4,128)S(1)}, u32[]{:S(2)}, u32[]{:S(2)}) async-start(f32[32,3,4,128]{3,2,1,0:T(4,128)} %bitcast.35), calls=%async_computation | async-start | bytes 393216 | tf_op jit(solution)/shard_map/all_to_all | solution.py:1027
  19.9 1.8 %collective-permute-start.3 = (f32[2,72,128]{2,1,0:T(8,128)}, f32[2,72,128]{2,1,0:T(8,128)S(1)}, u32[]{:S(2)}, u32[]{:S(2)}) collective-permute-start(f32[2,72,128]{2,1,0:T(8,128)} %get-tuple-element.104), channel_id=1, source_target_pairs={{0,16},{16,0},{1,17},{17,1},{2,18},{18,2},{3,19},{19,3},{4,20},{20... | collective-permute-start | bytes 221192 | tf_op jit(solution)/shard_map/ppermute | solution.py:978
  22.4 2.3 %shard_map.133 = (bf16[2,384,384]{2,1,0:T(8,128)(2,1)S(1)}, bf16[2,384,384]{2,1,0:T(8,128)(2,1)S(1)}, bf16[2,384,384]{2,1,0:T(8,128)(2,1)}, bf16[2,384,384]{2,1,0:T(8,128)(2,1)}) custom-call(f32[384,384]{1,0:T(8,128)} %bitcast.34, f32[6,128,128]{2,1,0:T(8,128)S(1)} %collective-permute-done.6.refs_1_), custom_call_target="tpu_custom_call" | custom-call | flops 1000000000 | bytes 1953125 | tf_op jit(solution)/shard_map/pallas_call | solution.py:960
  25.6 3.2 %all-to-all-done = f32[32,3,4,128]{3,2,1,0:T(4,128)S(1)} async-done(((f32[32,3,4,128]{3,2,1,0:T(4,128)}), f32[32,3,4,128]{3,2,1,0:T(4,128)S(1)}, u32[]{:S(2)}, u32[]{:S(2)}) %all-to-all-start) | async-done | bytes 196640 | tf_op jit(solution)/shard_map/all_to_all | solution.py:1027
  28.9 3.3 %shard_map.134 = (bf16[32,512]{1,0:T(8,128)(2,1)S(1)}, bf16[32,512]{1,0:T(8,128)(2,1)S(1)}, f32[128,128]{1,0:T(8,128)S(1)}, f32[128,128]{1,0:T(8,128)S(1)}, f32[...) custom-call(f32[48,8,128]{2,1,0:T(8,128)S(1)} %bitcast.25, ...), custom_call_target="tpu_custom_call" | custom-call | tf_op jit(solution)/shard_map/pallas_call | solution.py:960
  32.2 3.1 %all-to-all-start.1 = ((f32[32,4,128]{2,1,0:T(4,128)}), f32[32,4,128]{2,1,0:T(4,128)S(1)}, u32[]{:S(2)}, u32[]{:S(2)}) async-start(f32[32,4,128]{2,1,0:T(4,128)} %bitcast.40), calls=%async_computation.1 | async-start | bytes 131072 | tf_op jit(solution)/shard_map/all_to_all | solution.py:1046
  35.4 1.8 %collective-permute-start.7 = (f32[2,16,128]{2,1,0:T(8,128)}, f32[2,16,128]{2,1,0:T(8,128)S(1)}, u32[]{:S(2)}, u32[]{:S(2)}) collective-permute-start(f32[2,16,128]{2,1,0:T(8,128)} %get-tuple-element.117), channel_id=1, source_target_pairs={{0,16},{16,0},{1,17},{17,1},{2,18},{18,2},{3,19},{19,3},{4,20},{20... | collective-permute-start | bytes 49160 | tf_op jit(solution)/shard_map/ppermute | solution.py:978
  37.9 3.9 %shard_map.135 = (bf16[2,2,256,512]{3,2,1,0:T(8,128)(2,1)S(1)}, bf16[2,2,256,512]{3,2,1,0:T(8,128)(2,1)S(1)}) custom-call(f32[48,8,128]{2,1,0:T(8,128)} %bitcast.26, bf16[2,384,384]{2,1,0:T(8,128)(2,1)} %get-tuple-element.124.refs_1_, bf16[2,384,384]{2,1,0:T(8,128)(2,1)} %get-tuple-element.125.refs_2_), custom_call_target="tpu_custom_call" | custom-call | flops 3000000000 | bytes 5859375 | tf_op jit(solution)/shard_map/pallas_call | solution.py:960
  42.8 2.9 %shard_map.136 = (f32[128,128]{1,0:T(8,128)S(1)}, f32[128,128]{1,0:T(8,128)S(1)}, f32[8,16,256]{2,1,0:T(8,128)S(1)}, f32[8,16,256]{2,1,0:T(8,128)}, f32[5,16,128...) custom-call(f32[16,8,128]{2,1,0:T(8,128)S(1)} %bitcast.27, ...), custom_call_target="tpu_custom_call" | custom-call | tf_op jit(solution)/shard_map/pallas_call | solution.py:960
  45.7 5.6 %all-to-all-start.2 = ((f32[32,4,128]{2,1,0:T(4,128)}), f32[32,4,128]{2,1,0:T(4,128)S(1)}, u32[]{:S(2)}, u32[]{:S(2)}) async-start(f32[32,4,128]{2,1,0:T(4,128)} %bitcast.42), calls=%async_computation.2 | async-start | bytes 131072 | tf_op jit(solution)/shard_map/all_to_all | solution.py:1046
  51.3 1.8 %collective-permute-start.10 = (f32[2,16,128]{2,1,0:T(8,128)}, f32[2,16,128]{2,1,0:T(8,128)S(1)}, u32[]{:S(2)}, u32[]{:S(2)}) collective-permute-start(f32[2,16,128]{2,1,0:T(8,128)} %get-tuple-element.133), channel_id=1, source_target_pairs={{0,16},{16,0},{1,17},{17,1},{2,18},{18,2},{3,19},{19,3},{4,20},{20... | collective-permute-start | bytes 49160 | tf_op jit(solution)/shard_map/ppermute | solution.py:978
  55.3 3.4 %all-to-all-done.2 = f32[32,4,128]{2,1,0:T(4,128)S(1)} async-done(((f32[32,4,128]{2,1,0:T(4,128)}), f32[32,4,128]{2,1,0:T(4,128)S(1)}, u32[]{:S(2)}, u32[]{:S(2)}) %all-to-all-start.2) | async-done | bytes 65568 | tf_op jit(solution)/shard_map/all_to_all | solution.py:1046
  58.7 2.9 %shard_map.137 = (f32[128,128]{1,0:T(8,128)S(1)}, f32[128,128]{1,0:T(8,128)S(1)}, f32[8,16,256]{2,1,0:T(8,128)S(1)}, f32[8,16,256]{2,1,0:T(8,128)}, f32[5,16,128...) custom-call(f32[16,8,128]{2,1,0:T(8,128)S(1)} %bitcast.29, ...), custom_call_target="tpu_custom_call" | custom-call | tf_op jit(solution)/shard_map/pallas_call | solution.py:960
  61.6 4.3 %all-to-all-start.3 = ((f32[32,4,128]{2,1,0:T(4,128)}), f32[32,4,128]{2,1,0:T(4,128)S(1)}, u32[]{:S(2)}, u32[]{:S(2)}) async-start(f32[32,4,128]{2,1,0:T(4,128)} %bitcast.43), calls=%async_computation.3 | async-start | bytes 131072 | tf_op jit(solution)/shard_map/all_to_all | solution.py:1046
  69.9 3.4 %all-to-all-done.3 = f32[32,4,128]{2,1,0:T(4,128)S(1)} async-done(((f32[32,4,128]{2,1,0:T(4,128)}), f32[32,4,128]{2,1,0:T(4,128)S(1)}, u32[]{:S(2)}, u32[]{:S(2)}) %all-to-all-start.3) | async-done | bytes 65568 | tf_op jit(solution)/shard_map/all_to_all | solution.py:1046
  73.3 2.9 %shard_map.138 = (f32[128,128]{1,0:T(8,128)S(1)}, f32[128,128]{1,0:T(8,128)S(1)}, f32[8,16,256]{2,1,0:T(8,128)S(1)}, f32[8,16,256]{2,1,0:T(8,128)}, f32[5,16,128...) custom-call(f32[16,8,128]{2,1,0:T(8,128)S(1)} %bitcast.30, ...), custom_call_target="tpu_custom_call" | custom-call | tf_op jit(solution)/shard_map/pallas_call | solution.py:960
  76.2 4.3 %all-to-all-start.4 = ((f32[32,4,128]{2,1,0:T(4,128)}), f32[32,4,128]{2,1,0:T(4,128)S(1)}, u32[]{:S(2)}, u32[]{:S(2)}) async-start(f32[32,4,128]{2,1,0:T(4,128)} %bitcast.44), calls=%async_computation.4 | async-start | bytes 131072 | tf_op jit(solution)/shard_map/all_to_all | solution.py:1046
  84.5 3.4 %all-to-all-done.4 = f32[32,4,128]{2,1,0:T(4,128)S(1)} async-done(((f32[32,4,128]{2,1,0:T(4,128)}), f32[32,4,128]{2,1,0:T(4,128)S(1)}, u32[]{:S(2)}, u32[]{:S(2)}) %all-to-all-start.4) | async-done | bytes 65568 | tf_op jit(solution)/shard_map/all_to_all | solution.py:1046
  87.9 2.9 %shard_map.139 = (f32[128,128]{1,0:T(8,128)S(1)}, f32[128,128]{1,0:T(8,128)S(1)}, f32[8,16,256]{2,1,0:T(8,128)S(1)}, f32[8,16,256]{2,1,0:T(8,128)}, f32[5,16,128...) custom-call(f32[16,8,128]{2,1,0:T(8,128)S(1)} %bitcast.28, ...), custom_call_target="tpu_custom_call" | custom-call | tf_op jit(solution)/shard_map/pallas_call | solution.py:960
  90.8 4.3 %all-to-all-start.5 = ((f32[32,4,128]{2,1,0:T(4,128)}), f32[32,4,128]{2,1,0:T(4,128)S(1)}, u32[]{:S(2)}, u32[]{:S(2)}) async-start(f32[32,4,128]{2,1,0:T(4,128)} %bitcast.41), calls=%async_computation.5 | async-start | bytes 131072 | tf_op jit(solution)/shard_map/all_to_all | solution.py:1046
  99.1 3.4 %all-to-all-done.5 = f32[32,4,128]{2,1,0:T(4,128)S(1)} async-done(((f32[32,4,128]{2,1,0:T(4,128)}), f32[32,4,128]{2,1,0:T(4,128)S(1)}, u32[]{:S(2)}, u32[]{:S(2)}) %all-to-all-start.5) | async-done | bytes 65568 | tf_op jit(solution)/shard_map/all_to_all | solution.py:1046
  (45 shorter events, 21.5 us)
Async XLA Ops:
  3.4 6.9 %collective-permute-start = (f32[2,40,128]{2,1,0:T(8,128)}, f32[2,40,128]{2,1,0:T(8,128)S(1)}, u32[]{:S(2)}, u32[]{:S(2)}) collective-permute-start(f32[2,40,128]{2,1,0:T(8,128)} %get-tuple-element.90), channel_id=1, source_target_pairs={{0,16},{16,0},{1,17},{17,1},{2,18},{18,2},{3,19},{19,3},{4,20},{20... | collective-permute-start | bytes 122888 | tf_op jit(solution)/shard_map/ppermute | solution.py:978
  6.4 3.8 %collective-permute-start.1 = (f32[40,128]{1,0:T(8,128)}, f32[40,128]{1,0:T(8,128)S(1)}, u32[]{:S(2)}, u32[]{:S(2)}) collective-permute-start(f32[40,128]{1,0:T(8,128)} %get-tuple-element.91), channel_id=1, source_target_pairs={{0,1},{2,3},{4,5},{6,7},{8,9},{10,11},{12,13},{14,15},{1,0},{3,2},... | collective-permute-start | bytes 61448 | tf_op jit(solution)/shard_map/ppermute | solution.py:979
  6.4 3.8 %collective-permute-start.2 = (f32[40,128]{1,0:T(8,128)}, f32[40,128]{1,0:T(8,128)S(1)}, u32[]{:S(2)}, u32[]{:S(2)}) collective-permute-start(f32[40,128]{1,0:T(8,128)} %get-tuple-element.92), channel_id=1, source_target_pairs={{1,2},{3,4},{5,6},{7,8},{9,10},{11,12},{13,14},{2,1},{4,3},{6,5},{... | collective-permute-start | bytes 61448 | tf_op jit(solution)/shard_map/ppermute | solution.py:980
  7.1 15.4 %collective-permute-start.6 = (f32[6,128,128]{2,1,0:T(8,128)}, f32[6,128,128]{2,1,0:T(8,128)S(1)}, u32[]{:S(2)}, u32[]{:S(2)}) collective-permute-start(f32[6,128,128]{2,1,0:T(8,128)} %get-tuple-element.111), channel_id=1, source_target_pairs={{0,16},{16,0},{1,17},{17,1},{2,18},{18,2},{3,19},{19,3},{4,20},{20... | collective-permute-start | bytes 1179656 | tf_op jit(solution)/shard_map/ppermute | solution.py:1004
  11.8 17.1 %all-to-all-start = ((f32[32,3,4,128]{3,2,1,0:T(4,128)}), f32[32,3,4,128]{3,2,1,0:T(4,128)S(1)}, u32[]{:S(2)}, u32[]{:S(2)}) async-start(f32[32,3,4,128]{3,2,1,0:T(4,128)} %bitcast.35), calls=%async_computation | async-start | bytes 393216 | tf_op jit(solution)/shard_map/all_to_all | solution.py:1027
  19.9 5.7 %collective-permute-start.3 = (f32[2,72,128]{2,1,0:T(8,128)}, f32[2,72,128]{2,1,0:T(8,128)S(1)}, u32[]{:S(2)}, u32[]{:S(2)}) collective-permute-start(f32[2,72,128]{2,1,0:T(8,128)} %get-tuple-element.104), channel_id=1, source_target_pairs={{0,16},{16,0},{1,17},{17,1},{2,18},{18,2},{3,19},{19,3},{4,20},{20... | collective-permute-start | bytes 221192 | tf_op jit(solution)/shard_map/ppermute | solution.py:978
  21.8 3.0 %collective-permute-start.4 = (f32[72,128]{1,0:T(8,128)}, f32[72,128]{1,0:T(8,128)S(1)}, u32[]{:S(2)}, u32[]{:S(2)}) collective-permute-start(f32[72,128]{1,0:T(8,128)} %get-tuple-element.105), channel_id=1, source_target_pairs={{0,1},{2,3},{4,5},{6,7},{8,9},{10,11},{12,13},{14,15},{1,0},{3,2},... | collective-permute-start | bytes 110600 | tf_op jit(solution)/shard_map/ppermute | solution.py:979
  21.8 3.0 %collective-permute-start.5 = (f32[72,128]{1,0:T(8,128)}, f32[72,128]{1,0:T(8,128)S(1)}, u32[]{:S(2)}, u32[]{:S(2)}) collective-permute-start(f32[72,128]{1,0:T(8,128)} %get-tuple-element.106), channel_id=1, source_target_pairs={{1,2},{3,4},{5,6},{7,8},{9,10},{11,12},{13,14},{2,1},{4,3},{6,5},{... | collective-permute-start | bytes 110600 | tf_op jit(solution)/shard_map/ppermute | solution.py:980
  32.2 10.6 %all-to-all-start.1 = ((f32[32,4,128]{2,1,0:T(4,128)}), f32[32,4,128]{2,1,0:T(4,128)S(1)}, u32[]{:S(2)}, u32[]{:S(2)}) async-start(f32[32,4,128]{2,1,0:T(4,128)} %bitcast.40), calls=%async_computation.1 | async-start | bytes 131072 | tf_op jit(solution)/shard_map/all_to_all | solution.py:1046
  35.4 6.4 %collective-permute-start.7 = (f32[2,16,128]{2,1,0:T(8,128)}, f32[2,16,128]{2,1,0:T(8,128)S(1)}, u32[]{:S(2)}, u32[]{:S(2)}) collective-permute-start(f32[2,16,128]{2,1,0:T(8,128)} %get-tuple-element.117), channel_id=1, source_target_pairs={{0,16},{16,0},{1,17},{17,1},{2,18},{18,2},{3,19},{19,3},{4,20},{20... | collective-permute-start | bytes 49160 | tf_op jit(solution)/shard_map/ppermute | solution.py:978
  37.2 4.6 %collective-permute-start.8 = (f32[16,128]{1,0:T(8,128)}, f32[16,128]{1,0:T(8,128)S(1)}, u32[]{:S(2)}, u32[]{:S(2)}) collective-permute-start(f32[16,128]{1,0:T(8,128)} %get-tuple-element.118), channel_id=1, source_target_pairs={{0,1},{2,3},{4,5},{6,7},{8,9},{10,11},{12,13},{14,15},{1,0},{3,2},... | collective-permute-start | bytes 24584 | tf_op jit(solution)/shard_map/ppermute | solution.py:979
  37.2 4.6 %collective-permute-start.9 = (f32[16,128]{1,0:T(8,128)}, f32[16,128]{1,0:T(8,128)S(1)}, u32[]{:S(2)}, u32[]{:S(2)}) collective-permute-start(f32[16,128]{1,0:T(8,128)} %get-tuple-element.119), channel_id=1, source_target_pairs={{1,2},{3,4},{5,6},{7,8},{9,10},{11,12},{13,14},{2,1},{4,3},{6,5},{... | collective-permute-start | bytes 24584 | tf_op jit(solution)/shard_map/ppermute | solution.py:980
  45.7 13.0 %all-to-all-start.2 = ((f32[32,4,128]{2,1,0:T(4,128)}), f32[32,4,128]{2,1,0:T(4,128)S(1)}, u32[]{:S(2)}, u32[]{:S(2)}) async-start(f32[32,4,128]{2,1,0:T(4,128)} %bitcast.42), calls=%async_computation.2 | async-start | bytes 131072 | tf_op jit(solution)/shard_map/all_to_all | solution.py:1046
  51.3 4.0 %collective-permute-start.10 = (f32[2,16,128]{2,1,0:T(8,128)}, f32[2,16,128]{2,1,0:T(8,128)S(1)}, u32[]{:S(2)}, u32[]{:S(2)}) collective-permute-start(f32[2,16,128]{2,1,0:T(8,128)} %get-tuple-element.133), channel_id=1, source_target_pairs={{0,16},{16,0},{1,17},{17,1},{2,18},{18,2},{3,19},{19,3},{4,20},{20... | collective-permute-start | bytes 49160 | tf_op jit(solution)/shard_map/ppermute | solution.py:978
  53.1 1.4 %collective-permute-start.11 = (f32[16,128]{1,0:T(8,128)}, f32[16,128]{1,0:T(8,128)S(1)}, u32[]{:S(2)}, u32[]{:S(2)}) collective-permute-start(f32[16,128]{1,0:T(8,128)} %get-tuple-element.134), channel_id=1, source_target_pairs={{0,1},{2,3},{4,5},{6,7},{8,9},{10,11},{12,13},{14,15},{1,0},{3,2},... | collective-permute-start | bytes 24584 | tf_op jit(solution)/shard_map/ppermute | solution.py:979
  61.6 11.7 %all-to-all-start.3 = ((f32[32,4,128]{2,1,0:T(4,128)}), f32[32,4,128]{2,1,0:T(4,128)S(1)}, u32[]{:S(2)}, u32[]{:S(2)}) async-start(f32[32,4,128]{2,1,0:T(4,128)} %bitcast.43), calls=%async_computation.3 | async-start | bytes 131072 | tf_op jit(solution)/shard_map/all_to_all | solution.py:1046
  65.9 4.0 %collective-permute-start.13 = (f32[2,16,128]{2,1,0:T(8,128)}, f32[2,16,128]{2,1,0:T(8,128)S(1)}, u32[]{:S(2)}, u32[]{:S(2)}) collective-permute-start(f32[2,16,128]{2,1,0:T(8,128)} %get-tuple-element.143), channel_id=1, source_target_pairs={{0,16},{16,0},{1,17},{17,1},{2,18},{18,2},{3,19},{19,3},{4,20},{20... | collective-permute-start | bytes 49160 | tf_op jit(solution)/shard_map/ppermute | solution.py:978
  67.7 1.4 %collective-permute-start.14 = (f32[16,128]{1,0:T(8,128)}, f32[16,128]{1,0:T(8,128)S(1)}, u32[]{:S(2)}, u32[]{:S(2)}) collective-permute-start(f32[16,128]{1,0:T(8,128)} %get-tuple-element.144), channel_id=1, source_target_pairs={{0,1},{2,3},{4,5},{6,7},{8,9},{10,11},{12,13},{14,15},{1,0},{3,2},... | collective-permute-start | bytes 24584 | tf_op jit(solution)/shard_map/ppermute | solution.py:979
  67.7 1.4 %collective-permute-start.15 = (f32[16,128]{1,0:T(8,128)}, f32[16,128]{1,0:T(8,128)S(1)}, u32[]{:S(2)}, u32[]{:S(2)}) collective-permute-start(f32[16,128]{1,0:T(8,128)} %get-tuple-element.145), channel_id=1, source_target_pairs={{1,2},{3,4},{5,6},{7,8},{9,10},{11,12},{13,14},{2,1},{4,3},{6,5},{... | collective-permute-start | bytes 24584 | tf_op jit(solution)/shard_map/ppermute | solution.py:980
  76.2 11.7 %all-to-all-start.4 = ((f32[32,4,128]{2,1,0:T(4,128)}), f32[32,4,128]{2,1,0:T(4,128)S(1)}, u32[]{:S(2)}, u32[]{:S(2)}) async-start(f32[32,4,128]{2,1,0:T(4,128)} %bitcast.44), calls=%async_computation.4 | async-start | bytes 131072 | tf_op jit(solution)/shard_map/all_to_all | solution.py:1046
  80.5 4.0 %collective-permute-start.16 = (f32[2,16,128]{2,1,0:T(8,128)}, f32[2,16,128]{2,1,0:T(8,128)S(1)}, u32[]{:S(2)}, u32[]{:S(2)}) collective-permute-start(f32[2,16,128]{2,1,0:T(8,128)} %get-tuple-element.153), channel_id=1, source_target_pairs={{0,16},{16,0},{1,17},{17,1},{2,18},{18,2},{3,19},{19,3},{4,20},{20... | collective-permute-start | bytes 49160 | tf_op jit(solution)/shard_map/ppermute | solution.py:978
  82.3 1.4 %collective-permute-start.18 = (f32[16,128]{1,0:T(8,128)}, f32[16,128]{1,0:T(8,128)S(1)}, u32[]{:S(2)}, u32[]{:S(2)}) collective-permute-start(f32[16,128]{1,0:T(8,128)} %get-tuple-element.155), channel_id=1, source_target_pairs={{1,2},{3,4},{5,6},{7,8},{9,10},{11,12},{13,14},{2,1},{4,3},{6,5},{... | collective-permute-start | bytes 24584 | tf_op jit(solution)/shard_map/ppermute | solution.py:980
  90.8 11.7 %all-to-all-start.5 = ((f32[32,4,128]{2,1,0:T(4,128)}), f32[32,4,128]{2,1,0:T(4,128)S(1)}, u32[]{:S(2)}, u32[]{:S(2)}) async-start(f32[32,4,128]{2,1,0:T(4,128)} %bitcast.41), calls=%async_computation.5 | async-start | bytes 131072 | tf_op jit(solution)/shard_map/all_to_all | solution.py:1046
  95.1 4.0 %collective-permute-start.19 = (f32[2,16,128]{2,1,0:T(8,128)}, f32[2,16,128]{2,1,0:T(8,128)S(1)}, u32[]{:S(2)}, u32[]{:S(2)}) collective-permute-start(f32[2,16,128]{2,1,0:T(8,128)} %get-tuple-element.163), channel_id=1, source_target_pairs={{0,16},{16,0},{1,17},{17,1},{2,18},{18,2},{3,19},{19,3},{4,20},{20... | collective-permute-start | bytes 49160 | tf_op jit(solution)/shard_map/ppermute | solution.py:978
  (5 other events, 8.9 us)

commit v6 on v5

--- a/solution.py
+++ b/solution.py
@@ -259,6 +259,7 @@
 SPAN_X, SPAN_Y = 2, 4
 SUBS = SPAN_X * SPAN_Y
 CASES = 16
+STAY = 2
 SLOTS = 32
 USED = 2 * (SPAN_X + 1) * (SPAN_Y + 1)
 CAST = 40
@@ -324,6 +325,9 @@
         x_ref[t, rows, :] = jnp.where(first, east[t], west[t])
     a_ref[rows, :] = jnp.where(even, north, south)
     b_ref[rows, :] = jnp.where(even, south, north)
+    if at == 0:
+        rest = pl.ds(b_ref.shape[0] * 2 // 3, b_ref.shape[0] - b_ref.shape[0] * 2 // 3)
+        b_ref[rest, :] = jnp.zeros((rest.size, 128), F32)
 
 
 def received(x_ref, a_ref, b_ref, at, n, side=None):
@@ -422,7 +426,7 @@
 
 
 def operator_kernel(
-    schur_ref, couple_ref, map_ref, slot_ref, high_ref, low_ref, cc_ref, ch_ref, cl_ref, name_ref,
+    schur_ref, couple_ref, map_ref, slot_ref, ha_ref, la_ref, hb_ref, lb_ref, cc_ref, ch_ref, cl_ref, name_ref,
 ):
     none = 384
     slot = slot_ref[...].astype(F32)
@@ -463,7 +467,10 @@
         s1, s2 = split(schur_ref[i])
         tall = dot_turned(jnp.concatenate([s1, s2, c1, c2, c3], 0), place)
         high, low = (dot(place, tall[t : t + 256].astype(BF16)).astype(BF16) for t in (0, 256))
-        high_ref[i], low_ref[i] = high, low
+        if i < STAY:
+            ha_ref[i], la_ref[i] = high, low
+        else:
+            hb_ref[i - STAY], lb_ref[i - STAY] = high, low
         cc = tall[512 : 512 + SLOTS] + tall[512 + SLOTS : 512 + 2 * SLOTS] + tall[512 + 2 * SLOTS :]
         cc_ref[i] = cc
         ch_ref[i], cl_ref[i] = split(cc)
@@ -529,8 +536,11 @@
     return total + pltpu.roll(total, 32, 1)
 
 
-def by_schur(us, high_ref, low_ref):
-    return [dot_split(us[i], high_ref[i], low_ref[i]) for i in range(SUBS)]
+def by_schur(us, ha_ref, la_ref, hb_ref, lb_ref):
+    return [
+        dot_split(us[i], ha_ref[i], la_ref[i]) if i < STAY else dot_split(us[i], hb_ref[i - STAY], lb_ref[i - STAY])
+        for i in range(SUBS)
+    ]
 
 
 def over_lanes(terms):
@@ -632,17 +642,18 @@
         which = lax.rem(lax.axis_index("gx") + region, 2)
         for whole_ref, out_ref in ((gh_ref, dh_ref), (gl_ref, dl_ref)):
             half = dot(whole_ref[which], picks).astype(BF16)
-            for par in range(2):
-                out_ref[region, par] = dot(rows[par], half).astype(BF16)
+            top = dot(rows[0], half).astype(BF16)
+            out_ref[region, 0], out_ref[region, 1] = top[:, :256], top[:, 256:]
+            out_ref[region, 2] = dot(rows[1], half[:, 256:]).astype(BF16)
 
 
 def solve_dense(spots, dh_ref, dl_ref):
     total, sols = None, []
     for region in range(2):
         v = spots[region]
-        one, two = (dot_split(v, dh_ref[region, par], dl_ref[region, par]) for par in range(2))
+        block = lambda t, dot=dot: dot_split(v, dh_ref[region, t], dl_ref[region, t], dot)
         first = (iota(v.shape, 0) // 4) % 2 == 0
-        sol = jnp.where(first, one[:, :256] + swap_pairs(two[:, :256]), two[:, 256:] + swap_pairs(one[:, 256:]))
+        sol = jnp.where(first, block(0) + swap_pairs(block(1, dot_turned)), block(2) + swap_pairs(block(1)))
         total = v * sol if total is None else total + v * sol
         sols.append(sol)
     total = jnp.sum(total, 1, keepdims=True)
@@ -662,11 +673,11 @@
     return first_of_pairs(jnp.sum(both, 1, keepdims=True))
 
 
-def emit(rs, mk_ref, high_ref, low_ref, ch_ref, cl_ref, block_ref, y_ref, x_ref, a_ref, b_ref):
+def emit(rs, mk_ref, schur_refs, ch_ref, cl_ref, block_ref, y_ref, x_ref, a_ref, b_ref):
     us = [mk_ref[i, 0:1, :] * rs[i] for i in range(SUBS)]
     corner = corners(us, ch_ref, cl_ref)
     rho = over_lanes([jnp.where(owned_lanes(i, CASES), rs[i] * us[i], 0.0) for i in range(SUBS)])
-    ys = by_schur(us, high_ref, low_ref)
+    ys = by_schur(us, *schur_refs)
     send(ys, x_ref, a_ref, b_ref, 0)
     for i in range(SUBS):
         y_ref[i] = ys[i]
@@ -677,12 +688,14 @@
     twice = jnp.concatenate([block, block], 0)
     for j in range(16):
         block_ref[j] = twice
+    block_ref.flush()
 
 
 def first_kernel(
-    own_ref, x_ref, a_ref, b_ref, high_ref, low_ref, cc_ref, ch_ref, cl_ref, name_ref,
+    own_ref, x_ref, a_ref, b_ref, ha_ref, la_ref, hb_ref, lb_ref, cc_ref, ch_ref, cl_ref, name_ref,
     r_ref, mk_ref, y_ref, block_ref, sx_ref, sa_ref, sb_ref, high_out_ref, low_out_ref,
 ):
+    schur_refs = ha_ref, la_ref, hb_ref, lb_ref
     own = [own_ref[i] for i in range(SUBS)]
     other = across(own, received(x_ref, a_ref, b_ref, 0, CAST), CAST)
     rs, vs = [], []
@@ -693,7 +706,7 @@
         mk_ref[i] = full[2 * CASES : 2 * CASES + 8]
         vs.append(jnp.concatenate([full[2 * CASES : 2 * CASES + 1] * full[:CASES], full[CASES : 2 * CASES]], 0))
     corner = corners(vs, ch_ref, cl_ref)
-    ys = by_schur(vs, high_ref, low_ref)
+    ys = by_schur(vs, *schur_refs)
     names = name_ref[...]
     send([jnp.concatenate([ys[i], cc_ref[i]], 0) for i in range(SUBS)], sx_ref, sa_ref, sb_ref, 0)
     at = pl.ds(2 * CASES + SLOTS, 8)
@@ -732,7 +745,7 @@
 
 def second_kernel(
     got_ref, x_ref, a_ref, b_ref, y_ref, r_ref, mk_ref, p_ref, l_ref, rho_ref, gh_ref, gl_ref, name_ref,
-    high_ref, low_ref, ch_ref, cl_ref,
+    ha_ref, la_ref, hb_ref, lb_ref, ch_ref, cl_ref,
     nh_ref, nl_ref, po_ref, lo_ref, ro_ref, so_ref, scal_ref, block_ref, yo_ref, sx_ref, sa_ref, sb_ref,
 ):
     near_ref, pick_ref = near_names(name_ref, x_ref, a_ref, b_ref), {}
@@ -786,8 +799,11 @@
     scalars = rho, pi, beta, skew, alpha
     keep_scalars(scal_ref, scalars)
     so_ref.flush()
-    track(r_ref, scalars, mk_ref, p_ref, l_ref, po_ref, lo_ref)
-    emit(rs, mk_ref, high_ref, low_ref, ch_ref, cl_ref, block_ref, yo_ref, sx_ref, sa_ref, sb_ref)
+    emit(rs, mk_ref, (ha_ref, la_ref, hb_ref, lb_ref), ch_ref, cl_ref, block_ref, yo_ref, sx_ref, sa_ref, sb_ref)
+
+    @pl.when(lax.axis_index("gx") >= 0)
+    def _():
+        track(r_ref, scalars, mk_ref, p_ref, l_ref, po_ref, lo_ref)
 
 
 def absorb(got_ref, x_ref, a_ref, b_ref, y_ref, r_ref, s_ref, scal_ref, mk_ref, dh_ref, dl_ref, nh_ref, nl_ref, ch_ref, cl_ref):
@@ -817,7 +833,7 @@
 
 def round_kernel(
     got_ref, x_ref, a_ref, b_ref, y_ref, r_ref, s_ref, scal_ref, mk_ref, dh_ref, dl_ref,
-    nh_ref, nl_ref, ch_ref, cl_ref, p_ref, l_ref, high_ref, low_ref,
+    nh_ref, nl_ref, ch_ref, cl_ref, p_ref, l_ref, ha_ref, la_ref, hb_ref, lb_ref,
     po_ref, lo_ref, ro_ref, so_ref, scalo_ref, block_ref, yo_ref, sx_ref, sa_ref, sb_ref,
 ):
     rs, ss, scalars = absorb(
@@ -827,8 +843,11 @@
         ro_ref[i], so_ref[i] = rs[i], ss[i]
     so_ref.flush()
     keep_scalars(scalo_ref, scalars)
-    track(r_ref, scalars, mk_ref, p_ref, l_ref, po_ref, lo_ref)
-    emit(rs, mk_ref, high_ref, low_ref, ch_ref, cl_ref, block_ref, yo_ref, sx_ref, sa_ref, sb_ref)
+    emit(rs, mk_ref, (ha_ref, la_ref, hb_ref, lb_ref), ch_ref, cl_ref, block_ref, yo_ref, sx_ref, sa_ref, sb_ref)
+
+    @pl.when(lax.axis_index("gx") >= 0)
+    def _():
+        track(r_ref, scalars, mk_ref, p_ref, l_ref, po_ref, lo_ref)
 
 
 def last_kernel(
@@ -892,6 +911,10 @@
 
     def __getitem__(self, index):
         return self.buffer[index]
+
+    @property
+    def shape(self):
+        return self.buffer.shape
 
     def flush(self):
         if not self.sent:
@@ -987,7 +1010,7 @@
     native = lambda v: v.reshape(CASES * SUBS, 128)
     by_sub = lambda v: v.reshape((SUBS,) + v.shape[2:])
     width = coarse_inverse.shape[-1]
-    sends = lambda rows: [((SPAN_Y // 2, rows, 128), F32), ((rows, 128), F32), ((rows, 128), F32)]
+    sends = lambda rows: [((SPAN_Y // 2, rows, 128), F32), ((rows, 128), F32), ((-(-3 * rows // 16) * 8, 128), F32)]
     state = ((SUBS, CASES, 256), F32)
     plain = ((CASES * SUBS, 128), F32)
 
@@ -1002,45 +1025,45 @@
     )
     come = trade(*out)
     other = lax.ppermute(inverse, "gx", [(0, 1), (1, 0)])
-    matrix = ((SUBS, 256, 256), BF16)
+    first_part, rest = ((STAY, 256, 256), BF16), ((SUBS - STAY, 256, 256), BF16)
     couple = ((SUBS, SLOTS, 256), BF16)
-    high, low, cc, ch, cl, names = call(
+    ha, la, hb, lb, cc, ch, cl, names = call(
         operator_kernel,
         [schur, coupled, placed, slotted],
-        [matrix, matrix, ((SUBS, SLOTS, 256), F32), couple, couple, ((8, 128), F32)],
+        [first_part, first_part, rest, rest, ((SUBS, SLOTS, 256), F32), couple, couple, ((8, 128), F32)],
         kept=range(4),
-        kept_out=range(6),
+        kept_out=range(8),
         flops=5 * 10**9,
     )
     rows = 2 * CASES + SLOTS + 8
-    r, mk, y, block, *out, high, low = call(
+    r, mk, y, block, *out, hb, lb = call(
         first_kernel,
-        [own, *come, high, low, cc, ch, cl, names],
+        [own, *come, ha, la, hb, lb, cc, ch, cl, names],
         [state, ((SUBS, 8, 256), F32), ((SUBS, 2 * CASES, 256), F32), ((48, 8, 128), F32)]
         + sends(rows)
-        + [matrix, matrix],
-        kept=range(10),
+        + [rest, rest],
+        kept=range(12),
         kept_out=(0, 1, 2),
-        through={7: lambda v: v[4], 8: lambda v: v[5]},
+        through={7: lambda v: v[6], 8: lambda v: v[7]},
         late=2,
     )
     got = lax.all_to_all(block.reshape(32, 3, 4, 128), BOTH, 0, 0, tiled=False).reshape(48, 8, 128)
     come = trade(*out)
     square = ((2, width, width), BF16)
     gh, gl, gh_far, gl_far = call(
-        inverse_kernel, [coarse_inverse[0], other], [square] * 4, kept=(1,), kept_out=(0, 1), flops=10**9
+        inverse_kernel, [coarse_inverse[0], other], [square] * 4, kept_out=(0, 1), flops=10**9
     )
     side = ((SLOTS, 512), BF16)
     onward = [plain, plain, state, state, ((5, CASES, 128), F32), ((16, 8, 128), F32), state] + sends(CASES)
     nh, nl, p, lam, r, s, scal, block, y, *out = call(
         second_kernel,
-        [got, *come, y, r, mk, p, native(duals), prev_rho.reshape(1, CASES), gh, gl, names, high, low, ch, cl],
+        [got, *come, y, r, mk, p, native(duals), prev_rho.reshape(1, CASES), gh, gl, names, ha, la, hb, lb, ch, cl],
         [side, side] + onward,
-        kept=(0, 1, 2, 3, 4, 5, 6, 10, 11, 12, 15, 16),
+        kept=(0, 1, 2, 3, 4, 5, 6, 10, 11, 12, 13, 14, 17, 18),
         kept_out=(0, 1, 2, 3, 4, 6, 8),
         late=3,
     )
-    dense = ((2, 2, 256, 512), BF16)
+    dense = ((2, 3, 256, 256), BF16)
     dh, dl = call(dense_kernel, [got, gh_far, gl_far], [dense, dense], kept_out=(0, 1), flops=3 * 10**9)
     for step in range(1, ITERS):
         got = lax.all_to_all(block.reshape(32, 4, 128), BOTH, 0, 0, tiled=False).reshape(16, 8, 128)
@@ -1049,7 +1072,7 @@
         kept = (*range(6), *range(7, 17))
         if step < ITERS - 1:
             p, lam, r, s, scal, block, y, *out = call(
-                round_kernel, args + [high, low], onward, kept, kept_out=(0, 1, 2, 4, 6), late=3
+                round_kernel, args + [ha, la, hb, lb], onward, (*kept, 17, 18), kept_out=(0, 1, 2, 4, 6), late=3
             )
         else:
             results = call(last_kernel, args, [plain, plain, plain], kept)

time: 105 us -> 104 us (level)
  starting transfers between devices: 48.5 us -> 60.1 us
  waiting for transfers between devices: 24.7 us -> 13.3 us
  Pallas kernels: 30.1 us -> 28.6 us
    ppermute x7, starting transfers between devices: 0.02 us -> 11.6 us  [trade(): lax.ppermute(a, 'gy', both_ways(pairs_from(0, peers)))]
    all_to_all x5, waiting for transfers between devices: 14.4 us -> 5.13 us  [two_regions(): lax.all_to_all(block.reshape(32, 4, 128), BOTH, 0, 0, tiled=False)]
    ppermute x7, waiting for transfers between devices: 4.12 us -> 0.7 us  [trade(): lax.ppermute(x, 'gx', [(0, 1), (1, 0)])]
    pallas_call x11, Pallas kernels: 30.1 us -> 28.6 us  [call(): pl.pallas_call(body, out_shape=[jax.ShapeDtypeStruct(*out) if i in kept_o...]
    ppermute x7, waiting for transfers between devices: 2.9 us -> 4.16 us  [trade(): lax.ppermute(a, 'gy', both_ways(pairs_from(0, peers)))]
  transfers between devices with their start and end apart: 28 -> 28, of which waited for: 15 -> 11; matrix products, arithmetic and copies ran while one was open for 0% -> 0% of each run, Pallas kernels for 10% -> 10%
where the time goes in v6:
time: 104 us; the launch traced here: 103 us
  starting transfers between devices  60.1 us (58%)
  Pallas kernels  28.6 us (28%)
  waiting for transfers between devices  13.3 us (13%)
  between operations  1.07 us (1%)
    pallas_call x11, Pallas kernels, call(): pl.pallas_call(body, out_shape=[jax.ShapeDtypeStruct(*out) if i in kept_o...  28.6 us
    all_to_all x5, starting transfers between devices, two_regions(): lax.all_to_all(block.reshape(32, 4, 128), BOTH, 0, 0, tiled=False)  21.6 us
    ppermute x7, starting transfers between devices, trade(): lax.ppermute(x, 'gx', [(0, 1), (1, 0)])  14 us
    ppermute x7, starting transfers between devices, trade(): lax.ppermute(a, 'gy', both_ways(pairs_from(0, peers)))  11.6 us
    all_to_all x1, starting transfers between devices, two_regions(): lax.all_to_all(block.reshape(32, 3, 4, 128), BOTH, 0, 0, tiled=False)  8.15 us
    all_to_all x5, waiting for transfers between devices, two_regions(): lax.all_to_all(block.reshape(32, 4, 128), BOTH, 0, 0, tiled=False)  5.13 us
    ppermute x7, starting transfers between devices, trade(): lax.ppermute(b, 'gy', both_ways(pairs_from(1, peers)))  4.55 us
    ppermute x7, waiting for transfers between devices, trade(): lax.ppermute(a, 'gy', both_ways(pairs_from(0, peers)))  4.16 us
  transfers between devices with their start and end apart: 28, of which 11 were waited for; matrix products, arithmetic and copies ran while one was open for 0% of the time, Pallas kernels for 10%

profile of v6, /device:TPU:0, one launch (start us, length us, event | category | flops | bytes accessed | tf_op | source)
XLA Modules:
  0.0 103.0 jit_solution(10462096563900618411)
XLA Ops:
  0.6 2.7 %shard_map.130 = (f32[8,40,256]{2,1,0:T(8,128)S(1)}, f32[2,40,128]{2,1,0:T(8,128)}, f32[40,128]{1,0:T(8,128)}, f32[64,128]{1,0:T(8,128)}, f32[8,256,256]{2,1,0:T...) custom-call(f32[128,128]{1,0:T(8,128)} %bitcast.37, ...), custom_call_target="tpu_custom_call" | custom-call | tf_op jit(solution)/shard_map/pallas_call | solution.py:983
  3.4 3.0 %collective-permute-start = (f32[2,40,128]{2,1,0:T(8,128)}, f32[2,40,128]{2,1,0:T(8,128)S(1)}, u32[]{:S(2)}, u32[]{:S(2)}) collective-permute-start(f32[2,40,128]{2,1,0:T(8,128)} %get-tuple-element.92), channel_id=1, source_target_pairs={{0,16},{16,0},{1,17},{17,1},{2,18},{18,2},{3,19},{19,3},{4,20},{20... | collective-permute-start | bytes 122888 | tf_op jit(solution)/shard_map/ppermute | solution.py:1001
  7.2 3.0 %shard_map.131 = (bf16[2,256,256]{2,1,0:T(8,128)(2,1)S(1)}, bf16[2,256,256]{2,1,0:T(8,128)(2,1)S(1)}, bf16[6,256,256]{2,1,0:T(8,128)(2,1)S(1)}, bf16[6,256,256]{...) custom-call(f32[8,256,256]{2,1,0:T(8,128)S(1)} %get-tuple-element.95, ...), custom_call_target="tpu_custom_call" | custom-call | flops 5000000000 | bytes 9765625 | tf_op jit(solution)/shard_map/pallas_call | solution.py:983
  11.7 8.2 %all-to-all-start = ((f32[32,3,4,128]{3,2,1,0:T(4,128)}), f32[32,3,4,128]{3,2,1,0:T(4,128)S(1)}, u32[]{:S(2)}, u32[]{:S(2)}) async-start(f32[32,3,4,128]{3,2,1,0:T(4,128)} %bitcast.35), calls=%async_computation | async-start | bytes 393216 | tf_op jit(solution)/shard_map/all_to_all | solution.py:1050
  19.9 1.8 %collective-permute-start.3 = (f32[2,72,128]{2,1,0:T(8,128)}, f32[2,72,128]{2,1,0:T(8,128)S(1)}, u32[]{:S(2)}, u32[]{:S(2)}) collective-permute-start(f32[2,72,128]{2,1,0:T(8,128)} %get-tuple-element.108), channel_id=1, source_target_pairs={{0,16},{16,0},{1,17},{17,1},{2,18},{18,2},{3,19},{19,3},{4,20},{20... | collective-permute-start | bytes 221192 | tf_op jit(solution)/shard_map/ppermute | solution.py:1001
  22.4 2.5 %shard_map.133 = (bf16[2,384,384]{2,1,0:T(8,128)(2,1)S(1)}, bf16[2,384,384]{2,1,0:T(8,128)(2,1)S(1)}, bf16[2,384,384]{2,1,0:T(8,128)(2,1)}, bf16[2,384,384]{2,1,0:T(8,128)(2,1)}) custom-call(f32[384,384]{1,0:T(8,128)} %bitcast.34, f32[6,128,128]{2,1,0:T(8,128)} %collective-permute-done.6.refs_1_), custom_call_target="tpu_custom_call" | custom-call | flops 1000000000 | bytes 1953125 | tf_op jit(solution)/shard_map/pallas_call | solution.py:983
  25.6 3.2 %all-to-all-done = f32[32,3,4,128]{3,2,1,0:T(4,128)S(1)} async-done(((f32[32,3,4,128]{3,2,1,0:T(4,128)}), f32[32,3,4,128]{3,2,1,0:T(4,128)S(1)}, u32[]{:S(2)}, u32[]{:S(2)}) %all-to-all-start) | async-done | bytes 196640 | tf_op jit(solution)/shard_map/all_to_all | solution.py:1050
  28.8 3.1 %shard_map.134 = (bf16[32,512]{1,0:T(8,128)(2,1)S(1)}, bf16[32,512]{1,0:T(8,128)(2,1)S(1)}, f32[128,128]{1,0:T(8,128)S(1)}, f32[128,128]{1,0:T(8,128)S(1)}, f32[...) custom-call(f32[48,8,128]{2,1,0:T(8,128)S(1)} %bitcast.25, ...), custom_call_target="tpu_custom_call" | custom-call | tf_op jit(solution)/shard_map/pallas_call | solution.py:983
  31.9 3.4 %all-to-all-start.1 = ((f32[32,4,128]{2,1,0:T(4,128)}), f32[32,4,128]{2,1,0:T(4,128)S(1)}, u32[]{:S(2)}, u32[]{:S(2)}) async-start(f32[32,4,128]{2,1,0:T(4,128)} %bitcast.40), calls=%async_computation.1 | async-start | bytes 131072 | tf_op jit(solution)/shard_map/all_to_all | solution.py:1069
  37.8 3.7 %shard_map.135 = (bf16[2,3,256,256]{3,2,1,0:T(8,128)(2,1)S(1)}, bf16[2,3,256,256]{3,2,1,0:T(8,128)(2,1)S(1)}) custom-call(f32[48,8,128]{2,1,0:T(8,128)} %bitcast.26, bf16[2,384,384]{2,1,0:T(8,128)(2,1)} %get-tuple-element.128.refs_1_, bf16[2,384,384]{2,1,0:T(8,128)(2,1)} %get-tuple-element.129.refs_2_), custom_call_target="tpu_custom_call" | custom-call | flops 3000000000 | bytes 5859375 | tf_op jit(solution)/shard_map/pallas_call | solution.py:983
  42.8 2.6 %shard_map.136 = (f32[128,128]{1,0:T(8,128)S(1)}, f32[128,128]{1,0:T(8,128)S(1)}, f32[8,16,256]{2,1,0:T(8,128)S(1)}, f32[8,16,256]{2,1,0:T(8,128)}, f32[5,16,128...) custom-call(f32[16,8,128]{2,1,0:T(8,128)S(1)} %bitcast.27, ...), custom_call_target="tpu_custom_call" | custom-call | tf_op jit(solution)/shard_map/pallas_call | solution.py:983
  45.4 5.4 %all-to-all-start.2 = ((f32[32,4,128]{2,1,0:T(4,128)}), f32[32,4,128]{2,1,0:T(4,128)S(1)}, u32[]{:S(2)}, u32[]{:S(2)}) async-start(f32[32,4,128]{2,1,0:T(4,128)} %bitcast.42), calls=%async_computation.2 | async-start | bytes 131072 | tf_op jit(solution)/shard_map/all_to_all | solution.py:1069
  53.3 2.9 %collective-permute-start.11 = (f32[16,128]{1,0:T(8,128)}, f32[16,128]{1,0:T(8,128)S(1)}, u32[]{:S(2)}, u32[]{:S(2)}) collective-permute-start(f32[16,128]{1,0:T(8,128)} %get-tuple-element.138), channel_id=1, source_target_pairs={{0,1},{2,3},{4,5},{6,7},{8,9},{10,11},{12,13},{14,15},{1,0},{3,2},... | collective-permute-start | bytes 24584 | tf_op jit(solution)/shard_map/ppermute | solution.py:1002
  58.2 2.6 %shard_map.137 = (f32[128,128]{1,0:T(8,128)S(1)}, f32[128,128]{1,0:T(8,128)S(1)}, f32[8,16,256]{2,1,0:T(8,128)S(1)}, f32[8,16,256]{2,1,0:T(8,128)}, f32[5,16,128...) custom-call(f32[16,8,128]{2,1,0:T(8,128)S(1)} %bitcast.29, ...), custom_call_target="tpu_custom_call" | custom-call | tf_op jit(solution)/shard_map/pallas_call | solution.py:983
  60.8 4.3 %all-to-all-start.3 = ((f32[32,4,128]{2,1,0:T(4,128)}), f32[32,4,128]{2,1,0:T(4,128)S(1)}, u32[]{:S(2)}, u32[]{:S(2)}) async-start(f32[32,4,128]{2,1,0:T(4,128)} %bitcast.43), calls=%async_computation.3 | async-start | bytes 131072 | tf_op jit(solution)/shard_map/all_to_all | solution.py:1069
  67.6 2.9 %collective-permute-start.14 = (f32[16,128]{1,0:T(8,128)}, f32[16,128]{1,0:T(8,128)S(1)}, u32[]{:S(2)}, u32[]{:S(2)}) collective-permute-start(f32[16,128]{1,0:T(8,128)} %get-tuple-element.148), channel_id=1, source_target_pairs={{0,1},{2,3},{4,5},{6,7},{8,9},{10,11},{12,13},{14,15},{1,0},{3,2},... | collective-permute-start | bytes 24584 | tf_op jit(solution)/shard_map/ppermute | solution.py:1002
  72.5 2.6 %shard_map.138 = (f32[128,128]{1,0:T(8,128)S(1)}, f32[128,128]{1,0:T(8,128)S(1)}, f32[8,16,256]{2,1,0:T(8,128)S(1)}, f32[8,16,256]{2,1,0:T(8,128)}, f32[5,16,128...) custom-call(f32[16,8,128]{2,1,0:T(8,128)S(1)} %bitcast.30, ...), custom_call_target="tpu_custom_call" | custom-call | tf_op jit(solution)/shard_map/pallas_call | solution.py:983
  75.1 4.3 %all-to-all-start.4 = ((f32[32,4,128]{2,1,0:T(4,128)}), f32[32,4,128]{2,1,0:T(4,128)S(1)}, u32[]{:S(2)}, u32[]{:S(2)}) async-start(f32[32,4,128]{2,1,0:T(4,128)} %bitcast.44), calls=%async_computation.4 | async-start | bytes 131072 | tf_op jit(solution)/shard_map/all_to_all | solution.py:1069
  79.4 1.8 %collective-permute-start.16 = (f32[2,16,128]{2,1,0:T(8,128)}, f32[2,16,128]{2,1,0:T(8,128)S(1)}, u32[]{:S(2)}, u32[]{:S(2)}) collective-permute-start(f32[2,16,128]{2,1,0:T(8,128)} %get-tuple-element.157), channel_id=1, source_target_pairs={{0,16},{16,0},{1,17},{17,1},{2,18},{18,2},{3,19},{19,3},{4,20},{20... | collective-permute-start | bytes 49160 | tf_op jit(solution)/shard_map/ppermute | solution.py:1001
  81.9 2.9 %collective-permute-start.17 = (f32[16,128]{1,0:T(8,128)}, f32[16,128]{1,0:T(8,128)S(1)}, u32[]{:S(2)}, u32[]{:S(2)}) collective-permute-start(f32[16,128]{1,0:T(8,128)} %get-tuple-element.158), channel_id=1, source_target_pairs={{0,1},{2,3},{4,5},{6,7},{8,9},{10,11},{12,13},{14,15},{1,0},{3,2},... | collective-permute-start | bytes 24584 | tf_op jit(solution)/shard_map/ppermute | solution.py:1002
  86.8 2.6 %shard_map.139 = (f32[128,128]{1,0:T(8,128)S(1)}, f32[128,128]{1,0:T(8,128)S(1)}, f32[8,16,256]{2,1,0:T(8,128)S(1)}, f32[8,16,256]{2,1,0:T(8,128)}, f32[5,16,128...) custom-call(f32[16,8,128]{2,1,0:T(8,128)S(1)} %bitcast.28, ...), custom_call_target="tpu_custom_call" | custom-call | tf_op jit(solution)/shard_map/pallas_call | solution.py:983
  89.4 4.3 %all-to-all-start.5 = ((f32[32,4,128]{2,1,0:T(4,128)}), f32[32,4,128]{2,1,0:T(4,128)S(1)}, u32[]{:S(2)}, u32[]{:S(2)}) async-start(f32[32,4,128]{2,1,0:T(4,128)} %bitcast.41), calls=%async_computation.5 | async-start | bytes 131072 | tf_op jit(solution)/shard_map/all_to_all | solution.py:1069
  93.7 1.8 %collective-permute-start.19 = (f32[2,16,128]{2,1,0:T(8,128)}, f32[2,16,128]{2,1,0:T(8,128)S(1)}, u32[]{:S(2)}, u32[]{:S(2)}) collective-permute-start(f32[2,16,128]{2,1,0:T(8,128)} %get-tuple-element.167), channel_id=1, source_target_pairs={{0,16},{16,0},{1,17},{17,1},{2,18},{18,2},{3,19},{19,3},{4,20},{20... | collective-permute-start | bytes 49160 | tf_op jit(solution)/shard_map/ppermute | solution.py:1001
  96.2 2.9 %collective-permute-start.20 = (f32[16,128]{1,0:T(8,128)}, f32[16,128]{1,0:T(8,128)S(1)}, u32[]{:S(2)}, u32[]{:S(2)}) collective-permute-start(f32[16,128]{1,0:T(8,128)} %get-tuple-element.168), channel_id=1, source_target_pairs={{0,1},{2,3},{4,5},{6,7},{8,9},{10,11},{12,13},{14,15},{1,0},{3,2},... | collective-permute-start | bytes 24584 | tf_op jit(solution)/shard_map/ppermute | solution.py:1002
  (45 shorter events, 23.5 us)
Async XLA Ops:
  3.4 6.9 %collective-permute-start = (f32[2,40,128]{2,1,0:T(8,128)}, f32[2,40,128]{2,1,0:T(8,128)S(1)}, u32[]{:S(2)}, u32[]{:S(2)}) collective-permute-start(f32[2,40,128]{2,1,0:T(8,128)} %get-tuple-element.92), channel_id=1, source_target_pairs={{0,16},{16,0},{1,17},{17,1},{2,18},{18,2},{3,19},{19,3},{4,20},{20... | collective-permute-start | bytes 122888 | tf_op jit(solution)/shard_map/ppermute | solution.py:1001
  7.0 15.3 %collective-permute-start.6 = (f32[6,128,128]{2,1,0:T(8,128)}, f32[6,128,128]{2,1,0:T(8,128)}, u32[]{:S(2)}, u32[]{:S(2)}) collective-permute-start(f32[6,128,128]{2,1,0:T(8,128)} %get-tuple-element.115), channel_id=1, source_target_pairs={{0,16},{16,0},{1,17},{17,1},{2,18},{18,2},{3,19},{19,3},{4,20},{20... | collective-permute-start | bytes 1179656 | tf_op jit(solution)/shard_map/ppermute | solution.py:1027
  11.7 17.1 %all-to-all-start = ((f32[32,3,4,128]{3,2,1,0:T(4,128)}), f32[32,3,4,128]{3,2,1,0:T(4,128)S(1)}, u32[]{:S(2)}, u32[]{:S(2)}) async-start(f32[32,3,4,128]{3,2,1,0:T(4,128)} %bitcast.35), calls=%async_computation | async-start | bytes 393216 | tf_op jit(solution)/shard_map/all_to_all | solution.py:1050
  19.9 5.7 %collective-permute-start.3 = (f32[2,72,128]{2,1,0:T(8,128)}, f32[2,72,128]{2,1,0:T(8,128)S(1)}, u32[]{:S(2)}, u32[]{:S(2)}) collective-permute-start(f32[2,72,128]{2,1,0:T(8,128)} %get-tuple-element.108), channel_id=1, source_target_pairs={{0,16},{16,0},{1,17},{17,1},{2,18},{18,2},{3,19},{19,3},{4,20},{20... | collective-permute-start | bytes 221192 | tf_op jit(solution)/shard_map/ppermute | solution.py:1001
  31.9 10.9 %all-to-all-start.1 = ((f32[32,4,128]{2,1,0:T(4,128)}), f32[32,4,128]{2,1,0:T(4,128)S(1)}, u32[]{:S(2)}, u32[]{:S(2)}) async-start(f32[32,4,128]{2,1,0:T(4,128)} %bitcast.40), calls=%async_computation.1 | async-start | bytes 131072 | tf_op jit(solution)/shard_map/all_to_all | solution.py:1069
  35.4 6.2 %collective-permute-start.7 = (f32[2,16,128]{2,1,0:T(8,128)}, f32[2,16,128]{2,1,0:T(8,128)S(1)}, u32[]{:S(2)}, u32[]{:S(2)}) collective-permute-start(f32[2,16,128]{2,1,0:T(8,128)} %get-tuple-element.121), channel_id=1, source_target_pairs={{0,16},{16,0},{1,17},{17,1},{2,18},{18,2},{3,19},{19,3},{4,20},{20... | collective-permute-start | bytes 49160 | tf_op jit(solution)/shard_map/ppermute | solution.py:1001
  37.2 4.4 %collective-permute-start.8 = (f32[16,128]{1,0:T(8,128)}, f32[16,128]{1,0:T(8,128)S(1)}, u32[]{:S(2)}, u32[]{:S(2)}) collective-permute-start(f32[16,128]{1,0:T(8,128)} %get-tuple-element.122), channel_id=1, source_target_pairs={{0,1},{2,3},{4,5},{6,7},{8,9},{10,11},{12,13},{14,15},{1,0},{3,2},... | collective-permute-start | bytes 24584 | tf_op jit(solution)/shard_map/ppermute | solution.py:1002
  37.2 4.4 %collective-permute-start.9 = (f32[24,128]{1,0:T(8,128)}, f32[24,128]{1,0:T(8,128)S(1)}, u32[]{:S(2)}, u32[]{:S(2)}) collective-permute-start(f32[24,128]{1,0:T(8,128)} %get-tuple-element.123), channel_id=1, source_target_pairs={{1,2},{3,4},{5,6},{7,8},{9,10},{11,12},{13,14},{2,1},{4,3},{6,5},{... | collective-permute-start | bytes 36872 | tf_op jit(solution)/shard_map/ppermute | solution.py:1003
  45.4 12.8 %all-to-all-start.2 = ((f32[32,4,128]{2,1,0:T(4,128)}), f32[32,4,128]{2,1,0:T(4,128)S(1)}, u32[]{:S(2)}, u32[]{:S(2)}) async-start(f32[32,4,128]{2,1,0:T(4,128)} %bitcast.42), calls=%async_computation.2 | async-start | bytes 131072 | tf_op jit(solution)/shard_map/all_to_all | solution.py:1069
  50.8 6.4 %collective-permute-start.10 = (f32[2,16,128]{2,1,0:T(8,128)}, f32[2,16,128]{2,1,0:T(8,128)S(1)}, u32[]{:S(2)}, u32[]{:S(2)}) collective-permute-start(f32[2,16,128]{2,1,0:T(8,128)} %get-tuple-element.137), channel_id=1, source_target_pairs={{0,16},{16,0},{1,17},{17,1},{2,18},{18,2},{3,19},{19,3},{4,20},{20... | collective-permute-start | bytes 49160 | tf_op jit(solution)/shard_map/ppermute | solution.py:1001
  52.6 4.6 %collective-permute-start.12 = (f32[24,128]{1,0:T(8,128)}, f32[24,128]{1,0:T(8,128)S(1)}, u32[]{:S(2)}, u32[]{:S(2)}) collective-permute-start(f32[24,128]{1,0:T(8,128)} %get-tuple-element.139), channel_id=1, source_target_pairs={{1,2},{3,4},{5,6},{7,8},{9,10},{11,12},{13,14},{2,1},{4,3},{6,5},{... | collective-permute-start | bytes 36872 | tf_op jit(solution)/shard_map/ppermute | solution.py:1003
  53.3 3.9 %collective-permute-start.11 = (f32[16,128]{1,0:T(8,128)}, f32[16,128]{1,0:T(8,128)S(1)}, u32[]{:S(2)}, u32[]{:S(2)}) collective-permute-start(f32[16,128]{1,0:T(8,128)} %get-tuple-element.138), channel_id=1, source_target_pairs={{0,1},{2,3},{4,5},{6,7},{8,9},{10,11},{12,13},{14,15},{1,0},{3,2},... | collective-permute-start | bytes 24584 | tf_op jit(solution)/shard_map/ppermute | solution.py:1002
  60.8 11.7 %all-to-all-start.3 = ((f32[32,4,128]{2,1,0:T(4,128)}), f32[32,4,128]{2,1,0:T(4,128)S(1)}, u32[]{:S(2)}, u32[]{:S(2)}) async-start(f32[32,4,128]{2,1,0:T(4,128)} %bitcast.43), calls=%async_computation.3 | async-start | bytes 131072 | tf_op jit(solution)/shard_map/all_to_all | solution.py:1069
  65.1 6.4 %collective-permute-start.13 = (f32[2,16,128]{2,1,0:T(8,128)}, f32[2,16,128]{2,1,0:T(8,128)S(1)}, u32[]{:S(2)}, u32[]{:S(2)}) collective-permute-start(f32[2,16,128]{2,1,0:T(8,128)} %get-tuple-element.147), channel_id=1, source_target_pairs={{0,16},{16,0},{1,17},{17,1},{2,18},{18,2},{3,19},{19,3},{4,20},{20... | collective-permute-start | bytes 49160 | tf_op jit(solution)/shard_map/ppermute | solution.py:1001
  66.9 4.6 %collective-permute-start.15 = (f32[24,128]{1,0:T(8,128)}, f32[24,128]{1,0:T(8,128)S(1)}, u32[]{:S(2)}, u32[]{:S(2)}) collective-permute-start(f32[24,128]{1,0:T(8,128)} %get-tuple-element.149), channel_id=1, source_target_pairs={{1,2},{3,4},{5,6},{7,8},{9,10},{11,12},{13,14},{2,1},{4,3},{6,5},{... | collective-permute-start | bytes 36872 | tf_op jit(solution)/shard_map/ppermute | solution.py:1003
  67.6 3.9 %collective-permute-start.14 = (f32[16,128]{1,0:T(8,128)}, f32[16,128]{1,0:T(8,128)S(1)}, u32[]{:S(2)}, u32[]{:S(2)}) collective-permute-start(f32[16,128]{1,0:T(8,128)} %get-tuple-element.148), channel_id=1, source_target_pairs={{0,1},{2,3},{4,5},{6,7},{8,9},{10,11},{12,13},{14,15},{1,0},{3,2},... | collective-permute-start | bytes 24584 | tf_op jit(solution)/shard_map/ppermute | solution.py:1002
  75.1 11.7 %all-to-all-start.4 = ((f32[32,4,128]{2,1,0:T(4,128)}), f32[32,4,128]{2,1,0:T(4,128)S(1)}, u32[]{:S(2)}, u32[]{:S(2)}) async-start(f32[32,4,128]{2,1,0:T(4,128)} %bitcast.44), calls=%async_computation.4 | async-start | bytes 131072 | tf_op jit(solution)/shard_map/all_to_all | solution.py:1069
  79.4 6.4 %collective-permute-start.16 = (f32[2,16,128]{2,1,0:T(8,128)}, f32[2,16,128]{2,1,0:T(8,128)S(1)}, u32[]{:S(2)}, u32[]{:S(2)}) collective-permute-start(f32[2,16,128]{2,1,0:T(8,128)} %get-tuple-element.157), channel_id=1, source_target_pairs={{0,16},{16,0},{1,17},{17,1},{2,18},{18,2},{3,19},{19,3},{4,20},{20... | collective-permute-start | bytes 49160 | tf_op jit(solution)/shard_map/ppermute | solution.py:1001
  81.2 4.6 %collective-permute-start.18 = (f32[24,128]{1,0:T(8,128)}, f32[24,128]{1,0:T(8,128)S(1)}, u32[]{:S(2)}, u32[]{:S(2)}) collective-permute-start(f32[24,128]{1,0:T(8,128)} %get-tuple-element.159), channel_id=1, source_target_pairs={{1,2},{3,4},{5,6},{7,8},{9,10},{11,12},{13,14},{2,1},{4,3},{6,5},{... | collective-permute-start | bytes 36872 | tf_op jit(solution)/shard_map/ppermute | solution.py:1003
  81.9 3.9 %collective-permute-start.17 = (f32[16,128]{1,0:T(8,128)}, f32[16,128]{1,0:T(8,128)S(1)}, u32[]{:S(2)}, u32[]{:S(2)}) collective-permute-start(f32[16,128]{1,0:T(8,128)} %get-tuple-element.158), channel_id=1, source_target_pairs={{0,1},{2,3},{4,5},{6,7},{8,9},{10,11},{12,13},{14,15},{1,0},{3,2},... | collective-permute-start | bytes 24584 | tf_op jit(solution)/shard_map/ppermute | solution.py:1002
  89.4 11.7 %all-to-all-start.5 = ((f32[32,4,128]{2,1,0:T(4,128)}), f32[32,4,128]{2,1,0:T(4,128)S(1)}, u32[]{:S(2)}, u32[]{:S(2)}) async-start(f32[32,4,128]{2,1,0:T(4,128)} %bitcast.41), calls=%async_computation.5 | async-start | bytes 131072 | tf_op jit(solution)/shard_map/all_to_all | solution.py:1069
  93.7 6.4 %collective-permute-start.19 = (f32[2,16,128]{2,1,0:T(8,128)}, f32[2,16,128]{2,1,0:T(8,128)S(1)}, u32[]{:S(2)}, u32[]{:S(2)}) collective-permute-start(f32[2,16,128]{2,1,0:T(8,128)} %get-tuple-element.167), channel_id=1, source_target_pairs={{0,16},{16,0},{1,17},{17,1},{2,18},{18,2},{3,19},{19,3},{4,20},{20... | collective-permute-start | bytes 49160 | tf_op jit(solution)/shard_map/ppermute | solution.py:1001
  95.5 4.6 %collective-permute-start.21 = (f32[24,128]{1,0:T(8,128)}, f32[24,128]{1,0:T(8,128)S(1)}, u32[]{:S(2)}, u32[]{:S(2)}) collective-permute-start(f32[24,128]{1,0:T(8,128)} %get-tuple-element.169), channel_id=1, source_target_pairs={{1,2},{3,4},{5,6},{7,8},{9,10},{11,12},{13,14},{2,1},{4,3},{6,5},{... | collective-permute-start | bytes 36872 | tf_op jit(solution)/shard_map/ppermute | solution.py:1003
  96.2 3.9 %collective-permute-start.20 = (f32[16,128]{1,0:T(8,128)}, f32[16,128]{1,0:T(8,128)S(1)}, u32[]{:S(2)}, u32[]{:S(2)}) collective-permute-start(f32[16,128]{1,0:T(8,128)} %get-tuple-element.168), channel_id=1, source_target_pairs={{0,1},{2,3},{4,5},{6,7},{8,9},{10,11},{12,13},{14,15},{1,0},{3,2},... | collective-permute-start | bytes 24584 | tf_op jit(solution)/shard_map/ppermute | solution.py:1002
  (5 other events, 17.1 us)

commit v7 on v6

--- a/solution.py
+++ b/solution.py
@@ -259,6 +259,7 @@
 SPAN_X, SPAN_Y = 2, 4
 SUBS = SPAN_X * SPAN_Y
 CASES = 16
+EARLY = 4
 STAY = 2
 SLOTS = 32
 USED = 2 * (SPAN_X + 1) * (SPAN_Y + 1)
@@ -325,9 +326,6 @@
         x_ref[t, rows, :] = jnp.where(first, east[t], west[t])
     a_ref[rows, :] = jnp.where(even, north, south)
     b_ref[rows, :] = jnp.where(even, south, north)
-    if at == 0:
-        rest = pl.ds(b_ref.shape[0] * 2 // 3, b_ref.shape[0] - b_ref.shape[0] * 2 // 3)
-        b_ref[rest, :] = jnp.zeros((rest.size, 128), F32)
 
 
 def received(x_ref, a_ref, b_ref, at, n, side=None):
@@ -426,7 +424,7 @@
 
 
 def operator_kernel(
-    schur_ref, couple_ref, map_ref, slot_ref, ha_ref, la_ref, hb_ref, lb_ref, cc_ref, ch_ref, cl_ref, name_ref,
+    schur_ref, couple_ref, map_ref, slot_ref, rest_ref, ha_ref, la_ref, hb_ref, lb_ref, cc_ref, ch_ref, cl_ref, name_ref,
 ):
     none = 384
     slot = slot_ref[...].astype(F32)
@@ -464,7 +462,7 @@
         cc = jnp.dot(compact, couple_ref[i], precision=EXACT, preferred_element_type=F32)
         c1, rest = split(cc)
         c2, c3 = split(cc - c1.astype(F32))
-        s1, s2 = split(schur_ref[i])
+        s1, s2 = split(schur_ref[i] if i < EARLY else rest_ref[i - EARLY])
         tall = dot_turned(jnp.concatenate([s1, s2, c1, c2, c3], 0), place)
         high, low = (dot(place, tall[t : t + 256].astype(BF16)).astype(BF16) for t in (0, 256))
         if i < STAY:
@@ -476,16 +474,14 @@
         ch_ref[i], cl_ref[i] = split(cc)
 
 
-def inverse_kernel(mine_ref, upper_ref, high_ref, low_ref, high_out_ref, low_out_ref):
+def inverse_kernel(mine_ref, upper_ref, high_ref, low_ref):
     first = lax.axis_index("gx") == 0
     mine = mine_ref[...]
     blocks = {spot: upper_ref[t] for t, spot in enumerate(UPPER)}
     side = lambda i, j: blocks[i, j] if i <= j else jnp.transpose(blocks[j, i])
     other = jnp.concatenate([jnp.concatenate([side(i, j) for j in range(3)], 1) for i in range(3)], 0)
     for region, v in enumerate((jnp.where(first, mine, other), jnp.where(first, other, mine))):
-        high, low = split(v)
-        high_ref[region], low_ref[region] = high, low
-        high_out_ref[region], low_out_ref[region] = high, low
+        high_ref[region], low_ref[region] = split(v)
 
 
 def near_names(name_ref, x_ref, a_ref, b_ref):
@@ -623,6 +619,7 @@
 
 def dense_kernel(got_ref, gh_ref, gl_ref, dh_ref, dl_ref):
     group = iota((8, 128), 1) // SLOTS
+    picks, rows = [], []
     for region in range(2):
         hits = []
         for par in range(2):
@@ -637,14 +634,15 @@
                 halves.append(acc[0:1])
             wanted = jnp.concatenate(halves, 1)
             hits.append(jnp.where(iota((384, 256), 0).astype(F32) == wanted, 1.0, 0.0))
-        picks = jnp.concatenate(hits, 1).astype(BF16)
-        rows = [jnp.transpose(hit).astype(BF16) for hit in hits]
-        which = lax.rem(lax.axis_index("gx") + region, 2)
-        for whole_ref, out_ref in ((gh_ref, dh_ref), (gl_ref, dl_ref)):
-            half = dot(whole_ref[which], picks).astype(BF16)
-            top = dot(rows[0], half).astype(BF16)
+        picks.append(jnp.concatenate(hits, 1).astype(BF16))
+        rows.append([jnp.transpose(hit).astype(BF16) for hit in hits])
+    for whole_ref, out_ref in ((gh_ref, dh_ref), (gl_ref, dl_ref)):
+        for region in range(2):
+            which = lax.rem(lax.axis_index("gx") + region, 2)
+            half = dot(whole_ref[which], picks[region]).astype(BF16)
+            top = dot(rows[region][0], half).astype(BF16)
             out_ref[region, 0], out_ref[region, 1] = top[:, :256], top[:, 256:]
-            out_ref[region, 2] = dot(rows[1], half[:, 256:]).astype(BF16)
+            out_ref[region, 2] = dot(rows[region][1], half[:, 256:]).astype(BF16)
 
 
 def solve_dense(spots, dh_ref, dl_ref):
@@ -746,7 +744,7 @@
 def second_kernel(
     got_ref, x_ref, a_ref, b_ref, y_ref, r_ref, mk_ref, p_ref, l_ref, rho_ref, gh_ref, gl_ref, name_ref,
     ha_ref, la_ref, hb_ref, lb_ref, ch_ref, cl_ref,
-    nh_ref, nl_ref, po_ref, lo_ref, ro_ref, so_ref, scal_ref, block_ref, yo_ref, sx_ref, sa_ref, sb_ref,
+    nh_ref, nl_ref, po_ref, lo_ref, ro_ref, so_ref, scal_ref, block_ref, yo_ref, sx_ref, sa_ref, sb_ref, *_,
 ):
     near_ref, pick_ref = near_names(name_ref, x_ref, a_ref, b_ref), {}
     near_spread(x_ref, a_ref, b_ref, nh_ref, nl_ref)
@@ -879,27 +877,6 @@
         return self.buffer[index]
 
 
-class FetchedPieces:
-    def __init__(self, source, buffer, semaphore, count):
-        self.buffer = buffer
-        step = buffer.shape[0] // count
-        self.parts = [
-            Fetched(source.at[pl.ds(i * step, step)], buffer.at[pl.ds(i * step, step)], semaphore.at[i])
-            for i in range(count)
-        ]
-        self.here = False
-
-    def wait(self):
-        for part in self.parts:
-            part.copy.wait()
-        self.here = True
-
-    def __getitem__(self, index):
-        if not self.here:
-            self.wait()
-        return self.buffer[index]
-
-
 class Stored:
     def __init__(self, target, buffer, semaphore):
         self.buffer = buffer
@@ -912,10 +889,6 @@
     def __getitem__(self, index):
         return self.buffer[index]
 
-    @property
-    def shape(self):
-        return self.buffer.shape
-
     def flush(self):
         if not self.sent:
             self.copy.start()
@@ -936,8 +909,8 @@
         pass
 
 
-def call(kernel, args, outs, kept=(), kept_out=(), raw=(), through=None, flops=None, late=0, pieces=None):
-    through, pieces = through or {}, pieces or {}
+def call(kernel, args, outs, kept=(), kept_out=(), raw=(), through=None, flops=None, late=0, parts=None):
+    through, parts = through or {}, parts or {}
     moved = [i for i in range(len(args)) if i not in kept and i not in raw]
     written = [i for i in range(len(outs)) if i not in kept_out and i not in through]
 
@@ -945,12 +918,9 @@
         ins, results = refs[: len(args)], refs[len(args) : len(args) + len(outs)]
         buffers, (in_sem, out_sem, through_sem) = refs[len(args) + len(outs) : -3], refs[-3:]
         fetched, stored = list(ins), [Kept(ref) for ref in results]
-        for i in sorted(moved, key=lambda i: i not in pieces):
-            t, at = moved.index(i), sum(pieces.get(m, 1) for m in moved[: moved.index(i)])
-            if i in pieces:
-                fetched[i] = FetchedPieces(ins[i], buffers[t], in_sem.at[pl.ds(at, pieces[i])], pieces[i])
-            else:
-                fetched[i] = Fetched(ins[i], buffers[t], in_sem.at[at])
+        for t, i in enumerate(moved):
+            source = ins[i].at[pl.ds(*parts[i])] if i in parts else ins[i]
+            fetched[i] = Fetched(source, buffers[t], in_sem.at[t])
         for t, i in enumerate(written):
             stored[i] = Stored(results[i], buffers[len(moved) + t], out_sem.at[t])
         passing = [
@@ -987,9 +957,11 @@
         ],
         in_specs=[place(i in kept) for i in range(len(args))],
         out_specs=[place(i in kept_out) for i in range(len(outs))],
-        scratch_shapes=[pltpu.VMEM(args[i].shape, args[i].dtype) for i in moved]
+        scratch_shapes=[
+            pltpu.VMEM((parts[i][1],) + args[i].shape[1:] if i in parts else args[i].shape, args[i].dtype) for i in moved
+        ]
         + [pltpu.VMEM(*outs[i]) for i in written]
-        + [semaphores(sum(pieces.get(i, 1) for i in moved)), semaphores(len(written)), semaphores(len(through))],
+        + [semaphores(len(moved)), semaphores(len(written)), semaphores(len(through))],
         compiler_params=pltpu.CompilerParams(vmem_limit_bytes=LIMIT),
         cost_estimate=flops and pl.CostEstimate(flops=flops, bytes_accessed=flops // 512, transcendentals=0),
     )(*args)
@@ -1010,7 +982,7 @@
     native = lambda v: v.reshape(CASES * SUBS, 128)
     by_sub = lambda v: v.reshape((SUBS,) + v.shape[2:])
     width = coarse_inverse.shape[-1]
-    sends = lambda rows: [((SPAN_Y // 2, rows, 128), F32), ((rows, 128), F32), ((-(-3 * rows // 16) * 8, 128), F32)]
+    sends = lambda rows: [((SPAN_Y // 2, rows, 128), F32), ((rows, 128), F32), ((rows, 128), F32)]
     state = ((SUBS, CASES, 256), F32)
     plain = ((CASES * SUBS, 128), F32)
 
@@ -1018,10 +990,10 @@
     own, *out, schur, coupled, placed, slotted, inverse, p = call(
         start_kernel,
         [native(residual), native(direction), by_sub(active), by_sub(scaling), *raw, coarse_inverse[0]],
-        [((SUBS, CAST, 256), F32)] + sends(CAST) + [(v.shape, v.dtype) for v in raw] + [((len(UPPER), 128, 128), F32), plain],
+        [((SUBS, CAST, 256), F32)] + sends(CAST) + [((EARLY,) + raw[0].shape[1:], F32)] + [(v.shape, v.dtype) for v in raw[1:]] + [((len(UPPER), 128, 128), F32), plain],
         kept_out=(0, 4, 5, 6, 7),
         raw=(4, 5, 6, 7),
-        through={4: lambda v: v[4], 5: lambda v: v[5], 6: lambda v: v[6], 7: lambda v: v[7]},
+        through={4: lambda v: v[4].at[pl.ds(0, EARLY)], 5: lambda v: v[5], 6: lambda v: v[6], 7: lambda v: v[7]},
     )
     come = trade(*out)
     other = lax.ppermute(inverse, "gx", [(0, 1), (1, 0)])
@@ -1029,10 +1001,11 @@
     couple = ((SUBS, SLOTS, 256), BF16)
     ha, la, hb, lb, cc, ch, cl, names = call(
         operator_kernel,
-        [schur, coupled, placed, slotted],
+        [schur, coupled, placed, slotted, by_sub(dual_schur)],
         [first_part, first_part, rest, rest, ((SUBS, SLOTS, 256), F32), couple, couple, ((8, 128), F32)],
         kept=range(4),
         kept_out=range(8),
+        parts={4: (EARLY, SUBS - EARLY)},
         flops=5 * 10**9,
     )
     rows = 2 * CASES + SLOTS + 8
@@ -1050,21 +1023,20 @@
     got = lax.all_to_all(block.reshape(32, 3, 4, 128), BOTH, 0, 0, tiled=False).reshape(48, 8, 128)
     come = trade(*out)
     square = ((2, width, width), BF16)
-    gh, gl, gh_far, gl_far = call(
-        inverse_kernel, [coarse_inverse[0], other], [square] * 4, kept_out=(0, 1), flops=10**9
-    )
+    gh, gl = call(inverse_kernel, [coarse_inverse[0], other], [square, square], kept_out=(0, 1), flops=10**9)
     side = ((SLOTS, 512), BF16)
     onward = [plain, plain, state, state, ((5, CASES, 128), F32), ((16, 8, 128), F32), state] + sends(CASES)
-    nh, nl, p, lam, r, s, scal, block, y, *out = call(
+    nh, nl, p, lam, r, s, scal, block, y, *out, gh, gl = call(
         second_kernel,
         [got, *come, y, r, mk, p, native(duals), prev_rho.reshape(1, CASES), gh, gl, names, ha, la, hb, lb, ch, cl],
-        [side, side] + onward,
+        [side, side] + onward + [square, square],
         kept=(0, 1, 2, 3, 4, 5, 6, 10, 11, 12, 13, 14, 17, 18),
         kept_out=(0, 1, 2, 3, 4, 6, 8),
-        late=3,
+        through={12: lambda v: v[10], 13: lambda v: v[11]},
+        late=5,
     )
     dense = ((2, 3, 256, 256), BF16)
-    dh, dl = call(dense_kernel, [got, gh_far, gl_far], [dense, dense], kept_out=(0, 1), flops=3 * 10**9)
+    dh, dl = call(dense_kernel, [got, gh, gl], [dense, dense], kept=(0,), kept_out=(0, 1), flops=10**8)
     for step in range(1, ITERS):
         got = lax.all_to_all(block.reshape(32, 4, 128), BOTH, 0, 0, tiled=False).reshape(16, 8, 128)
         come = trade(*out)

time: 104 us -> 103 us (level)
  starting transfers between devices: 60.1 us -> 48 us
  waiting for transfers between devices: 13.3 us -> 25.4 us
  Pallas kernels: 28.6 us -> 27.1 us
    ppermute x7, starting transfers between devices: 11.6 us -> 0.02 us  [trade(): lax.ppermute(a, 'gy', both_ways(pairs_from(0, peers)))]
    all_to_all x5, waiting for transfers between devices: 5.13 us -> 14.9 us  [two_regions(): lax.all_to_all(block.reshape(32, 4, 128), BOTH, 0, 0, tiled=False)]
    ppermute x7, waiting for transfers between devices: 0.7 us -> 4.3 us  [trade(): lax.ppermute(x, 'gx', [(0, 1), (1, 0)])]
    pallas_call x11, Pallas kernels: 28.6 us -> 27.1 us  [call(): pl.pallas_call(body, out_shape=[jax.ShapeDtypeStruct(*out) if i in kept_o...]
    ppermute x7, waiting for transfers between devices: 4.16 us -> 2.9 us  [trade(): lax.ppermute(a, 'gy', both_ways(pairs_from(0, peers)))]
  transfers between devices with their start and end apart: 28 -> 28, of which waited for: 11 -> 15; matrix products, arithmetic and copies ran while one was open for 0% -> 0% of each run, Pallas kernels for 10% -> 9%
where the time goes in v7:
time: 103 us; the launch traced here: 102 us
  starting transfers between devices  48 us (47%)
  Pallas kernels  27.1 us (26%)
  waiting for transfers between devices  25.4 us (25%)
  between operations  1.07 us (1%)
    pallas_call x11, Pallas kernels, call(): pl.pallas_call(body, out_shape=[jax.ShapeDtypeStruct(*out) if i in kept_o...  27.1 us
    all_to_all x5, starting transfers between devices, two_regions(): lax.all_to_all(block.reshape(32, 4, 128), BOTH, 0, 0, tiled=False)  21.1 us
    all_to_all x5, waiting for transfers between devices, two_regions(): lax.all_to_all(block.reshape(32, 4, 128), BOTH, 0, 0, tiled=False)  14.9 us
    ppermute x7, starting transfers between devices, trade(): lax.ppermute(x, 'gx', [(0, 1), (1, 0)])  14 us
    all_to_all x1, starting transfers between devices, two_regions(): lax.all_to_all(block.reshape(32, 3, 4, 128), BOTH, 0, 0, tiled=False)  8.15 us
    ppermute x7, starting transfers between devices, trade(): lax.ppermute(b, 'gy', both_ways(pairs_from(1, peers)))  4.55 us
    ppermute x7, waiting for transfers between devices, trade(): lax.ppermute(x, 'gx', [(0, 1), (1, 0)])  4.3 us
    all_to_all x1, waiting for transfers between devices, two_regions(): lax.all_to_all(block.reshape(32, 3, 4, 128), BOTH, 0, 0, tiled=False)  3.24 us
  transfers between devices with their start and end apart: 28, of which 15 were waited for; matrix products, arithmetic and copies ran while one was open for 0% of the time, Pallas kernels for 9%

profile of v7, /device:TPU:0, one launch (start us, length us, event | category | flops | bytes accessed | tf_op | source)
XLA Modules:
  0.0 102.3 jit_solution(12265182384186567707)
XLA Ops:
  0.6 2.4 %shard_map.130 = (f32[8,40,256]{2,1,0:T(8,128)S(1)}, f32[2,40,128]{2,1,0:T(8,128)}, f32[40,128]{1,0:T(8,128)}, f32[40,128]{1,0:T(8,128)}, f32[4,256,256]{2,1,0:T...) custom-call(f32[128,128]{1,0:T(8,128)} %bitcast.38, ...), custom_call_target="tpu_custom_call" | custom-call | tf_op jit(solution)/shard_map/pallas_call | solution.py:953
  3.0 3.0 %collective-permute-start = (f32[2,40,128]{2,1,0:T(8,128)}, f32[2,40,128]{2,1,0:T(8,128)S(1)}, u32[]{:S(2)}, u32[]{:S(2)}) collective-permute-start(f32[2,40,128]{2,1,0:T(8,128)} %get-tuple-element.92), channel_id=1, source_target_pairs={{0,16},{16,0},{1,17},{17,1},{2,18},{18,2},{3,19},{19,3},{4,20},{20... | collective-permute-start | bytes 122888 | tf_op jit(solution)/shard_map/ppermute | solution.py:973
  6.9 3.1 %shard_map.131 = (bf16[2,256,256]{2,1,0:T(8,128)(2,1)S(1)}, bf16[2,256,256]{2,1,0:T(8,128)(2,1)S(1)}, bf16[6,256,256]{2,1,0:T(8,128)(2,1)S(1)}, bf16[6,256,256]{...) custom-call(f32[4,256,256]{2,1,0:T(8,128)S(1)} %get-tuple-element.95, ...), custom_call_target="tpu_custom_call" | custom-call | flops 5000000000 | bytes 9765625 | tf_op jit(solution)/shard_map/pallas_call | solution.py:953
  11.6 8.2 %all-to-all-start = ((f32[32,3,4,128]{3,2,1,0:T(4,128)}), f32[32,3,4,128]{3,2,1,0:T(4,128)S(1)}, u32[]{:S(2)}, u32[]{:S(2)}) async-start(f32[32,3,4,128]{3,2,1,0:T(4,128)} %bitcast.36), calls=%async_computation | async-start | bytes 393216 | tf_op jit(solution)/shard_map/all_to_all | solution.py:1023
  19.7 1.8 %collective-permute-start.3 = (f32[2,72,128]{2,1,0:T(8,128)}, f32[2,72,128]{2,1,0:T(8,128)S(1)}, u32[]{:S(2)}, u32[]{:S(2)}) collective-permute-start(f32[2,72,128]{2,1,0:T(8,128)} %get-tuple-element.108), channel_id=1, source_target_pairs={{0,16},{16,0},{1,17},{17,1},{2,18},{18,2},{3,19},{19,3},{4,20},{20... | collective-permute-start | bytes 221192 | tf_op jit(solution)/shard_map/ppermute | solution.py:973
  25.4 3.2 %all-to-all-done = f32[32,3,4,128]{3,2,1,0:T(4,128)S(1)} async-done(((f32[32,3,4,128]{3,2,1,0:T(4,128)}), f32[32,3,4,128]{3,2,1,0:T(4,128)S(1)}, u32[]{:S(2)}, u32[]{:S(2)}) %all-to-all-start) | async-done | bytes 196640 | tf_op jit(solution)/shard_map/all_to_all | solution.py:1023
  28.6 3.1 %shard_map.134 = (bf16[32,512]{1,0:T(8,128)(2,1)S(1)}, bf16[32,512]{1,0:T(8,128)(2,1)S(1)}, f32[128,128]{1,0:T(8,128)S(1)}, f32[128,128]{1,0:T(8,128)S(1)}, f32[...) custom-call(f32[48,8,128]{2,1,0:T(8,128)S(1)} %bitcast.25, ...), custom_call_target="tpu_custom_call" | custom-call | tf_op jit(solution)/shard_map/pallas_call | solution.py:953
  31.8 3.1 %all-to-all-start.1 = ((f32[32,4,128]{2,1,0:T(4,128)}), f32[32,4,128]{2,1,0:T(4,128)S(1)}, u32[]{:S(2)}, u32[]{:S(2)}) async-start(f32[32,4,128]{2,1,0:T(4,128)} %bitcast.41), calls=%async_computation.1 | async-start | bytes 131072 | tf_op jit(solution)/shard_map/all_to_all | solution.py:1041
  34.9 1.8 %collective-permute-start.7 = (f32[2,16,128]{2,1,0:T(8,128)}, f32[2,16,128]{2,1,0:T(8,128)S(1)}, u32[]{:S(2)}, u32[]{:S(2)}) collective-permute-start(f32[2,16,128]{2,1,0:T(8,128)} %get-tuple-element.121), channel_id=1, source_target_pairs={{0,16},{16,0},{1,17},{17,1},{2,18},{18,2},{3,19},{19,3},{4,20},{20... | collective-permute-start | bytes 49160 | tf_op jit(solution)/shard_map/ppermute | solution.py:973
  37.4 3.4 %shard_map.135 = (bf16[2,3,256,256]{3,2,1,0:T(8,128)(2,1)S(1)}, bf16[2,3,256,256]{3,2,1,0:T(8,128)(2,1)S(1)}) custom-call(f32[48,8,128]{2,1,0:T(8,128)S(1)} %bitcast.26, bf16[2,384,384]{2,1,0:T(8,128)(2,1)} %get-tuple-element.128.refs_1_, bf16[2,384,384]{2,1,0:T(8,128)(2,1)} %get-tuple-element.129.refs_2_), custom_call_target="tpu_custom_call" | custom-call | flops 100000000 | bytes 195312 | tf_op jit(solution)/shard_map/pallas_call | solution.py:953
  42.3 2.6 %shard_map.136 = (f32[128,128]{1,0:T(8,128)S(1)}, f32[128,128]{1,0:T(8,128)S(1)}, f32[8,16,256]{2,1,0:T(8,128)S(1)}, f32[8,16,256]{2,1,0:T(8,128)}, f32[5,16,128...) custom-call(f32[16,8,128]{2,1,0:T(8,128)S(1)} %bitcast.27, ...), custom_call_target="tpu_custom_call" | custom-call | tf_op jit(solution)/shard_map/pallas_call | solution.py:953
  44.9 5.1 %all-to-all-start.2 = ((f32[32,4,128]{2,1,0:T(4,128)}), f32[32,4,128]{2,1,0:T(4,128)S(1)}, u32[]{:S(2)}, u32[]{:S(2)}) async-start(f32[32,4,128]{2,1,0:T(4,128)} %bitcast.43), calls=%async_computation.2 | async-start | bytes 131072 | tf_op jit(solution)/shard_map/all_to_all | solution.py:1041
  50.1 1.8 %collective-permute-start.10 = (f32[2,16,128]{2,1,0:T(8,128)}, f32[2,16,128]{2,1,0:T(8,128)S(1)}, u32[]{:S(2)}, u32[]{:S(2)}) collective-permute-start(f32[2,16,128]{2,1,0:T(8,128)} %get-tuple-element.137), channel_id=1, source_target_pairs={{0,16},{16,0},{1,17},{17,1},{2,18},{18,2},{3,19},{19,3},{4,20},{20... | collective-permute-start | bytes 49160 | tf_op jit(solution)/shard_map/ppermute | solution.py:973
  54.1 3.4 %all-to-all-done.2 = f32[32,4,128]{2,1,0:T(4,128)S(1)} async-done(((f32[32,4,128]{2,1,0:T(4,128)}), f32[32,4,128]{2,1,0:T(4,128)S(1)}, u32[]{:S(2)}, u32[]{:S(2)}) %all-to-all-start.2) | async-done | bytes 65568 | tf_op jit(solution)/shard_map/all_to_all | solution.py:1041
  57.5 2.6 %shard_map.137 = (f32[128,128]{1,0:T(8,128)S(1)}, f32[128,128]{1,0:T(8,128)S(1)}, f32[8,16,256]{2,1,0:T(8,128)S(1)}, f32[8,16,256]{2,1,0:T(8,128)}, f32[5,16,128...) custom-call(f32[16,8,128]{2,1,0:T(8,128)S(1)} %bitcast.29, ...), custom_call_target="tpu_custom_call" | custom-call | tf_op jit(solution)/shard_map/pallas_call | solution.py:953
  60.1 4.3 %all-to-all-start.3 = ((f32[32,4,128]{2,1,0:T(4,128)}), f32[32,4,128]{2,1,0:T(4,128)S(1)}, u32[]{:S(2)}, u32[]{:S(2)}) async-start(f32[32,4,128]{2,1,0:T(4,128)} %bitcast.44), calls=%async_computation.3 | async-start | bytes 131072 | tf_op jit(solution)/shard_map/all_to_all | solution.py:1041
  64.4 1.8 %collective-permute-start.13 = (f32[2,16,128]{2,1,0:T(8,128)}, f32[2,16,128]{2,1,0:T(8,128)S(1)}, u32[]{:S(2)}, u32[]{:S(2)}) collective-permute-start(f32[2,16,128]{2,1,0:T(8,128)} %get-tuple-element.147), channel_id=1, source_target_pairs={{0,16},{16,0},{1,17},{17,1},{2,18},{18,2},{3,19},{19,3},{4,20},{20... | collective-permute-start | bytes 49160 | tf_op jit(solution)/shard_map/ppermute | solution.py:973
  68.4 3.4 %all-to-all-done.3 = f32[32,4,128]{2,1,0:T(4,128)S(1)} async-done(((f32[32,4,128]{2,1,0:T(4,128)}), f32[32,4,128]{2,1,0:T(4,128)S(1)}, u32[]{:S(2)}, u32[]{:S(2)}) %all-to-all-start.3) | async-done | bytes 65568 | tf_op jit(solution)/shard_map/all_to_all | solution.py:1041
  71.8 2.6 %shard_map.138 = (f32[128,128]{1,0:T(8,128)S(1)}, f32[128,128]{1,0:T(8,128)S(1)}, f32[8,16,256]{2,1,0:T(8,128)S(1)}, f32[8,16,256]{2,1,0:T(8,128)}, f32[5,16,128...) custom-call(f32[16,8,128]{2,1,0:T(8,128)S(1)} %bitcast.30, ...), custom_call_target="tpu_custom_call" | custom-call | tf_op jit(solution)/shard_map/pallas_call | solution.py:953
  74.4 4.3 %all-to-all-start.4 = ((f32[32,4,128]{2,1,0:T(4,128)}), f32[32,4,128]{2,1,0:T(4,128)S(1)}, u32[]{:S(2)}, u32[]{:S(2)}) async-start(f32[32,4,128]{2,1,0:T(4,128)} %bitcast.45), calls=%async_computation.4 | async-start | bytes 131072 | tf_op jit(solution)/shard_map/all_to_all | solution.py:1041
  82.7 3.4 %all-to-all-done.4 = f32[32,4,128]{2,1,0:T(4,128)S(1)} async-done(((f32[32,4,128]{2,1,0:T(4,128)}), f32[32,4,128]{2,1,0:T(4,128)S(1)}, u32[]{:S(2)}, u32[]{:S(2)}) %all-to-all-start.4) | async-done | bytes 65568 | tf_op jit(solution)/shard_map/all_to_all | solution.py:1041
  86.1 2.6 %shard_map.139 = (f32[128,128]{1,0:T(8,128)S(1)}, f32[128,128]{1,0:T(8,128)S(1)}, f32[8,16,256]{2,1,0:T(8,128)S(1)}, f32[8,16,256]{2,1,0:T(8,128)}, f32[5,16,128...) custom-call(f32[16,8,128]{2,1,0:T(8,128)S(1)} %bitcast.28, ...), custom_call_target="tpu_custom_call" | custom-call | tf_op jit(solution)/shard_map/pallas_call | solution.py:953
  88.7 4.3 %all-to-all-start.5 = ((f32[32,4,128]{2,1,0:T(4,128)}), f32[32,4,128]{2,1,0:T(4,128)S(1)}, u32[]{:S(2)}, u32[]{:S(2)}) async-start(f32[32,4,128]{2,1,0:T(4,128)} %bitcast.42), calls=%async_computation.5 | async-start | bytes 131072 | tf_op jit(solution)/shard_map/all_to_all | solution.py:1041
  97.0 3.4 %all-to-all-done.5 = f32[32,4,128]{2,1,0:T(4,128)S(1)} async-done(((f32[32,4,128]{2,1,0:T(4,128)}), f32[32,4,128]{2,1,0:T(4,128)S(1)}, u32[]{:S(2)}, u32[]{:S(2)}) %all-to-all-start.5) | async-done | bytes 65568 | tf_op jit(solution)/shard_map/all_to_all | solution.py:1041
  (45 shorter events, 22.5 us)
Async XLA Ops:
  3.0 7.0 %collective-permute-start = (f32[2,40,128]{2,1,0:T(8,128)}, f32[2,40,128]{2,1,0:T(8,128)S(1)}, u32[]{:S(2)}, u32[]{:S(2)}) collective-permute-start(f32[2,40,128]{2,1,0:T(8,128)} %get-tuple-element.92), channel_id=1, source_target_pairs={{0,16},{16,0},{1,17},{17,1},{2,18},{18,2},{3,19},{19,3},{4,20},{20... | collective-permute-start | bytes 122888 | tf_op jit(solution)/shard_map/ppermute | solution.py:973
  6.1 4.0 %collective-permute-start.1 = (f32[40,128]{1,0:T(8,128)}, f32[40,128]{1,0:T(8,128)S(1)}, u32[]{:S(2)}, u32[]{:S(2)}) collective-permute-start(f32[40,128]{1,0:T(8,128)} %get-tuple-element.93), channel_id=1, source_target_pairs={{0,1},{2,3},{4,5},{6,7},{8,9},{10,11},{12,13},{14,15},{1,0},{3,2},... | collective-permute-start | bytes 61448 | tf_op jit(solution)/shard_map/ppermute | solution.py:974
  6.1 4.0 %collective-permute-start.2 = (f32[40,128]{1,0:T(8,128)}, f32[40,128]{1,0:T(8,128)S(1)}, u32[]{:S(2)}, u32[]{:S(2)}) collective-permute-start(f32[40,128]{1,0:T(8,128)} %get-tuple-element.94), channel_id=1, source_target_pairs={{1,2},{3,4},{5,6},{7,8},{9,10},{11,12},{13,14},{2,1},{4,3},{6,5},{... | collective-permute-start | bytes 61448 | tf_op jit(solution)/shard_map/ppermute | solution.py:975
  6.7 15.5 %collective-permute-start.6 = (f32[6,128,128]{2,1,0:T(8,128)}, f32[6,128,128]{2,1,0:T(8,128)S(1)}, u32[]{:S(2)}, u32[]{:S(2)}) collective-permute-start(f32[6,128,128]{2,1,0:T(8,128)} %get-tuple-element.115), channel_id=1, source_target_pairs={{0,16},{16,0},{1,17},{17,1},{2,18},{18,2},{3,19},{19,3},{4,20},{20... | collective-permute-start | bytes 1179656 | tf_op jit(solution)/shard_map/ppermute | solution.py:999
  11.6 17.1 %all-to-all-start = ((f32[32,3,4,128]{3,2,1,0:T(4,128)}), f32[32,3,4,128]{3,2,1,0:T(4,128)S(1)}, u32[]{:S(2)}, u32[]{:S(2)}) async-start(f32[32,3,4,128]{3,2,1,0:T(4,128)} %bitcast.36), calls=%async_computation | async-start | bytes 393216 | tf_op jit(solution)/shard_map/all_to_all | solution.py:1023
  19.7 5.7 %collective-permute-start.3 = (f32[2,72,128]{2,1,0:T(8,128)}, f32[2,72,128]{2,1,0:T(8,128)S(1)}, u32[]{:S(2)}, u32[]{:S(2)}) collective-permute-start(f32[2,72,128]{2,1,0:T(8,128)} %get-tuple-element.108), channel_id=1, source_target_pairs={{0,16},{16,0},{1,17},{17,1},{2,18},{18,2},{3,19},{19,3},{4,20},{20... | collective-permute-start | bytes 221192 | tf_op jit(solution)/shard_map/ppermute | solution.py:973
  21.6 2.8 %collective-permute-start.4 = (f32[72,128]{1,0:T(8,128)}, f32[72,128]{1,0:T(8,128)S(1)}, u32[]{:S(2)}, u32[]{:S(2)}) collective-permute-start(f32[72,128]{1,0:T(8,128)} %get-tuple-element.109), channel_id=1, source_target_pairs={{0,1},{2,3},{4,5},{6,7},{8,9},{10,11},{12,13},{14,15},{1,0},{3,2},... | collective-permute-start | bytes 110600 | tf_op jit(solution)/shard_map/ppermute | solution.py:974
  21.6 2.8 %collective-permute-start.5 = (f32[72,128]{1,0:T(8,128)}, f32[72,128]{1,0:T(8,128)S(1)}, u32[]{:S(2)}, u32[]{:S(2)}) collective-permute-start(f32[72,128]{1,0:T(8,128)} %get-tuple-element.110), channel_id=1, source_target_pairs={{1,2},{3,4},{5,6},{7,8},{9,10},{11,12},{13,14},{2,1},{4,3},{6,5},{... | collective-permute-start | bytes 110600 | tf_op jit(solution)/shard_map/ppermute | solution.py:975
  31.8 10.5 %all-to-all-start.1 = ((f32[32,4,128]{2,1,0:T(4,128)}), f32[32,4,128]{2,1,0:T(4,128)S(1)}, u32[]{:S(2)}, u32[]{:S(2)}) async-start(f32[32,4,128]{2,1,0:T(4,128)} %bitcast.41), calls=%async_computation.1 | async-start | bytes 131072 | tf_op jit(solution)/shard_map/all_to_all | solution.py:1041
  34.9 5.9 %collective-permute-start.7 = (f32[2,16,128]{2,1,0:T(8,128)}, f32[2,16,128]{2,1,0:T(8,128)S(1)}, u32[]{:S(2)}, u32[]{:S(2)}) collective-permute-start(f32[2,16,128]{2,1,0:T(8,128)} %get-tuple-element.121), channel_id=1, source_target_pairs={{0,16},{16,0},{1,17},{17,1},{2,18},{18,2},{3,19},{19,3},{4,20},{20... | collective-permute-start | bytes 49160 | tf_op jit(solution)/shard_map/ppermute | solution.py:973
  36.8 4.1 %collective-permute-start.8 = (f32[16,128]{1,0:T(8,128)}, f32[16,128]{1,0:T(8,128)S(1)}, u32[]{:S(2)}, u32[]{:S(2)}) collective-permute-start(f32[16,128]{1,0:T(8,128)} %get-tuple-element.122), channel_id=1, source_target_pairs={{0,1},{2,3},{4,5},{6,7},{8,9},{10,11},{12,13},{14,15},{1,0},{3,2},... | collective-permute-start | bytes 24584 | tf_op jit(solution)/shard_map/ppermute | solution.py:974
  36.8 4.1 %collective-permute-start.9 = (f32[16,128]{1,0:T(8,128)}, f32[16,128]{1,0:T(8,128)S(1)}, u32[]{:S(2)}, u32[]{:S(2)}) collective-permute-start(f32[16,128]{1,0:T(8,128)} %get-tuple-element.123), channel_id=1, source_target_pairs={{1,2},{3,4},{5,6},{7,8},{9,10},{11,12},{13,14},{2,1},{4,3},{6,5},{... | collective-permute-start | bytes 24584 | tf_op jit(solution)/shard_map/ppermute | solution.py:975
  44.9 12.5 %all-to-all-start.2 = ((f32[32,4,128]{2,1,0:T(4,128)}), f32[32,4,128]{2,1,0:T(4,128)S(1)}, u32[]{:S(2)}, u32[]{:S(2)}) async-start(f32[32,4,128]{2,1,0:T(4,128)} %bitcast.43), calls=%async_computation.2 | async-start | bytes 131072 | tf_op jit(solution)/shard_map/all_to_all | solution.py:1041
  50.1 4.0 %collective-permute-start.10 = (f32[2,16,128]{2,1,0:T(8,128)}, f32[2,16,128]{2,1,0:T(8,128)S(1)}, u32[]{:S(2)}, u32[]{:S(2)}) collective-permute-start(f32[2,16,128]{2,1,0:T(8,128)} %get-tuple-element.137), channel_id=1, source_target_pairs={{0,16},{16,0},{1,17},{17,1},{2,18},{18,2},{3,19},{19,3},{4,20},{20... | collective-permute-start | bytes 49160 | tf_op jit(solution)/shard_map/ppermute | solution.py:973
  51.9 1.4 %collective-permute-start.11 = (f32[16,128]{1,0:T(8,128)}, f32[16,128]{1,0:T(8,128)S(1)}, u32[]{:S(2)}, u32[]{:S(2)}) collective-permute-start(f32[16,128]{1,0:T(8,128)} %get-tuple-element.138), channel_id=1, source_target_pairs={{0,1},{2,3},{4,5},{6,7},{8,9},{10,11},{12,13},{14,15},{1,0},{3,2},... | collective-permute-start | bytes 24584 | tf_op jit(solution)/shard_map/ppermute | solution.py:974
  51.9 1.4 %collective-permute-start.12 = (f32[16,128]{1,0:T(8,128)}, f32[16,128]{1,0:T(8,128)S(1)}, u32[]{:S(2)}, u32[]{:S(2)}) collective-permute-start(f32[16,128]{1,0:T(8,128)} %get-tuple-element.139), channel_id=1, source_target_pairs={{1,2},{3,4},{5,6},{7,8},{9,10},{11,12},{13,14},{2,1},{4,3},{6,5},{... | collective-permute-start | bytes 24584 | tf_op jit(solution)/shard_map/ppermute | solution.py:975
  60.1 11.7 %all-to-all-start.3 = ((f32[32,4,128]{2,1,0:T(4,128)}), f32[32,4,128]{2,1,0:T(4,128)S(1)}, u32[]{:S(2)}, u32[]{:S(2)}) async-start(f32[32,4,128]{2,1,0:T(4,128)} %bitcast.44), calls=%async_computation.3 | async-start | bytes 131072 | tf_op jit(solution)/shard_map/all_to_all | solution.py:1041
  64.4 4.0 %collective-permute-start.13 = (f32[2,16,128]{2,1,0:T(8,128)}, f32[2,16,128]{2,1,0:T(8,128)S(1)}, u32[]{:S(2)}, u32[]{:S(2)}) collective-permute-start(f32[2,16,128]{2,1,0:T(8,128)} %get-tuple-element.147), channel_id=1, source_target_pairs={{0,16},{16,0},{1,17},{17,1},{2,18},{18,2},{3,19},{19,3},{4,20},{20... | collective-permute-start | bytes 49160 | tf_op jit(solution)/shard_map/ppermute | solution.py:973
  66.2 1.4 %collective-permute-start.14 = (f32[16,128]{1,0:T(8,128)}, f32[16,128]{1,0:T(8,128)S(1)}, u32[]{:S(2)}, u32[]{:S(2)}) collective-permute-start(f32[16,128]{1,0:T(8,128)} %get-tuple-element.148), channel_id=1, source_target_pairs={{0,1},{2,3},{4,5},{6,7},{8,9},{10,11},{12,13},{14,15},{1,0},{3,2},... | collective-permute-start | bytes 24584 | tf_op jit(solution)/shard_map/ppermute | solution.py:974
  66.2 1.4 %collective-permute-start.15 = (f32[16,128]{1,0:T(8,128)}, f32[16,128]{1,0:T(8,128)S(1)}, u32[]{:S(2)}, u32[]{:S(2)}) collective-permute-start(f32[16,128]{1,0:T(8,128)} %get-tuple-element.149), channel_id=1, source_target_pairs={{1,2},{3,4},{5,6},{7,8},{9,10},{11,12},{13,14},{2,1},{4,3},{6,5},{... | collective-permute-start | bytes 24584 | tf_op jit(solution)/shard_map/ppermute | solution.py:975
  74.4 11.7 %all-to-all-start.4 = ((f32[32,4,128]{2,1,0:T(4,128)}), f32[32,4,128]{2,1,0:T(4,128)S(1)}, u32[]{:S(2)}, u32[]{:S(2)}) async-start(f32[32,4,128]{2,1,0:T(4,128)} %bitcast.45), calls=%async_computation.4 | async-start | bytes 131072 | tf_op jit(solution)/shard_map/all_to_all | solution.py:1041
  78.7 4.0 %collective-permute-start.16 = (f32[2,16,128]{2,1,0:T(8,128)}, f32[2,16,128]{2,1,0:T(8,128)S(1)}, u32[]{:S(2)}, u32[]{:S(2)}) collective-permute-start(f32[2,16,128]{2,1,0:T(8,128)} %get-tuple-element.157), channel_id=1, source_target_pairs={{0,16},{16,0},{1,17},{17,1},{2,18},{18,2},{3,19},{19,3},{4,20},{20... | collective-permute-start | bytes 49160 | tf_op jit(solution)/shard_map/ppermute | solution.py:973
  88.7 11.7 %all-to-all-start.5 = ((f32[32,4,128]{2,1,0:T(4,128)}), f32[32,4,128]{2,1,0:T(4,128)S(1)}, u32[]{:S(2)}, u32[]{:S(2)}) async-start(f32[32,4,128]{2,1,0:T(4,128)} %bitcast.42), calls=%async_computation.5 | async-start | bytes 131072 | tf_op jit(solution)/shard_map/all_to_all | solution.py:1041
  93.0 4.0 %collective-permute-start.19 = (f32[2,16,128]{2,1,0:T(8,128)}, f32[2,16,128]{2,1,0:T(8,128)S(1)}, u32[]{:S(2)}, u32[]{:S(2)}) collective-permute-start(f32[2,16,128]{2,1,0:T(8,128)} %get-tuple-element.167), channel_id=1, source_target_pairs={{0,16},{16,0},{1,17},{17,1},{2,18},{18,2},{3,19},{19,3},{4,20},{20... | collective-permute-start | bytes 49160 | tf_op jit(solution)/shard_map/ppermute | solution.py:973
  (5 other events, 6.3 us)

commit v8 on v7

--- a/solution.py
+++ b/solution.py
@@ -636,10 +636,11 @@
             hits.append(jnp.where(iota((384, 256), 0).astype(F32) == wanted, 1.0, 0.0))
         picks.append(jnp.concatenate(hits, 1).astype(BF16))
         rows.append([jnp.transpose(hit).astype(BF16) for hit in hits])
-    for whole_ref, out_ref in ((gh_ref, dh_ref), (gl_ref, dl_ref)):
-        for region in range(2):
-            which = lax.rem(lax.axis_index("gx") + region, 2)
-            half = dot(whole_ref[which], picks[region]).astype(BF16)
+    size = 384
+    for region in range(2):
+        which = lax.rem(lax.axis_index("gx") + region, 2)
+        both = dot(jnp.concatenate([gh_ref[which], gl_ref[which]], 0), picks[region]).astype(BF16)
+        for half, out_ref in ((both[:size], dh_ref), (both[size:], dl_ref)):
             top = dot(rows[region][0], half).astype(BF16)
             out_ref[region, 0], out_ref[region, 1] = top[:, :256], top[:, 256:]
             out_ref[region, 2] = dot(rows[region][1], half[:, 256:]).astype(BF16)

time: 103 us -> 103 us (level)
  no operation moved by 1% of the time
where the time goes in v8:
time: 103 us; the launch traced here: 102 us
  starting transfers between devices  47.7 us (46%)
  Pallas kernels  26.7 us (26%)
  waiting for transfers between devices  25.7 us (25%)
  between operations  1.07 us (1%)
    pallas_call x11, Pallas kernels, call(): pl.pallas_call(body, out_shape=[jax.ShapeDtypeStruct(*out) if i in kept_o...  26.7 us
    all_to_all x5, starting transfers between devices, two_regions(): lax.all_to_all(block.reshape(32, 4, 128), BOTH, 0, 0, tiled=False)  20.7 us
    all_to_all x5, waiting for transfers between devices, two_regions(): lax.all_to_all(block.reshape(32, 4, 128), BOTH, 0, 0, tiled=False)  15.3 us
    ppermute x7, starting transfers between devices, trade(): lax.ppermute(x, 'gx', [(0, 1), (1, 0)])  14 us
    all_to_all x1, starting transfers between devices, two_regions(): lax.all_to_all(block.reshape(32, 3, 4, 128), BOTH, 0, 0, tiled=False)  8.15 us
    ppermute x7, starting transfers between devices, trade(): lax.ppermute(b, 'gy', both_ways(pairs_from(1, peers)))  4.55 us
    ppermute x7, waiting for transfers between devices, trade(): lax.ppermute(x, 'gx', [(0, 1), (1, 0)])  4.3 us
    all_to_all x1, waiting for transfers between devices, two_regions(): lax.all_to_all(block.reshape(32, 3, 4, 128), BOTH, 0, 0, tiled=False)  3.24 us
  transfers between devices with their start and end apart: 28, of which 15 were waited for; matrix products, arithmetic and copies ran while one was open for 0% of the time, Pallas kernels for 9%

profile of v8, /device:TPU:0, one launch (start us, length us, event | category | flops | bytes accessed | tf_op | source)
XLA Modules:
  0.0 101.9 jit_solution(15231036049582400226)
XLA Ops:
  0.6 2.4 %shard_map.130 = (f32[8,40,256]{2,1,0:T(8,128)S(1)}, f32[2,40,128]{2,1,0:T(8,128)}, f32[40,128]{1,0:T(8,128)}, f32[40,128]{1,0:T(8,128)}, f32[4,256,256]{2,1,0:T...) custom-call(f32[128,128]{1,0:T(8,128)} %bitcast.38, ...), custom_call_target="tpu_custom_call" | custom-call | tf_op jit(solution)/shard_map/pallas_call | solution.py:954
  3.0 3.0 %collective-permute-start = (f32[2,40,128]{2,1,0:T(8,128)}, f32[2,40,128]{2,1,0:T(8,128)S(1)}, u32[]{:S(2)}, u32[]{:S(2)}) collective-permute-start(f32[2,40,128]{2,1,0:T(8,128)} %get-tuple-element.92), channel_id=1, source_target_pairs={{0,16},{16,0},{1,17},{17,1},{2,18},{18,2},{3,19},{19,3},{4,20},{20... | collective-permute-start | bytes 122888 | tf_op jit(solution)/shard_map/ppermute | solution.py:974
  6.9 3.1 %shard_map.131 = (bf16[2,256,256]{2,1,0:T(8,128)(2,1)S(1)}, bf16[2,256,256]{2,1,0:T(8,128)(2,1)S(1)}, bf16[6,256,256]{2,1,0:T(8,128)(2,1)S(1)}, bf16[6,256,256]{...) custom-call(f32[4,256,256]{2,1,0:T(8,128)S(1)} %get-tuple-element.95, ...), custom_call_target="tpu_custom_call" | custom-call | flops 5000000000 | bytes 9765625 | tf_op jit(solution)/shard_map/pallas_call | solution.py:954
  11.6 8.2 %all-to-all-start = ((f32[32,3,4,128]{3,2,1,0:T(4,128)}), f32[32,3,4,128]{3,2,1,0:T(4,128)S(1)}, u32[]{:S(2)}, u32[]{:S(2)}) async-start(f32[32,3,4,128]{3,2,1,0:T(4,128)} %bitcast.36), calls=%async_computation | async-start | bytes 393216 | tf_op jit(solution)/shard_map/all_to_all | solution.py:1024
  19.7 1.8 %collective-permute-start.3 = (f32[2,72,128]{2,1,0:T(8,128)}, f32[2,72,128]{2,1,0:T(8,128)S(1)}, u32[]{:S(2)}, u32[]{:S(2)}) collective-permute-start(f32[2,72,128]{2,1,0:T(8,128)} %get-tuple-element.108), channel_id=1, source_target_pairs={{0,16},{16,0},{1,17},{17,1},{2,18},{18,2},{3,19},{19,3},{4,20},{20... | collective-permute-start | bytes 221192 | tf_op jit(solution)/shard_map/ppermute | solution.py:974
  25.4 3.2 %all-to-all-done = f32[32,3,4,128]{3,2,1,0:T(4,128)S(1)} async-done(((f32[32,3,4,128]{3,2,1,0:T(4,128)}), f32[32,3,4,128]{3,2,1,0:T(4,128)S(1)}, u32[]{:S(2)}, u32[]{:S(2)}) %all-to-all-start) | async-done | bytes 196640 | tf_op jit(solution)/shard_map/all_to_all | solution.py:1024
  28.6 3.1 %shard_map.134 = (bf16[32,512]{1,0:T(8,128)(2,1)S(1)}, bf16[32,512]{1,0:T(8,128)(2,1)S(1)}, f32[128,128]{1,0:T(8,128)S(1)}, f32[128,128]{1,0:T(8,128)S(1)}, f32[...) custom-call(f32[48,8,128]{2,1,0:T(8,128)S(1)} %bitcast.25, ...), custom_call_target="tpu_custom_call" | custom-call | tf_op jit(solution)/shard_map/pallas_call | solution.py:954
  31.8 3.1 %all-to-all-start.1 = ((f32[32,4,128]{2,1,0:T(4,128)}), f32[32,4,128]{2,1,0:T(4,128)S(1)}, u32[]{:S(2)}, u32[]{:S(2)}) async-start(f32[32,4,128]{2,1,0:T(4,128)} %bitcast.41), calls=%async_computation.1 | async-start | bytes 131072 | tf_op jit(solution)/shard_map/all_to_all | solution.py:1042
  34.9 1.8 %collective-permute-start.7 = (f32[2,16,128]{2,1,0:T(8,128)}, f32[2,16,128]{2,1,0:T(8,128)S(1)}, u32[]{:S(2)}, u32[]{:S(2)}) collective-permute-start(f32[2,16,128]{2,1,0:T(8,128)} %get-tuple-element.121), channel_id=1, source_target_pairs={{0,16},{16,0},{1,17},{17,1},{2,18},{18,2},{3,19},{19,3},{4,20},{20... | collective-permute-start | bytes 49160 | tf_op jit(solution)/shard_map/ppermute | solution.py:974
  37.4 3.0 %shard_map.135 = (bf16[2,3,256,256]{3,2,1,0:T(8,128)(2,1)S(1)}, bf16[2,3,256,256]{3,2,1,0:T(8,128)(2,1)S(1)}) custom-call(f32[48,8,128]{2,1,0:T(8,128)S(1)} %bitcast.26, bf16[2,384,384]{2,1,0:T(8,128)(2,1)} %get-tuple-element.128.refs_1_, bf16[2,384,384]{2,1,0:T(8,128)(2,1)} %get-tuple-element.129.refs_2_), custom_call_target="tpu_custom_call" | custom-call | flops 100000000 | bytes 195312 | tf_op jit(solution)/shard_map/pallas_call | solution.py:954
  42.3 2.6 %shard_map.136 = (f32[128,128]{1,0:T(8,128)S(1)}, f32[128,128]{1,0:T(8,128)S(1)}, f32[8,16,256]{2,1,0:T(8,128)S(1)}, f32[8,16,256]{2,1,0:T(8,128)}, f32[5,16,128...) custom-call(f32[16,8,128]{2,1,0:T(8,128)S(1)} %bitcast.27, ...), custom_call_target="tpu_custom_call" | custom-call | tf_op jit(solution)/shard_map/pallas_call | solution.py:954
  44.9 4.8 %all-to-all-start.2 = ((f32[32,4,128]{2,1,0:T(4,128)}), f32[32,4,128]{2,1,0:T(4,128)S(1)}, u32[]{:S(2)}, u32[]{:S(2)}) async-start(f32[32,4,128]{2,1,0:T(4,128)} %bitcast.43), calls=%async_computation.2 | async-start | bytes 131072 | tf_op jit(solution)/shard_map/all_to_all | solution.py:1042
  49.7 1.8 %collective-permute-start.10 = (f32[2,16,128]{2,1,0:T(8,128)}, f32[2,16,128]{2,1,0:T(8,128)S(1)}, u32[]{:S(2)}, u32[]{:S(2)}) collective-permute-start(f32[2,16,128]{2,1,0:T(8,128)} %get-tuple-element.137), channel_id=1, source_target_pairs={{0,16},{16,0},{1,17},{17,1},{2,18},{18,2},{3,19},{19,3},{4,20},{20... | collective-permute-start | bytes 49160 | tf_op jit(solution)/shard_map/ppermute | solution.py:974
  53.7 3.4 %all-to-all-done.2 = f32[32,4,128]{2,1,0:T(4,128)S(1)} async-done(((f32[32,4,128]{2,1,0:T(4,128)}), f32[32,4,128]{2,1,0:T(4,128)S(1)}, u32[]{:S(2)}, u32[]{:S(2)}) %all-to-all-start.2) | async-done | bytes 65568 | tf_op jit(solution)/shard_map/all_to_all | solution.py:1042
  57.1 2.6 %shard_map.137 = (f32[128,128]{1,0:T(8,128)S(1)}, f32[128,128]{1,0:T(8,128)S(1)}, f32[8,16,256]{2,1,0:T(8,128)S(1)}, f32[8,16,256]{2,1,0:T(8,128)}, f32[5,16,128...) custom-call(f32[16,8,128]{2,1,0:T(8,128)S(1)} %bitcast.29, ...), custom_call_target="tpu_custom_call" | custom-call | tf_op jit(solution)/shard_map/pallas_call | solution.py:954
  59.7 4.3 %all-to-all-start.3 = ((f32[32,4,128]{2,1,0:T(4,128)}), f32[32,4,128]{2,1,0:T(4,128)S(1)}, u32[]{:S(2)}, u32[]{:S(2)}) async-start(f32[32,4,128]{2,1,0:T(4,128)} %bitcast.44), calls=%async_computation.3 | async-start | bytes 131072 | tf_op jit(solution)/shard_map/all_to_all | solution.py:1042
  64.0 1.8 %collective-permute-start.13 = (f32[2,16,128]{2,1,0:T(8,128)}, f32[2,16,128]{2,1,0:T(8,128)S(1)}, u32[]{:S(2)}, u32[]{:S(2)}) collective-permute-start(f32[2,16,128]{2,1,0:T(8,128)} %get-tuple-element.147), channel_id=1, source_target_pairs={{0,16},{16,0},{1,17},{17,1},{2,18},{18,2},{3,19},{19,3},{4,20},{20... | collective-permute-start | bytes 49160 | tf_op jit(solution)/shard_map/ppermute | solution.py:974
  68.0 3.4 %all-to-all-done.3 = f32[32,4,128]{2,1,0:T(4,128)S(1)} async-done(((f32[32,4,128]{2,1,0:T(4,128)}), f32[32,4,128]{2,1,0:T(4,128)S(1)}, u32[]{:S(2)}, u32[]{:S(2)}) %all-to-all-start.3) | async-done | bytes 65568 | tf_op jit(solution)/shard_map/all_to_all | solution.py:1042
  71.4 2.6 %shard_map.138 = (f32[128,128]{1,0:T(8,128)S(1)}, f32[128,128]{1,0:T(8,128)S(1)}, f32[8,16,256]{2,1,0:T(8,128)S(1)}, f32[8,16,256]{2,1,0:T(8,128)}, f32[5,16,128...) custom-call(f32[16,8,128]{2,1,0:T(8,128)S(1)} %bitcast.30, ...), custom_call_target="tpu_custom_call" | custom-call | tf_op jit(solution)/shard_map/pallas_call | solution.py:954
  74.0 4.3 %all-to-all-start.4 = ((f32[32,4,128]{2,1,0:T(4,128)}), f32[32,4,128]{2,1,0:T(4,128)S(1)}, u32[]{:S(2)}, u32[]{:S(2)}) async-start(f32[32,4,128]{2,1,0:T(4,128)} %bitcast.45), calls=%async_computation.4 | async-start | bytes 131072 | tf_op jit(solution)/shard_map/all_to_all | solution.py:1042
  82.3 3.4 %all-to-all-done.4 = f32[32,4,128]{2,1,0:T(4,128)S(1)} async-done(((f32[32,4,128]{2,1,0:T(4,128)}), f32[32,4,128]{2,1,0:T(4,128)S(1)}, u32[]{:S(2)}, u32[]{:S(2)}) %all-to-all-start.4) | async-done | bytes 65568 | tf_op jit(solution)/shard_map/all_to_all | solution.py:1042
  85.7 2.6 %shard_map.139 = (f32[128,128]{1,0:T(8,128)S(1)}, f32[128,128]{1,0:T(8,128)S(1)}, f32[8,16,256]{2,1,0:T(8,128)S(1)}, f32[8,16,256]{2,1,0:T(8,128)}, f32[5,16,128...) custom-call(f32[16,8,128]{2,1,0:T(8,128)S(1)} %bitcast.28, ...), custom_call_target="tpu_custom_call" | custom-call | tf_op jit(solution)/shard_map/pallas_call | solution.py:954
  88.3 4.3 %all-to-all-start.5 = ((f32[32,4,128]{2,1,0:T(4,128)}), f32[32,4,128]{2,1,0:T(4,128)S(1)}, u32[]{:S(2)}, u32[]{:S(2)}) async-start(f32[32,4,128]{2,1,0:T(4,128)} %bitcast.42), calls=%async_computation.5 | async-start | bytes 131072 | tf_op jit(solution)/shard_map/all_to_all | solution.py:1042
  96.6 3.4 %all-to-all-done.5 = f32[32,4,128]{2,1,0:T(4,128)S(1)} async-done(((f32[32,4,128]{2,1,0:T(4,128)}), f32[32,4,128]{2,1,0:T(4,128)S(1)}, u32[]{:S(2)}, u32[]{:S(2)}) %all-to-all-start.5) | async-done | bytes 65568 | tf_op jit(solution)/shard_map/all_to_all | solution.py:1042
  (45 shorter events, 22.9 us)
Async XLA Ops:
  3.0 7.0 %collective-permute-start = (f32[2,40,128]{2,1,0:T(8,128)}, f32[2,40,128]{2,1,0:T(8,128)S(1)}, u32[]{:S(2)}, u32[]{:S(2)}) collective-permute-start(f32[2,40,128]{2,1,0:T(8,128)} %get-tuple-element.92), channel_id=1, source_target_pairs={{0,16},{16,0},{1,17},{17,1},{2,18},{18,2},{3,19},{19,3},{4,20},{20... | collective-permute-start | bytes 122888 | tf_op jit(solution)/shard_map/ppermute | solution.py:974
  6.1 4.0 %collective-permute-start.1 = (f32[40,128]{1,0:T(8,128)}, f32[40,128]{1,0:T(8,128)S(1)}, u32[]{:S(2)}, u32[]{:S(2)}) collective-permute-start(f32[40,128]{1,0:T(8,128)} %get-tuple-element.93), channel_id=1, source_target_pairs={{0,1},{2,3},{4,5},{6,7},{8,9},{10,11},{12,13},{14,15},{1,0},{3,2},... | collective-permute-start | bytes 61448 | tf_op jit(solution)/shard_map/ppermute | solution.py:975
  6.1 4.0 %collective-permute-start.2 = (f32[40,128]{1,0:T(8,128)}, f32[40,128]{1,0:T(8,128)S(1)}, u32[]{:S(2)}, u32[]{:S(2)}) collective-permute-start(f32[40,128]{1,0:T(8,128)} %get-tuple-element.94), channel_id=1, source_target_pairs={{1,2},{3,4},{5,6},{7,8},{9,10},{11,12},{13,14},{2,1},{4,3},{6,5},{... | collective-permute-start | bytes 61448 | tf_op jit(solution)/shard_map/ppermute | solution.py:976
  6.7 15.5 %collective-permute-start.6 = (f32[6,128,128]{2,1,0:T(8,128)}, f32[6,128,128]{2,1,0:T(8,128)S(1)}, u32[]{:S(2)}, u32[]{:S(2)}) collective-permute-start(f32[6,128,128]{2,1,0:T(8,128)} %get-tuple-element.115), channel_id=1, source_target_pairs={{0,16},{16,0},{1,17},{17,1},{2,18},{18,2},{3,19},{19,3},{4,20},{20... | collective-permute-start | bytes 1179656 | tf_op jit(solution)/shard_map/ppermute | solution.py:1000
  11.6 17.1 %all-to-all-start = ((f32[32,3,4,128]{3,2,1,0:T(4,128)}), f32[32,3,4,128]{3,2,1,0:T(4,128)S(1)}, u32[]{:S(2)}, u32[]{:S(2)}) async-start(f32[32,3,4,128]{3,2,1,0:T(4,128)} %bitcast.36), calls=%async_computation | async-start | bytes 393216 | tf_op jit(solution)/shard_map/all_to_all | solution.py:1024
  19.7 5.7 %collective-permute-start.3 = (f32[2,72,128]{2,1,0:T(8,128)}, f32[2,72,128]{2,1,0:T(8,128)S(1)}, u32[]{:S(2)}, u32[]{:S(2)}) collective-permute-start(f32[2,72,128]{2,1,0:T(8,128)} %get-tuple-element.108), channel_id=1, source_target_pairs={{0,16},{16,0},{1,17},{17,1},{2,18},{18,2},{3,19},{19,3},{4,20},{20... | collective-permute-start | bytes 221192 | tf_op jit(solution)/shard_map/ppermute | solution.py:974
  21.6 2.8 %collective-permute-start.4 = (f32[72,128]{1,0:T(8,128)}, f32[72,128]{1,0:T(8,128)S(1)}, u32[]{:S(2)}, u32[]{:S(2)}) collective-permute-start(f32[72,128]{1,0:T(8,128)} %get-tuple-element.109), channel_id=1, source_target_pairs={{0,1},{2,3},{4,5},{6,7},{8,9},{10,11},{12,13},{14,15},{1,0},{3,2},... | collective-permute-start | bytes 110600 | tf_op jit(solution)/shard_map/ppermute | solution.py:975
  21.6 2.8 %collective-permute-start.5 = (f32[72,128]{1,0:T(8,128)}, f32[72,128]{1,0:T(8,128)S(1)}, u32[]{:S(2)}, u32[]{:S(2)}) collective-permute-start(f32[72,128]{1,0:T(8,128)} %get-tuple-element.110), channel_id=1, source_target_pairs={{1,2},{3,4},{5,6},{7,8},{9,10},{11,12},{13,14},{2,1},{4,3},{6,5},{... | collective-permute-start | bytes 110600 | tf_op jit(solution)/shard_map/ppermute | solution.py:976
  31.8 10.5 %all-to-all-start.1 = ((f32[32,4,128]{2,1,0:T(4,128)}), f32[32,4,128]{2,1,0:T(4,128)S(1)}, u32[]{:S(2)}, u32[]{:S(2)}) async-start(f32[32,4,128]{2,1,0:T(4,128)} %bitcast.41), calls=%async_computation.1 | async-start | bytes 131072 | tf_op jit(solution)/shard_map/all_to_all | solution.py:1042
  34.9 5.6 %collective-permute-start.7 = (f32[2,16,128]{2,1,0:T(8,128)}, f32[2,16,128]{2,1,0:T(8,128)S(1)}, u32[]{:S(2)}, u32[]{:S(2)}) collective-permute-start(f32[2,16,128]{2,1,0:T(8,128)} %get-tuple-element.121), channel_id=1, source_target_pairs={{0,16},{16,0},{1,17},{17,1},{2,18},{18,2},{3,19},{19,3},{4,20},{20... | collective-permute-start | bytes 49160 | tf_op jit(solution)/shard_map/ppermute | solution.py:974
  36.8 3.7 %collective-permute-start.8 = (f32[16,128]{1,0:T(8,128)}, f32[16,128]{1,0:T(8,128)S(1)}, u32[]{:S(2)}, u32[]{:S(2)}) collective-permute-start(f32[16,128]{1,0:T(8,128)} %get-tuple-element.122), channel_id=1, source_target_pairs={{0,1},{2,3},{4,5},{6,7},{8,9},{10,11},{12,13},{14,15},{1,0},{3,2},... | collective-permute-start | bytes 24584 | tf_op jit(solution)/shard_map/ppermute | solution.py:975
  36.8 3.7 %collective-permute-start.9 = (f32[16,128]{1,0:T(8,128)}, f32[16,128]{1,0:T(8,128)S(1)}, u32[]{:S(2)}, u32[]{:S(2)}) collective-permute-start(f32[16,128]{1,0:T(8,128)} %get-tuple-element.123), channel_id=1, source_target_pairs={{1,2},{3,4},{5,6},{7,8},{9,10},{11,12},{13,14},{2,1},{4,3},{6,5},{... | collective-permute-start | bytes 24584 | tf_op jit(solution)/shard_map/ppermute | solution.py:976
  44.9 12.2 %all-to-all-start.2 = ((f32[32,4,128]{2,1,0:T(4,128)}), f32[32,4,128]{2,1,0:T(4,128)S(1)}, u32[]{:S(2)}, u32[]{:S(2)}) async-start(f32[32,4,128]{2,1,0:T(4,128)} %bitcast.43), calls=%async_computation.2 | async-start | bytes 131072 | tf_op jit(solution)/shard_map/all_to_all | solution.py:1042
  49.7 4.0 %collective-permute-start.10 = (f32[2,16,128]{2,1,0:T(8,128)}, f32[2,16,128]{2,1,0:T(8,128)S(1)}, u32[]{:S(2)}, u32[]{:S(2)}) collective-permute-start(f32[2,16,128]{2,1,0:T(8,128)} %get-tuple-element.137), channel_id=1, source_target_pairs={{0,16},{16,0},{1,17},{17,1},{2,18},{18,2},{3,19},{19,3},{4,20},{20... | collective-permute-start | bytes 49160 | tf_op jit(solution)/shard_map/ppermute | solution.py:974
  51.5 1.4 %collective-permute-start.11 = (f32[16,128]{1,0:T(8,128)}, f32[16,128]{1,0:T(8,128)S(1)}, u32[]{:S(2)}, u32[]{:S(2)}) collective-permute-start(f32[16,128]{1,0:T(8,128)} %get-tuple-element.138), channel_id=1, source_target_pairs={{0,1},{2,3},{4,5},{6,7},{8,9},{10,11},{12,13},{14,15},{1,0},{3,2},... | collective-permute-start | bytes 24584 | tf_op jit(solution)/shard_map/ppermute | solution.py:975
  59.7 11.7 %all-to-all-start.3 = ((f32[32,4,128]{2,1,0:T(4,128)}), f32[32,4,128]{2,1,0:T(4,128)S(1)}, u32[]{:S(2)}, u32[]{:S(2)}) async-start(f32[32,4,128]{2,1,0:T(4,128)} %bitcast.44), calls=%async_computation.3 | async-start | bytes 131072 | tf_op jit(solution)/shard_map/all_to_all | solution.py:1042
  64.0 4.0 %collective-permute-start.13 = (f32[2,16,128]{2,1,0:T(8,128)}, f32[2,16,128]{2,1,0:T(8,128)S(1)}, u32[]{:S(2)}, u32[]{:S(2)}) collective-permute-start(f32[2,16,128]{2,1,0:T(8,128)} %get-tuple-element.147), channel_id=1, source_target_pairs={{0,16},{16,0},{1,17},{17,1},{2,18},{18,2},{3,19},{19,3},{4,20},{20... | collective-permute-start | bytes 49160 | tf_op jit(solution)/shard_map/ppermute | solution.py:974
  65.8 1.4 %collective-permute-start.14 = (f32[16,128]{1,0:T(8,128)}, f32[16,128]{1,0:T(8,128)S(1)}, u32[]{:S(2)}, u32[]{:S(2)}) collective-permute-start(f32[16,128]{1,0:T(8,128)} %get-tuple-element.148), channel_id=1, source_target_pairs={{0,1},{2,3},{4,5},{6,7},{8,9},{10,11},{12,13},{14,15},{1,0},{3,2},... | collective-permute-start | bytes 24584 | tf_op jit(solution)/shard_map/ppermute | solution.py:975
  65.8 1.4 %collective-permute-start.15 = (f32[16,128]{1,0:T(8,128)}, f32[16,128]{1,0:T(8,128)S(1)}, u32[]{:S(2)}, u32[]{:S(2)}) collective-permute-start(f32[16,128]{1,0:T(8,128)} %get-tuple-element.149), channel_id=1, source_target_pairs={{1,2},{3,4},{5,6},{7,8},{9,10},{11,12},{13,14},{2,1},{4,3},{6,5},{... | collective-permute-start | bytes 24584 | tf_op jit(solution)/shard_map/ppermute | solution.py:976
  74.0 11.7 %all-to-all-start.4 = ((f32[32,4,128]{2,1,0:T(4,128)}), f32[32,4,128]{2,1,0:T(4,128)S(1)}, u32[]{:S(2)}, u32[]{:S(2)}) async-start(f32[32,4,128]{2,1,0:T(4,128)} %bitcast.45), calls=%async_computation.4 | async-start | bytes 131072 | tf_op jit(solution)/shard_map/all_to_all | solution.py:1042
  78.3 4.0 %collective-permute-start.16 = (f32[2,16,128]{2,1,0:T(8,128)}, f32[2,16,128]{2,1,0:T(8,128)S(1)}, u32[]{:S(2)}, u32[]{:S(2)}) collective-permute-start(f32[2,16,128]{2,1,0:T(8,128)} %get-tuple-element.157), channel_id=1, source_target_pairs={{0,16},{16,0},{1,17},{17,1},{2,18},{18,2},{3,19},{19,3},{4,20},{20... | collective-permute-start | bytes 49160 | tf_op jit(solution)/shard_map/ppermute | solution.py:974
  80.1 1.4 %collective-permute-start.18 = (f32[16,128]{1,0:T(8,128)}, f32[16,128]{1,0:T(8,128)S(1)}, u32[]{:S(2)}, u32[]{:S(2)}) collective-permute-start(f32[16,128]{1,0:T(8,128)} %get-tuple-element.159), channel_id=1, source_target_pairs={{1,2},{3,4},{5,6},{7,8},{9,10},{11,12},{13,14},{2,1},{4,3},{6,5},{... | collective-permute-start | bytes 24584 | tf_op jit(solution)/shard_map/ppermute | solution.py:976
  88.3 11.7 %all-to-all-start.5 = ((f32[32,4,128]{2,1,0:T(4,128)}), f32[32,4,128]{2,1,0:T(4,128)S(1)}, u32[]{:S(2)}, u32[]{:S(2)}) async-start(f32[32,4,128]{2,1,0:T(4,128)} %bitcast.42), calls=%async_computation.5 | async-start | bytes 131072 | tf_op jit(solution)/shard_map/all_to_all | solution.py:1042
  92.6 4.0 %collective-permute-start.19 = (f32[2,16,128]{2,1,0:T(8,128)}, f32[2,16,128]{2,1,0:T(8,128)S(1)}, u32[]{:S(2)}, u32[]{:S(2)}) collective-permute-start(f32[2,16,128]{2,1,0:T(8,128)} %get-tuple-element.167), channel_id=1, source_target_pairs={{0,16},{16,0},{1,17},{17,1},{2,18},{18,2},{3,19},{19,3},{4,20},{20... | collective-permute-start | bytes 49160 | tf_op jit(solution)/shard_map/ppermute | solution.py:974
  (5 other events, 6.3 us)

commit v9 on v8

--- a/solution.py
+++ b/solution.py
@@ -713,6 +713,8 @@
         sx_ref[t, at, :] = names
     sa_ref[at, :] = names
     sb_ref[at, :] = names
+    for ref in (sx_ref, sa_ref, sb_ref):
+        ref.flush()
     us = [v[:CASES] for v in vs]
     ps = [v[CASES:] for v in vs]
     rho = over_lanes([jnp.where(owned_lanes(i, CASES), rs[i] * us[i], 0.0) for i in range(SUBS)])
@@ -857,6 +859,8 @@
         got_ref, x_ref, a_ref, b_ref, y_ref, r_ref, s_ref, scal_ref, mk_ref, dh_ref, dl_ref, nh_ref, nl_ref, ch_ref, cl_ref
     )
     track(r_ref, scalars, mk_ref, p_ref, l_ref, po_ref, lo_ref)
+    po_ref.flush()
+    lo_ref.flush()
     for i in range(SUBS):
         ro_ref[pl.ds(i, CASES, stride=SUBS), :] = take_owned(rs[i], i)
 

time: 103 us -> 103 us (level)
  no operation moved by 1% of the time
where the time goes in v9:
time: 103 us; the launch traced here: 102 us
  starting transfers between devices  47.7 us (46%)
  Pallas kernels  26.7 us (26%)
  waiting for transfers between devices  25.7 us (25%)
  between operations  1.07 us (1%)
    pallas_call x11, Pallas kernels, call(): pl.pallas_call(body, out_shape=[jax.ShapeDtypeStruct(*out) if i in kept_o...  26.7 us
    all_to_all x5, starting transfers between devices, two_regions(): lax.all_to_all(block.reshape(32, 4, 128), BOTH, 0, 0, tiled=False)  20.7 us
    all_to_all x5, waiting for transfers between devices, two_regions(): lax.all_to_all(block.reshape(32, 4, 128), BOTH, 0, 0, tiled=False)  15.3 us
    ppermute x7, starting transfers between devices, trade(): lax.ppermute(x, 'gx', [(0, 1), (1, 0)])  14 us
    all_to_all x1, starting transfers between devices, two_regions(): lax.all_to_all(block.reshape(32, 3, 4, 128), BOTH, 0, 0, tiled=False)  8.15 us
    ppermute x7, starting transfers between devices, trade(): lax.ppermute(b, 'gy', both_ways(pairs_from(1, peers)))  4.55 us
    ppermute x7, waiting for transfers between devices, trade(): lax.ppermute(x, 'gx', [(0, 1), (1, 0)])  4.3 us
    all_to_all x1, waiting for transfers between devices, two_regions(): lax.all_to_all(block.reshape(32, 3, 4, 128), BOTH, 0, 0, tiled=False)  3.24 us
  transfers between devices with their start and end apart: 28, of which 15 were waited for; matrix products, arithmetic and copies ran while one was open for 0% of the time, Pallas kernels for 9%

profile of v9, /device:TPU:0, one launch (start us, length us, event | category | flops | bytes accessed | tf_op | source)
XLA Modules:
  0.0 101.9 jit_solution(11937693983237638494)
XLA Ops:
  0.6 2.4 %shard_map.130 = (f32[8,40,256]{2,1,0:T(8,128)S(1)}, f32[2,40,128]{2,1,0:T(8,128)}, f32[40,128]{1,0:T(8,128)}, f32[40,128]{1,0:T(8,128)}, f32[4,256,256]{2,1,0:T...) custom-call(f32[128,128]{1,0:T(8,128)} %bitcast.38, ...), custom_call_target="tpu_custom_call" | custom-call | tf_op jit(solution)/shard_map/pallas_call | solution.py:958
  3.0 3.0 %collective-permute-start = (f32[2,40,128]{2,1,0:T(8,128)}, f32[2,40,128]{2,1,0:T(8,128)S(1)}, u32[]{:S(2)}, u32[]{:S(2)}) collective-permute-start(f32[2,40,128]{2,1,0:T(8,128)} %get-tuple-element.92), channel_id=1, source_target_pairs={{0,16},{16,0},{1,17},{17,1},{2,18},{18,2},{3,19},{19,3},{4,20},{20... | collective-permute-start | bytes 122888 | tf_op jit(solution)/shard_map/ppermute | solution.py:978
  6.9 3.1 %shard_map.131 = (bf16[2,256,256]{2,1,0:T(8,128)(2,1)S(1)}, bf16[2,256,256]{2,1,0:T(8,128)(2,1)S(1)}, bf16[6,256,256]{2,1,0:T(8,128)(2,1)S(1)}, bf16[6,256,256]{...) custom-call(f32[4,256,256]{2,1,0:T(8,128)S(1)} %get-tuple-element.95, ...), custom_call_target="tpu_custom_call" | custom-call | flops 5000000000 | bytes 9765625 | tf_op jit(solution)/shard_map/pallas_call | solution.py:958
  11.5 8.2 %all-to-all-start = ((f32[32,3,4,128]{3,2,1,0:T(4,128)}), f32[32,3,4,128]{3,2,1,0:T(4,128)S(1)}, u32[]{:S(2)}, u32[]{:S(2)}) async-start(f32[32,3,4,128]{3,2,1,0:T(4,128)} %bitcast.36), calls=%async_computation | async-start | bytes 393216 | tf_op jit(solution)/shard_map/all_to_all | solution.py:1028
  19.7 1.8 %collective-permute-start.3 = (f32[2,72,128]{2,1,0:T(8,128)}, f32[2,72,128]{2,1,0:T(8,128)S(1)}, u32[]{:S(2)}, u32[]{:S(2)}) collective-permute-start(f32[2,72,128]{2,1,0:T(8,128)} %get-tuple-element.108), channel_id=1, source_target_pairs={{0,16},{16,0},{1,17},{17,1},{2,18},{18,2},{3,19},{19,3},{4,20},{20... | collective-permute-start | bytes 221192 | tf_op jit(solution)/shard_map/ppermute | solution.py:978
  25.4 3.2 %all-to-all-done = f32[32,3,4,128]{3,2,1,0:T(4,128)S(1)} async-done(((f32[32,3,4,128]{3,2,1,0:T(4,128)}), f32[32,3,4,128]{3,2,1,0:T(4,128)S(1)}, u32[]{:S(2)}, u32[]{:S(2)}) %all-to-all-start) | async-done | bytes 196640 | tf_op jit(solution)/shard_map/all_to_all | solution.py:1028
  28.6 3.1 %shard_map.134 = (bf16[32,512]{1,0:T(8,128)(2,1)S(1)}, bf16[32,512]{1,0:T(8,128)(2,1)S(1)}, f32[128,128]{1,0:T(8,128)S(1)}, f32[128,128]{1,0:T(8,128)S(1)}, f32[...) custom-call(f32[48,8,128]{2,1,0:T(8,128)S(1)} %bitcast.25, ...), custom_call_target="tpu_custom_call" | custom-call | tf_op jit(solution)/shard_map/pallas_call | solution.py:958
  31.8 3.1 %all-to-all-start.1 = ((f32[32,4,128]{2,1,0:T(4,128)}), f32[32,4,128]{2,1,0:T(4,128)S(1)}, u32[]{:S(2)}, u32[]{:S(2)}) async-start(f32[32,4,128]{2,1,0:T(4,128)} %bitcast.41), calls=%async_computation.1 | async-start | bytes 131072 | tf_op jit(solution)/shard_map/all_to_all | solution.py:1046
  34.9 1.8 %collective-permute-start.7 = (f32[2,16,128]{2,1,0:T(8,128)}, f32[2,16,128]{2,1,0:T(8,128)S(1)}, u32[]{:S(2)}, u32[]{:S(2)}) collective-permute-start(f32[2,16,128]{2,1,0:T(8,128)} %get-tuple-element.121), channel_id=1, source_target_pairs={{0,16},{16,0},{1,17},{17,1},{2,18},{18,2},{3,19},{19,3},{4,20},{20... | collective-permute-start | bytes 49160 | tf_op jit(solution)/shard_map/ppermute | solution.py:978
  37.4 3.0 %shard_map.135 = (bf16[2,3,256,256]{3,2,1,0:T(8,128)(2,1)S(1)}, bf16[2,3,256,256]{3,2,1,0:T(8,128)(2,1)S(1)}) custom-call(f32[48,8,128]{2,1,0:T(8,128)S(1)} %bitcast.26, bf16[2,384,384]{2,1,0:T(8,128)(2,1)} %get-tuple-element.128.refs_1_, bf16[2,384,384]{2,1,0:T(8,128)(2,1)} %get-tuple-element.129.refs_2_), custom_call_target="tpu_custom_call" | custom-call | flops 100000000 | bytes 195312 | tf_op jit(solution)/shard_map/pallas_call | solution.py:958
  42.3 2.6 %shard_map.136 = (f32[128,128]{1,0:T(8,128)S(1)}, f32[128,128]{1,0:T(8,128)S(1)}, f32[8,16,256]{2,1,0:T(8,128)S(1)}, f32[8,16,256]{2,1,0:T(8,128)}, f32[5,16,128...) custom-call(f32[16,8,128]{2,1,0:T(8,128)S(1)} %bitcast.27, ...), custom_call_target="tpu_custom_call" | custom-call | tf_op jit(solution)/shard_map/pallas_call | solution.py:958
  44.9 4.8 %all-to-all-start.2 = ((f32[32,4,128]{2,1,0:T(4,128)}), f32[32,4,128]{2,1,0:T(4,128)S(1)}, u32[]{:S(2)}, u32[]{:S(2)}) async-start(f32[32,4,128]{2,1,0:T(4,128)} %bitcast.43), calls=%async_computation.2 | async-start | bytes 131072 | tf_op jit(solution)/shard_map/all_to_all | solution.py:1046
  49.7 1.8 %collective-permute-start.10 = (f32[2,16,128]{2,1,0:T(8,128)}, f32[2,16,128]{2,1,0:T(8,128)S(1)}, u32[]{:S(2)}, u32[]{:S(2)}) collective-permute-start(f32[2,16,128]{2,1,0:T(8,128)} %get-tuple-element.137), channel_id=1, source_target_pairs={{0,16},{16,0},{1,17},{17,1},{2,18},{18,2},{3,19},{19,3},{4,20},{20... | collective-permute-start | bytes 49160 | tf_op jit(solution)/shard_map/ppermute | solution.py:978
  53.7 3.4 %all-to-all-done.2 = f32[32,4,128]{2,1,0:T(4,128)S(1)} async-done(((f32[32,4,128]{2,1,0:T(4,128)}), f32[32,4,128]{2,1,0:T(4,128)S(1)}, u32[]{:S(2)}, u32[]{:S(2)}) %all-to-all-start.2) | async-done | bytes 65568 | tf_op jit(solution)/shard_map/all_to_all | solution.py:1046
  57.1 2.6 %shard_map.137 = (f32[128,128]{1,0:T(8,128)S(1)}, f32[128,128]{1,0:T(8,128)S(1)}, f32[8,16,256]{2,1,0:T(8,128)S(1)}, f32[8,16,256]{2,1,0:T(8,128)}, f32[5,16,128...) custom-call(f32[16,8,128]{2,1,0:T(8,128)S(1)} %bitcast.29, ...), custom_call_target="tpu_custom_call" | custom-call | tf_op jit(solution)/shard_map/pallas_call | solution.py:958
  59.7 4.3 %all-to-all-start.3 = ((f32[32,4,128]{2,1,0:T(4,128)}), f32[32,4,128]{2,1,0:T(4,128)S(1)}, u32[]{:S(2)}, u32[]{:S(2)}) async-start(f32[32,4,128]{2,1,0:T(4,128)} %bitcast.44), calls=%async_computation.3 | async-start | bytes 131072 | tf_op jit(solution)/shard_map/all_to_all | solution.py:1046
  64.0 1.8 %collective-permute-start.13 = (f32[2,16,128]{2,1,0:T(8,128)}, f32[2,16,128]{2,1,0:T(8,128)S(1)}, u32[]{:S(2)}, u32[]{:S(2)}) collective-permute-start(f32[2,16,128]{2,1,0:T(8,128)} %get-tuple-element.147), channel_id=1, source_target_pairs={{0,16},{16,0},{1,17},{17,1},{2,18},{18,2},{3,19},{19,3},{4,20},{20... | collective-permute-start | bytes 49160 | tf_op jit(solution)/shard_map/ppermute | solution.py:978
  68.0 3.4 %all-to-all-done.3 = f32[32,4,128]{2,1,0:T(4,128)S(1)} async-done(((f32[32,4,128]{2,1,0:T(4,128)}), f32[32,4,128]{2,1,0:T(4,128)S(1)}, u32[]{:S(2)}, u32[]{:S(2)}) %all-to-all-start.3) | async-done | bytes 65568 | tf_op jit(solution)/shard_map/all_to_all | solution.py:1046
  71.4 2.6 %shard_map.138 = (f32[128,128]{1,0:T(8,128)S(1)}, f32[128,128]{1,0:T(8,128)S(1)}, f32[8,16,256]{2,1,0:T(8,128)S(1)}, f32[8,16,256]{2,1,0:T(8,128)}, f32[5,16,128...) custom-call(f32[16,8,128]{2,1,0:T(8,128)S(1)} %bitcast.30, ...), custom_call_target="tpu_custom_call" | custom-call | tf_op jit(solution)/shard_map/pallas_call | solution.py:958
  74.0 4.3 %all-to-all-start.4 = ((f32[32,4,128]{2,1,0:T(4,128)}), f32[32,4,128]{2,1,0:T(4,128)S(1)}, u32[]{:S(2)}, u32[]{:S(2)}) async-start(f32[32,4,128]{2,1,0:T(4,128)} %bitcast.45), calls=%async_computation.4 | async-start | bytes 131072 | tf_op jit(solution)/shard_map/all_to_all | solution.py:1046
  82.3 3.4 %all-to-all-done.4 = f32[32,4,128]{2,1,0:T(4,128)S(1)} async-done(((f32[32,4,128]{2,1,0:T(4,128)}), f32[32,4,128]{2,1,0:T(4,128)S(1)}, u32[]{:S(2)}, u32[]{:S(2)}) %all-to-all-start.4) | async-done | bytes 65568 | tf_op jit(solution)/shard_map/all_to_all | solution.py:1046
  85.7 2.6 %shard_map.139 = (f32[128,128]{1,0:T(8,128)S(1)}, f32[128,128]{1,0:T(8,128)S(1)}, f32[8,16,256]{2,1,0:T(8,128)S(1)}, f32[8,16,256]{2,1,0:T(8,128)}, f32[5,16,128...) custom-call(f32[16,8,128]{2,1,0:T(8,128)S(1)} %bitcast.28, ...), custom_call_target="tpu_custom_call" | custom-call | tf_op jit(solution)/shard_map/pallas_call | solution.py:958
  88.3 4.3 %all-to-all-start.5 = ((f32[32,4,128]{2,1,0:T(4,128)}), f32[32,4,128]{2,1,0:T(4,128)S(1)}, u32[]{:S(2)}, u32[]{:S(2)}) async-start(f32[32,4,128]{2,1,0:T(4,128)} %bitcast.42), calls=%async_computation.5 | async-start | bytes 131072 | tf_op jit(solution)/shard_map/all_to_all | solution.py:1046
  96.6 3.4 %all-to-all-done.5 = f32[32,4,128]{2,1,0:T(4,128)S(1)} async-done(((f32[32,4,128]{2,1,0:T(4,128)}), f32[32,4,128]{2,1,0:T(4,128)S(1)}, u32[]{:S(2)}, u32[]{:S(2)}) %all-to-all-start.5) | async-done | bytes 65568 | tf_op jit(solution)/shard_map/all_to_all | solution.py:1046
  (45 shorter events, 22.8 us)
Async XLA Ops:
  3.0 7.0 %collective-permute-start = (f32[2,40,128]{2,1,0:T(8,128)}, f32[2,40,128]{2,1,0:T(8,128)S(1)}, u32[]{:S(2)}, u32[]{:S(2)}) collective-permute-start(f32[2,40,128]{2,1,0:T(8,128)} %get-tuple-element.92), channel_id=1, source_target_pairs={{0,16},{16,0},{1,17},{17,1},{2,18},{18,2},{3,19},{19,3},{4,20},{20... | collective-permute-start | bytes 122888 | tf_op jit(solution)/shard_map/ppermute | solution.py:978
  6.1 4.0 %collective-permute-start.1 = (f32[40,128]{1,0:T(8,128)}, f32[40,128]{1,0:T(8,128)S(1)}, u32[]{:S(2)}, u32[]{:S(2)}) collective-permute-start(f32[40,128]{1,0:T(8,128)} %get-tuple-element.93), channel_id=1, source_target_pairs={{0,1},{2,3},{4,5},{6,7},{8,9},{10,11},{12,13},{14,15},{1,0},{3,2},... | collective-permute-start | bytes 61448 | tf_op jit(solution)/shard_map/ppermute | solution.py:979
  6.1 4.0 %collective-permute-start.2 = (f32[40,128]{1,0:T(8,128)}, f32[40,128]{1,0:T(8,128)S(1)}, u32[]{:S(2)}, u32[]{:S(2)}) collective-permute-start(f32[40,128]{1,0:T(8,128)} %get-tuple-element.94), channel_id=1, source_target_pairs={{1,2},{3,4},{5,6},{7,8},{9,10},{11,12},{13,14},{2,1},{4,3},{6,5},{... | collective-permute-start | bytes 61448 | tf_op jit(solution)/shard_map/ppermute | solution.py:980
  6.7 15.5 %collective-permute-start.6 = (f32[6,128,128]{2,1,0:T(8,128)}, f32[6,128,128]{2,1,0:T(8,128)S(1)}, u32[]{:S(2)}, u32[]{:S(2)}) collective-permute-start(f32[6,128,128]{2,1,0:T(8,128)} %get-tuple-element.115), channel_id=1, source_target_pairs={{0,16},{16,0},{1,17},{17,1},{2,18},{18,2},{3,19},{19,3},{4,20},{20... | collective-permute-start | bytes 1179656 | tf_op jit(solution)/shard_map/ppermute | solution.py:1004
  11.5 17.1 %all-to-all-start = ((f32[32,3,4,128]{3,2,1,0:T(4,128)}), f32[32,3,4,128]{3,2,1,0:T(4,128)S(1)}, u32[]{:S(2)}, u32[]{:S(2)}) async-start(f32[32,3,4,128]{3,2,1,0:T(4,128)} %bitcast.36), calls=%async_computation | async-start | bytes 393216 | tf_op jit(solution)/shard_map/all_to_all | solution.py:1028
  19.7 5.7 %collective-permute-start.3 = (f32[2,72,128]{2,1,0:T(8,128)}, f32[2,72,128]{2,1,0:T(8,128)S(1)}, u32[]{:S(2)}, u32[]{:S(2)}) collective-permute-start(f32[2,72,128]{2,1,0:T(8,128)} %get-tuple-element.108), channel_id=1, source_target_pairs={{0,16},{16,0},{1,17},{17,1},{2,18},{18,2},{3,19},{19,3},{4,20},{20... | collective-permute-start | bytes 221192 | tf_op jit(solution)/shard_map/ppermute | solution.py:978
  21.5 2.8 %collective-permute-start.4 = (f32[72,128]{1,0:T(8,128)}, f32[72,128]{1,0:T(8,128)S(1)}, u32[]{:S(2)}, u32[]{:S(2)}) collective-permute-start(f32[72,128]{1,0:T(8,128)} %get-tuple-element.109), channel_id=1, source_target_pairs={{0,1},{2,3},{4,5},{6,7},{8,9},{10,11},{12,13},{14,15},{1,0},{3,2},... | collective-permute-start | bytes 110600 | tf_op jit(solution)/shard_map/ppermute | solution.py:979
  21.5 2.8 %collective-permute-start.5 = (f32[72,128]{1,0:T(8,128)}, f32[72,128]{1,0:T(8,128)S(1)}, u32[]{:S(2)}, u32[]{:S(2)}) collective-permute-start(f32[72,128]{1,0:T(8,128)} %get-tuple-element.110), channel_id=1, source_target_pairs={{1,2},{3,4},{5,6},{7,8},{9,10},{11,12},{13,14},{2,1},{4,3},{6,5},{... | collective-permute-start | bytes 110600 | tf_op jit(solution)/shard_map/ppermute | solution.py:980
  31.8 10.5 %all-to-all-start.1 = ((f32[32,4,128]{2,1,0:T(4,128)}), f32[32,4,128]{2,1,0:T(4,128)S(1)}, u32[]{:S(2)}, u32[]{:S(2)}) async-start(f32[32,4,128]{2,1,0:T(4,128)} %bitcast.41), calls=%async_computation.1 | async-start | bytes 131072 | tf_op jit(solution)/shard_map/all_to_all | solution.py:1046
  34.9 5.6 %collective-permute-start.7 = (f32[2,16,128]{2,1,0:T(8,128)}, f32[2,16,128]{2,1,0:T(8,128)S(1)}, u32[]{:S(2)}, u32[]{:S(2)}) collective-permute-start(f32[2,16,128]{2,1,0:T(8,128)} %get-tuple-element.121), channel_id=1, source_target_pairs={{0,16},{16,0},{1,17},{17,1},{2,18},{18,2},{3,19},{19,3},{4,20},{20... | collective-permute-start | bytes 49160 | tf_op jit(solution)/shard_map/ppermute | solution.py:978
  36.7 3.7 %collective-permute-start.8 = (f32[16,128]{1,0:T(8,128)}, f32[16,128]{1,0:T(8,128)S(1)}, u32[]{:S(2)}, u32[]{:S(2)}) collective-permute-start(f32[16,128]{1,0:T(8,128)} %get-tuple-element.122), channel_id=1, source_target_pairs={{0,1},{2,3},{4,5},{6,7},{8,9},{10,11},{12,13},{14,15},{1,0},{3,2},... | collective-permute-start | bytes 24584 | tf_op jit(solution)/shard_map/ppermute | solution.py:979
  36.7 3.7 %collective-permute-start.9 = (f32[16,128]{1,0:T(8,128)}, f32[16,128]{1,0:T(8,128)S(1)}, u32[]{:S(2)}, u32[]{:S(2)}) collective-permute-start(f32[16,128]{1,0:T(8,128)} %get-tuple-element.123), channel_id=1, source_target_pairs={{1,2},{3,4},{5,6},{7,8},{9,10},{11,12},{13,14},{2,1},{4,3},{6,5},{... | collective-permute-start | bytes 24584 | tf_op jit(solution)/shard_map/ppermute | solution.py:980
  44.9 12.2 %all-to-all-start.2 = ((f32[32,4,128]{2,1,0:T(4,128)}), f32[32,4,128]{2,1,0:T(4,128)S(1)}, u32[]{:S(2)}, u32[]{:S(2)}) async-start(f32[32,4,128]{2,1,0:T(4,128)} %bitcast.43), calls=%async_computation.2 | async-start | bytes 131072 | tf_op jit(solution)/shard_map/all_to_all | solution.py:1046
  49.7 4.0 %collective-permute-start.10 = (f32[2,16,128]{2,1,0:T(8,128)}, f32[2,16,128]{2,1,0:T(8,128)S(1)}, u32[]{:S(2)}, u32[]{:S(2)}) collective-permute-start(f32[2,16,128]{2,1,0:T(8,128)} %get-tuple-element.137), channel_id=1, source_target_pairs={{0,16},{16,0},{1,17},{17,1},{2,18},{18,2},{3,19},{19,3},{4,20},{20... | collective-permute-start | bytes 49160 | tf_op jit(solution)/shard_map/ppermute | solution.py:978
  51.5 1.4 %collective-permute-start.11 = (f32[16,128]{1,0:T(8,128)}, f32[16,128]{1,0:T(8,128)S(1)}, u32[]{:S(2)}, u32[]{:S(2)}) collective-permute-start(f32[16,128]{1,0:T(8,128)} %get-tuple-element.138), channel_id=1, source_target_pairs={{0,1},{2,3},{4,5},{6,7},{8,9},{10,11},{12,13},{14,15},{1,0},{3,2},... | collective-permute-start | bytes 24584 | tf_op jit(solution)/shard_map/ppermute | solution.py:979
  51.5 1.4 %collective-permute-start.12 = (f32[16,128]{1,0:T(8,128)}, f32[16,128]{1,0:T(8,128)S(1)}, u32[]{:S(2)}, u32[]{:S(2)}) collective-permute-start(f32[16,128]{1,0:T(8,128)} %get-tuple-element.139), channel_id=1, source_target_pairs={{1,2},{3,4},{5,6},{7,8},{9,10},{11,12},{13,14},{2,1},{4,3},{6,5},{... | collective-permute-start | bytes 24584 | tf_op jit(solution)/shard_map/ppermute | solution.py:980
  59.7 11.7 %all-to-all-start.3 = ((f32[32,4,128]{2,1,0:T(4,128)}), f32[32,4,128]{2,1,0:T(4,128)S(1)}, u32[]{:S(2)}, u32[]{:S(2)}) async-start(f32[32,4,128]{2,1,0:T(4,128)} %bitcast.44), calls=%async_computation.3 | async-start | bytes 131072 | tf_op jit(solution)/shard_map/all_to_all | solution.py:1046
  64.0 4.0 %collective-permute-start.13 = (f32[2,16,128]{2,1,0:T(8,128)}, f32[2,16,128]{2,1,0:T(8,128)S(1)}, u32[]{:S(2)}, u32[]{:S(2)}) collective-permute-start(f32[2,16,128]{2,1,0:T(8,128)} %get-tuple-element.147), channel_id=1, source_target_pairs={{0,16},{16,0},{1,17},{17,1},{2,18},{18,2},{3,19},{19,3},{4,20},{20... | collective-permute-start | bytes 49160 | tf_op jit(solution)/shard_map/ppermute | solution.py:978
  65.8 1.4 %collective-permute-start.14 = (f32[16,128]{1,0:T(8,128)}, f32[16,128]{1,0:T(8,128)S(1)}, u32[]{:S(2)}, u32[]{:S(2)}) collective-permute-start(f32[16,128]{1,0:T(8,128)} %get-tuple-element.148), channel_id=1, source_target_pairs={{0,1},{2,3},{4,5},{6,7},{8,9},{10,11},{12,13},{14,15},{1,0},{3,2},... | collective-permute-start | bytes 24584 | tf_op jit(solution)/shard_map/ppermute | solution.py:979
  65.8 1.4 %collective-permute-start.15 = (f32[16,128]{1,0:T(8,128)}, f32[16,128]{1,0:T(8,128)S(1)}, u32[]{:S(2)}, u32[]{:S(2)}) collective-permute-start(f32[16,128]{1,0:T(8,128)} %get-tuple-element.149), channel_id=1, source_target_pairs={{1,2},{3,4},{5,6},{7,8},{9,10},{11,12},{13,14},{2,1},{4,3},{6,5},{... | collective-permute-start | bytes 24584 | tf_op jit(solution)/shard_map/ppermute | solution.py:980
  74.0 11.7 %all-to-all-start.4 = ((f32[32,4,128]{2,1,0:T(4,128)}), f32[32,4,128]{2,1,0:T(4,128)S(1)}, u32[]{:S(2)}, u32[]{:S(2)}) async-start(f32[32,4,128]{2,1,0:T(4,128)} %bitcast.45), calls=%async_computation.4 | async-start | bytes 131072 | tf_op jit(solution)/shard_map/all_to_all | solution.py:1046
  78.3 4.0 %collective-permute-start.16 = (f32[2,16,128]{2,1,0:T(8,128)}, f32[2,16,128]{2,1,0:T(8,128)S(1)}, u32[]{:S(2)}, u32[]{:S(2)}) collective-permute-start(f32[2,16,128]{2,1,0:T(8,128)} %get-tuple-element.157), channel_id=1, source_target_pairs={{0,16},{16,0},{1,17},{17,1},{2,18},{18,2},{3,19},{19,3},{4,20},{20... | collective-permute-start | bytes 49160 | tf_op jit(solution)/shard_map/ppermute | solution.py:978
  88.3 11.7 %all-to-all-start.5 = ((f32[32,4,128]{2,1,0:T(4,128)}), f32[32,4,128]{2,1,0:T(4,128)S(1)}, u32[]{:S(2)}, u32[]{:S(2)}) async-start(f32[32,4,128]{2,1,0:T(4,128)} %bitcast.42), calls=%async_computation.5 | async-start | bytes 131072 | tf_op jit(solution)/shard_map/all_to_all | solution.py:1046
  92.6 4.0 %collective-permute-start.19 = (f32[2,16,128]{2,1,0:T(8,128)}, f32[2,16,128]{2,1,0:T(8,128)S(1)}, u32[]{:S(2)}, u32[]{:S(2)}) collective-permute-start(f32[2,16,128]{2,1,0:T(8,128)} %get-tuple-element.167), channel_id=1, source_target_pairs={{0,16},{16,0},{1,17},{17,1},{2,18},{18,2},{3,19},{19,3},{4,20},{20... | collective-permute-start | bytes 49160 | tf_op jit(solution)/shard_map/ppermute | solution.py:978
  (5 other events, 6.3 us)
